TPU v7x, 256 devices: a whole 4x4x8 slice. The times are simulated.
256 devices in a mesh: ctx: 16 (over x_hi, z), head: 2 (over core), exp: 8 (over y, x_lo).
Axes of the slice: x: 4 (x_hi: 2, x_lo: 2; x = x_hi * 2 + x_lo), y: 4, z: 8, core: 2. Of those that a mesh axis runs over, the one named last changes fastest.
Arguments:
- queries: bfloat16 [4096, 32, 128], P('ctx', ('head', 'exp')), may hold values from -6 to 6
- key_rows: bfloat16 [4096, 2, 128], P(('ctx', 'exp'), 'head'), may hold values from -6 to 6
- value_vector_rows: bfloat16 [4096, 2, 128], P(('ctx', 'exp'), 'head'), may hold values from -6 to 6
- grad_attn: bfloat16 [4096, 32, 128], P('ctx', ('head', 'exp')), may hold values from -6 to 6
- moe_input: bfloat16 [4096, 4096], P('exp', 'ctx'), may hold values from -6 to 6
- moe_grad: bfloat16 [4096, 4096], P('exp', 'ctx'), may hold values from -6 to 6
- expert_ids: int32 [4096, 8], P('exp'), may hold values from 0 to 127, as said below
- router_weight: float32 [4096, 8], P('exp'), may hold values from 0.02 to 0.5
- gate_weight: bfloat16 [8, 4096, 1536], P('exp', 'ctx'), may hold values from -0.09375 to 0.09375
- up_weight: bfloat16 [8, 4096, 1536], P('exp', 'ctx'), may hold values from -0.09375 to 0.09375
- down_weight: bfloat16 [8, 1536, 4096], P('exp', None, 'ctx'), may hold values from -0.15625 to 0.15625
Outputs:
- grad_query: bfloat16 [4096, 32, 128], P('ctx', ('head', 'exp'))
- grad_key: bfloat16 [4096, 2, 128], P(('ctx', 'exp'), 'head')
- grad_value: bfloat16 [4096, 2, 128], P(('ctx', 'exp'), 'head')
- grad_input: bfloat16 [4096, 4096], P('exp', ('ctx', 'head'))
- grad_gate: bfloat16 [8, 4096, 1536], P('exp', 'ctx', 'head')
- grad_up: bfloat16 [8, 4096, 1536], P('exp', 'ctx', 'head')
- grad_down: bfloat16 [8, 1536, 4096], P('exp', 'head', 'ctx')
Inputs may be any that keep to these rules, and one draw needn't show every extreme that they name: `expert_ids`: each row names 8 different experts. In each aligned block of 512 rows every expert below 8 is named by at most 48 rows, and some expert below 8 is named by exactly 48 rows in every block.
All inputs are finite; a program needn't handle non-finite values.
Results may differ from a plain program's by a relative error of at most 0.0083.
Values may be sent and summed in bfloat16 or wider, within the bound.
No kernel may reach another device: no remote copies, remote signals or barrier semaphores. Data moves between devices by JAX's collectives and lax.ppermute only.
A program may use at most 128 MiB of HBM per device.

v0:
```python
import jax
import jax.numpy as jnp
from jax import lax
from jax.sharding import PartitionSpec as P

CAP = 48


def activate(gate_val, up_val, back_val):
    sigmoid_gate = jax.nn.sigmoid(gate_val)
    hidden = (gate_val * sigmoid_gate * up_val).astype(jnp.bfloat16)
    d_up = (back_val * gate_val * sigmoid_gate).astype(jnp.bfloat16)
    d_gate = (back_val * up_val * sigmoid_gate * (1.0 + gate_val * (1.0 - sigmoid_gate))).astype(
        jnp.bfloat16
    )
    return (hidden, d_gate, d_up)


def shards(
    queries,
    key_rows,
    value_vector_rows,
    grad_attn,
    moe_input,
    moe_grad,
    expert_ids,
    router_weight,
    gate_weight,
    up_weight,
    down_weight,
):
    tok_rows = queries.shape[0]
    head_dim = queries.shape[2]
    inv_root = head_dim ** (-0.5)
    all_keys, all_values = (
        lax.all_gather(key_rows, ("ctx", "exp"), axis=0, tiled=True),
        lax.all_gather(value_vector_rows, ("ctx", "exp"), axis=0, tiled=True),
    )
    key_flat = all_keys[:, 0, :]
    value_flat = all_values[:, 0, :]
    seq_len = key_flat.shape[0]
    row_offset = lax.axis_index("ctx") * tok_rows
    query_pos = row_offset + jnp.arange(tok_rows)
    key_pos = jnp.arange(seq_len)
    allowed = key_pos[None, :] <= query_pos[:, None]
    scores = (
        jnp.einsum("phd,td->hpt", queries, key_flat, preferred_element_type=jnp.float32) * inv_root
    )
    scores = jnp.where(allowed[None], scores, -jnp.inf)
    probs_full = jax.nn.softmax(scores, axis=-1)
    probs_low = probs_full.astype(jnp.bfloat16)
    attn_out = jnp.einsum("hpt,td->phd", probs_low, value_flat, preferred_element_type=jnp.float32)
    row_delta = jnp.sum(grad_attn.astype(jnp.float32) * attn_out, axis=-1)
    grad_prob = jnp.einsum("phd,td->hpt", grad_attn, value_flat, preferred_element_type=jnp.float32)
    dscore = (probs_full * (grad_prob - jnp.transpose(row_delta)[:, :, None])).astype(jnp.bfloat16)
    grad_query = (
        jnp.einsum("hpt,td->phd", dscore, key_flat, preferred_element_type=jnp.float32) * inv_root
    ).astype(jnp.bfloat16)
    key_grad = jnp.einsum("hpt,phd->td", dscore, queries, preferred_element_type=jnp.float32)
    value_grad = jnp.einsum("hpt,phd->td", probs_low, grad_attn, preferred_element_type=jnp.float32)
    summed = lax.psum_scatter(
        jnp.concatenate([key_grad, value_grad], axis=1),
        ("ctx", "exp"),
        scatter_dimension=0,
        tiled=True,
    )
    grad_key = (summed[:, :head_dim] * inv_root).astype(jnp.bfloat16)[:, None, :]
    grad_value = summed[:, head_dim:].astype(jnp.bfloat16)[:, None, :]
    experts_here = lax.axis_size("exp")
    local_dim = moe_input.shape[1]
    half_slots = CAP // lax.axis_size("head")
    slot_start = lax.axis_index("head") * half_slots
    labels = jnp.arange(experts_here)
    matches = expert_ids[:, :, None] == labels[None, None, :]
    member = jnp.sum(matches.astype(jnp.int32), axis=1)
    weight_row = jnp.sum(jnp.where(matches, router_weight[:, :, None], 0.0), axis=1)
    slot_rank = jnp.cumsum(member, axis=0) - member
    slot_targets = slot_start + jnp.arange(half_slots)
    placed = (member[:, :, None] == 1) & (slot_rank[:, :, None] == slot_targets[None, None, :])
    placed_low = placed.astype(jnp.bfloat16)
    grad_spread = (weight_row[:, :, None] * moe_grad.astype(jnp.float32)[:, None, :]).astype(
        jnp.bfloat16
    )
    send_input = jnp.einsum(
        "bwc,bd->wcd", placed_low, moe_input, preferred_element_type=jnp.float32
    ).astype(jnp.bfloat16)
    send_grad = jnp.einsum(
        "bwc,bwd->wcd", placed_low, grad_spread, preferred_element_type=jnp.float32
    ).astype(jnp.bfloat16)
    got_input, got_grad = (
        lax.all_to_all(send_input, "exp", split_axis=0, concat_axis=0, tiled=True),
        lax.all_to_all(send_grad, "exp", split_axis=0, concat_axis=0, tiled=True),
    )
    input_rows = got_input.reshape(-1, local_dim)
    grad_rows = got_grad.reshape(-1, local_dim)
    gate_mat = gate_weight[0]
    up_mat = up_weight[0]
    down_mat = down_weight[0]
    gate_part = jnp.dot(input_rows, gate_mat, preferred_element_type=jnp.float32)
    up_part = jnp.dot(input_rows, up_mat, preferred_element_type=jnp.float32)
    back_part = jnp.einsum("rd,fd->rf", grad_rows, down_mat, preferred_element_type=jnp.float32)
    gate_sum, up_sum, back_sum = lax.psum((gate_part, up_part, back_part), "ctx")
    hidden, d_gate, d_up = activate(gate_sum, up_sum, back_sum)
    gate_terms = jnp.einsum("rd,rf->df", input_rows, d_gate, preferred_element_type=jnp.float32)
    up_terms = jnp.einsum("rd,rf->df", input_rows, d_up, preferred_element_type=jnp.float32)
    down_terms = jnp.einsum("rf,rd->fd", hidden, grad_rows, preferred_element_type=jnp.float32)
    contrib = jnp.einsum("rf,df->rd", d_gate, gate_mat, preferred_element_type=jnp.float32)
    contrib = contrib + jnp.einsum("rf,df->rd", d_up, up_mat, preferred_element_type=jnp.float32)
    contrib = contrib.astype(jnp.bfloat16).reshape(experts_here, half_slots, local_dim)
    back_rows = lax.all_to_all(contrib, "exp", split_axis=0, concat_axis=0, tiled=True)
    input_terms = jnp.einsum(
        "bwc,wcd->bd", placed_low, back_rows, preferred_element_type=jnp.float32
    )
    gate_sum_w, up_sum_w, down_sum_w, input_sum = (
        lax.psum_scatter(gate_terms, "head", scatter_dimension=1, tiled=True),
        lax.psum_scatter(up_terms, "head", scatter_dimension=1, tiled=True),
        lax.psum_scatter(down_terms, "head", scatter_dimension=0, tiled=True),
        lax.psum_scatter(input_terms, "head", scatter_dimension=1, tiled=True),
    )
    grad_gate = gate_sum_w.astype(jnp.bfloat16)[None]
    grad_up = up_sum_w.astype(jnp.bfloat16)[None]
    grad_down = down_sum_w.astype(jnp.bfloat16)[None]
    grad_input = input_sum.astype(jnp.bfloat16)
    return (grad_query, grad_key, grad_value, grad_input, grad_gate, grad_up, grad_down)


def solution(mesh):
    placed = (
        P("ctx", ("head", "exp"), None),
        P(("ctx", "exp"), "head", None),
        P(("ctx", "exp"), "head", None),
        P("ctx", ("head", "exp"), None),
        P("exp", "ctx"),
        P("exp", "ctx"),
        P("exp", None),
        P("exp", None),
        P("exp", "ctx", None),
        P("exp", "ctx", None),
        P("exp", None, "ctx"),
    )
    return jax.shard_map(
        shards,
        mesh=mesh,
        in_specs=placed,
        out_specs=(
            P("ctx", ("head", "exp"), None),
            P(("ctx", "exp"), "head", None),
            P(("ctx", "exp"), "head", None),
            P("exp", ("ctx", "head")),
            P("exp", "ctx", "head"),
            P("exp", "ctx", "head"),
            P("exp", "head", "ctx"),
        ),
        check_vma=False,
    )
```

profile of v0, /device:TPU:2, one launch (start us, length us, event | category | flops | bytes accessed | tf_op | source)
XLA Modules:
  0.0 2054.7 jit_solution(6566922613953287510)
XLA Ops:
  8.0 0.8 convert_reduce_fusion
  8.9 1.1 reduce-window.6
  10.0 0.2 slice_reduce_fusion
  10.3 0.1 bitcast_subtract_fusion.1
  10.3 1.9 convolution_convert_fusion
  12.2 5.9 all-to-all-start.1
  18.1 0.8 select_reduce_fusion
  18.9 1.0 convert_element_type.66
  19.9 1.4 fusion.16
  21.3 2.1 all-to-all-done.1
  23.4 4.6 all-to-all-start
  27.9 1.3 fusion.30
  29.3 1.4 fusion.33
  30.6 2.6 all-to-all-done
  33.2 1.5 fusion.35
  34.7 0.0 all-reduce.3.cloned.1.call-update
  34.7 0.0 all-gather.3.cloned.1.call-start
  34.8 0.5 all-gather.3.cloned.1.call-update
  35.3 0.0 all-gather.5.cloned.1.call-start
  35.3 0.5 all-gather.5.cloned.1.call-update
  35.9 0.0 reduce-scatter.8.cloned.1.call-start
  35.9 169.6 %all-reduce.3.cloned.1.call-done = (f32[192,1536]{1,0:T(8,128)}, f32[192,1536]{1,0:T(8,128)}, f32[192,1536]{1,0:T(8,128)}) async-done(((f32[192,1536]{1,0:T(8,128)}, f32[192,1536]{1,0:T(8,128)}, f32[192,1536]{1,0:T(8,128)}), (f32[192,1536]{1,0:T(8,128)}, f32[192,1536]{1,0:T(8,128)}, f32[192,1536]{1,0:T(8,128)})) %all-reduce.3.cloned.1.call-update) | async-done | bytes 3538960 | tf_op jit(solution)/shard_map/psum | solution.py:102
  205.5 2.6 multiply_convert_fusion.3
  208.1 0.4 fusion.28
  208.5 0.4 fusion.15
  208.9 12.6 all_to_all.15
  221.6 1.2 convolution_bitcast_fusion.2
  222.8 0.0 reduce-scatter.14.cloned.1.call-start
  222.9 3.4 fusion.37
  226.3 0.0 reduce-scatter.14.cloned.1.call-update
  226.3 0.0 reduce-scatter.12.cloned.1.call-start
  226.4 1.5 fusion.56
  227.9 0.0 reduce-scatter.10.cloned.1.call-start
  228.0 0.1 copy.65
  228.1 0.1 copy.70
  228.3 0.7 iota_compare_fusion
  229.0 459.3 %all-gather.3.cloned.1.call-done = bf16[4096,1,128]{2,0,1:T(8,128)(2,1)} async-done(((bf16[32,1,128]{2,0,1:T(8,128)(2,1)}), bf16[4096,1,128]{2,0,1:T(8,128)(2,1)}) %all-gather.3.cloned.1.call-update) | async-done | bytes 1048592 | tf_op jit(solution)/shard_map/all_gather | solution.py:36
  688.2 7.0 fusion.52
  695.2 1.5 fusion.55
  696.8 0.2 reduce-scatter.16.cloned.1.call-start
  697.0 4.1 fusion.7
  701.1 2.0 copy-done.1
  703.0 1.5 convolution_bitcast_fusion
  704.5 628.3 %all-gather.5.cloned.1.call-done = bf16[4096,1,128]{2,0,1:T(8,128)(2,1)} async-done(((bf16[32,1,128]{2,0,1:T(8,128)(2,1)}), bf16[4096,1,128]{2,0,1:T(8,128)(2,1)}) %all-gather.5.cloned.1.call-update) | async-done | bytes 1048592 | tf_op jit(solution)/shard_map/all_gather | solution.py:37
  1332.8 3.4 fusion.17
  1336.2 4.6 fusion.2
  1340.8 1.5 convolution_bitcast_fusion.1
  1342.3 0.5 copy-done.2
  1342.8 2.3 pad_maximum_fusion
  1345.1 5.6 copy.82
  1350.7 1.2 copy-done.7
  1351.9 3.5 fusion.18
  1355.4 0.8 copy.73
  1356.2 1.6 convert_element_type.73
  1357.8 1.9 convert_bitcast_fusion
  1359.8 1.9 convert_bitcast_fusion.1
  1361.7 1.9 convert_bitcast_fusion.2
  1363.6 680.6 %reduce-scatter.16.cloned.1.call-done = f32[32,256]{1,0:T(8,128)} async-done(((f32[4096,256]{1,0:T(8,128)}), f32[32,256]{1,0:T(8,128)}) %reduce-scatter.16.cloned.1.call-update) | async-done | bytes 32784
  2044.2 0.7 slice.18
  2044.9 0.1 copy.85
  2045.0 0.7 copy.75
  2045.7 0.7 slice.17
  2046.4 0.1 copy.84
  2046.6 0.7 copy.74
  (30 shorter events, 0.2 us)
Async XLA Ops:
  8.0 19.9 copy-start
  12.2 11.2 all-to-all-start.1
  19.9 9.4 copy-start.3
  23.4 9.8 all-to-all-start
  27.9 5.3 copy-start.4
  27.9 177.5 %all-reduce.3.cloned.1.call-start = ((), (), s32[]{:S(2)}) async-start(), calls=%async_computation.15 | async-start | bytes 7077888 | tf_op jit(solution)/shard_map/psum | solution.py:102
  34.7 653.5 %all-gather.3.cloned.1.call-start = ((), (), s32[]{:S(2)}) async-start(), calls=%async_computation.8 | async-start | bytes 1056768 | tf_op jit(solution)/shard_map/all_gather | solution.py:36
  35.3 1297.5 %all-gather.5.cloned.1.call-start = ((), (), s32[]{:S(2)}) async-start(), calls=%async_computation.9 | async-start | bytes 1056768 | tf_op jit(solution)/shard_map/all_gather | solution.py:37
  35.9 1320.3 %reduce-scatter.8.cloned.1.call-start = ((), (), s32[]{:S(2)}) async-start(), calls=%async_computation.10 | async-start | bytes 786432 | tf_op jit(solution)/shard_map/reduce_scatter | solution.py:118
  222.8 1135.0 %reduce-scatter.14.cloned.1.call-start = ((), (), s32[]{:S(2)}) async-start(), calls=%async_computation.13 | async-start | bytes 2359296 | tf_op jit(solution)/shard_map/reduce_scatter | solution.py:117
  226.3 1.7 copy-start.5
  226.3 1.8 copy-start.6
  226.3 1133.4 %reduce-scatter.12.cloned.1.call-start = ((), (), s32[]{:S(2)}) async-start(), calls=%async_computation.12 | async-start | bytes 2359296 | tf_op jit(solution)/shard_map/reduce_scatter | solution.py:116
  227.9 1133.7 %reduce-scatter.10.cloned.1.call-start = ((), (), s32[]{:S(2)}) async-start(), calls=%async_computation.11 | async-start | bytes 2359296 | tf_op jit(solution)/shard_map/reduce_scatter | solution.py:115
  696.8 1347.4 %reduce-scatter.16.cloned.1.call-start = ((), (), s32[]{:S(2)}) async-start(), calls=%async_computation.14 | async-start | bytes 4227072
  701.1 2.0 copy-start.1
  1332.8 3.4 copy-start.8
  1340.8 2.0 copy-start.2
  1350.7 1.2 copy-start.7
Sparse Core Ops, SparseCore 0:
  34.8 170.6 all-reduce.2
  222.9 8.2 reduce-scatter.7
  233.9 15.7 reduce-scatter.13
  252.0 15.6 reduce-scatter.11
  696.9 12.0 reduce-scatter.9
  1350.9 693.2 reduce-scatter.15
Sparse Core Ops, SparseCore 1:
  37.0 651.2 all-gather.2
  689.9 642.8 all-gather.4
where the time goes:
time: 2060 us; the launch traced here: 2050 us
  waiting for transfers between devices  1940 us (94%)
  matrix products  37.3 us (2%)
  other arithmetic  20.9 us (1%)
    unnamed x9, waiting for transfers between devices  682 us
    all_gather x1, waiting for transfers between devices, shards(): lax.all_gather(value_vector_rows, ('ctx', 'exp'), axis=0, tiled=True)  628 us
    all_gather x1, waiting for transfers between devices, shards(): lax.all_gather(key_rows, ('ctx', 'exp'), axis=0, tiled=True)  459 us
    psum x1, waiting for transfers between devices, shards(): lax.psum((gate_part, up_part, back_part), 'ctx')  170 us
  transfers between devices with their start and end apart: 10, of which 6 were waited for; matrix products, arithmetic and copies ran while one was open for 3% of the time, Pallas kernels for 0%

commit v1 on v0

v1 whole, which is shorter than its diff:
```python
import jax
import jax.numpy as jnp
from jax import lax
from jax.sharding import PartitionSpec as P

CAP = 48
BF = jnp.bfloat16
F32 = jnp.float32


def activate(gate_val, up_val, back_val):
    sigmoid_gate = jax.nn.sigmoid(gate_val)
    hidden = (gate_val * sigmoid_gate * up_val).astype(BF)
    d_up = (back_val * gate_val * sigmoid_gate).astype(BF)
    d_gate = (back_val * up_val * sigmoid_gate * (1.0 + gate_val * (1.0 - sigmoid_gate))).astype(BF)
    return (hidden, d_gate, d_up)


def spread(block, axis):
    n = lax.axis_size(axis)
    copies = jnp.broadcast_to(block[None], (n,) + block.shape)
    return lax.all_to_all(copies, axis, 0, 0, tiled=True)


def gather_sum(parts, axis):
    return jnp.sum(lax.all_to_all(parts, axis, 0, 0, tiled=True).astype(F32), axis=0)


def attention(queries, key_rows, value_vector_rows, grad_attn):
    tok_rows = queries.shape[0]
    head_dim = queries.shape[2]
    inv_root = head_dim ** (-0.5)
    ctx_size, exp_size = lax.axis_size("ctx"), lax.axis_size("exp")
    own = key_rows.shape[0]
    pair = jnp.concatenate([key_rows[:, 0, :], value_vector_rows[:, 0, :]], axis=1)
    everyone = spread(spread(pair, "ctx"), "exp")
    flat = everyone.reshape(-1, 2 * head_dim)
    key_flat, value_flat = flat[:, :head_dim], flat[:, head_dim:]
    place = jnp.arange(flat.shape[0])
    key_pos = (
        (place // own) % ctx_size * (own * exp_size) + place // (own * ctx_size) * own + place % own
    )
    query_pos = lax.axis_index("ctx") * tok_rows + jnp.arange(tok_rows)
    allowed = key_pos[None, :] <= query_pos[:, None]
    scores = (
        jnp.einsum("phd,td->hpt", queries, key_flat, preferred_element_type=F32) * inv_root
    )
    scores = jnp.where(allowed[None], scores, -jnp.inf)
    probs_full = jax.nn.softmax(scores, axis=-1)
    probs_low = probs_full.astype(BF)
    attn_out = jnp.einsum("hpt,td->phd", probs_low, value_flat, preferred_element_type=F32)
    row_delta = jnp.sum(grad_attn.astype(F32) * attn_out, axis=-1)
    grad_prob = jnp.einsum("phd,td->hpt", grad_attn, value_flat, preferred_element_type=F32)
    dscore = (probs_full * (grad_prob - jnp.transpose(row_delta)[:, :, None])).astype(BF)
    grad_query = (
        jnp.einsum("hpt,td->phd", dscore, key_flat, preferred_element_type=F32) * inv_root
    ).astype(BF)
    key_grad = jnp.einsum("hpt,phd->td", dscore, queries, preferred_element_type=F32)
    value_grad = jnp.einsum("hpt,phd->td", probs_low, grad_attn, preferred_element_type=F32)
    both = jnp.concatenate([key_grad.astype(BF), value_grad.astype(BF)], axis=1)
    both = gather_sum(both.reshape(exp_size, ctx_size * own, 2 * head_dim), "exp").astype(BF)
    summed = gather_sum(both.reshape(ctx_size, own, 2 * head_dim), "ctx")
    grad_key = (summed[:, :head_dim] * inv_root).astype(BF)[:, None, :]
    grad_value = summed[:, head_dim:].astype(BF)[:, None, :]
    return grad_query, grad_key, grad_value


def experts(moe_input, moe_grad, expert_ids, router_weight, gate_weight, up_weight, down_weight):
    width = moe_input.shape[1]
    exp_size, ctx_size, head_size = (lax.axis_size(a) for a in ("exp", "ctx", "head"))
    half = lax.axis_index("head")
    units = gate_weight.shape[2] // head_size
    columns = width // head_size
    matches = expert_ids[:, :, None] == jnp.arange(exp_size)[None, None, :]
    member = jnp.sum(matches.astype(jnp.int32), axis=1)
    weight_row = jnp.sum(jnp.where(matches, router_weight[:, :, None], 0.0), axis=1)
    slot_rank = jnp.cumsum(member, axis=0) - member
    placed = (member[:, :, None] == 1) & (
        slot_rank[:, :, None] == jnp.arange(CAP)[None, None, :]
    )
    slot_weight = jnp.sum(jnp.where(placed, weight_row[:, :, None], 0.0), axis=0)
    placed_low = placed.astype(BF).reshape(-1, exp_size * CAP)
    rows = jnp.concatenate([moe_input, moe_grad], axis=1)
    picked = jnp.einsum("bs,bd->sd", placed_low, rows, preferred_element_type=F32)
    scaled = picked[:, width:] * slot_weight.reshape(-1, 1)
    sent = jnp.concatenate([picked[:, :width].astype(BF), scaled.astype(BF)], axis=1)
    got = lax.all_to_all(sent.reshape(exp_size, CAP, 2 * width), "exp", 0, 0, tiled=True)
    got = got.reshape(exp_size * CAP, 2 * width)
    input_rows, grad_rows = got[:, :width], got[:, width:]
    gate_mat = lax.dynamic_slice_in_dim(gate_weight[0], half * units, units, 1)
    up_mat = lax.dynamic_slice_in_dim(up_weight[0], half * units, units, 1)
    down_mat = lax.dynamic_slice_in_dim(down_weight[0], half * units, units, 0)
    gate_part = jnp.dot(input_rows, gate_mat, preferred_element_type=F32).astype(BF)
    up_part = jnp.dot(input_rows, up_mat, preferred_element_type=F32).astype(BF)
    back_part = jnp.einsum("rd,fd->rf", grad_rows, down_mat, preferred_element_type=F32).astype(BF)
    parts = jnp.concatenate([gate_part, up_part, back_part], axis=1)
    total = gather_sum(parts.reshape(ctx_size, -1, 3 * units), "ctx")
    hidden, d_gate, d_up = activate(
        total[:, :units], total[:, units : 2 * units], total[:, 2 * units :]
    )
    full = spread(jnp.concatenate([hidden, d_gate, d_up], axis=1), "ctx").reshape(-1, 3 * units)
    hidden, d_gate, d_up = full[:, :units], full[:, units : 2 * units], full[:, 2 * units :]
    contrib = jnp.einsum("rf,df->rd", d_gate, gate_mat, preferred_element_type=F32)
    contrib = contrib + jnp.einsum("rf,df->rd", d_up, up_mat, preferred_element_type=F32)
    mine = lax.dynamic_slice_in_dim(contrib, half * columns, columns, 1)
    other = lax.dynamic_slice_in_dim(contrib, (1 - half) * columns, columns, 1).astype(BF)
    mine = (mine + lax.ppermute(other, "head", [(0, 1), (1, 0)]).astype(F32)).astype(BF)
    back_rows = lax.all_to_all(mine.reshape(exp_size, CAP, columns), "exp", 0, 0, tiled=True)
    grad_input = jnp.dot(
        placed_low, back_rows.reshape(-1, columns), preferred_element_type=F32
    ).astype(BF)
    grad_gate = jnp.einsum("rd,rf->df", input_rows, d_gate, preferred_element_type=F32).astype(BF)
    grad_up = jnp.einsum("rd,rf->df", input_rows, d_up, preferred_element_type=F32).astype(BF)
    grad_down = jnp.einsum("rf,rd->fd", hidden, grad_rows, preferred_element_type=F32).astype(BF)
    return grad_input, grad_gate[None], grad_up[None], grad_down[None]


def shards(
    queries,
    key_rows,
    value_vector_rows,
    grad_attn,
    moe_input,
    moe_grad,
    expert_ids,
    router_weight,
    gate_weight,
    up_weight,
    down_weight,
):
    of_attention = attention(queries, key_rows, value_vector_rows, grad_attn)
    of_experts = experts(
        moe_input, moe_grad, expert_ids, router_weight, gate_weight, up_weight, down_weight
    )
    return of_attention + of_experts


def solution(mesh):
    placed = (
        P("ctx", ("head", "exp"), None),
        P(("ctx", "exp"), "head", None),
        P(("ctx", "exp"), "head", None),
        P("ctx", ("head", "exp"), None),
        P("exp", "ctx"),
        P("exp", "ctx"),
        P("exp", None),
        P("exp", None),
        P("exp", "ctx", None),
        P("exp", "ctx", None),
        P("exp", None, "ctx"),
    )
    return jax.shard_map(
        shards,
        mesh=mesh,
        in_specs=placed,
        out_specs=(
            P("ctx", ("head", "exp"), None),
            P(("ctx", "exp"), "head", None),
            P(("ctx", "exp"), "head", None),
            P("exp", ("ctx", "head")),
            P("exp", "ctx", "head"),
            P("exp", "ctx", "head"),
            P("exp", "head", "ctx"),
        ),
        check_vma=False,
    )
```

time: 2060 us -> 240 us (0.12)
  waiting for transfers between devices: 1940 us -> 125 us
  starting transfers between devices: 11 us -> 50.9 us
    all_gather x2 -> x0, waiting for transfers between devices: 1090 us -> none  [the longest x1 628 us: shards(): lax.all_gather(value_vector_rows, ('ctx', 'exp'), axis=0, tiled=True)]
    unnamed x9 -> x0, waiting for transfers between devices: 682 us -> none
    psum x1 -> x0, waiting for transfers between devices: 170 us -> none  [shards(): lax.psum((gate_part, up_part, back_part), 'ctx')]
    all_to_all x2 -> x8, waiting for transfers between devices: 4.68 us -> 125 us  [the longest x3 60.7 us: spread(): return lax.all_to_all(copies, axis, 0, 0, tiled=True)]
    all_to_all x2 -> x8, starting transfers between devices: 10.5 us -> 50.8 us  [the longest x3 20.2 us: spread(): return lax.all_to_all(copies, axis, 0, 0, tiled=True)]
  transfers between devices with their start and end apart: 10 -> 9, of which waited for: 6 -> 8; matrix products, arithmetic and copies ran while one was open for 3% -> 17% of each run, Pallas kernels for 0% -> 0%
where the time goes in v1:
time: 240 us; the launch traced here: 238 us
  waiting for transfers between devices  125 us (52%)
  starting transfers between devices  50.9 us (21%)
  matrix products  29.9 us (12%)
  other arithmetic  21.2 us (9%)
  local copies, waits for them, and re-layouts  9.6 us (4%)
    all_to_all x3, waiting for transfers between devices, spread(): return lax.all_to_all(copies, axis, 0, 0, tiled=True)  60.7 us
    all_to_all x3, waiting for transfers between devices, gather_sum(): lax.all_to_all(parts, axis, 0, 0, tiled=True).astype(F32)  53.9 us
    all_to_all x3, starting transfers between devices, spread(): return lax.all_to_all(copies, axis, 0, 0, tiled=True)  20.2 us
    all_to_all x3, starting transfers between devices, gather_sum(): lax.all_to_all(parts, axis, 0, 0, tiled=True).astype(F32)  18.3 us
    all_to_all x1, waiting for transfers between devices, experts(): lax.all_to_all(sent.reshape(exp_size, CAP, 2 * width), 'exp', 0, 0, tiled...  7.49 us
    sub x1, matrix products, attention(): probs_full = jax.nn.softmax(scores, axis=-1)  6.97 us
    all_to_all x1, starting transfers between devices, experts(): lax.all_to_all(mine.reshape(exp_size, CAP, columns), 'exp', 0, 0, tiled=T...  6.47 us
    all_to_all x1, starting transfers between devices, experts(): lax.all_to_all(sent.reshape(exp_size, CAP, 2 * width), 'exp', 0, 0, tiled...  5.93 us
  transfers between devices with their start and end apart: 9, of which 8 were waited for; matrix products, arithmetic and copies ran while one was open for 17% of the time, Pallas kernels for 0%

profile of v1, /device:TPU:2, one launch (start us, length us, event | category | flops | bytes accessed | tf_op | source)
XLA Modules:
  0.0 237.9 jit_solution(9242471460687546822)
XLA Ops:
  0.8 0.8 convert_reduce_fusion.2
  1.6 1.1 reduce-window.6
  2.8 0.2 slice_reduce_fusion
  3.1 0.8 select_reduce_fusion.1
  3.9 0.3 select_reduce_fusion
  4.2 0.2 fusion.22
  4.4 1.4 fusion.25
  5.9 0.1 fusion.34
  6.0 0.8 pad_maximum_fusion.2
  6.8 5.9 %all-to-all-start.4 = ((bf16[8,48,512]{2,1,0:T(8,128)(2,1)}), bf16[8,48,512]{2,1,0:T(8,128)(2,1)S(1)}, u32[]{:S(2)}, u32[]{:S(2)}) async-start(bf16[8,48,512]{2,1,0:T(8,128)(2,1)} %bitcast.23), calls=%async_computation.4 | async-start | bytes 786432 | tf_op jit(solution)/shard_map/all_to_all | solution.py:87
  12.7 7.5 %all-to-all-done.4 = bf16[8,48,512]{2,1,0:T(8,128)(2,1)S(1)} async-done(((bf16[8,48,512]{2,1,0:T(8,128)(2,1)}), bf16[8,48,512]{2,1,0:T(8,128)(2,1)S(1)}, u32[]{:S(2)}, u32[]{:S(2)}) %all-to-all-start.4) | async-done | bytes 393248 | tf_op jit(solution)/shard_map/all_to_all | solution.py:87
  20.2 0.7 broadcast_in_dim.52
  21.0 10.1 %all-to-all-start = ((bf16[16,32,256]{2,1,0:T(8,128)(2,1)}), bf16[16,32,256]{2,1,0:T(8,128)(2,1)S(1)}, u32[]{:S(2)}, u32[]{:S(2)}) async-start(bf16[16,32,256]{2,1,0:T(8,128)(2,1)} %broadcast_in_dim.52), calls=%async_computation | async-start | bytes 524288 | tf_op jit(solution)/shard_map/all_to_all | solution.py:22
  31.1 0.1 copy.81
  31.3 0.1 copy.87
  31.4 0.6 iota_add_fusion
  31.9 0.6 fusion.62
  32.6 9.0 %all-to-all-done = bf16[16,32,256]{2,1,0:T(8,128)(2,1)S(1)} async-done(((bf16[16,32,256]{2,1,0:T(8,128)(2,1)}), bf16[16,32,256]{2,1,0:T(8,128)(2,1)S(1)}, u32[]{:S(2)}, u32[]{:S(2)}) %all-to-all-start) | async-done | bytes 262176 | tf_op jit(solution)/shard_map/all_to_all | solution.py:22
  41.6 1.6 broadcast_in_dim.53
  43.2 5.4 %all-to-all-start.1 = ((bf16[8,16,32,256]{3,2,1,0:T(8,128)(2,1)}), bf16[8,16,32,256]{3,2,1,0:T(8,128)(2,1)S(1)}, u32[]{:S(2)}, u32[]{:S(2)}) async-start(bf16[8,16,32,256]{3,2,1,0:T(8,128)(2,1)} %broadcast_in_dim.53), calls=%async_computation.1 | async-start | bytes 4194304 | tf_op jit(solution)/shard_map/all_to_all | solution.py:22
  48.6 3.3 %broadcast_compare_fusion = pred[256,4096]{0,1:T(8,128)(4,1)} fusion(s32[256]{0:T(256)} %iota_add_fusion, s32[4096]{0:T(1024)} %fusion.62), kind=kLoop, calls=%fused_computation.19 | loop fusion | flops 1048576 | bytes 1065984 | tf_op jit(solution)/shard_map/le | solution.py:44
  51.9 1.3 convolution_convert_fusion.1
  53.2 1.4 convolution_convert_fusion
  54.6 0.3 convolution_convert_fusion.2
  54.9 1.3 pad_maximum_fusion.1
  56.2 15.6 %all-to-all-done.1 = bf16[8,16,32,256]{3,2,1,0:T(8,128)(2,1)S(1)} async-done(((bf16[8,16,32,256]{3,2,1,0:T(8,128)(2,1)}), bf16[8,16,32,256]{3,2,1,0:T(8,128)(2,1)S(1)}, u32[]{:S(2)}, u32[]{:S(2)}) %all-to-all-start.1) | async-done | bytes 2097184 | tf_op jit(solution)/shard_map/all_to_all | solution.py:22
  71.9 5.2 %all-to-all-start.5 = ((bf16[16,24,2304]{2,1,0:T(8,128)(2,1)}), bf16[16,24,2304]{2,1,0:T(8,128)(2,1)}, u32[]{:S(2)}, u32[]{:S(2)}) async-start(bf16[16,24,2304]{2,1,0:T(8,128)(2,1)} %bitcast.117), calls=%async_computation.5 | async-start | bytes 3538944 | tf_op jit(solution)/shard_map/all_to_all | solution.py:26
  77.1 7.0 %fusion.78 = (f32[2,256]{1,0:T(2,128)}, f32[2,256,4096]{1,2,0:T(8,128)}) fusion(pred[256,4096]{0,1:T(8,128)(4,1)} %broadcast_compare_fusion, bf16[256,2,128]{0,2,1:T(8,128)(2,1)S(1)} %copy.87, bf16[4096,256]{1,0:T(8,128)(2,1)S(1)} %bitcast.111), kind=kOutput, calls=%fused_computation.133 | convolution fusion | flops 545263616 | bytes 10618880 | tf_op jit(solution)/shard_map/sub | solution.py:49
  84.0 4.3 %fusion.9 = bf16[2,256,4096]{1,2,0:T(8,128)(2,1)S(1)} fusion(f32[2,256,4096]{1,2,0:T(8,128)} %get-tuple-element.46, f32[2,256]{1,0:T(2,128)} %get-tuple-element.45), kind=kLoop, calls=%fused_computation.16 | loop fusion | flops 4194304 | bytes 12584960 | tf_op jit(solution)/shard_map/convert_element_type | solution.py:50
  88.3 1.5 fusion.5
  89.8 0.8 fusion.18
  90.7 1.4 fusion.2
  92.1 1.5 fusion.4
  93.6 0.4 copy-done.1
  94.0 0.2 pad_maximum_fusion
  94.2 1.5 copy.105
  95.8 23.2 %all-to-all-done.5 = bf16[16,24,2304]{2,1,0:T(8,128)(2,1)} async-done(((bf16[16,24,2304]{2,1,0:T(8,128)(2,1)}), bf16[16,24,2304]{2,1,0:T(8,128)(2,1)}, u32[]{:S(2)}, u32[]{:S(2)}) %all-to-all-start.5) | async-done | bytes 1769504 | tf_op jit(solution)/shard_map/all_to_all | solution.py:26
  118.9 6.2 %all-to-all-start.2 = ((bf16[8,512,256]{1,2,0:T(8,128)(2,1)}), bf16[8,512,256]{1,2,0:T(8,128)(2,1)S(1)}, u32[]{:S(2)}, u32[]{:S(2)}) async-start(bf16[8,512,256]{1,2,0:T(8,128)(2,1)} %bitcast.115), calls=%async_computation.2 | async-start | bytes 4194304 | tf_op jit(solution)/shard_map/all_to_all | solution.py:26
  125.1 2.4 %convert_reduce_fusion = f32[24,2304]{1,0:T(8,128)} fusion(bf16[16,24,2304]{2,1,0:T(8,128)(2,1)} %all-to-all-done.5), kind=kLoop, calls=%fused_computation.15 | loop fusion | flops 1714176 | bytes 1990656 | tf_op jit(solution)/shard_map/reduce_sum | solution.py:26
  127.5 21.6 %all-to-all-done.2 = bf16[8,512,256]{1,2,0:T(8,128)(2,1)S(1)} async-done(((bf16[8,512,256]{1,2,0:T(8,128)(2,1)}), bf16[8,512,256]{1,2,0:T(8,128)(2,1)S(1)}, u32[]{:S(2)}, u32[]{:S(2)}) %all-to-all-start.2) | async-done | bytes 2097184 | tf_op jit(solution)/shard_map/all_to_all | solution.py:26
  149.1 0.4 reduce_sum.77
  149.5 0.8 copy.92
  150.3 6.9 %all-to-all-start.3 = ((bf16[16,32,256]{2,1,0:T(8,128)(2,1)}), bf16[16,32,256]{2,1,0:T(8,128)(2,1)S(1)}, u32[]{:S(2)}, u32[]{:S(2)}) async-start(bf16[16,32,256]{2,1,0:T(8,128)(2,1)} %bitcast.124), calls=%async_computation.3 | async-start | bytes 524288 | tf_op jit(solution)/shard_map/all_to_all | solution.py:26
  157.3 1.0 multiply_convert_fusion.2
  158.3 0.7 pad_maximum_fusion.3
  159.0 9.1 %all-to-all-done.3 = bf16[16,32,256]{2,1,0:T(8,128)(2,1)S(1)} async-done(((bf16[16,32,256]{2,1,0:T(8,128)(2,1)}), bf16[16,32,256]{2,1,0:T(8,128)(2,1)S(1)}, u32[]{:S(2)}, u32[]{:S(2)}) %all-to-all-start.3) | async-done | bytes 262176 | tf_op jit(solution)/shard_map/all_to_all | solution.py:26
  168.1 2.3 broadcast_in_dim.92
  170.4 4.6 %all-to-all-start.6 = ((bf16[16,24,2304]{2,1,0:T(8,128)(2,1)}), bf16[16,24,2304]{2,1,0:T(8,128)(2,1)}, u32[]{:S(2)}, u32[]{:S(2)}) async-start(bf16[16,24,2304]{2,1,0:T(8,128)(2,1)} %broadcast_in_dim.92), calls=%async_computation.6 | async-start | bytes 3538944 | tf_op jit(solution)/shard_map/all_to_all | solution.py:22
  175.1 2.9 %fusion.19 = bf16[256,2,128]{0,2,1:T(8,128)(2,1)S(1)} fusion(bf16[2,256,4096]{1,2,0:T(8,128)(2,1)} %copy-done.1, bf16[4096,256]{1,0:T(8,128)(2,1)S(1)} %bitcast.114), kind=kOutput, calls=%fused_computation.39 | convolution fusion | flops 537001984 | bytes 5373952 | tf_op jit(solution)/shard_map/hpt,td->phd/dot_general | solution.py:56
  178.0 0.8 copy.93
  178.8 1.0 convert_reduce_fusion.1
  179.8 0.6 fusion.69
  180.4 0.6 fusion.68
  181.0 36.0 %all-to-all-done.6 = bf16[16,24,2304]{2,1,0:T(8,128)(2,1)} async-done(((bf16[16,24,2304]{2,1,0:T(8,128)(2,1)}), bf16[16,24,2304]{2,1,0:T(8,128)(2,1)}, u32[]{:S(2)}, u32[]{:S(2)}) %all-to-all-start.6) | async-done | bytes 1769504 | tf_op jit(solution)/shard_map/all_to_all | solution.py:22
  217.0 2.2 fusion.14
  219.2 1.4 fusion.32
  220.7 1.4 convolution_add_fusion
  222.1 0.1 collective-permute-start
  222.2 2.2 fusion.12
  224.5 0.7 add_convert_fusion
  225.1 6.5 %all-to-all-start.7 = ((bf16[8,48,128]{2,1,0:T(8,128)(2,1)}), bf16[8,48,128]{2,1,0:T(8,128)(2,1)S(1)}, u32[]{:S(2)}, u32[]{:S(2)}) async-start(bf16[8,48,128]{2,1,0:T(8,128)(2,1)} %bitcast.30), calls=%async_computation.7 | async-start | bytes 196608 | tf_op jit(solution)/shard_map/all_to_all | solution.py:108
  231.6 2.2 fusion.13
  233.8 3.0 %all-to-all-done.7 = bf16[8,48,128]{2,1,0:T(8,128)(2,1)S(1)} async-done(((bf16[8,48,128]{2,1,0:T(8,128)(2,1)}), bf16[8,48,128]{2,1,0:T(8,128)(2,1)S(1)}, u32[]{:S(2)}, u32[]{:S(2)}) %all-to-all-start.7) | async-done | bytes 98336 | tf_op jit(solution)/shard_map/all_to_all | solution.py:108
  236.8 1.1 fusion.16
  (41 shorter events, 0.4 us)
Async XLA Ops:
  0.6 53.9 %copy-start = (bf16[1,256,1536]{2,1,0:T(8,128)(2,1)S(1)}, bf16[1,256,1536]{2,1,0:T(8,128)(2,1)}, u32[]{:S(2)}) copy-start(bf16[1,256,1536]{2,1,0:T(8,128)(2,1)} %param.19) | copy-start | bytes 2359300
  0.6 12.1 %copy-start.10 = (bf16[32,1,128]{2,0,1:T(8,128)(2,1)S(1)}, bf16[32,1,128]{2,0,1:T(8,128)(2,1)}, u32[]{:S(2)}) copy-start(bf16[32,1,128]{2,0,1:T(8,128)(2,1)} %param.13) | copy-start | bytes 24580
  0.7 12.1 %copy-start.11 = (bf16[32,1,128]{2,0,1:T(8,128)(2,1)S(1)}, bf16[32,1,128]{2,0,1:T(8,128)(2,1)}, u32[]{:S(2)}) copy-start(bf16[32,1,128]{2,0,1:T(8,128)(2,1)} %param.12) | copy-start | bytes 24580
  0.7 30.4 %copy-start.6 = (bf16[256,2,128]{2,1,0:T(2,128)(2,1)S(1)}, bf16[256,2,128]{2,1,0:T(2,128)(2,1)}, u32[]{:S(2)}) copy-start(bf16[256,2,128]{2,1,0:T(2,128)(2,1)} %param.14) | copy-start | bytes 393220
  0.7 30.6 %copy-start.7 = (bf16[256,2,128]{2,1,0:T(2,128)(2,1)S(1)}, bf16[256,2,128]{2,1,0:T(2,128)(2,1)}, u32[]{:S(2)}) copy-start(bf16[256,2,128]{2,1,0:T(2,128)(2,1)} %param.11) | copy-start | bytes 393220
  1.6 19.3 %copy-start.8 = (pred[512,8]{0,1:T(8,128)(4,1)}, pred[512,8]{0,1:T(8,128)(4,1)S(1)}, u32[]{:S(2)}) copy-start(pred[512,8]{0,1:T(8,128)(4,1)S(1)} %broadcast_compare_fusion.1) | copy-start | bytes 12292
  6.8 13.4 %all-to-all-start.4 = ((bf16[8,48,512]{2,1,0:T(8,128)(2,1)}), bf16[8,48,512]{2,1,0:T(8,128)(2,1)S(1)}, u32[]{:S(2)}, u32[]{:S(2)}) async-start(bf16[8,48,512]{2,1,0:T(8,128)(2,1)} %bitcast.23), calls=%async_computation.4 | async-start | bytes 786432 | tf_op jit(solution)/shard_map/all_to_all | solution.py:87
  21.0 20.6 %all-to-all-start = ((bf16[16,32,256]{2,1,0:T(8,128)(2,1)}), bf16[16,32,256]{2,1,0:T(8,128)(2,1)S(1)}, u32[]{:S(2)}, u32[]{:S(2)}) async-start(bf16[16,32,256]{2,1,0:T(8,128)(2,1)} %broadcast_in_dim.52), calls=%async_computation | async-start | bytes 524288 | tf_op jit(solution)/shard_map/all_to_all | solution.py:22
  43.2 28.7 %all-to-all-start.1 = ((bf16[8,16,32,256]{3,2,1,0:T(8,128)(2,1)}), bf16[8,16,32,256]{3,2,1,0:T(8,128)(2,1)S(1)}, u32[]{:S(2)}, u32[]{:S(2)}) async-start(bf16[8,16,32,256]{3,2,1,0:T(8,128)(2,1)} %broadcast_in_dim.53), calls=%async_computation.1 | async-start | bytes 4194304 | tf_op jit(solution)/shard_map/all_to_all | solution.py:22
  71.9 18.7 %copy-start.2 = (bf16[8,16,32,256]{3,2,1,0:T(8,128)(2,1)}, bf16[8,16,32,256]{3,2,1,0:T(8,128)(2,1)S(1)}, u32[]{:S(2)}) copy-start(bf16[8,16,32,256]{3,2,1,0:T(8,128)(2,1)S(1)} %all-to-all-done.1) | copy-start | bytes 6291460
  71.9 47.1 %all-to-all-start.5 = ((bf16[16,24,2304]{2,1,0:T(8,128)(2,1)}), bf16[16,24,2304]{2,1,0:T(8,128)(2,1)}, u32[]{:S(2)}, u32[]{:S(2)}) async-start(bf16[16,24,2304]{2,1,0:T(8,128)(2,1)} %bitcast.117), calls=%async_computation.5 | async-start | bytes 3538944 | tf_op jit(solution)/shard_map/all_to_all | solution.py:26
  84.0 6.6 %slice-start = ((s8[8388608]{0:T(1024)(128)(4,1)}), s8[4194304]{0:T(1024)(128)(4,1)S(1)}, s32[]{:S(2)}) async-start(s8[8388608]{0:T(1024)(128)(4,1)} %bitcast.109), calls=%async_computation.8 | async-start | bytes 8388608
  88.3 2.3 slice-start.1
  89.8 0.9 copy-start.12
  92.1 1.9 copy-start.1
  118.9 30.2 %all-to-all-start.2 = ((bf16[8,512,256]{1,2,0:T(8,128)(2,1)}), bf16[8,512,256]{1,2,0:T(8,128)(2,1)S(1)}, u32[]{:S(2)}, u32[]{:S(2)}) async-start(bf16[8,512,256]{1,2,0:T(8,128)(2,1)} %bitcast.115), calls=%async_computation.2 | async-start | bytes 4194304 | tf_op jit(solution)/shard_map/all_to_all | solution.py:26
  149.5 25.6 %copy-start.3 = (bf16[8,16,32,256]{3,2,1,0:T(8,128)(2,1)S(1)}, bf16[8,16,32,256]{3,2,1,0:T(8,128)(2,1)}, u32[]{:S(2)}) copy-start(bf16[8,16,32,256]{3,2,1,0:T(8,128)(2,1)} %copy-done.2) | copy-start | bytes 6291460
  150.3 17.7 %all-to-all-start.3 = ((bf16[16,32,256]{2,1,0:T(8,128)(2,1)}), bf16[16,32,256]{2,1,0:T(8,128)(2,1)S(1)}, u32[]{:S(2)}, u32[]{:S(2)}) async-start(bf16[16,32,256]{2,1,0:T(8,128)(2,1)} %bitcast.124), calls=%async_computation.3 | async-start | bytes 524288 | tf_op jit(solution)/shard_map/all_to_all | solution.py:26
  168.1 7.0 %copy-start.4 = (bf16[16,32,256]{2,1,0:T(8,128)(2,1)}, bf16[16,32,256]{2,1,0:T(8,128)(2,1)S(1)}, u32[]{:S(2)}) copy-start(bf16[16,32,256]{2,1,0:T(8,128)(2,1)S(1)} %all-to-all-done.3) | copy-start | bytes 786436
  170.4 46.6 %all-to-all-start.6 = ((bf16[16,24,2304]{2,1,0:T(8,128)(2,1)}), bf16[16,24,2304]{2,1,0:T(8,128)(2,1)}, u32[]{:S(2)}, u32[]{:S(2)}) async-start(bf16[16,24,2304]{2,1,0:T(8,128)(2,1)} %broadcast_in_dim.92), calls=%async_computation.6 | async-start | bytes 3538944 | tf_op jit(solution)/shard_map/all_to_all | solution.py:22
  178.0 42.7 %copy-start.5 = (bf16[1,256,1536]{2,1,0:T(8,128)(2,1)S(1)}, bf16[1,256,1536]{2,1,0:T(8,128)(2,1)}, u32[]{:S(2)}) copy-start(bf16[1,256,1536]{2,1,0:T(8,128)(2,1)} %param.20) | copy-start | bytes 2359300
  219.2 17.6 %copy-start.9 = (pred[512,8]{0,1:T(8,128)(4,1)S(1)}, pred[512,8]{0,1:T(8,128)(4,1)}, u32[]{:S(2)}) copy-start(pred[512,8]{0,1:T(8,128)(4,1)} %copy-done.8) | copy-start | bytes 12292
  222.1 2.3 collective-permute-start
  225.1 11.7 %all-to-all-start.7 = ((bf16[8,48,128]{2,1,0:T(8,128)(2,1)}), bf16[8,48,128]{2,1,0:T(8,128)(2,1)S(1)}, u32[]{:S(2)}, u32[]{:S(2)}) async-start(bf16[8,48,128]{2,1,0:T(8,128)(2,1)} %bitcast.30), calls=%async_computation.7 | async-start | bytes 196608 | tf_op jit(solution)/shard_map/all_to_all | solution.py:108

commit v2 on v1

--- a/solution.py
+++ b/solution.py
@@ -4,6 +4,7 @@
 from jax.sharding import PartitionSpec as P
 
 CAP = 48
+X_HI = 2
 BF = jnp.bfloat16
 F32 = jnp.float32
 
@@ -26,20 +27,91 @@
     return jnp.sum(lax.all_to_all(parts, axis, 0, 0, tiled=True).astype(F32), axis=0)
 
 
-def attention(queries, key_rows, value_vector_rows, grad_attn):
+def z_shift(step):
+    n = lax.axis_size("ctx") // X_HI
+    return [(h * n + z, h * n + (z + step) % n) for h in range(X_HI) for z in range(n)]
+
+
+def right(block):
+    return lax.ppermute(block, "ctx", z_shift(1))
+
+
+def left(block):
+    return lax.ppermute(block, "ctx", z_shift(-1))
+
+
+def opposite(block):
+    n = lax.axis_size("ctx")
+    return lax.ppermute(block, "ctx", [(c, (c + n // X_HI) % n) for c in range(n)])
+
+
+def after(block, *others):
+    return lax.optimization_barrier((block,) + others)[0]
+
+
+def add_low(a, b):
+    return (a.astype(F32) + b.astype(F32)).astype(BF)
+
+
+def ring_sum(parts, beside):
+    n = len(parts)
+    far = n // 2
+    cut = parts[0].shape[1] // 2
+    onward, back = parts[far][:, :cut], parts[far][:, cut:]
+    for step in range(far):
+        if step in beside:
+            onward, back = after(onward, beside[step]), after(back, beside[step])
+        onward, back = right(onward), left(back)
+        ahead, behind = parts[far - 1 - step], parts[(far + 1 + step) % n]
+        if step == 0:
+            onward = jnp.concatenate([add_low(onward, ahead[:, :cut]), ahead[:, cut:]], axis=1)
+            back = jnp.concatenate([behind[:, :cut], add_low(back, behind[:, cut:])], axis=1)
+        elif step < far - 1:
+            onward, back = add_low(onward, ahead), add_low(back, behind)
+    return onward.astype(F32) + back.astype(F32) + parts[0].astype(F32)
+
+
+def ring_gather(block, beside=()):
+    n = lax.axis_size("ctx") // X_HI
+    far = n // 2
+    cut = block.shape[1] // 2
+    blocks = [block] + [None] * (n - 1)
+    onward = back = block
+    for step in range(1, far):
+        if step in beside:
+            onward, back = after(onward, beside[step]), after(back, beside[step])
+        onward, back = right(onward), left(back)
+        blocks[n - step], blocks[step] = onward, back
+    blocks[far] = jnp.concatenate([right(onward[:, :cut]), left(back[:, cut:])], axis=1)
+    return blocks
+
+
+def turn(blocks, places):
+    twice = jnp.concatenate([blocks, blocks], axis=0)
+    return lax.dynamic_slice_in_dim(twice, places, blocks.shape[0], 0)
+
+
+def ctx_gather(key_rows, value_vector_rows):
+    n = lax.axis_size("ctx") // X_HI
+    side = lax.axis_index("ctx") // n
+    pair = jnp.concatenate([key_rows[:, 0, :], value_vector_rows[:, 0, :]], axis=1)
+    partner = opposite(pair)
+    first, second = jnp.where(side == 0, pair, partner), jnp.where(side == 0, partner, pair)
+    return jnp.concatenate(ring_gather(jnp.concatenate([first, second], axis=0)), axis=0)
+
+
+def attention(queries, flat, grad_attn):
     tok_rows = queries.shape[0]
     head_dim = queries.shape[2]
     inv_root = head_dim ** (-0.5)
     ctx_size, exp_size = lax.axis_size("ctx"), lax.axis_size("exp")
-    own = key_rows.shape[0]
-    pair = jnp.concatenate([key_rows[:, 0, :], value_vector_rows[:, 0, :]], axis=1)
-    everyone = spread(spread(pair, "ctx"), "exp")
-    flat = everyone.reshape(-1, 2 * head_dim)
+    own = flat.shape[0] // (ctx_size * exp_size)
     key_flat, value_flat = flat[:, :head_dim], flat[:, head_dim:]
+    ring = ctx_size // X_HI
+    at = lax.axis_index("ctx") % ring
     place = jnp.arange(flat.shape[0])
-    key_pos = (
-        (place // own) % ctx_size * (own * exp_size) + place // (own * ctx_size) * own + place % own
-    )
+    of_ctx = place // own % X_HI * ring + (place // (own * X_HI) + at) % ring
+    key_pos = (of_ctx * exp_size + place // (own * ctx_size)) * own + place % own
     query_pos = lax.axis_index("ctx") * tok_rows + jnp.arange(tok_rows)
     allowed = key_pos[None, :] <= query_pos[:, None]
     scores = (
@@ -58,19 +130,25 @@
     key_grad = jnp.einsum("hpt,phd->td", dscore, queries, preferred_element_type=F32)
     value_grad = jnp.einsum("hpt,phd->td", probs_low, grad_attn, preferred_element_type=F32)
     both = jnp.concatenate([key_grad.astype(BF), value_grad.astype(BF)], axis=1)
-    both = gather_sum(both.reshape(exp_size, ctx_size * own, 2 * head_dim), "exp").astype(BF)
-    summed = gather_sum(both.reshape(ctx_size, own, 2 * head_dim), "ctx")
-    grad_key = (summed[:, :head_dim] * inv_root).astype(BF)[:, None, :]
+    return both, probs_low, grad_query
+
+
+def to_owners(both):
+    ctx_size = lax.axis_size("ctx")
+    ring, head_dim = ctx_size // X_HI, both.shape[1] // 2
+    own = both.shape[0] // ctx_size
+    at = lax.axis_index("ctx") % ring
+    both = turn(both.reshape(ring, X_HI, own, 2 * head_dim), (ring - at) % ring)
+    both = jnp.swapaxes(both, 0, 1).reshape(ctx_size, own, 2 * head_dim)
+    summed = gather_sum(both, "ctx")
+    grad_key = (summed[:, :head_dim] * head_dim ** (-0.5)).astype(BF)[:, None, :]
     grad_value = summed[:, head_dim:].astype(BF)[:, None, :]
-    return grad_query, grad_key, grad_value
-
-
-def experts(moe_input, moe_grad, expert_ids, router_weight, gate_weight, up_weight, down_weight):
+    return grad_key, grad_value
+
+
+def select(moe_input, moe_grad, expert_ids, router_weight):
     width = moe_input.shape[1]
-    exp_size, ctx_size, head_size = (lax.axis_size(a) for a in ("exp", "ctx", "head"))
-    half = lax.axis_index("head")
-    units = gate_weight.shape[2] // head_size
-    columns = width // head_size
+    exp_size = lax.axis_size("exp")
     matches = expert_ids[:, :, None] == jnp.arange(exp_size)[None, None, :]
     member = jnp.sum(matches.astype(jnp.int32), axis=1)
     weight_row = jnp.sum(jnp.where(matches, router_weight[:, :, None], 0.0), axis=1)
@@ -85,7 +163,16 @@
     scaled = picked[:, width:] * slot_weight.reshape(-1, 1)
     sent = jnp.concatenate([picked[:, :width].astype(BF), scaled.astype(BF)], axis=1)
     got = lax.all_to_all(sent.reshape(exp_size, CAP, 2 * width), "exp", 0, 0, tiled=True)
-    got = got.reshape(exp_size * CAP, 2 * width)
+    return placed_low, got
+
+
+def project(got, gate_weight, up_weight, down_weight):
+    ring = lax.axis_size("ctx") // X_HI
+    at = lax.axis_index("ctx") % ring
+    half = lax.axis_index("head")
+    units = gate_weight.shape[2] // lax.axis_size("head")
+    width = got.shape[2] // 2
+    got = turn(got.reshape(ring, -1, 2 * width), at).reshape(-1, 2 * width)
     input_rows, grad_rows = got[:, :width], got[:, width:]
     gate_mat = lax.dynamic_slice_in_dim(gate_weight[0], half * units, units, 1)
     up_mat = lax.dynamic_slice_in_dim(up_weight[0], half * units, units, 1)
@@ -93,19 +180,34 @@
     gate_part = jnp.dot(input_rows, gate_mat, preferred_element_type=F32).astype(BF)
     up_part = jnp.dot(input_rows, up_mat, preferred_element_type=F32).astype(BF)
     back_part = jnp.einsum("rd,fd->rf", grad_rows, down_mat, preferred_element_type=F32).astype(BF)
-    parts = jnp.concatenate([gate_part, up_part, back_part], axis=1)
-    total = gather_sum(parts.reshape(ctx_size, -1, 3 * units), "ctx")
+    parts = jnp.concatenate([gate_part, up_part, back_part], axis=1).reshape(ring, -1, 3 * units)
+    return input_rows, grad_rows, gate_mat, up_mat, [parts[j] for j in range(ring)]
+
+
+def act_block(total):
+    units = total.shape[1] // 3
+    total = total + opposite(total.astype(BF)).astype(F32)
     hidden, d_gate, d_up = activate(
         total[:, :units], total[:, units : 2 * units], total[:, 2 * units :]
     )
-    full = spread(jnp.concatenate([hidden, d_gate, d_up], axis=1), "ctx").reshape(-1, 3 * units)
+    return jnp.concatenate([hidden, d_gate, d_up], axis=1)
+
+
+def finish(full, input_rows, grad_rows, gate_mat, up_mat, placed_low):
+    exp_size, head_size = lax.axis_size("exp"), lax.axis_size("head")
+    ring = lax.axis_size("ctx") // X_HI
+    at = lax.axis_index("ctx") % ring
+    half = lax.axis_index("head")
+    units = full.shape[1] // 3
+    columns = input_rows.shape[1] // head_size
     hidden, d_gate, d_up = full[:, :units], full[:, units : 2 * units], full[:, 2 * units :]
     contrib = jnp.einsum("rf,df->rd", d_gate, gate_mat, preferred_element_type=F32)
     contrib = contrib + jnp.einsum("rf,df->rd", d_up, up_mat, preferred_element_type=F32)
     mine = lax.dynamic_slice_in_dim(contrib, half * columns, columns, 1)
     other = lax.dynamic_slice_in_dim(contrib, (1 - half) * columns, columns, 1).astype(BF)
     mine = (mine + lax.ppermute(other, "head", [(0, 1), (1, 0)]).astype(F32)).astype(BF)
-    back_rows = lax.all_to_all(mine.reshape(exp_size, CAP, columns), "exp", 0, 0, tiled=True)
+    mine = turn(mine.reshape(ring, -1, columns), (ring - at) % ring).reshape(exp_size, CAP, columns)
+    back_rows = lax.all_to_all(mine, "exp", 0, 0, tiled=True)
     grad_input = jnp.dot(
         placed_low, back_rows.reshape(-1, columns), preferred_element_type=F32
     ).astype(BF)
@@ -128,11 +230,23 @@
     up_weight,
     down_weight,
 ):
-    of_attention = attention(queries, key_rows, value_vector_rows, grad_attn)
-    of_experts = experts(
-        moe_input, moe_grad, expert_ids, router_weight, gate_weight, up_weight, down_weight
-    )
-    return of_attention + of_experts
+    near = ctx_gather(key_rows, value_vector_rows)
+    placed_low, got = select(moe_input, moe_grad, expert_ids, router_weight)
+    got, near = lax.optimization_barrier((got, near))
+    flat = spread(near, "exp").reshape(-1, near.shape[1])
+    input_rows, grad_rows, gate_mat, up_mat, parts = project(
+        got, gate_weight, up_weight, down_weight
+    )
+    both, probs_low, grad_query = attention(queries, flat, grad_attn)
+    exp_size = lax.axis_size("exp")
+    total = ring_sum(parts, {3: flat})
+    block = act_block(total)
+    blocks = ring_gather(block, {2: probs_low, 3: both})
+    both = gather_sum(both.reshape((exp_size, -1) + both.shape[1:]), "exp").astype(BF)
+    full = after(jnp.concatenate(blocks, axis=0), both)
+    of_experts = finish(full, input_rows, grad_rows, gate_mat, up_mat, placed_low)
+    grad_key, grad_value = to_owners(both)
+    return (grad_query, grad_key, grad_value) + of_experts
 
 
 def solution(mesh):

time: 240 us -> 193 us (0.80)
  waiting for transfers between devices: 125 us -> 53.8 us
  starting transfers between devices: 50.9 us -> 74.3 us
  local copies, waits for them, and re-layouts: 9.6 us -> 13 us
    all_to_all x3 -> x1, waiting for transfers between devices: 60.7 us -> 7.49 us  [spread(): return lax.all_to_all(copies, axis, 0, 0, tiled=True)]
    all_to_all x3 -> x2, waiting for transfers between devices: 53.9 us -> 7.38 us  [gather_sum(): lax.all_to_all(parts, axis, 0, 0, tiled=True).astype(F32)]
    ppermute x1 -> x27, starting transfers between devices: 0.09 us -> 44 us  [the longest x12 28.6 us: left(): return lax.ppermute(block, 'ctx', z_shift(-1))]
    ppermute x1 -> x27, waiting for transfers between devices: 0.01 us -> 34.8 us  [the longest x12 18.3 us: right(): return lax.ppermute(block, 'ctx', z_shift(1))]
    all_to_all x3 -> x1, starting transfers between devices: 20.2 us -> 5.68 us  [spread(): return lax.all_to_all(copies, axis, 0, 0, tiled=True)]
    all_to_all x2, waiting for transfers between devices: 10.5 us -> 4.1 us  [the longest x1 4.1 us: finish(): back_rows = lax.all_to_all(mine, 'exp', 0, 0, tiled=True)]
    all_to_all x3 -> x2, starting transfers between devices: 18.3 us -> 12.9 us  [gather_sum(): lax.all_to_all(parts, axis, 0, 0, tiled=True).astype(F32)]
    unnamed x33 -> x37, local copies, waits for them, and re-layouts: 1.53 us -> 6.44 us
  transfers between devices with their start and end apart: 9 -> 32, of which waited for: 8 -> 16; matrix products, arithmetic and copies ran while one was open for 17% -> 19% of each run, Pallas kernels for 0% -> 0%
where the time goes in v2:
time: 193 us; the launch traced here: 191 us
  starting transfers between devices  74.3 us (38%)
  waiting for transfers between devices  53.8 us (28%)
  matrix products  27.6 us (14%)
  other arithmetic  21 us (11%)
  local copies, waits for them, and re-layouts  13 us (7%)
    ppermute x12, starting transfers between devices, left(): return lax.ppermute(block, 'ctx', z_shift(-1))  28.6 us
    ppermute x12, waiting for transfers between devices, right(): return lax.ppermute(block, 'ctx', z_shift(1))  18.3 us
    all_to_all x2, starting transfers between devices, gather_sum(): lax.all_to_all(parts, axis, 0, 0, tiled=True).astype(F32)  12.9 us
    ppermute x12, starting transfers between devices, right(): return lax.ppermute(block, 'ctx', z_shift(1))  11.5 us
    ppermute x12, waiting for transfers between devices, left(): return lax.ppermute(block, 'ctx', z_shift(-1))  10.2 us
    all_to_all x1, waiting for transfers between devices, spread(): return lax.all_to_all(copies, axis, 0, 0, tiled=True)  7.49 us
    all_to_all x2, waiting for transfers between devices, gather_sum(): lax.all_to_all(parts, axis, 0, 0, tiled=True).astype(F32)  7.38 us
    sub x1, matrix products, attention(): probs_full = jax.nn.softmax(scores, axis=-1)  7.25 us
  transfers between devices with their start and end apart: 32, of which 16 were waited for; matrix products, arithmetic and copies ran while one was open for 19% of the time, Pallas kernels for 0%

profile of v2, /device:TPU:2, one launch (start us, length us, event | category | flops | bytes accessed | tf_op | source)
XLA Modules:
  0.0 190.9 jit_solution(16772943598426784142)
XLA Ops:
  0.7 0.8 pad_maximum_fusion.9
  1.5 2.1 %collective-permute-start = (bf16[32,256]{1,0:T(8,128)(2,1)S(1)}, bf16[32,256]{1,0:T(8,128)(2,1)S(1)}, u32[]{:S(2)}, u32[]{:S(2)}) collective-permute-start(bf16[32,256]{1,0:T(8,128)(2,1)S(1)} %pad_maximum_fusion.9), channel_id=1, source_target_pairs={{0,128},{16,144},{32,160},{48,176},{64,192},{80,208},{96,224},{112... | collective-permute-start | bytes 49160 | tf_op jit(solution)/shard_map/ppermute | solution.py:45
  4.4 1.1 reduce-window.6
  7.2 1.4 fusion.25
  8.9 2.0 %collective-permute-start.4 = (bf16[64,256]{1,0:T(8,128)(2,1)S(1)}, bf16[64,256]{1,0:T(8,128)(2,1)S(1)}, u32[]{:S(2)}, u32[]{:S(2)}) collective-permute-start(bf16[64,256]{1,0:T(8,128)(2,1)S(1)} %pad_maximum_fusion.8), channel_id=1, source_target_pairs={{0,16},{16,32},{32,48},{48,64},{64,80},{80,96},{96,112},{112,0},{1... | collective-permute-start | bytes 98312 | tf_op jit(solution)/shard_map/ppermute | solution.py:36
  10.9 4.0 %collective-permute-start.1 = (bf16[64,256]{1,0:T(8,128)(2,1)S(1)}, bf16[64,256]{1,0:T(8,128)(2,1)S(1)}, u32[]{:S(2)}, u32[]{:S(2)}) collective-permute-start(bf16[64,256]{1,0:T(8,128)(2,1)S(1)} %pad_maximum_fusion.8), channel_id=1, source_target_pairs={{0,112},{16,0},{32,16},{48,32},{64,48},{80,64},{96,80},{112,96},{1... | collective-permute-start | bytes 98312 | tf_op jit(solution)/shard_map/ppermute | solution.py:40
  15.7 5.9 %all-to-all-start = ((bf16[8,48,512]{2,1,0:T(8,128)(2,1)}), bf16[8,48,512]{2,1,0:T(8,128)(2,1)S(1)}, u32[]{:S(2)}, u32[]{:S(2)}) async-start(bf16[8,48,512]{2,1,0:T(8,128)(2,1)} %bitcast.6), calls=%async_computation | async-start | bytes 786432 | tf_op jit(solution)/shard_map/all_to_all | solution.py:165
  21.7 3.2 %collective-permute-start.2 = (bf16[64,256]{1,0:T(8,128)(2,1)S(1)}, bf16[64,256]{1,0:T(8,128)(2,1)S(1)}, u32[]{:S(2)}, u32[]{:S(2)}) collective-permute-start(bf16[64,256]{1,0:T(8,128)(2,1)S(1)} %collective-permute-done.1), channel_id=1, source_target_pairs={{0,112},{16,0},{32,16},{48,32},{64,48},{80,64},{96,80},{112,96},{1... | collective-permute-start | bytes 98312 | tf_op jit(solution)/shard_map/ppermute | solution.py:40
  24.9 1.9 collective-permute-done.5
  26.8 3.2 %collective-permute-start.3 = (bf16[64,256]{1,0:T(8,128)(2,1)S(1)}, bf16[64,256]{1,0:T(8,128)(2,1)S(1)}, u32[]{:S(2)}, u32[]{:S(2)}) collective-permute-start(bf16[64,256]{1,0:T(8,128)(2,1)S(1)} %collective-permute-done.2), channel_id=1, source_target_pairs={{0,112},{16,0},{32,16},{48,32},{64,48},{80,64},{96,80},{112,96},{1... | collective-permute-start | bytes 98312 | tf_op jit(solution)/shard_map/ppermute | solution.py:40
  30.0 1.9 collective-permute-done.6
  31.9 3.2 %collective-permute-start.8 = (bf16[64,128]{1,0:T(8,128)(2,1)S(1)}, bf16[64,128]{1,0:T(8,128)(2,1)S(1)}, u32[]{:S(2)}, u32[]{:S(2)}) collective-permute-start(bf16[64,128]{1,0:T(8,128)(2,1)S(1)} %slice.153), channel_id=1, source_target_pairs={{0,112},{16,0},{32,16},{48,32},{64,48},{80,64},{96,80},{112,96},{1... | collective-permute-start | bytes 49160 | tf_op jit(solution)/shard_map/ppermute | solution.py:40
  35.2 1.7 collective-permute-done.7
  37.4 1.3 convolution_convert_fusion
  39.3 3.3 %collective-permute-start.13 = (bf16[48,1152]{1,0:T(8,128)(2,1)S(1)}, bf16[48,1152]{1,0:T(8,128)(2,1)S(1)}, u32[]{:S(2)}, u32[]{:S(2)}) collective-permute-start(bf16[48,1152]{1,0:T(8,128)(2,1)S(1)} %get-tuple-element.73), channel_id=1, source_target_pairs={{0,112},{16,0},{32,16},{48,32},{64,48},{80,64},{96,80},{112,96},{1... | collective-permute-start | bytes 331784 | tf_op jit(solution)/shard_map/ppermute | solution.py:40
  42.6 3.4 %collective-permute-done.9 = bf16[48,1152]{1,0:T(8,128)(2,1)S(1)} collective-permute-done((bf16[48,1152]{1,0:T(8,128)(2,1)S(1)}, bf16[48,1152]{1,0:T(8,128)(2,1)S(1)}, u32[]{:S(2)}, u32[]{:S(2)}) %collective-permute-start.9) | collective-permute-done | bytes 110624 | tf_op jit(solution)/shard_map/ppermute | solution.py:36
  46.8 3.3 %collective-permute-start.10 = (bf16[48,2304]{1,0:T(8,128)(2,1)}, bf16[48,2304]{1,0:T(8,128)(2,1)}, u32[]{:S(2)}, u32[]{:S(2)}) collective-permute-start(bf16[48,2304]{1,0:T(8,128)(2,1)} %get-tuple-element.68), channel_id=1, source_target_pairs={{0,16},{16,32},{32,48},{48,64},{64,80},{80,96},{96,112},{112,0},{1... | collective-permute-start | bytes 663560 | tf_op jit(solution)/shard_map/ppermute | solution.py:36
  50.5 5.7 %collective-permute-done.10 = bf16[48,2304]{1,0:T(8,128)(2,1)} collective-permute-done((bf16[48,2304]{1,0:T(8,128)(2,1)}, bf16[48,2304]{1,0:T(8,128)(2,1)}, u32[]{:S(2)}, u32[]{:S(2)}) %collective-permute-start.10) | collective-permute-done | bytes 221216 | tf_op jit(solution)/shard_map/ppermute | solution.py:36
  56.2 1.7 add_convert_fusion.3
  57.8 1.4 collective-permute-start.11
  59.3 1.5 broadcast_in_dim.74
  60.8 5.7 %all-to-all-start.1 = ((bf16[8,512,256]{2,1,0:T(8,128)(2,1)}), bf16[8,512,256]{2,1,0:T(8,128)(2,1)}, u32[]{:S(2)}, u32[]{:S(2)}) async-start(bf16[8,512,256]{2,1,0:T(8,128)(2,1)} %broadcast_in_dim.74), calls=%async_computation.1 | async-start | bytes 4194304 | tf_op jit(solution)/shard_map/all_to_all | solution.py:23
  66.5 1.9 %add_convert_fusion.2 = (bf16[48,2304]{1,0:T(8,128)(2,1)}, bf16[48,2304]{1,0:T(8,128)(2,1)}) fusion(bf16[48,2304]{1,0:T(8,128)(2,1)} %collective-permute-done.11, bf16[384,768]{1,0:T(8,128)(2,1)S(1)} %convolution_convert_fusion, bf16[384,768]{1,0:T(8,128)(2,1)S(1)} %convolution_convert_fusion.1, bf16[384,768]{1,0:T(8,128)(2,1)S(1)} %convolution_convert_fusion.2, ...), kind=kLoop, calls=%fused_computation.67 | loop fusion | flops 1990656 | bytes 2654208 | tf_op jit(solution)/shard_map/convert_element_type | solution.py:53
  68.4 1.9 collective-permute-start.15
  70.3 2.7 %broadcast_compare_fusion = pred[256,4096]{0,1:T(8,128)(4,1)} fusion(s32[256]{0:T(256)S(1)} %iota_add_fusion, s32[4096]{0:T(1024)S(1)} %fusion.76), kind=kLoop, calls=%fused_computation.18 | loop fusion | flops 1048576 | bytes 1065984 | tf_op jit(solution)/shard_map/le | solution.py:116
  73.1 1.0 copy.87
  75.4 7.5 %all-to-all-done.1 = bf16[8,512,256]{2,1,0:T(8,128)(2,1)} async-done(((bf16[8,512,256]{2,1,0:T(8,128)(2,1)}), bf16[8,512,256]{2,1,0:T(8,128)(2,1)}, u32[]{:S(2)}, u32[]{:S(2)}) %all-to-all-start.1) | async-done | bytes 2097184 | tf_op jit(solution)/shard_map/all_to_all | solution.py:23
  82.9 7.2 %fusion.95 = (f32[2,256]{1,0:T(2,128)S(1)}, f32[2,256,4096]{1,2,0:T(8,128)}) fusion(pred[256,4096]{0,1:T(8,128)(4,1)} %broadcast_compare_fusion, bf16[256,2,128]{0,2,1:T(8,128)(2,1)S(1)} %copy.87, bf16[4096,256]{1,0:T(8,128)(2,1)} %bitcast.9), kind=kOutput, calls=%fused_computation.195 | convolution fusion | flops 545263616 | bytes 10618880 | tf_op jit(solution)/shard_map/sub | solution.py:121
  90.1 4.2 %fusion.9 = bf16[2,256,4096]{1,2,0:T(8,128)(2,1)S(1)} fusion(f32[2,256,4096]{1,2,0:T(8,128)} %get-tuple-element.80, f32[2,256]{1,0:T(2,128)S(1)} %get-tuple-element.79), kind=kLoop, calls=%fused_computation.15 | loop fusion | flops 4194304 | bytes 12584960 | tf_op jit(solution)/shard_map/convert_element_type | solution.py:122
  94.4 2.2 %fusion.18 = f32[256,2]{0,1:T(2,128)S(1)} fusion(bf16[2,256,4096]{1,2,0:T(8,128)(2,1)S(1)} %fusion.9, bf16[4096,256]{1,0:T(8,128)(2,1)} %bitcast.9, bf16[256,2,128]{0,2,1:T(8,128)(2,1)S(1)} %copy.81), kind=kOutput, calls=%fused_computation.36 | convolution fusion | flops 537067008 | bytes 5376000 | tf_op jit(solution)/shard_map/hpt,td->phd/dot_general | solution.py:123
  96.6 1.5 fusion.5
  98.1 2.2 %collective-permute-start.12 = (bf16[48,2304]{1,0:T(8,128)(2,1)S(1)}, bf16[48,2304]{1,0:T(8,128)(2,1)S(1)}, u32[]{:S(2)}, u32[]{:S(2)}) collective-permute-start(bf16[48,2304]{1,0:T(8,128)(2,1)S(1)} %copy-done.4), channel_id=1, source_target_pairs={{0,16},{16,32},{32,48},{48,64},{64,80},{80,96},{96,112},{112,0},{1... | collective-permute-start | bytes 663560 | tf_op jit(solution)/shard_map/ppermute | solution.py:36
  100.3 1.1 collective-permute-start.16
  101.4 2.5 %fusion.2 = bf16[2,256,4096]{1,2,0:T(8,128)(2,1)S(1)} fusion(bf16[256,2,128]{0,2,1:T(8,128)(2,1)S(1)} %copy.81, f32[2,256]{1,0:T(2,128)S(1)} %bitcast.129, f32[2,256,4096]{1,2,0:T(8,128)S(1)} %bitcast.111, f32[2,256]{1,0:T(2,128)S(1)} %get-tuple-element.79, bf16[4096,256]{1,0:T(8,128)(2,1)} %bitcast.9), kind=kOutput, calls=%fused_computation.3 | convolution fusion | flops 545259520 | bytes 13766656 | tf_op jit(solution)/shard_map/phd,td->hpt/dot_general | solution.py:125
  103.9 1.5 fusion.4
  105.4 2.8 %collective-permute-done.16 = bf16[48,2304]{1,0:T(8,128)(2,1)S(1)} collective-permute-done((bf16[48,2304]{1,0:T(8,128)(2,1)S(1)}, bf16[48,2304]{1,0:T(8,128)(2,1)S(1)}, u32[]{:S(2)}, u32[]{:S(2)}) %collective-permute-start.16) | collective-permute-done | bytes 221216 | tf_op jit(solution)/shard_map/ppermute | solution.py:40
  108.3 1.7 collective-permute-start.17
  110.1 5.9 %collective-permute-done.17 = bf16[48,2304]{1,0:T(8,128)(2,1)S(1)} collective-permute-done((bf16[48,2304]{1,0:T(8,128)(2,1)S(1)}, bf16[48,2304]{1,0:T(8,128)(2,1)S(1)}, u32[]{:S(2)}, u32[]{:S(2)}) %collective-permute-start.17) | collective-permute-done | bytes 221216 | tf_op jit(solution)/shard_map/ppermute | solution.py:45
  116.2 0.8 pad_maximum_fusion.4
  117.7 1.6 collective-permute-start.21
  119.3 2.0 %fusion.19 = bf16[256,2,128]{0,2,1:T(8,128)(2,1)S(1)} fusion(bf16[2,256,4096]{1,2,0:T(8,128)(2,1)S(1)} %fusion.2, bf16[4096,256]{1,0:T(8,128)(2,1)} %bitcast.9), kind=kOutput, calls=%fused_computation.37 | convolution fusion | flops 537001984 | bytes 5373952 | tf_op jit(solution)/shard_map/hpt,td->phd/dot_general | solution.py:128
  121.3 0.8 copy.94
  122.1 1.5 copy.106
  123.7 7.0 %all-to-all-start.2 = ((bf16[8,512,256]{1,2,0:T(8,128)(2,1)}), bf16[8,512,256]{1,2,0:T(8,128)(2,1)S(1)}, u32[]{:S(2)}, u32[]{:S(2)}) async-start(bf16[8,512,256]{1,2,0:T(8,128)(2,1)} %bitcast.112), calls=%async_computation.2 | async-start | bytes 4194304 | tf_op jit(solution)/shard_map/all_to_all | solution.py:27
  130.7 1.3 collective-permute-start.19
  132.0 0.8 collective-permute-start.22
  132.8 1.6 constant_dynamic-update-slice_fusion.14
  134.4 2.5 %collective-permute-done.19 = bf16[48,2304]{1,0:T(8,128)(2,1)S(1)} collective-permute-done((bf16[48,2304]{1,0:T(8,128)(2,1)}, bf16[48,2304]{1,0:T(8,128)(2,1)S(1)}, u32[]{:S(2)}, u32[]{:S(2)}) %collective-permute-start.19) | collective-permute-done | bytes 221216 | tf_op jit(solution)/shard_map/ppermute | solution.py:40
  136.9 2.4 %collective-permute-start.20 = (bf16[48,2304]{1,0:T(8,128)(2,1)S(1)}, bf16[48,2304]{1,0:T(8,128)(2,1)S(1)}, u32[]{:S(2)}, u32[]{:S(2)}) collective-permute-start(bf16[48,2304]{1,0:T(8,128)(2,1)S(1)} %collective-permute-done.19), channel_id=1, source_target_pairs={{0,112},{16,0},{32,16},{48,32},{64,48},{80,64},{96,80},{112,96},{1... | collective-permute-start | bytes 663560 | tf_op jit(solution)/shard_map/ppermute | solution.py:40
  140.0 2.8 %collective-permute-done.20 = bf16[48,2304]{1,0:T(8,128)(2,1)S(1)} collective-permute-done((bf16[48,2304]{1,0:T(8,128)(2,1)S(1)}, bf16[48,2304]{1,0:T(8,128)(2,1)S(1)}, u32[]{:S(2)}, u32[]{:S(2)}) %collective-permute-start.20) | collective-permute-done | bytes 221216 | tf_op jit(solution)/shard_map/ppermute | solution.py:40
  142.8 3.7 %collective-permute-start.25 = (bf16[48,1152]{1,0:T(8,128)(2,1)S(1)}, bf16[48,1152]{1,0:T(8,128)(2,1)S(1)}, u32[]{:S(2)}, u32[]{:S(2)}) collective-permute-start(bf16[48,1152]{1,0:T(8,128)(2,1)S(1)} %slice.164), channel_id=1, source_target_pairs={{0,112},{16,0},{32,16},{48,32},{64,48},{80,64},{96,80},{112,96},{1... | collective-permute-start | bytes 331784 | tf_op jit(solution)/shard_map/ppermute | solution.py:40
  147.4 1.5 collective-permute-done.25
  148.9 3.7 %collective-permute-done.24 = bf16[48,1152]{1,0:T(8,128)(2,1)S(1)} collective-permute-done((bf16[48,1152]{1,0:T(8,128)(2,1)S(1)}, bf16[48,1152]{1,0:T(8,128)(2,1)S(1)}, u32[]{:S(2)}, u32[]{:S(2)}) %collective-permute-start.24) | collective-permute-done | bytes 110624 | tf_op jit(solution)/shard_map/ppermute | solution.py:36
  154.7 1.6 constant_dynamic-update-slice_fusion.9
  156.9 1.5 fusion.32
  158.4 1.3 convolution_add_fusion
  162.0 5.7 %all-to-all-start.4 = ((bf16[8,48,128]{2,1,0:T(8,128)(2,1)}), bf16[8,48,128]{2,1,0:T(8,128)(2,1)S(1)}, u32[]{:S(2)}, u32[]{:S(2)}) async-start(bf16[8,48,128]{2,1,0:T(8,128)(2,1)} %fusion.63), calls=%async_computation.4 | async-start | bytes 196608 | tf_op jit(solution)/shard_map/all_to_all | solution.py:210
  167.7 1.1 fusion.12
  168.8 4.1 %all-to-all-done.4 = bf16[8,48,128]{2,1,0:T(8,128)(2,1)S(1)} async-done(((bf16[8,48,128]{2,1,0:T(8,128)(2,1)}), bf16[8,48,128]{2,1,0:T(8,128)(2,1)S(1)}, u32[]{:S(2)}, u32[]{:S(2)}) %all-to-all-start.4) | async-done | bytes 98336 | tf_op jit(solution)/shard_map/all_to_all | solution.py:210
  172.9 6.0 %all-to-all-start.3 = ((bf16[16,32,256]{2,1,0:T(8,128)(2,1)}), bf16[16,32,256]{2,1,0:T(8,128)(2,1)S(1)}, u32[]{:S(2)}, u32[]{:S(2)}) async-start(bf16[16,32,256]{2,1,0:T(8,128)(2,1)} %bitcast.23), calls=%async_computation.3 | async-start | bytes 524288 | tf_op jit(solution)/shard_map/all_to_all | solution.py:27
  178.9 1.1 fusion.13
  180.0 1.2 fusion.14
  181.2 1.1 fusion.16
  182.3 7.4 %all-to-all-done.3 = bf16[16,32,256]{2,1,0:T(8,128)(2,1)S(1)} async-done(((bf16[16,32,256]{2,1,0:T(8,128)(2,1)}), bf16[16,32,256]{2,1,0:T(8,128)(2,1)S(1)}, u32[]{:S(2)}, u32[]{:S(2)}) %all-to-all-start.3) | async-done | bytes 262176 | tf_op jit(solution)/shard_map/all_to_all | solution.py:27
  (110 shorter events, 15.8 us)
Async XLA Ops:
  0.6 38.2 %copy-start = (bf16[1,256,1536]{2,1,0:T(8,128)(2,1)S(1)}, bf16[1,256,1536]{2,1,0:T(8,128)(2,1)}, u32[]{:S(2)}) copy-start(bf16[1,256,1536]{2,1,0:T(8,128)(2,1)} %param.19) | copy-start | bytes 2359300
  0.6 8.2 %copy-start.6 = (bf16[32,1,128]{2,0,1:T(8,128)(2,1)S(1)}, bf16[32,1,128]{2,0,1:T(8,128)(2,1)}, u32[]{:S(2)}) copy-start(bf16[32,1,128]{2,0,1:T(8,128)(2,1)} %param.13) | copy-start | bytes 24580
  0.7 8.2 %copy-start.7 = (bf16[32,1,128]{2,0,1:T(8,128)(2,1)S(1)}, bf16[32,1,128]{2,0,1:T(8,128)(2,1)}, u32[]{:S(2)}) copy-start(bf16[32,1,128]{2,0,1:T(8,128)(2,1)} %param.12) | copy-start | bytes 24580
  1.5 7.4 %collective-permute-start = (bf16[32,256]{1,0:T(8,128)(2,1)S(1)}, bf16[32,256]{1,0:T(8,128)(2,1)S(1)}, u32[]{:S(2)}, u32[]{:S(2)}) collective-permute-start(bf16[32,256]{1,0:T(8,128)(2,1)S(1)} %pad_maximum_fusion.9), channel_id=1, source_target_pairs={{0,128},{16,144},{32,160},{48,176},{64,192},{80,208},{96,224},{112... | collective-permute-start | bytes 49160 | tf_op jit(solution)/shard_map/ppermute | solution.py:45
  4.4 2.8 %copy-start.8 = (pred[512,8]{0,1:T(8,128)(4,1)}, pred[512,8]{0,1:T(8,128)(4,1)S(1)}, u32[]{:S(2)}) copy-start(pred[512,8]{0,1:T(8,128)(4,1)S(1)} %broadcast_compare_fusion.1) | copy-start | bytes 12292
  8.7 28.4 %copy-start.2 = (bf16[1,256,1536]{2,1,0:T(8,128)(2,1)S(1)}, bf16[1,256,1536]{2,1,0:T(8,128)(2,1)}, u32[]{:S(2)}) copy-start(bf16[1,256,1536]{2,1,0:T(8,128)(2,1)} %param.20) | copy-start | bytes 2359300
  8.9 12.7 %collective-permute-start.4 = (bf16[64,256]{1,0:T(8,128)(2,1)S(1)}, bf16[64,256]{1,0:T(8,128)(2,1)S(1)}, u32[]{:S(2)}, u32[]{:S(2)}) collective-permute-start(bf16[64,256]{1,0:T(8,128)(2,1)S(1)} %pad_maximum_fusion.8), channel_id=1, source_target_pairs={{0,16},{16,32},{32,48},{48,64},{64,80},{80,96},{96,112},{112,0},{1... | collective-permute-start | bytes 98312 | tf_op jit(solution)/shard_map/ppermute | solution.py:36
  10.9 10.7 %collective-permute-start.1 = (bf16[64,256]{1,0:T(8,128)(2,1)S(1)}, bf16[64,256]{1,0:T(8,128)(2,1)S(1)}, u32[]{:S(2)}, u32[]{:S(2)}) collective-permute-start(bf16[64,256]{1,0:T(8,128)(2,1)S(1)} %pad_maximum_fusion.8), channel_id=1, source_target_pairs={{0,112},{16,0},{32,16},{48,32},{64,48},{80,64},{96,80},{112,96},{1... | collective-permute-start | bytes 98312 | tf_op jit(solution)/shard_map/ppermute | solution.py:40
  15.7 21.2 %all-to-all-start = ((bf16[8,48,512]{2,1,0:T(8,128)(2,1)}), bf16[8,48,512]{2,1,0:T(8,128)(2,1)S(1)}, u32[]{:S(2)}, u32[]{:S(2)}) async-start(bf16[8,48,512]{2,1,0:T(8,128)(2,1)} %bitcast.6), calls=%async_computation | async-start | bytes 786432 | tf_op jit(solution)/shard_map/all_to_all | solution.py:165
  21.7 5.1 %collective-permute-start.5 = (bf16[64,256]{1,0:T(8,128)(2,1)S(1)}, bf16[64,256]{1,0:T(8,128)(2,1)S(1)}, u32[]{:S(2)}, u32[]{:S(2)}) collective-permute-start(bf16[64,256]{1,0:T(8,128)(2,1)S(1)} %collective-permute-done.4), channel_id=1, source_target_pairs={{0,16},{16,32},{32,48},{48,64},{64,80},{80,96},{96,112},{112,0},{1... | collective-permute-start | bytes 98312 | tf_op jit(solution)/shard_map/ppermute | solution.py:36
  21.7 5.1 %collective-permute-start.2 = (bf16[64,256]{1,0:T(8,128)(2,1)S(1)}, bf16[64,256]{1,0:T(8,128)(2,1)S(1)}, u32[]{:S(2)}, u32[]{:S(2)}) collective-permute-start(bf16[64,256]{1,0:T(8,128)(2,1)S(1)} %collective-permute-done.1), channel_id=1, source_target_pairs={{0,112},{16,0},{32,16},{48,32},{64,48},{80,64},{96,80},{112,96},{1... | collective-permute-start | bytes 98312 | tf_op jit(solution)/shard_map/ppermute | solution.py:40
  26.8 5.1 %collective-permute-start.6 = (bf16[64,256]{1,0:T(8,128)(2,1)S(1)}, bf16[64,256]{1,0:T(8,128)(2,1)S(1)}, u32[]{:S(2)}, u32[]{:S(2)}) collective-permute-start(bf16[64,256]{1,0:T(8,128)(2,1)S(1)} %collective-permute-done.5), channel_id=1, source_target_pairs={{0,16},{16,32},{32,48},{48,64},{64,80},{80,96},{96,112},{112,0},{1... | collective-permute-start | bytes 98312 | tf_op jit(solution)/shard_map/ppermute | solution.py:36
  26.8 5.1 %collective-permute-start.3 = (bf16[64,256]{1,0:T(8,128)(2,1)S(1)}, bf16[64,256]{1,0:T(8,128)(2,1)S(1)}, u32[]{:S(2)}, u32[]{:S(2)}) collective-permute-start(bf16[64,256]{1,0:T(8,128)(2,1)S(1)} %collective-permute-done.2), channel_id=1, source_target_pairs={{0,112},{16,0},{32,16},{48,32},{64,48},{80,64},{96,80},{112,96},{1... | collective-permute-start | bytes 98312 | tf_op jit(solution)/shard_map/ppermute | solution.py:40
  31.9 4.9 %collective-permute-start.7 = (bf16[64,128]{1,0:T(8,128)(2,1)S(1)}, bf16[64,128]{1,0:T(8,128)(2,1)S(1)}, u32[]{:S(2)}, u32[]{:S(2)}) collective-permute-start(bf16[64,128]{1,0:T(8,128)(2,1)S(1)} %slice.152), channel_id=1, source_target_pairs={{0,16},{16,32},{32,48},{48,64},{64,80},{80,96},{96,112},{112,0},{1... | collective-permute-start | bytes 49160 | tf_op jit(solution)/shard_map/ppermute | solution.py:36
  31.9 4.9 %collective-permute-start.8 = (bf16[64,128]{1,0:T(8,128)(2,1)S(1)}, bf16[64,128]{1,0:T(8,128)(2,1)S(1)}, u32[]{:S(2)}, u32[]{:S(2)}) collective-permute-start(bf16[64,128]{1,0:T(8,128)(2,1)S(1)} %slice.153), channel_id=1, source_target_pairs={{0,112},{16,0},{32,16},{48,32},{64,48},{80,64},{96,80},{112,96},{1... | collective-permute-start | bytes 49160 | tf_op jit(solution)/shard_map/ppermute | solution.py:40
  39.2 6.8 %collective-permute-start.9 = (bf16[48,1152]{1,0:T(8,128)(2,1)S(1)}, bf16[48,1152]{1,0:T(8,128)(2,1)S(1)}, u32[]{:S(2)}, u32[]{:S(2)}) collective-permute-start(bf16[48,1152]{1,0:T(8,128)(2,1)S(1)} %get-tuple-element.72), channel_id=1, source_target_pairs={{0,16},{16,32},{32,48},{48,64},{64,80},{80,96},{96,112},{112,0},{1... | collective-permute-start | bytes 331784 | tf_op jit(solution)/shard_map/ppermute | solution.py:36
  39.3 6.8 %collective-permute-start.13 = (bf16[48,1152]{1,0:T(8,128)(2,1)S(1)}, bf16[48,1152]{1,0:T(8,128)(2,1)S(1)}, u32[]{:S(2)}, u32[]{:S(2)}) collective-permute-start(bf16[48,1152]{1,0:T(8,128)(2,1)S(1)} %get-tuple-element.73), channel_id=1, source_target_pairs={{0,112},{16,0},{32,16},{48,32},{64,48},{80,64},{96,80},{112,96},{1... | collective-permute-start | bytes 331784 | tf_op jit(solution)/shard_map/ppermute | solution.py:40
  46.8 9.4 %collective-permute-start.10 = (bf16[48,2304]{1,0:T(8,128)(2,1)}, bf16[48,2304]{1,0:T(8,128)(2,1)}, u32[]{:S(2)}, u32[]{:S(2)}) collective-permute-start(bf16[48,2304]{1,0:T(8,128)(2,1)} %get-tuple-element.68), channel_id=1, source_target_pairs={{0,16},{16,32},{32,48},{48,64},{64,80},{80,96},{96,112},{112,0},{1... | collective-permute-start | bytes 663560 | tf_op jit(solution)/shard_map/ppermute | solution.py:36
  50.1 16.3 %collective-permute-start.14 = (bf16[48,2304]{1,0:T(8,128)(2,1)S(1)}, bf16[48,2304]{1,0:T(8,128)(2,1)}, u32[]{:S(2)}, u32[]{:S(2)}) collective-permute-start(bf16[48,2304]{1,0:T(8,128)(2,1)S(1)} %get-tuple-element.69), channel_id=1, source_target_pairs={{0,112},{16,0},{32,16},{48,32},{64,48},{80,64},{96,80},{112,96},{1... | collective-permute-start | bytes 663560 | tf_op jit(solution)/shard_map/ppermute | solution.py:40
  57.8 8.6 %collective-permute-start.11 = (bf16[48,2304]{1,0:T(8,128)(2,1)}, bf16[48,2304]{1,0:T(8,128)(2,1)}, u32[]{:S(2)}, u32[]{:S(2)}) collective-permute-start(bf16[48,2304]{1,0:T(8,128)(2,1)} %add_convert_fusion.3), channel_id=1, source_target_pairs={{0,16},{16,32},{32,48},{48,64},{64,80},{80,96},{96,112},{112,0},{1... | collective-permute-start | bytes 663560 | tf_op jit(solution)/shard_map/ppermute | solution.py:36
  60.8 22.1 %all-to-all-start.1 = ((bf16[8,512,256]{2,1,0:T(8,128)(2,1)}), bf16[8,512,256]{2,1,0:T(8,128)(2,1)}, u32[]{:S(2)}, u32[]{:S(2)}) async-start(bf16[8,512,256]{2,1,0:T(8,128)(2,1)} %broadcast_in_dim.74), calls=%async_computation.1 | async-start | bytes 4194304 | tf_op jit(solution)/shard_map/all_to_all | solution.py:23
  66.4 6.5 %copy-start.5 = (bf16[256,2,128]{2,1,0:T(2,128)(2,1)S(1)}, bf16[256,2,128]{2,1,0:T(2,128)(2,1)}, u32[]{:S(2)}) copy-start(bf16[256,2,128]{2,1,0:T(2,128)(2,1)} %param.14) | copy-start | bytes 393220
  68.4 6.3 %collective-permute-start.15 = (bf16[48,2304]{1,0:T(8,128)(2,1)}, bf16[48,2304]{1,0:T(8,128)(2,1)S(1)}, u32[]{:S(2)}, u32[]{:S(2)}) collective-permute-start(bf16[48,2304]{1,0:T(8,128)(2,1)} %get-tuple-element.67), channel_id=1, source_target_pairs={{0,112},{16,0},{32,16},{48,32},{64,48},{80,64},{96,80},{112,96},{1... | collective-permute-start | bytes 663560 | tf_op jit(solution)/shard_map/ppermute | solution.py:40
  90.1 11.3 %slice-start = ((s8[8388608]{0:T(1024)(128)(4,1)}), s8[4194304]{0:T(1024)(128)(4,1)S(1)}, s32[]{:S(2)}) async-start(s8[8388608]{0:T(1024)(128)(4,1)} %bitcast.110), calls=%async_computation.5 | async-start | bytes 8388608
  94.4 7.0 %slice-start.1 = ((s8[8388608]{0:T(1024)(128)(4,1)}), s8[4194304]{0:T(1024)(128)(4,1)S(1)}, s32[]{:S(2)}) async-start(s8[8388608]{0:T(1024)(128)(4,1)} %bitcast.110), calls=%async_computation.6 | async-start | bytes 8388608
  96.5 1.5 copy-start.4
  96.5 3.7 %copy-start.3 = (bf16[48,2304]{1,0:T(8,128)(2,1)S(1)}, bf16[48,2304]{1,0:T(8,128)(2,1)}, u32[]{:S(2)}) copy-start(bf16[48,2304]{1,0:T(8,128)(2,1)} %add_convert_fusion) | copy-start | bytes 663556
  98.1 7.3 %collective-permute-start.12 = (bf16[48,2304]{1,0:T(8,128)(2,1)S(1)}, bf16[48,2304]{1,0:T(8,128)(2,1)S(1)}, u32[]{:S(2)}, u32[]{:S(2)}) collective-permute-start(bf16[48,2304]{1,0:T(8,128)(2,1)S(1)} %copy-done.4), channel_id=1, source_target_pairs={{0,16},{16,32},{32,48},{48,64},{64,80},{80,96},{96,112},{112,0},{1... | collective-permute-start | bytes 663560 | tf_op jit(solution)/shard_map/ppermute | solution.py:36
  100.3 7.9 %collective-permute-start.16 = (bf16[48,2304]{1,0:T(8,128)(2,1)S(1)}, bf16[48,2304]{1,0:T(8,128)(2,1)S(1)}, u32[]{:S(2)}, u32[]{:S(2)}) collective-permute-start(bf16[48,2304]{1,0:T(8,128)(2,1)S(1)} %copy-done.3), channel_id=1, source_target_pairs={{0,112},{16,0},{32,16},{48,32},{64,48},{80,64},{96,80},{112,96},{1... | collective-permute-start | bytes 663560 | tf_op jit(solution)/shard_map/ppermute | solution.py:40
  108.3 7.7 %collective-permute-start.17 = (bf16[48,2304]{1,0:T(8,128)(2,1)S(1)}, bf16[48,2304]{1,0:T(8,128)(2,1)S(1)}, u32[]{:S(2)}, u32[]{:S(2)}) collective-permute-start(bf16[48,2304]{1,0:T(8,128)(2,1)S(1)} %get-tuple-element.60), channel_id=1, source_target_pairs={{0,128},{16,144},{32,160},{48,176},{64,192},{80,208},{96,224},{112... | collective-permute-start | bytes 663560 | tf_op jit(solution)/shard_map/ppermute | solution.py:45
  117.0 13.7 %collective-permute-start.18 = (bf16[48,2304]{1,0:T(8,128)(2,1)}, bf16[48,2304]{1,0:T(8,128)(2,1)}, u32[]{:S(2)}, u32[]{:S(2)}) collective-permute-start(bf16[48,2304]{1,0:T(8,128)(2,1)} %get-tuple-element.77), channel_id=1, source_target_pairs={{0,112},{16,0},{32,16},{48,32},{64,48},{80,64},{96,80},{112,96},{1... | collective-permute-start | bytes 663560 | tf_op jit(solution)/shard_map/ppermute | solution.py:40
  117.7 12.9 %collective-permute-start.21 = (bf16[48,2304]{1,0:T(8,128)(2,1)}, bf16[48,2304]{1,0:T(8,128)(2,1)}, u32[]{:S(2)}, u32[]{:S(2)}) collective-permute-start(bf16[48,2304]{1,0:T(8,128)(2,1)} %get-tuple-element.77), channel_id=1, source_target_pairs={{0,16},{16,32},{32,48},{48,64},{64,80},{80,96},{96,112},{112,0},{1... | collective-permute-start | bytes 663560 | tf_op jit(solution)/shard_map/ppermute | solution.py:36
  123.7 32.7 %all-to-all-start.2 = ((bf16[8,512,256]{1,2,0:T(8,128)(2,1)}), bf16[8,512,256]{1,2,0:T(8,128)(2,1)S(1)}, u32[]{:S(2)}, u32[]{:S(2)}) async-start(bf16[8,512,256]{1,2,0:T(8,128)(2,1)} %bitcast.112), calls=%async_computation.2 | async-start | bytes 4194304 | tf_op jit(solution)/shard_map/all_to_all | solution.py:27
  130.7 6.2 %collective-permute-start.19 = (bf16[48,2304]{1,0:T(8,128)(2,1)}, bf16[48,2304]{1,0:T(8,128)(2,1)S(1)}, u32[]{:S(2)}, u32[]{:S(2)}) collective-permute-start(bf16[48,2304]{1,0:T(8,128)(2,1)} %collective-permute-done.18), channel_id=1, source_target_pairs={{0,112},{16,0},{32,16},{48,32},{64,48},{80,64},{96,80},{112,96},{1... | collective-permute-start | bytes 663560 | tf_op jit(solution)/shard_map/ppermute | solution.py:40
  132.0 7.4 %collective-permute-start.22 = (bf16[48,2304]{1,0:T(8,128)(2,1)}, bf16[48,2304]{1,0:T(8,128)(2,1)S(1)}, u32[]{:S(2)}, u32[]{:S(2)}) collective-permute-start(bf16[48,2304]{1,0:T(8,128)(2,1)} %collective-permute-done.21), channel_id=1, source_target_pairs={{0,16},{16,32},{32,48},{48,64},{64,80},{80,96},{96,112},{112,0},{1... | collective-permute-start | bytes 663560 | tf_op jit(solution)/shard_map/ppermute | solution.py:36
  136.9 5.9 %collective-permute-start.20 = (bf16[48,2304]{1,0:T(8,128)(2,1)S(1)}, bf16[48,2304]{1,0:T(8,128)(2,1)S(1)}, u32[]{:S(2)}, u32[]{:S(2)}) collective-permute-start(bf16[48,2304]{1,0:T(8,128)(2,1)S(1)} %collective-permute-done.19), channel_id=1, source_target_pairs={{0,112},{16,0},{32,16},{48,32},{64,48},{80,64},{96,80},{112,96},{1... | collective-permute-start | bytes 663560 | tf_op jit(solution)/shard_map/ppermute | solution.py:40
  139.3 7.2 %collective-permute-start.23 = (bf16[48,2304]{1,0:T(8,128)(2,1)S(1)}, bf16[48,2304]{1,0:T(8,128)(2,1)S(1)}, u32[]{:S(2)}, u32[]{:S(2)}) collective-permute-start(bf16[48,2304]{1,0:T(8,128)(2,1)S(1)} %collective-permute-done.22), channel_id=1, source_target_pairs={{0,16},{16,32},{32,48},{48,64},{64,80},{80,96},{96,112},{112,0},{1... | collective-permute-start | bytes 663560 | tf_op jit(solution)/shard_map/ppermute | solution.py:36
  142.8 6.0 %collective-permute-start.25 = (bf16[48,1152]{1,0:T(8,128)(2,1)S(1)}, bf16[48,1152]{1,0:T(8,128)(2,1)S(1)}, u32[]{:S(2)}, u32[]{:S(2)}) collective-permute-start(bf16[48,1152]{1,0:T(8,128)(2,1)S(1)} %slice.164), channel_id=1, source_target_pairs={{0,112},{16,0},{32,16},{48,32},{64,48},{80,64},{96,80},{112,96},{1... | collective-permute-start | bytes 331784 | tf_op jit(solution)/shard_map/ppermute | solution.py:40
  146.6 6.0 %collective-permute-start.24 = (bf16[48,1152]{1,0:T(8,128)(2,1)S(1)}, bf16[48,1152]{1,0:T(8,128)(2,1)S(1)}, u32[]{:S(2)}, u32[]{:S(2)}) collective-permute-start(bf16[48,1152]{1,0:T(8,128)(2,1)S(1)} %slice.163), channel_id=1, source_target_pairs={{0,16},{16,32},{32,48},{48,64},{64,80},{80,96},{96,112},{112,0},{1... | collective-permute-start | bytes 331784 | tf_op jit(solution)/shard_map/ppermute | solution.py:36
  156.8 1.7 copy-start.1
  159.8 1.4 collective-permute-start.26
  162.0 11.0 %all-to-all-start.4 = ((bf16[8,48,128]{2,1,0:T(8,128)(2,1)}), bf16[8,48,128]{2,1,0:T(8,128)(2,1)S(1)}, u32[]{:S(2)}, u32[]{:S(2)}) async-start(bf16[8,48,128]{2,1,0:T(8,128)(2,1)} %fusion.63), calls=%async_computation.4 | async-start | bytes 196608 | tf_op jit(solution)/shard_map/all_to_all | solution.py:210
  167.7 13.5 %copy-start.9 = (pred[512,8]{0,1:T(8,128)(4,1)S(1)}, pred[512,8]{0,1:T(8,128)(4,1)}, u32[]{:S(2)}) copy-start(pred[512,8]{0,1:T(8,128)(4,1)} %copy-done.8) | copy-start | bytes 12292
  172.9 16.7 %all-to-all-start.3 = ((bf16[16,32,256]{2,1,0:T(8,128)(2,1)}), bf16[16,32,256]{2,1,0:T(8,128)(2,1)S(1)}, u32[]{:S(2)}, u32[]{:S(2)}) async-start(bf16[16,32,256]{2,1,0:T(8,128)(2,1)} %bitcast.23), calls=%async_computation.3 | async-start | bytes 524288 | tf_op jit(solution)/shard_map/all_to_all | solution.py:27

commit v3 on v2

--- a/solution.py
+++ b/solution.py
@@ -5,6 +5,7 @@
 
 CAP = 48
 X_HI = 2
+MASKS = (4, 2, 8, 1)
 BF = jnp.bfloat16
 F32 = jnp.float32
 
@@ -53,25 +54,27 @@
     return (a.astype(F32) + b.astype(F32)).astype(BF)
 
 
-def ring_sum(parts, beside):
+def sum_start(parts):
+    far = len(parts) // 2
+    cut = parts[0].shape[1] // 2
+    return parts[far][:, :cut], parts[far][:, cut:]
+
+
+def sum_step(parts, step, onward, back):
     n = len(parts)
     far = n // 2
     cut = parts[0].shape[1] // 2
-    onward, back = parts[far][:, :cut], parts[far][:, cut:]
-    for step in range(far):
-        if step in beside:
-            onward, back = after(onward, beside[step]), after(back, beside[step])
-        onward, back = right(onward), left(back)
-        ahead, behind = parts[far - 1 - step], parts[(far + 1 + step) % n]
-        if step == 0:
-            onward = jnp.concatenate([add_low(onward, ahead[:, :cut]), ahead[:, cut:]], axis=1)
-            back = jnp.concatenate([behind[:, :cut], add_low(back, behind[:, cut:])], axis=1)
-        elif step < far - 1:
-            onward, back = add_low(onward, ahead), add_low(back, behind)
-    return onward.astype(F32) + back.astype(F32) + parts[0].astype(F32)
-
-
-def ring_gather(block, beside=()):
+    onward, back = right(onward), left(back)
+    ahead, behind = parts[far - 1 - step], parts[(far + 1 + step) % n]
+    if step == 0:
+        onward = jnp.concatenate([add_low(onward, ahead[:, :cut]), ahead[:, cut:]], axis=1)
+        back = jnp.concatenate([behind[:, :cut], add_low(back, behind[:, cut:])], axis=1)
+    elif step < far - 1:
+        onward, back = add_low(onward, ahead), add_low(back, behind)
+    return onward, back
+
+
+def ring_gather(block, beside):
     n = lax.axis_size("ctx") // X_HI
     far = n // 2
     cut = block.shape[1] // 2
@@ -91,58 +94,71 @@
     return lax.dynamic_slice_in_dim(twice, places, blocks.shape[0], 0)
 
 
+def swap(block, mask):
+    return lax.ppermute(block, "ctx", [(c, c ^ mask) for c in range(lax.axis_size("ctx"))])
+
+
 def ctx_gather(key_rows, value_vector_rows):
-    n = lax.axis_size("ctx") // X_HI
-    side = lax.axis_index("ctx") // n
-    pair = jnp.concatenate([key_rows[:, 0, :], value_vector_rows[:, 0, :]], axis=1)
-    partner = opposite(pair)
-    first, second = jnp.where(side == 0, pair, partner), jnp.where(side == 0, partner, pair)
-    return jnp.concatenate(ring_gather(jnp.concatenate([first, second], axis=0)), axis=0)
-
-
-def attention(queries, flat, grad_attn):
-    tok_rows = queries.shape[0]
-    head_dim = queries.shape[2]
-    inv_root = head_dim ** (-0.5)
+    block = jnp.concatenate([key_rows[:, 0, :], value_vector_rows[:, 0, :]], axis=1)
+    for mask in MASKS:
+        block = jnp.concatenate([block, swap(block, mask)], axis=0)
+    return block
+
+
+def mask_of(index):
+    return sum((index >> bit) % 2 * mask for bit, mask in enumerate(MASKS))
+
+
+def key_places(rows):
     ctx_size, exp_size = lax.axis_size("ctx"), lax.axis_size("exp")
-    own = flat.shape[0] // (ctx_size * exp_size)
-    key_flat, value_flat = flat[:, :head_dim], flat[:, head_dim:]
-    ring = ctx_size // X_HI
-    at = lax.axis_index("ctx") % ring
-    place = jnp.arange(flat.shape[0])
-    of_ctx = place // own % X_HI * ring + (place // (own * X_HI) + at) % ring
-    key_pos = (of_ctx * exp_size + place // (own * ctx_size)) * own + place % own
+    own = rows // (ctx_size * exp_size)
+    place = jnp.arange(rows)
+    of_ctx = lax.axis_index("ctx") ^ mask_of(place // own % ctx_size)
+    return (of_ctx * exp_size + place // (own * ctx_size)) * own + place % own
+
+
+def masked_scores(queries, flat):
+    tok_rows, _, head_dim = queries.shape
     query_pos = lax.axis_index("ctx") * tok_rows + jnp.arange(tok_rows)
-    allowed = key_pos[None, :] <= query_pos[:, None]
-    scores = (
-        jnp.einsum("phd,td->hpt", queries, key_flat, preferred_element_type=F32) * inv_root
-    )
-    scores = jnp.where(allowed[None], scores, -jnp.inf)
+    allowed = key_places(flat.shape[0])[None, :] <= query_pos[:, None]
+    scores = jnp.einsum("phd,td->hpt", queries, flat[:, :head_dim], preferred_element_type=F32)
+    return jnp.where(allowed[None], scores * head_dim ** (-0.5), -jnp.inf)
+
+
+def value_side(scores, flat, grad_attn):
+    value_flat = flat[:, grad_attn.shape[2] :]
     probs_full = jax.nn.softmax(scores, axis=-1)
     probs_low = probs_full.astype(BF)
     attn_out = jnp.einsum("hpt,td->phd", probs_low, value_flat, preferred_element_type=F32)
     row_delta = jnp.sum(grad_attn.astype(F32) * attn_out, axis=-1)
-    grad_prob = jnp.einsum("phd,td->hpt", grad_attn, value_flat, preferred_element_type=F32)
+    value_grad = jnp.einsum("hpt,phd->td", probs_low, grad_attn, preferred_element_type=F32)
+    return probs_full, row_delta, value_grad.astype(BF)
+
+
+def key_side(probs_full, row_delta, queries, flat, grad_attn):
+    head_dim = queries.shape[2]
+    grad_prob = jnp.einsum(
+        "phd,td->hpt", grad_attn, flat[:, head_dim:], preferred_element_type=F32
+    )
     dscore = (probs_full * (grad_prob - jnp.transpose(row_delta)[:, :, None])).astype(BF)
-    grad_query = (
-        jnp.einsum("hpt,td->phd", dscore, key_flat, preferred_element_type=F32) * inv_root
-    ).astype(BF)
     key_grad = jnp.einsum("hpt,phd->td", dscore, queries, preferred_element_type=F32)
-    value_grad = jnp.einsum("hpt,phd->td", probs_low, grad_attn, preferred_element_type=F32)
-    both = jnp.concatenate([key_grad.astype(BF), value_grad.astype(BF)], axis=1)
-    return both, probs_low, grad_query
+    return dscore, key_grad.astype(BF)
+
+
+def query_side(dscore, flat):
+    head_dim = flat.shape[1] // 2
+    grad_query = jnp.einsum("hpt,td->phd", dscore, flat[:, :head_dim], preferred_element_type=F32)
+    return (grad_query * head_dim ** (-0.5)).astype(BF)
 
 
 def to_owners(both):
-    ctx_size = lax.axis_size("ctx")
-    ring, head_dim = ctx_size // X_HI, both.shape[1] // 2
-    own = both.shape[0] // ctx_size
-    at = lax.axis_index("ctx") % ring
-    both = turn(both.reshape(ring, X_HI, own, 2 * head_dim), (ring - at) % ring)
-    both = jnp.swapaxes(both, 0, 1).reshape(ctx_size, own, 2 * head_dim)
-    summed = gather_sum(both, "ctx")
-    grad_key = (summed[:, :head_dim] * head_dim ** (-0.5)).astype(BF)[:, None, :]
-    grad_value = summed[:, head_dim:].astype(BF)[:, None, :]
+    head_dim = both.shape[1] // 2
+    for mask in reversed(MASKS):
+        half = both.shape[0] // 2
+        sent = both[half:].astype(BF if half >= both.shape[1] // 2 else F32)
+        both = both[:half] + swap(sent, mask).astype(F32)
+    grad_key = (both[:, :head_dim] * head_dim ** (-0.5)).astype(BF)[:, None, :]
+    grad_value = both[:, head_dim:].astype(BF)[:, None, :]
     return grad_key, grad_value
 
 
@@ -230,19 +246,28 @@
     up_weight,
     down_weight,
 ):
+    exp_size = lax.axis_size("exp")
     near = ctx_gather(key_rows, value_vector_rows)
     placed_low, got = select(moe_input, moe_grad, expert_ids, router_weight)
-    got, near = lax.optimization_barrier((got, near))
-    flat = spread(near, "exp").reshape(-1, near.shape[1])
+    flat = spread(after(near, got), "exp").reshape(-1, near.shape[1])
     input_rows, grad_rows, gate_mat, up_mat, parts = project(
         got, gate_weight, up_weight, down_weight
     )
-    both, probs_low, grad_query = attention(queries, flat, grad_attn)
-    exp_size = lax.axis_size("exp")
-    total = ring_sum(parts, {3: flat})
-    block = act_block(total)
-    blocks = ring_gather(block, {2: probs_low, 3: both})
-    both = gather_sum(both.reshape((exp_size, -1) + both.shape[1:]), "exp").astype(BF)
+    onward, back = sum_step(parts, 0, *sum_start(parts))
+    onward, back = sum_step(parts, 1, onward, back)
+    scores = masked_scores(queries, after(flat, onward, back))
+    onward, back = sum_step(parts, 2, onward, back)
+    probs_full, row_delta, value_grad = value_side(after(scores, onward, back), flat, grad_attn)
+    onward, back = sum_step(parts, 3, after(onward, scores), after(back, scores))
+    total = onward.astype(F32) + back.astype(F32) + parts[0].astype(F32)
+    dscore, key_grad = key_side(
+        probs_full, after(row_delta, total), queries, flat, grad_attn
+    )
+    block = act_block(after(total, value_grad))
+    grad_query = query_side(dscore, after(flat, block))
+    both = jnp.concatenate([key_grad, value_grad], axis=1)
+    blocks = ring_gather(block, {1: both, 2: grad_query})
+    both = gather_sum(both.reshape((exp_size, -1) + both.shape[1:]), "exp")
     full = after(jnp.concatenate(blocks, axis=0), both)
     of_experts = finish(full, input_rows, grad_rows, gate_mat, up_mat, placed_low)
     grad_key, grad_value = to_owners(both)

time: 193 us -> 171 us (0.89)
  starting transfers between devices: 74.3 us -> 66.6 us
  waiting for transfers between devices: 53.8 us -> 47.7 us
  matrix products: 27.6 us -> 22.1 us
    ppermute x0 -> x8, starting transfers between devices: none -> 17.9 us  [swap(): lax.ppermute(block, 'ctx', [(c, c ^ mask) for c in range(lax.axis_size('c...]
    ppermute x0 -> x8, waiting for transfers between devices: none -> 15.7 us  [swap(): lax.ppermute(block, 'ctx', [(c, c ^ mask) for c in range(lax.axis_size('c...]
    ppermute x12 -> x8, starting transfers between devices: 28.6 us -> 18.3 us  [left(): return lax.ppermute(block, 'ctx', z_shift(-1))]
    ppermute x12 -> x8, waiting for transfers between devices: 10.2 us -> 2.14 us  [left(): return lax.ppermute(block, 'ctx', z_shift(-1))]
    all_to_all x2 -> x1, starting transfers between devices: 12.9 us -> 5.34 us  [gather_sum(): lax.all_to_all(parts, axis, 0, 0, tiled=True).astype(F32)]
    all_to_all x2 -> x1, waiting for transfers between devices: 7.38 us -> 0.01 us  [gather_sum(): lax.all_to_all(parts, axis, 0, 0, tiled=True).astype(F32)]
    sub x1 -> x0, matrix products: 7.25 us -> none  [attention(): probs_full = jax.nn.softmax(scores, axis=-1)]
    ppermute x12 -> x8, starting transfers between devices: 11.5 us -> 5.54 us  [right(): return lax.ppermute(block, 'ctx', z_shift(1))]
  transfers between devices with their start and end apart: 32 -> 30, of which waited for: 16 -> 16; matrix products, arithmetic and copies ran while one was open for 19% -> 25% of each run, Pallas kernels for 0% -> 0%
where the time goes in v3:
time: 171 us; the launch traced here: 169 us
  starting transfers between devices  66.6 us (39%)
  waiting for transfers between devices  47.7 us (28%)
  matrix products  22.1 us (13%)
  other arithmetic  19.3 us (11%)
  local copies, waits for them, and re-layouts  12.4 us (7%)
    ppermute x8, starting transfers between devices, left(): return lax.ppermute(block, 'ctx', z_shift(-1))  18.3 us
    ppermute x8, starting transfers between devices, swap(): lax.ppermute(block, 'ctx', [(c, c ^ mask) for c in range(lax.axis_size('c...  17.9 us
    ppermute x8, waiting for transfers between devices, swap(): lax.ppermute(block, 'ctx', [(c, c ^ mask) for c in range(lax.axis_size('c...  15.7 us
    ppermute x8, waiting for transfers between devices, right(): return lax.ppermute(block, 'ctx', z_shift(1))  14.9 us
    all_to_all x1, waiting for transfers between devices, spread(): return lax.all_to_all(copies, axis, 0, 0, tiled=True)  11.7 us
    unnamed x37, local copies, waits for them, and re-layouts  8.01 us
    all_to_all x1, starting transfers between devices, select(): lax.all_to_all(sent.reshape(exp_size, CAP, 2 * width), 'exp', 0, 0, tiled...  5.92 us
    all_to_all x1, starting transfers between devices, spread(): return lax.all_to_all(copies, axis, 0, 0, tiled=True)  5.84 us
  transfers between devices with their start and end apart: 30, of which 16 were waited for; matrix products, arithmetic and copies ran while one was open for 25% of the time, Pallas kernels for 0%

profile of v3, /device:TPU:2, one launch (start us, length us, event | category | flops | bytes accessed | tf_op | source)
XLA Modules:
  0.0 169.3 jit_solution(8518445006726802843)
XLA Ops:
  0.6 0.8 pad_maximum_fusion.11
  1.4 7.2 %collective-permute-start = (bf16[32,256]{1,0:T(8,128)(2,1)S(1)}, bf16[32,256]{1,0:T(8,128)(2,1)S(1)}, u32[]{:S(2)}, u32[]{:S(2)}) collective-permute-start(bf16[32,256]{1,0:T(8,128)(2,1)S(1)} %get-tuple-element.74), channel_id=1, source_target_pairs={{0,64},{16,80},{32,96},{48,112},{64,0},{80,16},{96,32},{112,48},{1... | collective-permute-start | bytes 49160 | tf_op jit(solution)/shard_map/ppermute | solution.py:98
  8.7 0.7 convert_reduce_fusion.1
  9.5 1.1 reduce-window.6
  11.0 0.8 select_reduce_fusion.1
  12.3 1.4 fusion.22
  13.9 0.8 pad_maximum_fusion.1
  14.7 5.9 %all-to-all-start = ((bf16[8,48,512]{2,1,0:T(8,128)(2,1)}), bf16[8,48,512]{2,1,0:T(8,128)(2,1)S(1)}, u32[]{:S(2)}, u32[]{:S(2)}) async-start(bf16[8,48,512]{2,1,0:T(8,128)(2,1)} %bitcast.8), calls=%async_computation | async-start | bytes 786432 | tf_op jit(solution)/shard_map/all_to_all | solution.py:181
  20.7 1.6 collective-permute-start.1
  22.3 3.3 %collective-permute-done.1 = bf16[64,256]{1,0:T(8,128)(2,1)S(1)} collective-permute-done((bf16[64,256]{1,0:T(8,128)(2,1)S(1)}, bf16[64,256]{1,0:T(8,128)(2,1)S(1)}, u32[]{:S(2)}, u32[]{:S(2)}) %collective-permute-start.1) | collective-permute-done | bytes 32800 | tf_op jit(solution)/shard_map/ppermute | solution.py:98
  25.6 2.1 %collective-permute-start.2 = (bf16[128,256]{1,0:T(8,128)(2,1)S(1)}, bf16[128,256]{1,0:T(8,128)(2,1)S(1)}, u32[]{:S(2)}, u32[]{:S(2)}) collective-permute-start(bf16[128,256]{1,0:T(8,128)(2,1)S(1)} %pad_maximum_fusion.9), channel_id=1, source_target_pairs={{0,128},{16,144},{32,160},{48,176},{64,192},{80,208},{96,224},{112... | collective-permute-start | bytes 196616 | tf_op jit(solution)/shard_map/ppermute | solution.py:98
  28.3 1.3 convolution_convert_fusion
  30.3 1.9 %collective-permute-start.4 = (bf16[48,1152]{1,0:T(8,128)(2,1)S(1)}, bf16[48,1152]{1,0:T(8,128)(2,1)S(1)}, u32[]{:S(2)}, u32[]{:S(2)}) collective-permute-start(bf16[48,1152]{1,0:T(8,128)(2,1)S(1)} %get-tuple-element.68), channel_id=1, source_target_pairs={{0,16},{16,32},{32,48},{48,64},{64,80},{80,96},{96,112},{112,0},{1... | collective-permute-start | bytes 331784 | tf_op jit(solution)/shard_map/ppermute | solution.py:37
  32.2 1.1 collective-permute-start.3
  33.3 2.0 %collective-permute-done.7 = bf16[48,1152]{1,0:T(8,128)(2,1)S(1)} collective-permute-done((bf16[48,1152]{1,0:T(8,128)(2,1)S(1)}, bf16[48,1152]{1,0:T(8,128)(2,1)S(1)}, u32[]{:S(2)}, u32[]{:S(2)}) %collective-permute-start.7) | collective-permute-done | bytes 110624 | tf_op jit(solution)/shard_map/ppermute | solution.py:41
  35.3 1.0 collective-permute-done.4
  36.4 2.0 %collective-permute-start.5 = (bf16[48,2304]{1,0:T(8,128)(2,1)S(1)}, bf16[48,2304]{1,0:T(8,128)(2,1)}, u32[]{:S(2)}, u32[]{:S(2)}) collective-permute-start(bf16[48,2304]{1,0:T(8,128)(2,1)S(1)} %get-tuple-element.64), channel_id=1, source_target_pairs={{0,16},{16,32},{32,48},{48,64},{64,80},{80,96},{96,112},{112,0},{1... | collective-permute-start | bytes 663560 | tf_op jit(solution)/shard_map/ppermute | solution.py:37
  38.5 1.5 broadcast_in_dim.74
  39.9 5.8 %all-to-all-start.1 = ((bf16[8,512,256]{2,1,0:T(8,128)(2,1)}), bf16[8,512,256]{2,1,0:T(8,128)(2,1)}, u32[]{:S(2)}, u32[]{:S(2)}) async-start(bf16[8,512,256]{2,1,0:T(8,128)(2,1)} %broadcast_in_dim.74), calls=%async_computation.1 | async-start | bytes 4194304 | tf_op jit(solution)/shard_map/all_to_all | solution.py:24
  45.8 1.2 add_convert_fusion.1
  47.0 1.3 collective-permute-start.10
  48.3 0.8 collective-permute-start.6
  49.1 2.7 %broadcast_compare_fusion = pred[256,4096]{0,1:T(8,128)(4,1)} fusion(s32[256]{0:T(256)S(1)} %iota_add_fusion, s32[4096]{0:T(1024)S(1)} %fusion.77), kind=kLoop, calls=%fused_computation.15 | loop fusion | flops 1048576 | bytes 1065984 | tf_op jit(solution)/shard_map/le | solution.py:123
  51.9 1.0 copy.74
  53.0 2.6 %collective-permute-done.6 = bf16[48,2304]{1,0:T(8,128)(2,1)} collective-permute-done((bf16[48,2304]{1,0:T(8,128)(2,1)S(1)}, bf16[48,2304]{1,0:T(8,128)(2,1)}, u32[]{:S(2)}, u32[]{:S(2)}) %collective-permute-start.6) | collective-permute-done | bytes 221216 | tf_op jit(solution)/shard_map/ppermute | solution.py:37
  55.6 1.0 add_convert_fusion
  56.6 11.7 %all-to-all-done.1 = bf16[8,512,256]{2,1,0:T(8,128)(2,1)} async-done(((bf16[8,512,256]{2,1,0:T(8,128)(2,1)}), bf16[8,512,256]{2,1,0:T(8,128)(2,1)}, u32[]{:S(2)}, u32[]{:S(2)}) %all-to-all-start.1) | async-done | bytes 2097184 | tf_op jit(solution)/shard_map/all_to_all | solution.py:24
  68.3 2.8 %bitcast_select_fusion = f32[2,256,4096]{1,2,0:T(8,128)S(1)} fusion(bf16[256,2,128]{0,2,1:T(8,128)(2,1)S(1)} %copy.74, pred[256,4096]{0,1:T(8,128)(4,1)} %broadcast_compare_fusion, bf16[4096,256]{1,0:T(8,128)(2,1)} %bitcast.9), kind=kOutput, calls=%fused_computation.4 | convolution fusion | flops 541065216 | bytes 10616832 | tf_op jit(solution)/shard_map/phd,td->hpt/dot_general | solution.py:124
  71.1 0.7 collective-permute-start.9
  71.8 2.8 %collective-permute-start.11 = (bf16[48,2304]{1,0:T(8,128)(2,1)S(1)}, bf16[48,2304]{1,0:T(8,128)(2,1)S(1)}, u32[]{:S(2)}, u32[]{:S(2)}) collective-permute-start(bf16[48,2304]{1,0:T(8,128)(2,1)S(1)} %get-tuple-element.22), channel_id=1, source_target_pairs={{0,112},{16,0},{32,16},{48,32},{64,48},{80,64},{96,80},{112,96},{1... | collective-permute-start | bytes 663560 | tf_op jit(solution)/shard_map/ppermute | solution.py:41
  74.6 4.4 %fusion.95 = (f32[2,256]{1,0:T(2,128)S(1)}, f32[2,256,4096]{1,2,0:T(8,128)S(1)}) fusion(f32[2,256,4096]{1,2,0:T(8,128)S(1)} %bitcast_select_fusion), kind=kOutput, calls=%fused_computation.201 | output fusion | flops 4198399 | bytes 16779264 | tf_op jit(solution)/shard_map/sub | solution.py:130
  79.0 0.8 fusion.5
  79.8 2.0 %fusion.12 = f32[256,2]{0,1:T(2,128)S(1)} fusion(bf16[2,256,4096]{1,2,0:T(8,128)(2,1)S(1)} %fusion.5, bf16[4096,256]{1,0:T(8,128)(2,1)} %bitcast.9, bf16[256,2,128]{0,2,1:T(8,128)(2,1)S(1)} %copy.66), kind=kOutput, calls=%fused_computation.32 | convolution fusion | flops 537067008 | bytes 5376000 | tf_op jit(solution)/shard_map/hpt,td->phd/dot_general | solution.py:132
  81.8 1.5 fusion.3
  83.4 2.5 %fusion.2 = bf16[2,256,4096]{1,2,0:T(8,128)(2,1)S(1)} fusion(bf16[256,2,128]{0,2,1:T(8,128)(2,1)S(1)} %copy.66, f32[2,256]{1,0:T(2,128)S(1)} %bitcast.115, f32[2,256,4096]{1,2,0:T(8,128)S(1)} %get-tuple-element.77, f32[2,256]{1,0:T(2,128)S(1)} %get-tuple-element.76, bf16[4096,256]{1,0:T(8,128)(2,1)} %bitcast.9), kind=kOutput, calls=%fused_computation.3 | convolution fusion | flops 545259520 | bytes 13766656 | tf_op jit(solution)/shard_map/phd,td->hpt/dot_general | solution.py:140
  85.9 2.2 %collective-permute-start.12 = (bf16[48,2304]{1,0:T(8,128)(2,1)S(1)}, bf16[48,2304]{1,0:T(8,128)(2,1)}, u32[]{:S(2)}, u32[]{:S(2)}) collective-permute-start(bf16[48,2304]{1,0:T(8,128)(2,1)S(1)} %convert_element_type.180), channel_id=1, source_target_pairs={{0,128},{16,144},{32,160},{48,176},{64,192},{80,208},{96,224},{112... | collective-permute-start | bytes 663560 | tf_op jit(solution)/shard_map/ppermute | solution.py:46
  88.2 1.5 fusion.4
  89.8 1.5 copy.91
  91.3 5.3 %all-to-all-start.2 = ((bf16[8,512,256]{1,2,0:T(8,128)(2,1)}), bf16[8,512,256]{1,2,0:T(8,128)(2,1)S(1)}, u32[]{:S(2)}, u32[]{:S(2)}) async-start(bf16[8,512,256]{1,2,0:T(8,128)(2,1)} %bitcast.97), calls=%async_computation.2 | async-start | bytes 4194304 | tf_op jit(solution)/shard_map/all_to_all | solution.py:28
  96.7 1.0 convert_add_fusion
  97.8 0.8 constant_dynamic-update-slice_fusion.11
  98.6 3.2 %collective-permute-start.17 = (bf16[48,2304]{1,0:T(8,128)(2,1)}, bf16[48,2304]{1,0:T(8,128)(2,1)S(1)}, u32[]{:S(2)}, u32[]{:S(2)}) collective-permute-start(bf16[48,2304]{1,0:T(8,128)(2,1)} %get-tuple-element.27), channel_id=1, source_target_pairs={{0,112},{16,0},{32,16},{48,32},{64,48},{80,64},{96,80},{112,96},{1... | collective-permute-start | bytes 663560 | tf_op jit(solution)/shard_map/ppermute | solution.py:41
  101.8 3.3 %fusion.13 = bf16[256,2,128]{0,2,1:T(8,128)(2,1)S(1)} fusion(bf16[2,256,4096]{1,2,0:T(8,128)(2,1)} %copy-done.1, bf16[4096,256]{1,0:T(8,128)(2,1)} %bitcast.9), kind=kOutput, calls=%fused_computation.33 | convolution fusion | flops 537001984 | bytes 5373952 | tf_op jit(solution)/shard_map/hpt,td->phd/dot_general | solution.py:150
  105.1 0.8 copy.77
  105.8 1.2 collective-permute-done.20
  107.1 3.5 %collective-permute-start.18 = (bf16[48,2304]{1,0:T(8,128)(2,1)S(1)}, bf16[48,2304]{1,0:T(8,128)(2,1)S(1)}, u32[]{:S(2)}, u32[]{:S(2)}) collective-permute-start(bf16[48,2304]{1,0:T(8,128)(2,1)S(1)} %collective-permute-done.17), channel_id=1, source_target_pairs={{0,112},{16,0},{32,16},{48,32},{64,48},{80,64},{96,80},{112,96},{1... | collective-permute-start | bytes 663560 | tf_op jit(solution)/shard_map/ppermute | solution.py:41
  110.6 0.7 constant_dynamic-update-slice_fusion.10
  111.3 5.0 %collective-permute-done.21 = bf16[48,2304]{1,0:T(8,128)(2,1)S(1)} collective-permute-done((bf16[48,2304]{1,0:T(8,128)(2,1)S(1)}, bf16[48,2304]{1,0:T(8,128)(2,1)S(1)}, u32[]{:S(2)}, u32[]{:S(2)}) %collective-permute-start.21) | collective-permute-done | bytes 221216 | tf_op jit(solution)/shard_map/ppermute | solution.py:37
  116.4 3.7 %collective-permute-start.19 = (bf16[48,2304]{1,0:T(8,128)(2,1)S(1)}, bf16[48,2304]{1,0:T(8,128)(2,1)S(1)}, u32[]{:S(2)}, u32[]{:S(2)}) collective-permute-start(bf16[48,2304]{1,0:T(8,128)(2,1)S(1)} %collective-permute-done.18), channel_id=1, source_target_pairs={{0,112},{16,0},{32,16},{48,32},{64,48},{80,64},{96,80},{112,96},{1... | collective-permute-start | bytes 663560 | tf_op jit(solution)/shard_map/ppermute | solution.py:41
  120.8 3.4 %collective-permute-done.22 = bf16[48,2304]{1,0:T(8,128)(2,1)S(1)} collective-permute-done((bf16[48,2304]{1,0:T(8,128)(2,1)S(1)}, bf16[48,2304]{1,0:T(8,128)(2,1)S(1)}, u32[]{:S(2)}, u32[]{:S(2)}) %collective-permute-start.22) | collective-permute-done | bytes 221216 | tf_op jit(solution)/shard_map/ppermute | solution.py:37
  124.3 3.5 %collective-permute-start.24 = (bf16[48,1152]{1,0:T(8,128)(2,1)S(1)}, bf16[48,1152]{1,0:T(8,128)(2,1)S(1)}, u32[]{:S(2)}, u32[]{:S(2)}) collective-permute-start(bf16[48,1152]{1,0:T(8,128)(2,1)S(1)} %slice.200), channel_id=1, source_target_pairs={{0,112},{16,0},{32,16},{48,32},{64,48},{80,64},{96,80},{112,96},{1... | collective-permute-start | bytes 331784 | tf_op jit(solution)/shard_map/ppermute | solution.py:41
  128.4 1.8 %collective-permute-done.23 = bf16[48,1152]{1,0:T(8,128)(2,1)S(1)} collective-permute-done((bf16[48,1152]{1,0:T(8,128)(2,1)S(1)}, bf16[48,1152]{1,0:T(8,128)(2,1)S(1)}, u32[]{:S(2)}, u32[]{:S(2)}) %collective-permute-start.23) | collective-permute-done | bytes 110624 | tf_op jit(solution)/shard_map/ppermute | solution.py:37
  133.4 1.1 copy-done.4
  134.5 1.1 fusion.6
  135.6 1.2 fusion.8
  137.8 1.1 fusion.7
  138.9 3.3 %collective-permute-done.13 = bf16[256,256]{0,1:T(8,128)(2,1)S(1)} collective-permute-done((bf16[256,256]{0,1:T(8,128)(2,1)S(1)}, bf16[256,256]{0,1:T(8,128)(2,1)S(1)}, u32[]{:S(2)}, u32[]{:S(2)}) %collective-permute-start.13) | collective-permute-done | bytes 131104 | tf_op jit(solution)/shard_map/ppermute | solution.py:98
  142.4 5.7 %collective-permute-done.14 = bf16[128,256]{0,1:T(8,128)(2,1)S(1)} collective-permute-done((bf16[128,256]{0,1:T(8,128)(2,1)S(1)}, bf16[128,256]{0,1:T(8,128)(2,1)S(1)}, u32[]{:S(2)}, u32[]{:S(2)}) %collective-permute-start.14) | collective-permute-done | bytes 65568 | tf_op jit(solution)/shard_map/ppermute | solution.py:98
  148.2 3.8 %collective-permute-start.15 = (f32[64,256]{0,1:T(8,128)S(1)}, f32[64,256]{0,1:T(8,128)S(1)}, u32[]{:S(2)}, u32[]{:S(2)}) collective-permute-start(f32[64,256]{0,1:T(8,128)S(1)} %slice.194), channel_id=1, source_target_pairs={{0,32},{16,48},{32,0},{48,16},{64,96},{80,112},{96,64},{112,80},{1... | collective-permute-start | bytes 196616 | tf_op jit(solution)/shard_map/ppermute | solution.py:98
  152.8 5.5 %all-to-all-start.3 = ((bf16[8,48,128]{2,1,0:T(8,128)(2,1)}), bf16[8,48,128]{2,1,0:T(8,128)(2,1)S(1)}, u32[]{:S(2)}, u32[]{:S(2)}) async-start(bf16[8,48,128]{2,1,0:T(8,128)(2,1)} %fusion.57), calls=%async_computation.3 | async-start | bytes 196608 | tf_op jit(solution)/shard_map/all_to_all | solution.py:226
  158.4 2.0 %collective-permute-start.16 = (f32[32,256]{0,1:T(8,128)S(1)}, f32[32,256]{0,1:T(8,128)S(1)}, u32[]{:S(2)}, u32[]{:S(2)}) collective-permute-start(f32[32,256]{0,1:T(8,128)S(1)} %slice.196), channel_id=1, source_target_pairs={{0,64},{16,80},{32,96},{48,112},{64,0},{80,16},{96,32},{112,48},{1... | collective-permute-start | bytes 98312 | tf_op jit(solution)/shard_map/ppermute | solution.py:98
  160.3 3.2 %all-to-all-done.3 = bf16[8,48,128]{2,1,0:T(8,128)(2,1)S(1)} async-done(((bf16[8,48,128]{2,1,0:T(8,128)(2,1)}), bf16[8,48,128]{2,1,0:T(8,128)(2,1)S(1)}, u32[]{:S(2)}, u32[]{:S(2)}) %all-to-all-start.3) | async-done | bytes 98336 | tf_op jit(solution)/shard_map/all_to_all | solution.py:226
  163.5 1.1 fusion.10
  164.5 3.4 %collective-permute-done.16 = f32[32,256]{0,1:T(8,128)S(1)} collective-permute-done((f32[32,256]{0,1:T(8,128)S(1)}, f32[32,256]{0,1:T(8,128)S(1)}, u32[]{:S(2)}, u32[]{:S(2)}) %collective-permute-start.16) | collective-permute-done | bytes 32800 | tf_op jit(solution)/shard_map/ppermute | solution.py:98
  (107 shorter events, 11.2 us)
Async XLA Ops:
  0.6 29.1 %copy-start = (bf16[1,256,1536]{2,1,0:T(8,128)(2,1)S(1)}, bf16[1,256,1536]{2,1,0:T(8,128)(2,1)}, u32[]{:S(2)}) copy-start(bf16[1,256,1536]{2,1,0:T(8,128)(2,1)} %param.19) | copy-start | bytes 2359300
  1.4 19.2 %collective-permute-start = (bf16[32,256]{1,0:T(8,128)(2,1)S(1)}, bf16[32,256]{1,0:T(8,128)(2,1)S(1)}, u32[]{:S(2)}, u32[]{:S(2)}) collective-permute-start(bf16[32,256]{1,0:T(8,128)(2,1)S(1)} %get-tuple-element.74), channel_id=1, source_target_pairs={{0,64},{16,80},{32,96},{48,112},{64,0},{80,16},{96,32},{112,48},{1... | collective-permute-start | bytes 49160 | tf_op jit(solution)/shard_map/ppermute | solution.py:98
  11.0 3.7 %copy-start.7 = (s32[512,8]{0,1:T(8,128)}, s32[512,8]{0,1:T(8,128)S(1)}, u32[]{:S(2)}) copy-start(s32[512,8]{0,1:T(8,128)S(1)} %bitcast_subtract_fusion.1) | copy-start | bytes 49156
  12.3 8.4 %copy-start.10 = (bf16[32,1,128]{2,0,1:T(8,128)(2,1)S(1)}, bf16[32,1,128]{2,0,1:T(8,128)(2,1)}, u32[]{:S(2)}) copy-start(bf16[32,1,128]{2,0,1:T(8,128)(2,1)} %param.13) | copy-start | bytes 24580
  12.3 8.4 %copy-start.11 = (bf16[32,1,128]{2,0,1:T(8,128)(2,1)S(1)}, bf16[32,1,128]{2,0,1:T(8,128)(2,1)}, u32[]{:S(2)}) copy-start(bf16[32,1,128]{2,0,1:T(8,128)(2,1)} %param.12) | copy-start | bytes 24580
  13.7 14.3 %copy-start.5 = (bf16[1,256,1536]{2,1,0:T(8,128)(2,1)S(1)}, bf16[1,256,1536]{2,1,0:T(8,128)(2,1)}, u32[]{:S(2)}) copy-start(bf16[1,256,1536]{2,1,0:T(8,128)(2,1)} %param.20) | copy-start | bytes 2359300
  14.7 13.2 %all-to-all-start = ((bf16[8,48,512]{2,1,0:T(8,128)(2,1)}), bf16[8,48,512]{2,1,0:T(8,128)(2,1)S(1)}, u32[]{:S(2)}, u32[]{:S(2)}) async-start(bf16[8,48,512]{2,1,0:T(8,128)(2,1)} %bitcast.8), calls=%async_computation | async-start | bytes 786432 | tf_op jit(solution)/shard_map/all_to_all | solution.py:181
  20.7 4.9 %collective-permute-start.1 = (bf16[64,256]{1,0:T(8,128)(2,1)S(1)}, bf16[64,256]{1,0:T(8,128)(2,1)S(1)}, u32[]{:S(2)}, u32[]{:S(2)}) collective-permute-start(bf16[64,256]{1,0:T(8,128)(2,1)S(1)} %pad_maximum_fusion.10), channel_id=1, source_target_pairs={{0,32},{16,48},{32,0},{48,16},{64,96},{80,112},{96,64},{112,80},{1... | collective-permute-start | bytes 98312 | tf_op jit(solution)/shard_map/ppermute | solution.py:98
  25.6 6.6 %collective-permute-start.2 = (bf16[128,256]{1,0:T(8,128)(2,1)S(1)}, bf16[128,256]{1,0:T(8,128)(2,1)S(1)}, u32[]{:S(2)}, u32[]{:S(2)}) collective-permute-start(bf16[128,256]{1,0:T(8,128)(2,1)S(1)} %pad_maximum_fusion.9), channel_id=1, source_target_pairs={{0,128},{16,144},{32,160},{48,176},{64,192},{80,208},{96,224},{112... | collective-permute-start | bytes 196616 | tf_op jit(solution)/shard_map/ppermute | solution.py:98
  28.0 2.1 %copy-start.2 = (bf16[8,48,512]{2,1,0:T(8,128)(2,1)}, bf16[8,48,512]{2,1,0:T(8,128)(2,1)S(1)}, u32[]{:S(2)}) copy-start(bf16[8,48,512]{2,1,0:T(8,128)(2,1)S(1)} %fusion.33) | copy-start | bytes 1179652
  30.1 5.2 %collective-permute-start.7 = (bf16[48,1152]{1,0:T(8,128)(2,1)S(1)}, bf16[48,1152]{1,0:T(8,128)(2,1)S(1)}, u32[]{:S(2)}, u32[]{:S(2)}) collective-permute-start(bf16[48,1152]{1,0:T(8,128)(2,1)S(1)} %get-tuple-element.67), channel_id=1, source_target_pairs={{0,112},{16,0},{32,16},{48,32},{64,48},{80,64},{96,80},{112,96},{1... | collective-permute-start | bytes 331784 | tf_op jit(solution)/shard_map/ppermute | solution.py:41
  30.3 6.0 %collective-permute-start.4 = (bf16[48,1152]{1,0:T(8,128)(2,1)S(1)}, bf16[48,1152]{1,0:T(8,128)(2,1)S(1)}, u32[]{:S(2)}, u32[]{:S(2)}) collective-permute-start(bf16[48,1152]{1,0:T(8,128)(2,1)S(1)} %get-tuple-element.68), channel_id=1, source_target_pairs={{0,16},{16,32},{32,48},{48,64},{64,80},{80,96},{96,112},{112,0},{1... | collective-permute-start | bytes 331784 | tf_op jit(solution)/shard_map/ppermute | solution.py:37
  32.2 6.2 %collective-permute-start.3 = (bf16[256,256]{1,0:T(8,128)(2,1)S(1)}, bf16[256,256]{1,0:T(8,128)(2,1)S(1)}, u32[]{:S(2)}, u32[]{:S(2)}) collective-permute-start(bf16[256,256]{1,0:T(8,128)(2,1)S(1)} %pad_maximum_fusion.5), channel_id=1, source_target_pairs={{0,16},{16,0},{32,48},{48,32},{64,80},{80,64},{96,112},{112,96},{1... | collective-permute-start | bytes 393224 | tf_op jit(solution)/shard_map/ppermute | solution.py:98
  36.3 9.5 %collective-permute-start.8 = (bf16[48,2304]{1,0:T(8,128)(2,1)S(1)}, bf16[48,2304]{1,0:T(8,128)(2,1)}, u32[]{:S(2)}, u32[]{:S(2)}) collective-permute-start(bf16[48,2304]{1,0:T(8,128)(2,1)S(1)} %get-tuple-element.63), channel_id=1, source_target_pairs={{0,112},{16,0},{32,16},{48,32},{64,48},{80,64},{96,80},{112,96},{1... | collective-permute-start | bytes 663560 | tf_op jit(solution)/shard_map/ppermute | solution.py:41
  36.4 9.4 %collective-permute-start.5 = (bf16[48,2304]{1,0:T(8,128)(2,1)S(1)}, bf16[48,2304]{1,0:T(8,128)(2,1)}, u32[]{:S(2)}, u32[]{:S(2)}) collective-permute-start(bf16[48,2304]{1,0:T(8,128)(2,1)S(1)} %get-tuple-element.64), channel_id=1, source_target_pairs={{0,16},{16,32},{32,48},{48,64},{64,80},{80,96},{96,112},{112,0},{1... | collective-permute-start | bytes 663560 | tf_op jit(solution)/shard_map/ppermute | solution.py:37
  39.9 28.4 %all-to-all-start.1 = ((bf16[8,512,256]{2,1,0:T(8,128)(2,1)}), bf16[8,512,256]{2,1,0:T(8,128)(2,1)}, u32[]{:S(2)}, u32[]{:S(2)}) async-start(bf16[8,512,256]{2,1,0:T(8,128)(2,1)} %broadcast_in_dim.74), calls=%async_computation.1 | async-start | bytes 4194304 | tf_op jit(solution)/shard_map/all_to_all | solution.py:24
  45.8 6.0 %copy-start.9 = (bf16[256,2,128]{2,1,0:T(2,128)(2,1)S(1)}, bf16[256,2,128]{2,1,0:T(2,128)(2,1)}, u32[]{:S(2)}) copy-start(bf16[256,2,128]{2,1,0:T(2,128)(2,1)} %param.14) | copy-start | bytes 393220
  47.0 6.0 %collective-permute-start.10 = (bf16[48,2304]{1,0:T(8,128)(2,1)S(1)}, bf16[48,2304]{1,0:T(8,128)(2,1)S(1)}, u32[]{:S(2)}, u32[]{:S(2)}) collective-permute-start(bf16[48,2304]{1,0:T(8,128)(2,1)S(1)} %get-tuple-element.61), channel_id=1, source_target_pairs={{0,112},{16,0},{32,16},{48,32},{64,48},{80,64},{96,80},{112,96},{1... | collective-permute-start | bytes 663560 | tf_op jit(solution)/shard_map/ppermute | solution.py:41
  48.3 7.2 %collective-permute-start.6 = (bf16[48,2304]{1,0:T(8,128)(2,1)S(1)}, bf16[48,2304]{1,0:T(8,128)(2,1)}, u32[]{:S(2)}, u32[]{:S(2)}) collective-permute-start(bf16[48,2304]{1,0:T(8,128)(2,1)S(1)} %get-tuple-element.62), channel_id=1, source_target_pairs={{0,16},{16,32},{32,48},{48,64},{64,80},{80,96},{96,112},{112,0},{1... | collective-permute-start | bytes 663560 | tf_op jit(solution)/shard_map/ppermute | solution.py:37
  71.1 12.2 %collective-permute-start.9 = (bf16[48,2304]{1,0:T(8,128)(2,1)S(1)}, bf16[48,2304]{1,0:T(8,128)(2,1)S(1)}, u32[]{:S(2)}, u32[]{:S(2)}) collective-permute-start(bf16[48,2304]{1,0:T(8,128)(2,1)S(1)} %get-tuple-element.21), channel_id=1, source_target_pairs={{0,16},{16,32},{32,48},{48,64},{64,80},{80,96},{96,112},{112,0},{1... | collective-permute-start | bytes 663560 | tf_op jit(solution)/shard_map/ppermute | solution.py:37
  71.8 11.5 %collective-permute-start.11 = (bf16[48,2304]{1,0:T(8,128)(2,1)S(1)}, bf16[48,2304]{1,0:T(8,128)(2,1)S(1)}, u32[]{:S(2)}, u32[]{:S(2)}) collective-permute-start(bf16[48,2304]{1,0:T(8,128)(2,1)S(1)} %get-tuple-element.22), channel_id=1, source_target_pairs={{0,112},{16,0},{32,16},{48,32},{64,48},{80,64},{96,80},{112,96},{1... | collective-permute-start | bytes 663560 | tf_op jit(solution)/shard_map/ppermute | solution.py:41
  85.9 3.7 %copy-start.1 = (bf16[2,256,4096]{1,2,0:T(8,128)(2,1)}, bf16[2,256,4096]{1,2,0:T(8,128)(2,1)S(1)}, u32[]{:S(2)}) copy-start(bf16[2,256,4096]{1,2,0:T(8,128)(2,1)S(1)} %fusion.2) | copy-start | bytes 12582916
  85.9 10.7 %collective-permute-start.12 = (bf16[48,2304]{1,0:T(8,128)(2,1)S(1)}, bf16[48,2304]{1,0:T(8,128)(2,1)}, u32[]{:S(2)}, u32[]{:S(2)}) collective-permute-start(bf16[48,2304]{1,0:T(8,128)(2,1)S(1)} %convert_element_type.180), channel_id=1, source_target_pairs={{0,128},{16,144},{32,160},{48,176},{64,192},{80,208},{96,224},{112... | collective-permute-start | bytes 663560 | tf_op jit(solution)/shard_map/ppermute | solution.py:46
  91.3 41.7 %all-to-all-start.2 = ((bf16[8,512,256]{1,2,0:T(8,128)(2,1)}), bf16[8,512,256]{1,2,0:T(8,128)(2,1)S(1)}, u32[]{:S(2)}, u32[]{:S(2)}) async-start(bf16[8,512,256]{1,2,0:T(8,128)(2,1)} %bitcast.97), calls=%async_computation.2 | async-start | bytes 4194304 | tf_op jit(solution)/shard_map/all_to_all | solution.py:28
  98.6 8.5 %collective-permute-start.20 = (bf16[48,2304]{1,0:T(8,128)(2,1)}, bf16[48,2304]{1,0:T(8,128)(2,1)S(1)}, u32[]{:S(2)}, u32[]{:S(2)}) collective-permute-start(bf16[48,2304]{1,0:T(8,128)(2,1)} %get-tuple-element.27), channel_id=1, source_target_pairs={{0,16},{16,32},{32,48},{48,64},{64,80},{80,96},{96,112},{112,0},{1... | collective-permute-start | bytes 663560 | tf_op jit(solution)/shard_map/ppermute | solution.py:37
  98.6 8.5 %collective-permute-start.17 = (bf16[48,2304]{1,0:T(8,128)(2,1)}, bf16[48,2304]{1,0:T(8,128)(2,1)S(1)}, u32[]{:S(2)}, u32[]{:S(2)}) collective-permute-start(bf16[48,2304]{1,0:T(8,128)(2,1)} %get-tuple-element.27), channel_id=1, source_target_pairs={{0,112},{16,0},{32,16},{48,32},{64,48},{80,64},{96,80},{112,96},{1... | collective-permute-start | bytes 663560 | tf_op jit(solution)/shard_map/ppermute | solution.py:41
  107.1 9.2 %collective-permute-start.21 = (bf16[48,2304]{1,0:T(8,128)(2,1)S(1)}, bf16[48,2304]{1,0:T(8,128)(2,1)S(1)}, u32[]{:S(2)}, u32[]{:S(2)}) collective-permute-start(bf16[48,2304]{1,0:T(8,128)(2,1)S(1)} %collective-permute-done.20), channel_id=1, source_target_pairs={{0,16},{16,32},{32,48},{48,64},{64,80},{80,96},{96,112},{112,0},{1... | collective-permute-start | bytes 663560 | tf_op jit(solution)/shard_map/ppermute | solution.py:37
  107.1 9.3 %collective-permute-start.18 = (bf16[48,2304]{1,0:T(8,128)(2,1)S(1)}, bf16[48,2304]{1,0:T(8,128)(2,1)S(1)}, u32[]{:S(2)}, u32[]{:S(2)}) collective-permute-start(bf16[48,2304]{1,0:T(8,128)(2,1)S(1)} %collective-permute-done.17), channel_id=1, source_target_pairs={{0,112},{16,0},{32,16},{48,32},{64,48},{80,64},{96,80},{112,96},{1... | collective-permute-start | bytes 663560 | tf_op jit(solution)/shard_map/ppermute | solution.py:41
  116.3 7.8 %collective-permute-start.22 = (bf16[48,2304]{1,0:T(8,128)(2,1)S(1)}, bf16[48,2304]{1,0:T(8,128)(2,1)S(1)}, u32[]{:S(2)}, u32[]{:S(2)}) collective-permute-start(bf16[48,2304]{1,0:T(8,128)(2,1)S(1)} %collective-permute-done.21), channel_id=1, source_target_pairs={{0,16},{16,32},{32,48},{48,64},{64,80},{80,96},{96,112},{112,0},{1... | collective-permute-start | bytes 663560 | tf_op jit(solution)/shard_map/ppermute | solution.py:37
  116.4 7.9 %collective-permute-start.19 = (bf16[48,2304]{1,0:T(8,128)(2,1)S(1)}, bf16[48,2304]{1,0:T(8,128)(2,1)S(1)}, u32[]{:S(2)}, u32[]{:S(2)}) collective-permute-start(bf16[48,2304]{1,0:T(8,128)(2,1)S(1)} %collective-permute-done.18), channel_id=1, source_target_pairs={{0,112},{16,0},{32,16},{48,32},{64,48},{80,64},{96,80},{112,96},{1... | collective-permute-start | bytes 663560 | tf_op jit(solution)/shard_map/ppermute | solution.py:41
  124.2 6.0 %collective-permute-start.23 = (bf16[48,1152]{1,0:T(8,128)(2,1)S(1)}, bf16[48,1152]{1,0:T(8,128)(2,1)S(1)}, u32[]{:S(2)}, u32[]{:S(2)}) collective-permute-start(bf16[48,1152]{1,0:T(8,128)(2,1)S(1)} %slice.199), channel_id=1, source_target_pairs={{0,16},{16,32},{32,48},{48,64},{64,80},{80,96},{96,112},{112,0},{1... | collective-permute-start | bytes 331784 | tf_op jit(solution)/shard_map/ppermute | solution.py:37
  124.3 5.9 %collective-permute-start.24 = (bf16[48,1152]{1,0:T(8,128)(2,1)S(1)}, bf16[48,1152]{1,0:T(8,128)(2,1)S(1)}, u32[]{:S(2)}, u32[]{:S(2)}) collective-permute-start(bf16[48,1152]{1,0:T(8,128)(2,1)S(1)} %slice.200), channel_id=1, source_target_pairs={{0,112},{16,0},{32,16},{48,32},{64,48},{80,64},{96,80},{112,96},{1... | collective-permute-start | bytes 331784 | tf_op jit(solution)/shard_map/ppermute | solution.py:41
  130.9 2.4 %copy-start.3 = (bf16[8,48,512]{2,1,0:T(8,128)(2,1)S(1)}, bf16[8,48,512]{2,1,0:T(8,128)(2,1)}, u32[]{:S(2)}) copy-start(bf16[8,48,512]{2,1,0:T(8,128)(2,1)} %copy-done.2) | copy-start | bytes 1179652
  133.0 1.5 copy-start.4
  134.5 2.7 %copy-start.6 = (bf16[1,256,1536]{2,1,0:T(8,128)(2,1)S(1)}, bf16[1,256,1536]{2,1,0:T(8,128)(2,1)}, u32[]{:S(2)}) copy-start(bf16[1,256,1536]{2,1,0:T(8,128)(2,1)} %param.20) | copy-start | bytes 2359300
  137.1 5.1 %collective-permute-start.13 = (bf16[256,256]{0,1:T(8,128)(2,1)S(1)}, bf16[256,256]{0,1:T(8,128)(2,1)S(1)}, u32[]{:S(2)}, u32[]{:S(2)}) collective-permute-start(bf16[256,256]{0,1:T(8,128)(2,1)S(1)} %slice.261), channel_id=1, source_target_pairs={{0,16},{16,0},{32,48},{48,32},{64,80},{80,64},{96,112},{112,96},{1... | collective-permute-start | bytes 393224 | tf_op jit(solution)/shard_map/ppermute | solution.py:98
  137.6 25.9 %copy-start.8 = (s32[512,8]{0,1:T(8,128)S(1)}, s32[512,8]{0,1:T(8,128)}, u32[]{:S(2)}) copy-start(s32[512,8]{0,1:T(8,128)} %copy-done.7) | copy-start | bytes 49156
  137.7 4.7 %collective-permute-start.25 = (bf16[384,128]{1,0:T(8,128)(2,1)S(1)}, bf16[384,128]{1,0:T(8,128)(2,1)S(1)}, u32[]{:S(2)}, u32[]{:S(2)}) collective-permute-start(bf16[384,128]{1,0:T(8,128)(2,1)S(1)} %dynamic-slice_convert_fusion), channel_id=1, source_target_pairs={{0,8},{8,0},{1,9},{9,1},{2,10},{10,2},{3,11},{11,3},{4,12},{12,4},... | collective-permute-start | bytes 294920 | tf_op jit(solution)/shard_map/ppermute | solution.py:224
  142.3 5.9 %collective-permute-start.14 = (bf16[128,256]{0,1:T(8,128)(2,1)S(1)}, bf16[128,256]{0,1:T(8,128)(2,1)S(1)}, u32[]{:S(2)}, u32[]{:S(2)}) collective-permute-start(bf16[128,256]{0,1:T(8,128)(2,1)S(1)} %slice.262), channel_id=1, source_target_pairs={{0,128},{16,144},{32,160},{48,176},{64,192},{80,208},{96,224},{112... | collective-permute-start | bytes 196616 | tf_op jit(solution)/shard_map/ppermute | solution.py:98
  148.2 10.0 %collective-permute-start.15 = (f32[64,256]{0,1:T(8,128)S(1)}, f32[64,256]{0,1:T(8,128)S(1)}, u32[]{:S(2)}, u32[]{:S(2)}) collective-permute-start(f32[64,256]{0,1:T(8,128)S(1)} %slice.194), channel_id=1, source_target_pairs={{0,32},{16,48},{32,0},{48,16},{64,96},{80,112},{96,64},{112,80},{1... | collective-permute-start | bytes 196616 | tf_op jit(solution)/shard_map/ppermute | solution.py:98
  152.8 10.7 %all-to-all-start.3 = ((bf16[8,48,128]{2,1,0:T(8,128)(2,1)}), bf16[8,48,128]{2,1,0:T(8,128)(2,1)S(1)}, u32[]{:S(2)}, u32[]{:S(2)}) async-start(bf16[8,48,128]{2,1,0:T(8,128)(2,1)} %fusion.57), calls=%async_computation.3 | async-start | bytes 196608 | tf_op jit(solution)/shard_map/all_to_all | solution.py:226
  158.4 9.6 %collective-permute-start.16 = (f32[32,256]{0,1:T(8,128)S(1)}, f32[32,256]{0,1:T(8,128)S(1)}, u32[]{:S(2)}, u32[]{:S(2)}) collective-permute-start(f32[32,256]{0,1:T(8,128)S(1)} %slice.196), channel_id=1, source_target_pairs={{0,64},{16,80},{32,96},{48,112},{64,0},{80,16},{96,32},{112,48},{1... | collective-permute-start | bytes 98312 | tf_op jit(solution)/shard_map/ppermute | solution.py:98

commit v4 on v3

--- a/solution.py
+++ b/solution.py
@@ -1,6 +1,10 @@
+import functools
+
 import jax
 import jax.numpy as jnp
 from jax import lax
+from jax.experimental import pallas as pl
+from jax.experimental.pallas import tpu as pltpu
 from jax.sharding import PartitionSpec as P
 
 CAP = 48
@@ -81,10 +85,9 @@
     blocks = [block] + [None] * (n - 1)
     onward = back = block
     for step in range(1, far):
-        if step in beside:
-            onward, back = after(onward, beside[step]), after(back, beside[step])
         onward, back = right(onward), left(back)
         blocks[n - step], blocks[step] = onward, back
+    onward, back = after(onward, beside), after(back, beside)
     blocks[far] = jnp.concatenate([right(onward[:, :cut]), left(back[:, cut:])], axis=1)
     return blocks
 
@@ -98,9 +101,8 @@
     return lax.ppermute(block, "ctx", [(c, c ^ mask) for c in range(lax.axis_size("ctx"))])
 
 
-def ctx_gather(key_rows, value_vector_rows):
-    block = jnp.concatenate([key_rows[:, 0, :], value_vector_rows[:, 0, :]], axis=1)
-    for mask in MASKS:
+def ctx_gather(block, masks):
+    for mask in masks:
         block = jnp.concatenate([block, swap(block, mask)], axis=0)
     return block
 
@@ -109,60 +111,123 @@
     return sum((index >> bit) % 2 * mask for bit, mask in enumerate(MASKS))
 
 
-def key_places(rows):
+def attend_body(own, ctx_size, me_ref, q_ref, g_ref, kv_ref, both_ref, dq_ref, score_ref, dprob_ref):
+    size = kv_ref.shape[1] // 2
+    lanes = q_ref.shape[0]
+    tokens = lanes // 2
+    scale = size ** (-0.5)
+    chunk = 8 * own
+    me = me_ref[0]
+    across = (((1,), (1,)), ((), ()))
+    ahead = lax.broadcasted_iota(jnp.int32, (own, lanes), 1) % tokens - lax.broadcasted_iota(
+        jnp.int32, (own, lanes), 0
+    )
+
+    def at(step):
+        return pl.ds(pl.multiple_of(step * chunk, chunk), chunk)
+
+    def score(step, top):
+        found = lax.dot_general(
+            kv_ref[at(step), :size], q_ref[...], across, preferred_element_type=F32
+        )
+        for part in range(8):
+            place = step * 8 + part
+            start = (me ^ mask_of(place % ctx_size)) * tokens + place // ctx_size * own
+            masked = jnp.where(
+                ahead >= start - me * tokens,
+                found[part * own : (part + 1) * own] * scale,
+                -jnp.inf,
+            )
+            score_ref[pl.ds(pl.multiple_of(place * own, own), own), :] = masked
+            top = jnp.maximum(top, masked)
+        return top
+
+    steps = kv_ref.shape[0] // chunk
+    top = lax.fori_loop(0, steps, score, jnp.full((own, lanes), -jnp.inf, F32))
+    top = jnp.max(top, axis=0, keepdims=True)
+
+    def weigh(step, sums):
+        norm, delta = sums
+        prob = jnp.exp(score_ref[at(step), :] - top)
+        dprob = lax.dot_general(
+            kv_ref[at(step), size:], g_ref[...], across, preferred_element_type=F32
+        )
+        score_ref[at(step), :] = prob
+        dprob_ref[at(step), :] = dprob
+        norm = norm + jnp.sum(prob.reshape(-1, 8, lanes), axis=0)
+        delta = delta + jnp.sum((prob * dprob).reshape(-1, 8, lanes), axis=0)
+        return norm, delta
+
+    zero = jnp.zeros((8, lanes), F32)
+    norm, delta = lax.fori_loop(0, steps, weigh, (zero, zero))
+    inverse = 1.0 / jnp.sum(norm, axis=0, keepdims=True)
+    delta = jnp.sum(delta, axis=0, keepdims=True) * inverse
+
+    def back(step, total):
+        prob = score_ref[at(step), :] * inverse
+        both_ref[at(step), size:] = jnp.dot(
+            prob.astype(BF), g_ref[...], preferred_element_type=F32
+        ).astype(BF)
+        dscore = (prob * (dprob_ref[at(step), :] - delta)).astype(BF)
+        both_ref[at(step), :size] = jnp.dot(
+            dscore, q_ref[...], preferred_element_type=F32
+        ).astype(BF)
+        return total + lax.dot_general(
+            kv_ref[at(step), :size], dscore, (((0,), (0,)), ((), ())), preferred_element_type=F32
+        )
+
+    total = lax.fori_loop(0, steps, back, jnp.zeros((size, lanes), F32))
+    dq_ref[...] = (total * scale).T.astype(BF)
+
+
+def attend(queries, grad_attn, flat):
+    tok_rows, heads, size = queries.shape
+    lanes = tok_rows * heads
     ctx_size, exp_size = lax.axis_size("ctx"), lax.axis_size("exp")
-    own = rows // (ctx_size * exp_size)
-    place = jnp.arange(rows)
-    of_ctx = lax.axis_index("ctx") ^ mask_of(place // own % ctx_size)
-    return (of_ctx * exp_size + place // (own * ctx_size)) * own + place % own
-
-
-def masked_scores(queries, flat):
-    tok_rows, _, head_dim = queries.shape
-    query_pos = lax.axis_index("ctx") * tok_rows + jnp.arange(tok_rows)
-    allowed = key_places(flat.shape[0])[None, :] <= query_pos[:, None]
-    scores = jnp.einsum("phd,td->hpt", queries, flat[:, :head_dim], preferred_element_type=F32)
-    return jnp.where(allowed[None], scores * head_dim ** (-0.5), -jnp.inf)
-
-
-def value_side(scores, flat, grad_attn):
-    value_flat = flat[:, grad_attn.shape[2] :]
-    probs_full = jax.nn.softmax(scores, axis=-1)
-    probs_low = probs_full.astype(BF)
-    attn_out = jnp.einsum("hpt,td->phd", probs_low, value_flat, preferred_element_type=F32)
-    row_delta = jnp.sum(grad_attn.astype(F32) * attn_out, axis=-1)
-    value_grad = jnp.einsum("hpt,phd->td", probs_low, grad_attn, preferred_element_type=F32)
-    return probs_full, row_delta, value_grad.astype(BF)
-
-
-def key_side(probs_full, row_delta, queries, flat, grad_attn):
-    head_dim = queries.shape[2]
-    grad_prob = jnp.einsum(
-        "phd,td->hpt", grad_attn, flat[:, head_dim:], preferred_element_type=F32
-    )
-    dscore = (probs_full * (grad_prob - jnp.transpose(row_delta)[:, :, None])).astype(BF)
-    key_grad = jnp.einsum("hpt,phd->td", dscore, queries, preferred_element_type=F32)
-    return dscore, key_grad.astype(BF)
-
-
-def query_side(dscore, flat):
-    head_dim = flat.shape[1] // 2
-    grad_query = jnp.einsum("hpt,td->phd", dscore, flat[:, :head_dim], preferred_element_type=F32)
-    return (grad_query * head_dim ** (-0.5)).astype(BF)
-
-
-def to_owners(both):
-    head_dim = both.shape[1] // 2
-    for mask in reversed(MASKS):
+    keys = flat.shape[0]
+    own = keys // (ctx_size * exp_size)
+    vmem = pl.BlockSpec(memory_space=pltpu.VMEM)
+    both, grad_query = pl.pallas_call(
+        functools.partial(attend_body, own, ctx_size),
+        out_shape=(
+            jax.ShapeDtypeStruct((keys, 2 * size), BF),
+            jax.ShapeDtypeStruct((lanes, size), BF),
+        ),
+        in_specs=[pl.BlockSpec(memory_space=pltpu.SMEM), vmem, vmem, vmem],
+        out_specs=(vmem, vmem),
+        scratch_shapes=[pltpu.VMEM((keys, lanes), F32), pltpu.VMEM((keys, lanes), F32)],
+        compiler_params=pltpu.CompilerParams(vmem_limit_bytes=32 * 2**20),
+        cost_estimate=pl.CostEstimate(
+            flops=10 * keys * lanes * size,
+            bytes_accessed=8 * keys * size,
+            transcendentals=keys * lanes,
+        ),
+        name="attention_backward",
+    )(
+        lax.axis_index("ctx").astype(jnp.int32).reshape(1),
+        jnp.swapaxes(queries, 0, 1).reshape(lanes, size),
+        jnp.swapaxes(grad_attn, 0, 1).reshape(lanes, size),
+        flat,
+    )
+    return both, jnp.swapaxes(grad_query.reshape(heads, tok_rows, size), 0, 1)
+
+
+def ctx_sum(both, masks):
+    for mask in reversed(masks):
         half = both.shape[0] // 2
         sent = both[half:].astype(BF if half >= both.shape[1] // 2 else F32)
         both = both[:half] + swap(sent, mask).astype(F32)
+    return both
+
+
+def own_grads(both):
+    head_dim = both.shape[1] // 2
     grad_key = (both[:, :head_dim] * head_dim ** (-0.5)).astype(BF)[:, None, :]
     grad_value = both[:, head_dim:].astype(BF)[:, None, :]
     return grad_key, grad_value
 
 
-def select(moe_input, moe_grad, expert_ids, router_weight):
+def select(moe_input, moe_grad, expert_ids, router_weight, near):
     width = moe_input.shape[1]
     exp_size = lax.axis_size("exp")
     matches = expert_ids[:, :, None] == jnp.arange(exp_size)[None, None, :]
@@ -178,6 +243,7 @@
     picked = jnp.einsum("bs,bd->sd", placed_low, rows, preferred_element_type=F32)
     scaled = picked[:, width:] * slot_weight.reshape(-1, 1)
     sent = jnp.concatenate([picked[:, :width].astype(BF), scaled.astype(BF)], axis=1)
+    sent = after(sent, near)
     got = lax.all_to_all(sent.reshape(exp_size, CAP, 2 * width), "exp", 0, 0, tiled=True)
     return placed_low, got
 
@@ -247,30 +313,28 @@
     down_weight,
 ):
     exp_size = lax.axis_size("exp")
-    near = ctx_gather(key_rows, value_vector_rows)
-    placed_low, got = select(moe_input, moe_grad, expert_ids, router_weight)
+    pair = jnp.concatenate([key_rows[:, 0, :], value_vector_rows[:, 0, :]], axis=1)
+    near = ctx_gather(pair, MASKS[:2])
+    placed_low, got = select(moe_input, moe_grad, expert_ids, router_weight, near)
+    near = ctx_gather(near, MASKS[2:])
     flat = spread(after(near, got), "exp").reshape(-1, near.shape[1])
     input_rows, grad_rows, gate_mat, up_mat, parts = project(
         got, gate_weight, up_weight, down_weight
     )
-    onward, back = sum_step(parts, 0, *sum_start(parts))
+    onward, back = sum_start(parts)
+    onward, back = sum_step(parts, 0, after(onward, near), after(back, near))
     onward, back = sum_step(parts, 1, onward, back)
-    scores = masked_scores(queries, after(flat, onward, back))
     onward, back = sum_step(parts, 2, onward, back)
-    probs_full, row_delta, value_grad = value_side(after(scores, onward, back), flat, grad_attn)
-    onward, back = sum_step(parts, 3, after(onward, scores), after(back, scores))
+    both, grad_query = attend(queries, grad_attn, after(flat, onward, back))
+    onward, back = sum_step(parts, 3, after(onward, flat), after(back, flat))
     total = onward.astype(F32) + back.astype(F32) + parts[0].astype(F32)
-    dscore, key_grad = key_side(
-        probs_full, after(row_delta, total), queries, flat, grad_attn
-    )
-    block = act_block(after(total, value_grad))
-    grad_query = query_side(dscore, after(flat, block))
-    both = jnp.concatenate([key_grad, value_grad], axis=1)
-    blocks = ring_gather(block, {1: both, 2: grad_query})
+    block = act_block(after(total, both))
     both = gather_sum(both.reshape((exp_size, -1) + both.shape[1:]), "exp")
+    blocks = ring_gather(block, both)
+    both = ctx_sum(both, MASKS[3:])
     full = after(jnp.concatenate(blocks, axis=0), both)
     of_experts = finish(full, input_rows, grad_rows, gate_mat, up_mat, placed_low)
-    grad_key, grad_value = to_owners(both)
+    grad_key, grad_value = own_grads(ctx_sum(both, MASKS[:3]))
     return (grad_query, grad_key, grad_value) + of_experts
 
 

time: 171 us -> 167 us (0.977)
  Pallas kernels: 0 us -> 14.9 us
  matrix products: 22.1 us -> 7.6 us
  waiting for transfers between devices: 47.7 us -> 58.9 us
  other arithmetic: 19.3 us -> 11.8 us
  local copies, waits for them, and re-layouts: 12.4 us -> 6.88 us
  starting transfers between devices: 66.6 us -> 64.6 us
    pallas_call x0 -> x1, Pallas kernels: none -> 14.9 us  [attend(): pl.pallas_call(functools.partial(attend_body, own, ctx_size), out_shape=(...]
    dot_general x6 -> x0, matrix products: 13.5 us -> none  [the longest x1 3.25 us: query_side(): jnp.einsum('hpt,td->phd', dscore, flat[:, :head_dim], preferred_element_t...]
    ppermute x8, waiting for transfers between devices: 14.9 us -> 20.9 us  [right(): return lax.ppermute(block, 'ctx', z_shift(1))]
    ppermute x8, starting transfers between devices: 18.3 us -> 24.1 us  [left(): return lax.ppermute(block, 'ctx', z_shift(-1))]
    unnamed x37 -> x52, local copies, waits for them, and re-layouts: 8.01 us -> 3.46 us
    sub x1 -> x0, other arithmetic: 4.4 us -> none  [value_side(): probs_full = jax.nn.softmax(scores, axis=-1)]
    ppermute x1, waiting for transfers between devices: 0.01 us -> 3.4 us  [opposite(): lax.ppermute(block, 'ctx', [(c, (c + n // X_HI) % n) for c in range(n)])]
    ppermute x8, starting transfers between devices: 5.54 us -> 2.37 us  [right(): return lax.ppermute(block, 'ctx', z_shift(1))]
  transfers between devices with their start and end apart: 30 -> 30, of which waited for: 16 -> 17; matrix products, arithmetic and copies ran while one was open for 25% -> 11% of each run, Pallas kernels for 0% -> 9%
where the time goes in v4:
time: 167 us; the launch traced here: 166 us
  starting transfers between devices  64.6 us (39%)
  waiting for transfers between devices  58.9 us (35%)
  Pallas kernels  14.9 us (9%)
  other arithmetic  11.8 us (7%)
  matrix products  7.6 us (5%)
  local copies, waits for them, and re-layouts  6.88 us (4%)
    ppermute x8, starting transfers between devices, left(): return lax.ppermute(block, 'ctx', z_shift(-1))  24.1 us
    ppermute x8, waiting for transfers between devices, right(): return lax.ppermute(block, 'ctx', z_shift(1))  20.9 us
    ppermute x8, waiting for transfers between devices, swap(): lax.ppermute(block, 'ctx', [(c, c ^ mask) for c in range(lax.axis_size('c...  17.9 us
    pallas_call x1, Pallas kernels, attend(): pl.pallas_call(functools.partial(attend_body, own, ctx_size), out_shape=(...  14.9 us
    ppermute x8, starting transfers between devices, swap(): lax.ppermute(block, 'ctx', [(c, c ^ mask) for c in range(lax.axis_size('c...  14.8 us
    all_to_all x1, waiting for transfers between devices, spread(): return lax.all_to_all(copies, axis, 0, 0, tiled=True)  10.8 us
    all_to_all x1, starting transfers between devices, select(): lax.all_to_all(sent.reshape(exp_size, CAP, 2 * width), 'exp', 0, 0, tiled...  5.93 us
    all_to_all x1, starting transfers between devices, finish(): back_rows = lax.all_to_all(mine, 'exp', 0, 0, tiled=True)  5.88 us
  transfers between devices with their start and end apart: 30, of which 17 were waited for; matrix products, arithmetic and copies ran while one was open for 11% of the time, Pallas kernels for 9%

profile of v4, /device:TPU:2, one launch (start us, length us, event | category | flops | bytes accessed | tf_op | source)
XLA Modules:
  0.0 165.9 jit_solution(11378397225699367321)
XLA Ops:
  0.7 0.8 pad_maximum_fusion.10
  1.5 7.2 %collective-permute-start = (bf16[32,256]{1,0:T(8,128)(2,1)S(1)}, bf16[32,256]{1,0:T(8,128)(2,1)S(1)}, u32[]{:S(2)}, u32[]{:S(2)}) collective-permute-start(bf16[32,256]{1,0:T(8,128)(2,1)S(1)} %get-tuple-element.48), channel_id=1, source_target_pairs={{0,64},{16,80},{32,96},{48,112},{64,0},{80,16},{96,32},{112,48},{1... | collective-permute-start | bytes 49160 | tf_op jit(solution)/shard_map/ppermute | solution.py:101
  8.6 0.7 convert_reduce_fusion.1
  9.4 1.1 reduce-window.6
  11.0 0.8 select_reduce_fusion.1
  12.3 1.4 fusion.8
  13.9 1.6 collective-permute-start.1
  15.5 0.8 pad_maximum_fusion
  16.3 2.6 %collective-permute-done.1 = bf16[64,256]{1,0:T(8,128)(2,1)S(1)} collective-permute-done((bf16[64,256]{1,0:T(8,128)(2,1)S(1)}, bf16[64,256]{1,0:T(8,128)(2,1)S(1)}, u32[]{:S(2)}, u32[]{:S(2)}) %collective-permute-start.1) | collective-permute-done | bytes 32800 | tf_op jit(solution)/shard_map/ppermute | solution.py:101
  18.8 2.2 %collective-permute-start.2 = (bf16[128,256]{1,0:T(8,128)(2,1)S(1)}, bf16[128,256]{1,0:T(8,128)(2,1)S(1)}, u32[]{:S(2)}, u32[]{:S(2)}) collective-permute-start(bf16[128,256]{1,0:T(8,128)(2,1)S(1)} %pad_maximum_fusion.8), channel_id=1, source_target_pairs={{0,128},{16,144},{32,160},{48,176},{64,192},{80,208},{96,224},{112... | collective-permute-start | bytes 196616 | tf_op jit(solution)/shard_map/ppermute | solution.py:101
  21.1 5.9 %all-to-all-start = ((bf16[8,48,512]{2,1,0:T(8,128)(2,1)}), bf16[8,48,512]{2,1,0:T(8,128)(2,1)S(1)}, u32[]{:S(2)}, u32[]{:S(2)}) async-start(bf16[8,48,512]{2,1,0:T(8,128)(2,1)} %bitcast.13), calls=%async_computation | async-start | bytes 786432 | tf_op jit(solution)/shard_map/all_to_all | solution.py:247
  27.0 1.1 collective-permute-start.3
  28.1 3.9 %collective-permute-done.3 = bf16[256,256]{1,0:T(8,128)(2,1)S(1)} collective-permute-done((bf16[256,256]{1,0:T(8,128)(2,1)S(1)}, bf16[256,256]{1,0:T(8,128)(2,1)S(1)}, u32[]{:S(2)}, u32[]{:S(2)}) %collective-permute-start.3) | collective-permute-done | bytes 131104 | tf_op jit(solution)/shard_map/ppermute | solution.py:101
  32.1 1.7 %all-to-all-done = bf16[8,48,512]{2,1,0:T(8,128)(2,1)S(1)} async-done(((bf16[8,48,512]{2,1,0:T(8,128)(2,1)}), bf16[8,48,512]{2,1,0:T(8,128)(2,1)S(1)}, u32[]{:S(2)}, u32[]{:S(2)}) %all-to-all-start) | async-done | bytes 393248 | tf_op jit(solution)/shard_map/all_to_all | solution.py:247
  34.0 0.4 convolution_convert_fusion
  35.1 1.1 collective-permute-start.4
  36.2 2.2 %collective-permute-start.7 = (bf16[48,1152]{1,0:T(8,128)(2,1)S(1)}, bf16[48,1152]{1,0:T(8,128)(2,1)S(1)}, u32[]{:S(2)}, u32[]{:S(2)}) collective-permute-start(bf16[48,1152]{1,0:T(8,128)(2,1)S(1)} %get-tuple-element.23), channel_id=1, source_target_pairs={{0,112},{16,0},{32,16},{48,32},{64,48},{80,64},{96,80},{112,96},{1... | collective-permute-start | bytes 331784 | tf_op jit(solution)/shard_map/ppermute | solution.py:45
  38.4 3.2 %collective-permute-done.4 = bf16[48,1152]{1,0:T(8,128)(2,1)S(1)} collective-permute-done((bf16[48,1152]{1,0:T(8,128)(2,1)S(1)}, bf16[48,1152]{1,0:T(8,128)(2,1)S(1)}, u32[]{:S(2)}, u32[]{:S(2)}) %collective-permute-start.4) | collective-permute-done | bytes 110624 | tf_op jit(solution)/shard_map/ppermute | solution.py:41
  41.6 0.5 collective-permute-done.7
  42.3 1.1 collective-permute-start.5
  43.4 2.2 %collective-permute-start.8 = (bf16[48,2304]{1,0:T(8,128)(2,1)S(1)}, bf16[48,2304]{1,0:T(8,128)(2,1)}, u32[]{:S(2)}, u32[]{:S(2)}) collective-permute-start(bf16[48,2304]{1,0:T(8,128)(2,1)S(1)} %get-tuple-element.37), channel_id=1, source_target_pairs={{0,112},{16,0},{32,16},{48,32},{64,48},{80,64},{96,80},{112,96},{1... | collective-permute-start | bytes 663560 | tf_op jit(solution)/shard_map/ppermute | solution.py:45
  45.6 1.5 broadcast_in_dim.56
  47.1 4.7 %all-to-all-start.1 = ((bf16[8,512,256]{2,1,0:T(8,128)(2,1)}), bf16[8,512,256]{2,1,0:T(8,128)(2,1)S(1)}, u32[]{:S(2)}, u32[]{:S(2)}) async-start(bf16[8,512,256]{2,1,0:T(8,128)(2,1)} %broadcast_in_dim.56), calls=%async_computation.1 | async-start | bytes 4194304 | tf_op jit(solution)/shard_map/all_to_all | solution.py:28
  51.8 1.4 add_convert_fusion.1
  53.3 3.2 %collective-permute-start.9 = (bf16[48,2304]{1,0:T(8,128)(2,1)S(1)}, bf16[48,2304]{1,0:T(8,128)(2,1)S(1)}, u32[]{:S(2)}, u32[]{:S(2)}) collective-permute-start(bf16[48,2304]{1,0:T(8,128)(2,1)S(1)} %get-tuple-element.35), channel_id=1, source_target_pairs={{0,112},{16,0},{32,16},{48,32},{64,48},{80,64},{96,80},{112,96},{1... | collective-permute-start | bytes 663560 | tf_op jit(solution)/shard_map/ppermute | solution.py:45
  56.6 3.8 %collective-permute-done.6 = bf16[48,2304]{1,0:T(8,128)(2,1)S(1)} collective-permute-done((bf16[48,2304]{1,0:T(8,128)(2,1)S(1)}, bf16[48,2304]{1,0:T(8,128)(2,1)S(1)}, u32[]{:S(2)}, u32[]{:S(2)}) %collective-permute-start.6) | collective-permute-done | bytes 221216 | tf_op jit(solution)/shard_map/ppermute | solution.py:41
  60.4 0.8 add_convert_fusion
  61.2 10.8 %all-to-all-done.1 = bf16[8,512,256]{2,1,0:T(8,128)(2,1)S(1)} async-done(((bf16[8,512,256]{2,1,0:T(8,128)(2,1)}), bf16[8,512,256]{2,1,0:T(8,128)(2,1)S(1)}, u32[]{:S(2)}, u32[]{:S(2)}) %all-to-all-start.1) | async-done | bytes 2097184 | tf_op jit(solution)/shard_map/all_to_all | solution.py:28
  72.1 3.2 %collective-permute-start.15 = (bf16[48,2304]{1,0:T(8,128)(2,1)S(1)}, bf16[48,2304]{1,0:T(8,128)(2,1)S(1)}, u32[]{:S(2)}, u32[]{:S(2)}) collective-permute-start(bf16[48,2304]{1,0:T(8,128)(2,1)S(1)} %get-tuple-element.28), channel_id=1, source_target_pairs={{0,112},{16,0},{32,16},{48,32},{64,48},{80,64},{96,80},{112,96},{1... | collective-permute-start | bytes 663560 | tf_op jit(solution)/shard_map/ppermute | solution.py:45
  75.3 14.9 %attention_backward.1 = (bf16[4096,256]{1,0:T(8,128)(2,1)}, bf16[512,128]{1,0:T(8,128)(2,1)S(1)}) custom-call(s32[1]{0:T(128)} %bitcast.me_ref, bf16[512,128]{1,0:T(8,128)(2,1)S(1)} %bitcast.60, bf16[512,128]{1,0:T(8,128)(2,1)S(1)} %bitcast.61, bf16[4096,256]{1,0:T(8,128)(2,1)S(1)} %bitcast.58), custom_call_target="tpu_custom_call" | custom-call | flops 2684354560 | bytes 4194304 | tf_op jit(solution)/shard_map/attention_backward/pallas_call | solution.py:190
  90.3 0.7 convert_element_type.161
  91.1 1.4 collective-permute-start.16
  92.5 5.4 %all-to-all-start.2 = ((bf16[8,512,256]{2,1,0:T(8,128)(2,1)}), bf16[8,512,256]{2,1,0:T(8,128)(2,1)S(1)}, u32[]{:S(2)}, u32[]{:S(2)}) async-start(bf16[8,512,256]{2,1,0:T(8,128)(2,1)} %bitcast.21), calls=%async_computation.2 | async-start | bytes 4194304 | tf_op jit(solution)/shard_map/all_to_all | solution.py:32
  97.8 3.4 %collective-permute-done.16 = bf16[48,2304]{1,0:T(8,128)(2,1)} collective-permute-done((bf16[48,2304]{1,0:T(8,128)(2,1)}, bf16[48,2304]{1,0:T(8,128)(2,1)}, u32[]{:S(2)}, u32[]{:S(2)}) %collective-permute-start.16) | collective-permute-done | bytes 221216 | tf_op jit(solution)/shard_map/ppermute | solution.py:50
  101.2 1.0 convert_add_fusion
  102.3 0.8 pad_maximum_fusion.3
  103.1 3.2 %collective-permute-start.17 = (bf16[48,2304]{1,0:T(8,128)(2,1)}, bf16[48,2304]{1,0:T(8,128)(2,1)S(1)}, u32[]{:S(2)}, u32[]{:S(2)}) collective-permute-start(bf16[48,2304]{1,0:T(8,128)(2,1)} %get-tuple-element.46), channel_id=1, source_target_pairs={{0,112},{16,0},{32,16},{48,32},{64,48},{80,64},{96,80},{112,96},{1... | collective-permute-start | bytes 663560 | tf_op jit(solution)/shard_map/ppermute | solution.py:45
  106.3 0.8 copy.32
  107.1 5.4 %collective-permute-done.20 = bf16[48,2304]{1,0:T(8,128)(2,1)S(1)} collective-permute-done((bf16[48,2304]{1,0:T(8,128)(2,1)}, bf16[48,2304]{1,0:T(8,128)(2,1)S(1)}, u32[]{:S(2)}, u32[]{:S(2)}) %collective-permute-start.20) | collective-permute-done | bytes 221216 | tf_op jit(solution)/shard_map/ppermute | solution.py:41
  112.5 3.4 %collective-permute-start.18 = (bf16[48,2304]{1,0:T(8,128)(2,1)S(1)}, bf16[48,2304]{1,0:T(8,128)(2,1)}, u32[]{:S(2)}, u32[]{:S(2)}) collective-permute-start(bf16[48,2304]{1,0:T(8,128)(2,1)S(1)} %collective-permute-done.17), channel_id=1, source_target_pairs={{0,112},{16,0},{32,16},{48,32},{64,48},{80,64},{96,80},{112,96},{1... | collective-permute-start | bytes 663560 | tf_op jit(solution)/shard_map/ppermute | solution.py:45
  115.9 0.7 constant_dynamic-update-slice_fusion.10
  116.6 3.9 %collective-permute-done.21 = bf16[48,2304]{1,0:T(8,128)(2,1)} collective-permute-done((bf16[48,2304]{1,0:T(8,128)(2,1)S(1)}, bf16[48,2304]{1,0:T(8,128)(2,1)}, u32[]{:S(2)}, u32[]{:S(2)}) %collective-permute-start.21) | collective-permute-done | bytes 221216 | tf_op jit(solution)/shard_map/ppermute | solution.py:41
  120.5 3.2 %collective-permute-start.19 = (bf16[48,2304]{1,0:T(8,128)(2,1)}, bf16[48,2304]{1,0:T(8,128)(2,1)S(1)}, u32[]{:S(2)}, u32[]{:S(2)}) collective-permute-start(bf16[48,2304]{1,0:T(8,128)(2,1)} %collective-permute-done.18), channel_id=1, source_target_pairs={{0,112},{16,0},{32,16},{48,32},{64,48},{80,64},{96,80},{112,96},{1... | collective-permute-start | bytes 663560 | tf_op jit(solution)/shard_map/ppermute | solution.py:45
  123.7 1.7 %constant_dynamic-update-slice_fusion.9 = bf16[384,2304]{1,0:T(8,128)(2,1)} fusion(bf16[384,2304]{1,0:T(8,128)(2,1)} %constant_dynamic-update-slice_fusion.10, bf16[48,2304]{1,0:T(8,128)(2,1)} %collective-permute-done.18), kind=kLoop, calls=%fused_computation.107 | loop fusion | bytes 442368
  125.7 2.1 %collective-permute-done.22 = bf16[48,2304]{1,0:T(8,128)(2,1)S(1)} collective-permute-done((bf16[48,2304]{1,0:T(8,128)(2,1)}, bf16[48,2304]{1,0:T(8,128)(2,1)S(1)}, u32[]{:S(2)}, u32[]{:S(2)}) %collective-permute-start.22) | collective-permute-done | bytes 221216 | tf_op jit(solution)/shard_map/ppermute | solution.py:41
  128.0 3.3 %collective-permute-start.24 = (bf16[48,1152]{1,0:T(8,128)(2,1)S(1)}, bf16[48,1152]{1,0:T(8,128)(2,1)S(1)}, u32[]{:S(2)}, u32[]{:S(2)}) collective-permute-start(bf16[48,1152]{1,0:T(8,128)(2,1)S(1)} %slice.163), channel_id=1, source_target_pairs={{0,112},{16,0},{32,16},{48,32},{64,48},{80,64},{96,80},{112,96},{1... | collective-permute-start | bytes 331784 | tf_op jit(solution)/shard_map/ppermute | solution.py:45
  131.4 2.5 %collective-permute-done.23 = bf16[48,1152]{1,0:T(8,128)(2,1)S(1)} collective-permute-done((bf16[48,1152]{1,0:T(8,128)(2,1)S(1)}, bf16[48,1152]{1,0:T(8,128)(2,1)S(1)}, u32[]{:S(2)}, u32[]{:S(2)}) %collective-permute-start.23) | collective-permute-done | bytes 110624 | tf_op jit(solution)/shard_map/ppermute | solution.py:41
  134.0 1.0 constant_dynamic-update-slice_fusion.6
  134.9 1.4 collective-permute-done.10
  136.4 1.2 fusion.2
  137.6 1.1 fusion.1
  138.7 1.1 fusion
  140.3 0.4 convolution_add_fusion
  140.6 1.5 collective-permute-start.11
  142.2 4.2 %collective-permute-done.11 = bf16[128,256]{1,0:T(8,128)(2,1)S(1)} collective-permute-done((bf16[128,256]{1,0:T(8,128)(2,1)S(1)}, bf16[128,256]{1,0:T(8,128)(2,1)S(1)}, u32[]{:S(2)}, u32[]{:S(2)}) %collective-permute-start.11) | collective-permute-done | bytes 65568 | tf_op jit(solution)/shard_map/ppermute | solution.py:101
  146.7 5.3 %collective-permute-done.12 = f32[64,256]{1,0:T(8,128)S(1)} collective-permute-done((f32[64,256]{1,0:T(8,128)S(1)}, f32[64,256]{1,0:T(8,128)S(1)}, u32[]{:S(2)}, u32[]{:S(2)}) %collective-permute-start.12) | collective-permute-done | bytes 65568 | tf_op jit(solution)/shard_map/ppermute | solution.py:101
  151.9 1.0 collective-permute-start.13
  153.0 0.7 fusion.43
  153.7 5.9 %all-to-all-start.3 = ((bf16[8,48,128]{2,1,0:T(8,128)(2,1)}), bf16[8,48,128]{2,1,0:T(8,128)(2,1)S(1)}, u32[]{:S(2)}, u32[]{:S(2)}) async-start(bf16[8,48,128]{2,1,0:T(8,128)(2,1)} %fusion.43), calls=%async_computation.3 | async-start | bytes 196608 | tf_op jit(solution)/shard_map/all_to_all | solution.py:292
  159.5 0.4 collective-permute-done.13
  160.0 0.6 fusion.45
  160.6 0.6 fusion.46
  161.2 3.6 %all-to-all-done.3 = bf16[8,48,128]{2,1,0:T(8,128)(2,1)S(1)} async-done(((bf16[8,48,128]{2,1,0:T(8,128)(2,1)}), bf16[8,48,128]{2,1,0:T(8,128)(2,1)S(1)}, u32[]{:S(2)}, u32[]{:S(2)}) %all-to-all-start.3) | async-done | bytes 98336 | tf_op jit(solution)/shard_map/all_to_all | solution.py:292
  164.8 1.1 fusion.3
  (113 shorter events, 3.7 us)
Async XLA Ops:
  0.6 34.1 %copy-start = (bf16[1,256,1536]{2,1,0:T(8,128)(2,1)S(1)}, bf16[1,256,1536]{2,1,0:T(8,128)(2,1)}, u32[]{:S(2)}) copy-start(bf16[1,256,1536]{2,1,0:T(8,128)(2,1)} %param.19) | copy-start | bytes 2359300
  0.6 13.2 %copy-start.21 = (bf16[32,1,128]{2,0,1:T(8,128)(2,1)S(1)}, bf16[32,1,128]{2,0,1:T(8,128)(2,1)}, u32[]{:S(2)}) copy-start(bf16[32,1,128]{2,0,1:T(8,128)(2,1)} %param.12) | copy-start | bytes 24580
  0.7 13.2 %copy-start.20 = (bf16[32,1,128]{2,0,1:T(8,128)(2,1)S(1)}, bf16[32,1,128]{2,0,1:T(8,128)(2,1)}, u32[]{:S(2)}) copy-start(bf16[32,1,128]{2,0,1:T(8,128)(2,1)} %param.13) | copy-start | bytes 24580
  1.5 12.4 %collective-permute-start = (bf16[32,256]{1,0:T(8,128)(2,1)S(1)}, bf16[32,256]{1,0:T(8,128)(2,1)S(1)}, u32[]{:S(2)}, u32[]{:S(2)}) collective-permute-start(bf16[32,256]{1,0:T(8,128)(2,1)S(1)} %get-tuple-element.48), channel_id=1, source_target_pairs={{0,64},{16,80},{32,96},{48,112},{64,0},{80,16},{96,32},{112,48},{1... | collective-permute-start | bytes 49160 | tf_op jit(solution)/shard_map/ppermute | solution.py:101
  10.9 3.0 %copy-start.16 = (s32[512,8]{0,1:T(8,128)}, s32[512,8]{0,1:T(8,128)S(1)}, u32[]{:S(2)}) copy-start(s32[512,8]{0,1:T(8,128)S(1)} %bitcast_subtract_fusion) | copy-start | bytes 49156
  13.9 20.1 %copy-start.15 = (bf16[1,1536,256]{2,1,0:T(8,128)(2,1)S(1)}, bf16[1,1536,256]{2,1,0:T(8,128)(2,1)}, u32[]{:S(2)}) copy-start(bf16[1,1536,256]{2,1,0:T(8,128)(2,1)} %param.21) | copy-start | bytes 2359300
  13.9 4.9 %collective-permute-start.1 = (bf16[64,256]{1,0:T(8,128)(2,1)S(1)}, bf16[64,256]{1,0:T(8,128)(2,1)S(1)}, u32[]{:S(2)}, u32[]{:S(2)}) collective-permute-start(bf16[64,256]{1,0:T(8,128)(2,1)S(1)} %pad_maximum_fusion.9), channel_id=1, source_target_pairs={{0,32},{16,48},{32,0},{48,16},{64,96},{80,112},{96,64},{112,80},{1... | collective-permute-start | bytes 98312 | tf_op jit(solution)/shard_map/ppermute | solution.py:101
  18.8 15.5 %copy-start.13 = (bf16[1,256,1536]{2,1,0:T(8,128)(2,1)S(1)}, bf16[1,256,1536]{2,1,0:T(8,128)(2,1)}, u32[]{:S(2)}) copy-start(bf16[1,256,1536]{2,1,0:T(8,128)(2,1)} %param.20) | copy-start | bytes 2359300
  18.8 8.2 %collective-permute-start.2 = (bf16[128,256]{1,0:T(8,128)(2,1)S(1)}, bf16[128,256]{1,0:T(8,128)(2,1)S(1)}, u32[]{:S(2)}, u32[]{:S(2)}) collective-permute-start(bf16[128,256]{1,0:T(8,128)(2,1)S(1)} %pad_maximum_fusion.8), channel_id=1, source_target_pairs={{0,128},{16,144},{32,160},{48,176},{64,192},{80,208},{96,224},{112... | collective-permute-start | bytes 196616 | tf_op jit(solution)/shard_map/ppermute | solution.py:101
  21.1 12.8 %all-to-all-start = ((bf16[8,48,512]{2,1,0:T(8,128)(2,1)}), bf16[8,48,512]{2,1,0:T(8,128)(2,1)S(1)}, u32[]{:S(2)}, u32[]{:S(2)}) async-start(bf16[8,48,512]{2,1,0:T(8,128)(2,1)} %bitcast.13), calls=%async_computation | async-start | bytes 786432 | tf_op jit(solution)/shard_map/all_to_all | solution.py:247
  27.0 5.1 %collective-permute-start.3 = (bf16[256,256]{1,0:T(8,128)(2,1)S(1)}, bf16[256,256]{1,0:T(8,128)(2,1)S(1)}, u32[]{:S(2)}, u32[]{:S(2)}) collective-permute-start(bf16[256,256]{1,0:T(8,128)(2,1)S(1)} %pad_maximum_fusion.4), channel_id=1, source_target_pairs={{0,16},{16,0},{32,48},{48,32},{64,80},{80,64},{96,112},{112,96},{1... | collective-permute-start | bytes 393224 | tf_op jit(solution)/shard_map/ppermute | solution.py:101
  34.0 1.1 copy-start.10
  34.4 7.8 %copy-start.1 = (bf16[384,768]{1,0:T(8,128)(2,1)}, bf16[384,768]{1,0:T(8,128)(2,1)S(1)}, u32[]{:S(2)}) copy-start(bf16[384,768]{1,0:T(8,128)(2,1)S(1)} %convolution_convert_fusion) | copy-start | bytes 1769476
  34.7 7.5 %copy-start.4 = (bf16[384,768]{1,0:T(8,128)(2,1)}, bf16[384,768]{1,0:T(8,128)(2,1)S(1)}, u32[]{:S(2)}) copy-start(bf16[384,768]{1,0:T(8,128)(2,1)S(1)} %convolution_convert_fusion.1) | copy-start | bytes 1769476
  35.1 7.1 %copy-start.7 = (bf16[384,768]{1,0:T(8,128)(2,1)}, bf16[384,768]{1,0:T(8,128)(2,1)S(1)}, u32[]{:S(2)}) copy-start(bf16[384,768]{1,0:T(8,128)(2,1)S(1)} %convolution_convert_fusion.2) | copy-start | bytes 1769476
  35.1 6.5 %collective-permute-start.4 = (bf16[48,1152]{1,0:T(8,128)(2,1)S(1)}, bf16[48,1152]{1,0:T(8,128)(2,1)S(1)}, u32[]{:S(2)}, u32[]{:S(2)}) collective-permute-start(bf16[48,1152]{1,0:T(8,128)(2,1)S(1)} %get-tuple-element.22), channel_id=1, source_target_pairs={{0,16},{16,32},{32,48},{48,64},{64,80},{80,96},{96,112},{112,0},{1... | collective-permute-start | bytes 331784 | tf_op jit(solution)/shard_map/ppermute | solution.py:41
  36.2 5.9 %collective-permute-start.7 = (bf16[48,1152]{1,0:T(8,128)(2,1)S(1)}, bf16[48,1152]{1,0:T(8,128)(2,1)S(1)}, u32[]{:S(2)}, u32[]{:S(2)}) collective-permute-start(bf16[48,1152]{1,0:T(8,128)(2,1)S(1)} %get-tuple-element.23), channel_id=1, source_target_pairs={{0,112},{16,0},{32,16},{48,32},{64,48},{80,64},{96,80},{112,96},{1... | collective-permute-start | bytes 331784 | tf_op jit(solution)/shard_map/ppermute | solution.py:45
  42.3 9.5 %collective-permute-start.5 = (bf16[48,2304]{1,0:T(8,128)(2,1)S(1)}, bf16[48,2304]{1,0:T(8,128)(2,1)S(1)}, u32[]{:S(2)}, u32[]{:S(2)}) collective-permute-start(bf16[48,2304]{1,0:T(8,128)(2,1)S(1)} %get-tuple-element.38), channel_id=1, source_target_pairs={{0,16},{16,32},{32,48},{48,64},{64,80},{80,96},{96,112},{112,0},{1... | collective-permute-start | bytes 663560 | tf_op jit(solution)/shard_map/ppermute | solution.py:41
  43.4 8.4 %collective-permute-start.8 = (bf16[48,2304]{1,0:T(8,128)(2,1)S(1)}, bf16[48,2304]{1,0:T(8,128)(2,1)}, u32[]{:S(2)}, u32[]{:S(2)}) collective-permute-start(bf16[48,2304]{1,0:T(8,128)(2,1)S(1)} %get-tuple-element.37), channel_id=1, source_target_pairs={{0,112},{16,0},{32,16},{48,32},{64,48},{80,64},{96,80},{112,96},{1... | collective-permute-start | bytes 663560 | tf_op jit(solution)/shard_map/ppermute | solution.py:45
  47.1 25.0 %all-to-all-start.1 = ((bf16[8,512,256]{2,1,0:T(8,128)(2,1)}), bf16[8,512,256]{2,1,0:T(8,128)(2,1)S(1)}, u32[]{:S(2)}, u32[]{:S(2)}) async-start(bf16[8,512,256]{2,1,0:T(8,128)(2,1)} %broadcast_in_dim.56), calls=%async_computation.1 | async-start | bytes 4194304 | tf_op jit(solution)/shard_map/all_to_all | solution.py:28
  51.7 4.8 %copy-start.18 = (bf16[256,2,128]{2,1,0:T(2,128)(2,1)S(1)}, bf16[256,2,128]{2,1,0:T(2,128)(2,1)}, u32[]{:S(2)}) copy-start(bf16[256,2,128]{2,1,0:T(2,128)(2,1)} %param.11) | copy-start | bytes 393220
  51.7 4.8 %copy-start.19 = (bf16[256,2,128]{2,1,0:T(2,128)(2,1)S(1)}, bf16[256,2,128]{2,1,0:T(2,128)(2,1)}, u32[]{:S(2)}) copy-start(bf16[256,2,128]{2,1,0:T(2,128)(2,1)} %param.14) | copy-start | bytes 393220
  51.7 8.7 %copy-start.2 = (bf16[384,768]{1,0:T(8,128)(2,1)S(1)}, bf16[384,768]{1,0:T(8,128)(2,1)}, u32[]{:S(2)}) copy-start(bf16[384,768]{1,0:T(8,128)(2,1)} %copy-done.1) | copy-start | bytes 1769476
  51.7 8.7 %copy-start.5 = (bf16[384,768]{1,0:T(8,128)(2,1)S(1)}, bf16[384,768]{1,0:T(8,128)(2,1)}, u32[]{:S(2)}) copy-start(bf16[384,768]{1,0:T(8,128)(2,1)} %copy-done.4) | copy-start | bytes 1769476
  51.8 8.7 %copy-start.8 = (bf16[384,768]{1,0:T(8,128)(2,1)S(1)}, bf16[384,768]{1,0:T(8,128)(2,1)}, u32[]{:S(2)}) copy-start(bf16[384,768]{1,0:T(8,128)(2,1)} %copy-done.7) | copy-start | bytes 1769476
  53.2 7.2 %collective-permute-start.6 = (bf16[48,2304]{1,0:T(8,128)(2,1)S(1)}, bf16[48,2304]{1,0:T(8,128)(2,1)S(1)}, u32[]{:S(2)}, u32[]{:S(2)}) collective-permute-start(bf16[48,2304]{1,0:T(8,128)(2,1)S(1)} %get-tuple-element.36), channel_id=1, source_target_pairs={{0,16},{16,32},{32,48},{48,64},{64,80},{80,96},{96,112},{112,0},{1... | collective-permute-start | bytes 663560 | tf_op jit(solution)/shard_map/ppermute | solution.py:41
  53.3 7.1 %collective-permute-start.9 = (bf16[48,2304]{1,0:T(8,128)(2,1)S(1)}, bf16[48,2304]{1,0:T(8,128)(2,1)S(1)}, u32[]{:S(2)}, u32[]{:S(2)}) collective-permute-start(bf16[48,2304]{1,0:T(8,128)(2,1)S(1)} %get-tuple-element.35), channel_id=1, source_target_pairs={{0,112},{16,0},{32,16},{48,32},{64,48},{80,64},{96,80},{112,96},{1... | collective-permute-start | bytes 663560 | tf_op jit(solution)/shard_map/ppermute | solution.py:45
  72.1 18.2 %collective-permute-start.14 = (bf16[48,2304]{1,0:T(8,128)(2,1)}, bf16[48,2304]{1,0:T(8,128)(2,1)S(1)}, u32[]{:S(2)}, u32[]{:S(2)}) collective-permute-start(bf16[48,2304]{1,0:T(8,128)(2,1)} %get-tuple-element.27), channel_id=1, source_target_pairs={{0,16},{16,32},{32,48},{48,64},{64,80},{80,96},{96,112},{112,0},{1... | collective-permute-start | bytes 663560 | tf_op jit(solution)/shard_map/ppermute | solution.py:41
  72.1 18.2 %collective-permute-start.15 = (bf16[48,2304]{1,0:T(8,128)(2,1)S(1)}, bf16[48,2304]{1,0:T(8,128)(2,1)S(1)}, u32[]{:S(2)}, u32[]{:S(2)}) collective-permute-start(bf16[48,2304]{1,0:T(8,128)(2,1)S(1)} %get-tuple-element.28), channel_id=1, source_target_pairs={{0,112},{16,0},{32,16},{48,32},{64,48},{80,64},{96,80},{112,96},{1... | collective-permute-start | bytes 663560 | tf_op jit(solution)/shard_map/ppermute | solution.py:45
  75.3 14.9 %copy-start.3 = (bf16[384,768]{1,0:T(8,128)(2,1)S(1)}, bf16[384,768]{1,0:T(8,128)(2,1)}, u32[]{:S(2)}) copy-start(bf16[384,768]{1,0:T(8,128)(2,1)} %copy-done.1) | copy-start | bytes 1769476
  75.3 14.9 %copy-start.6 = (bf16[384,768]{1,0:T(8,128)(2,1)S(1)}, bf16[384,768]{1,0:T(8,128)(2,1)}, u32[]{:S(2)}) copy-start(bf16[384,768]{1,0:T(8,128)(2,1)} %copy-done.4) | copy-start | bytes 1769476
  75.3 15.0 %copy-start.9 = (bf16[384,768]{1,0:T(8,128)(2,1)S(1)}, bf16[384,768]{1,0:T(8,128)(2,1)}, u32[]{:S(2)}) copy-start(bf16[384,768]{1,0:T(8,128)(2,1)} %copy-done.7) | copy-start | bytes 1769476
  91.1 10.2 %collective-permute-start.16 = (bf16[48,2304]{1,0:T(8,128)(2,1)}, bf16[48,2304]{1,0:T(8,128)(2,1)}, u32[]{:S(2)}, u32[]{:S(2)}) collective-permute-start(bf16[48,2304]{1,0:T(8,128)(2,1)} %convert_element_type.161), channel_id=1, source_target_pairs={{0,128},{16,144},{32,160},{48,176},{64,192},{80,208},{96,224},{112... | collective-permute-start | bytes 663560 | tf_op jit(solution)/shard_map/ppermute | solution.py:50
  92.5 32.9 %all-to-all-start.2 = ((bf16[8,512,256]{2,1,0:T(8,128)(2,1)}), bf16[8,512,256]{2,1,0:T(8,128)(2,1)S(1)}, u32[]{:S(2)}, u32[]{:S(2)}) async-start(bf16[8,512,256]{2,1,0:T(8,128)(2,1)} %bitcast.21), calls=%async_computation.2 | async-start | bytes 4194304 | tf_op jit(solution)/shard_map/all_to_all | solution.py:32
  103.1 9.4 %collective-permute-start.20 = (bf16[48,2304]{1,0:T(8,128)(2,1)}, bf16[48,2304]{1,0:T(8,128)(2,1)S(1)}, u32[]{:S(2)}, u32[]{:S(2)}) collective-permute-start(bf16[48,2304]{1,0:T(8,128)(2,1)} %get-tuple-element.46), channel_id=1, source_target_pairs={{0,16},{16,32},{32,48},{48,64},{64,80},{80,96},{96,112},{112,0},{1... | collective-permute-start | bytes 663560 | tf_op jit(solution)/shard_map/ppermute | solution.py:41
  103.1 9.4 %collective-permute-start.17 = (bf16[48,2304]{1,0:T(8,128)(2,1)}, bf16[48,2304]{1,0:T(8,128)(2,1)S(1)}, u32[]{:S(2)}, u32[]{:S(2)}) collective-permute-start(bf16[48,2304]{1,0:T(8,128)(2,1)} %get-tuple-element.46), channel_id=1, source_target_pairs={{0,112},{16,0},{32,16},{48,32},{64,48},{80,64},{96,80},{112,96},{1... | collective-permute-start | bytes 663560 | tf_op jit(solution)/shard_map/ppermute | solution.py:45
  112.5 8.0 %collective-permute-start.21 = (bf16[48,2304]{1,0:T(8,128)(2,1)S(1)}, bf16[48,2304]{1,0:T(8,128)(2,1)}, u32[]{:S(2)}, u32[]{:S(2)}) collective-permute-start(bf16[48,2304]{1,0:T(8,128)(2,1)S(1)} %collective-permute-done.20), channel_id=1, source_target_pairs={{0,16},{16,32},{32,48},{48,64},{64,80},{80,96},{96,112},{112,0},{1... | collective-permute-start | bytes 663560 | tf_op jit(solution)/shard_map/ppermute | solution.py:41
  112.5 8.0 %collective-permute-start.18 = (bf16[48,2304]{1,0:T(8,128)(2,1)S(1)}, bf16[48,2304]{1,0:T(8,128)(2,1)}, u32[]{:S(2)}, u32[]{:S(2)}) collective-permute-start(bf16[48,2304]{1,0:T(8,128)(2,1)S(1)} %collective-permute-done.17), channel_id=1, source_target_pairs={{0,112},{16,0},{32,16},{48,32},{64,48},{80,64},{96,80},{112,96},{1... | collective-permute-start | bytes 663560 | tf_op jit(solution)/shard_map/ppermute | solution.py:45
  120.5 7.4 %collective-permute-start.22 = (bf16[48,2304]{1,0:T(8,128)(2,1)}, bf16[48,2304]{1,0:T(8,128)(2,1)S(1)}, u32[]{:S(2)}, u32[]{:S(2)}) collective-permute-start(bf16[48,2304]{1,0:T(8,128)(2,1)} %collective-permute-done.21), channel_id=1, source_target_pairs={{0,16},{16,32},{32,48},{48,64},{64,80},{80,96},{96,112},{112,0},{1... | collective-permute-start | bytes 663560 | tf_op jit(solution)/shard_map/ppermute | solution.py:41
  120.5 7.5 %collective-permute-start.19 = (bf16[48,2304]{1,0:T(8,128)(2,1)}, bf16[48,2304]{1,0:T(8,128)(2,1)S(1)}, u32[]{:S(2)}, u32[]{:S(2)}) collective-permute-start(bf16[48,2304]{1,0:T(8,128)(2,1)} %collective-permute-done.18), channel_id=1, source_target_pairs={{0,112},{16,0},{32,16},{48,32},{64,48},{80,64},{96,80},{112,96},{1... | collective-permute-start | bytes 663560 | tf_op jit(solution)/shard_map/ppermute | solution.py:45
  125.4 5.9 %copy-start.12 = (bf16[384,2304]{1,0:T(8,128)(2,1)S(1)}, bf16[384,2304]{1,0:T(8,128)(2,1)}, u32[]{:S(2)}) copy-start(bf16[384,2304]{1,0:T(8,128)(2,1)} %constant_dynamic-update-slice_fusion.9) | copy-start | bytes 5308420
  125.7 10.7 %copy-start.11 = (bf16[8,48,512]{2,1,0:T(8,128)(2,1)S(1)}, bf16[8,48,512]{2,1,0:T(8,128)(2,1)}, u32[]{:S(2)}) copy-start(bf16[8,48,512]{2,1,0:T(8,128)(2,1)} %copy-done.10) | copy-start | bytes 1179652
  127.9 6.0 %collective-permute-start.23 = (bf16[48,1152]{1,0:T(8,128)(2,1)S(1)}, bf16[48,1152]{1,0:T(8,128)(2,1)S(1)}, u32[]{:S(2)}, u32[]{:S(2)}) collective-permute-start(bf16[48,1152]{1,0:T(8,128)(2,1)S(1)} %slice.162), channel_id=1, source_target_pairs={{0,16},{16,32},{32,48},{48,64},{64,80},{80,96},{96,112},{112,0},{1... | collective-permute-start | bytes 331784 | tf_op jit(solution)/shard_map/ppermute | solution.py:41
  128.0 5.9 %collective-permute-start.24 = (bf16[48,1152]{1,0:T(8,128)(2,1)S(1)}, bf16[48,1152]{1,0:T(8,128)(2,1)S(1)}, u32[]{:S(2)}, u32[]{:S(2)}) collective-permute-start(bf16[48,1152]{1,0:T(8,128)(2,1)S(1)} %slice.163), channel_id=1, source_target_pairs={{0,112},{16,0},{32,16},{48,32},{64,48},{80,64},{96,80},{112,96},{1... | collective-permute-start | bytes 331784 | tf_op jit(solution)/shard_map/ppermute | solution.py:45
  131.3 5.1 %collective-permute-start.10 = (bf16[256,256]{1,0:T(8,128)(2,1)S(1)}, bf16[256,256]{1,0:T(8,128)(2,1)S(1)}, u32[]{:S(2)}, u32[]{:S(2)}) collective-permute-start(bf16[256,256]{1,0:T(8,128)(2,1)S(1)} %slice.234), channel_id=1, source_target_pairs={{0,16},{16,0},{32,48},{48,32},{64,80},{80,64},{96,112},{112,96},{1... | collective-permute-start | bytes 393224 | tf_op jit(solution)/shard_map/ppermute | solution.py:101
  137.6 2.7 %copy-start.14 = (bf16[1,256,1536]{2,1,0:T(8,128)(2,1)S(1)}, bf16[1,256,1536]{2,1,0:T(8,128)(2,1)}, u32[]{:S(2)}) copy-start(bf16[1,256,1536]{2,1,0:T(8,128)(2,1)} %param.20) | copy-start | bytes 2359300
  140.2 24.6 %copy-start.17 = (s32[512,8]{0,1:T(8,128)S(1)}, s32[512,8]{0,1:T(8,128)}, u32[]{:S(2)}) copy-start(s32[512,8]{0,1:T(8,128)} %copy-done.16) | copy-start | bytes 49156
  140.6 5.9 %collective-permute-start.11 = (bf16[128,256]{1,0:T(8,128)(2,1)S(1)}, bf16[128,256]{1,0:T(8,128)(2,1)S(1)}, u32[]{:S(2)}, u32[]{:S(2)}) collective-permute-start(bf16[128,256]{1,0:T(8,128)(2,1)S(1)} %slice.235), channel_id=1, source_target_pairs={{0,128},{16,144},{32,160},{48,176},{64,192},{80,208},{96,224},{112... | collective-permute-start | bytes 196616 | tf_op jit(solution)/shard_map/ppermute | solution.py:101
  142.1 4.5 %collective-permute-start.25 = (bf16[384,128]{1,0:T(8,128)(2,1)S(1)}, bf16[384,128]{1,0:T(8,128)(2,1)S(1)}, u32[]{:S(2)}, u32[]{:S(2)}) collective-permute-start(bf16[384,128]{1,0:T(8,128)(2,1)S(1)} %dynamic-slice_convert_fusion), channel_id=1, source_target_pairs={{0,8},{8,0},{1,9},{9,1},{2,10},{10,2},{3,11},{11,3},{4,12},{12,4},... | collective-permute-start | bytes 294920 | tf_op jit(solution)/shard_map/ppermute | solution.py:290
  146.5 5.4 %collective-permute-start.12 = (f32[64,256]{1,0:T(8,128)S(1)}, f32[64,256]{1,0:T(8,128)S(1)}, u32[]{:S(2)}, u32[]{:S(2)}) collective-permute-start(f32[64,256]{1,0:T(8,128)S(1)} %slice.177), channel_id=1, source_target_pairs={{0,32},{16,48},{32,0},{48,16},{64,96},{80,112},{96,64},{112,80},{1... | collective-permute-start | bytes 196616 | tf_op jit(solution)/shard_map/ppermute | solution.py:101
  151.9 8.0 %collective-permute-start.13 = (f32[32,256]{1,0:T(8,128)S(1)}, f32[32,256]{1,0:T(8,128)S(1)}, u32[]{:S(2)}, u32[]{:S(2)}) collective-permute-start(f32[32,256]{1,0:T(8,128)S(1)} %slice.179), channel_id=1, source_target_pairs={{0,64},{16,80},{32,96},{48,112},{64,0},{80,16},{96,32},{112,48},{1... | collective-permute-start | bytes 98312 | tf_op jit(solution)/shard_map/ppermute | solution.py:101
  153.7 11.1 %all-to-all-start.3 = ((bf16[8,48,128]{2,1,0:T(8,128)(2,1)}), bf16[8,48,128]{2,1,0:T(8,128)(2,1)S(1)}, u32[]{:S(2)}, u32[]{:S(2)}) async-start(bf16[8,48,128]{2,1,0:T(8,128)(2,1)} %fusion.43), calls=%async_computation.3 | async-start | bytes 196608 | tf_op jit(solution)/shard_map/all_to_all | solution.py:292

commit v5 on v3

--- a/solution.py
+++ b/solution.py
@@ -1,10 +1,16 @@
+import functools
+
 import jax
 import jax.numpy as jnp
 from jax import lax
+from jax.experimental import pallas as pl
+from jax.experimental.pallas import tpu as pltpu
 from jax.sharding import PartitionSpec as P
 
 CAP = 48
 X_HI = 2
+X_LO = 2
+MASKED = -1e30
 MASKS = (4, 2, 8, 1)
 BF = jnp.bfloat16
 F32 = jnp.float32
@@ -18,14 +24,24 @@
     return (hidden, d_gate, d_up)
 
 
-def spread(block, axis):
-    n = lax.axis_size(axis)
+def y_groups():
+    n = lax.axis_size("exp")
+    return [list(range(x, n, X_LO)) for x in range(X_LO)]
+
+
+def y_gather(block):
+    n = lax.axis_size("exp") // X_LO
     copies = jnp.broadcast_to(block[None], (n,) + block.shape)
-    return lax.all_to_all(copies, axis, 0, 0, tiled=True)
-
-
-def gather_sum(parts, axis):
-    return jnp.sum(lax.all_to_all(parts, axis, 0, 0, tiled=True).astype(F32), axis=0)
+    return lax.all_to_all(copies, "exp", 0, 0, tiled=True, axis_index_groups=y_groups())
+
+
+def y_sum(parts):
+    got = lax.all_to_all(parts, "exp", 0, 0, tiled=True, axis_index_groups=y_groups())
+    return jnp.sum(got.astype(F32), axis=0)
+
+
+def beside(block):
+    return lax.ppermute(block, "exp", [(e, e ^ 1) for e in range(lax.axis_size("exp"))])
 
 
 def z_shift(step):
@@ -74,17 +90,19 @@
     return onward, back
 
 
-def ring_gather(block, beside):
+def ring_gather(block, waits):
     n = lax.axis_size("ctx") // X_HI
     far = n // 2
     cut = block.shape[1] // 2
     blocks = [block] + [None] * (n - 1)
     onward = back = block
     for step in range(1, far):
-        if step in beside:
-            onward, back = after(onward, beside[step]), after(back, beside[step])
+        if step in waits:
+            onward, back = after(onward, waits[step]), after(back, waits[step])
         onward, back = right(onward), left(back)
         blocks[n - step], blocks[step] = onward, back
+    if far in waits:
+        onward, back = after(onward, waits[far]), after(back, waits[far])
     blocks[far] = jnp.concatenate([right(onward[:, :cut]), left(back[:, cut:])], axis=1)
     return blocks
 
@@ -98,9 +116,8 @@
     return lax.ppermute(block, "ctx", [(c, c ^ mask) for c in range(lax.axis_size("ctx"))])
 
 
-def ctx_gather(key_rows, value_vector_rows):
-    block = jnp.concatenate([key_rows[:, 0, :], value_vector_rows[:, 0, :]], axis=1)
-    for mask in MASKS:
+def ctx_gather(block, masks):
+    for mask in masks:
         block = jnp.concatenate([block, swap(block, mask)], axis=0)
     return block
 
@@ -109,54 +126,152 @@
     return sum((index >> bit) % 2 * mask for bit, mask in enumerate(MASKS))
 
 
-def key_places(rows):
-    ctx_size, exp_size = lax.axis_size("ctx"), lax.axis_size("exp")
-    own = rows // (ctx_size * exp_size)
-    place = jnp.arange(rows)
-    of_ctx = lax.axis_index("ctx") ^ mask_of(place // own % ctx_size)
-    return (of_ctx * exp_size + place // (own * ctx_size)) * own + place % own
-
-
-def masked_scores(queries, flat):
-    tok_rows, _, head_dim = queries.shape
-    query_pos = lax.axis_index("ctx") * tok_rows + jnp.arange(tok_rows)
-    allowed = key_places(flat.shape[0])[None, :] <= query_pos[:, None]
-    scores = jnp.einsum("phd,td->hpt", queries, flat[:, :head_dim], preferred_element_type=F32)
-    return jnp.where(allowed[None], scores * head_dim ** (-0.5), -jnp.inf)
-
-
-def value_side(scores, flat, grad_attn):
-    value_flat = flat[:, grad_attn.shape[2] :]
-    probs_full = jax.nn.softmax(scores, axis=-1)
-    probs_low = probs_full.astype(BF)
-    attn_out = jnp.einsum("hpt,td->phd", probs_low, value_flat, preferred_element_type=F32)
-    row_delta = jnp.sum(grad_attn.astype(F32) * attn_out, axis=-1)
-    value_grad = jnp.einsum("hpt,phd->td", probs_low, grad_attn, preferred_element_type=F32)
-    return probs_full, row_delta, value_grad.astype(BF)
-
-
-def key_side(probs_full, row_delta, queries, flat, grad_attn):
-    head_dim = queries.shape[2]
-    grad_prob = jnp.einsum(
-        "phd,td->hpt", grad_attn, flat[:, head_dim:], preferred_element_type=F32
-    )
-    dscore = (probs_full * (grad_prob - jnp.transpose(row_delta)[:, :, None])).astype(BF)
-    key_grad = jnp.einsum("hpt,phd->td", dscore, queries, preferred_element_type=F32)
-    return dscore, key_grad.astype(BF)
-
-
-def query_side(dscore, flat):
-    head_dim = flat.shape[1] // 2
-    grad_query = jnp.einsum("hpt,td->phd", dscore, flat[:, :head_dim], preferred_element_type=F32)
-    return (grad_query * head_dim ** (-0.5)).astype(BF)
-
-
-def to_owners(both):
-    head_dim = both.shape[1] // 2
-    for mask in reversed(MASKS):
+def scores_of(step, own, ctx_size, tokens, here_ref, k, q):
+    lanes = q.shape[0]
+    found = lax.dot_general(k, q, (((1,), (1,)), ((), ())), preferred_element_type=F32)
+    ahead = lax.broadcasted_iota(jnp.int32, (own, lanes), 1) % tokens - lax.broadcasted_iota(
+        jnp.int32, (own, lanes), 0
+    )
+    me, side = here_ref[0], here_ref[1]
+    parts = k.shape[0] // own
+    masked = []
+    for part in range(parts):
+        place = step * parts + part
+        start = (me ^ mask_of(place % ctx_size)) * tokens + (place // ctx_size * X_LO + side) * own
+        masked.append(
+            jnp.where(
+                ahead >= start - me * tokens,
+                found[part * own : (part + 1) * own] * k.shape[1] ** (-0.5),
+                MASKED,
+            )
+        )
+    return jnp.concatenate(masked, axis=0)
+
+
+def stats_body(own, ctx_size, tokens, here_ref, q_ref, g_ref, kv_ref, stats_ref):
+    size = kv_ref.shape[1] // 2
+    lanes = q_ref.shape[0]
+    chunk = 8 * own
+
+    def one(step, held):
+        top, norm, delta = held
+        rows = pl.ds(pl.multiple_of(step * chunk, chunk), chunk)
+        scores = scores_of(step, own, ctx_size, tokens, here_ref, kv_ref[rows, :size], q_ref[...])
+        dprob = lax.dot_general(
+            kv_ref[rows, size:], g_ref[...], (((1,), (1,)), ((), ())), preferred_element_type=F32
+        )
+        scores, dprob = scores.reshape(-1, 8, lanes), dprob.reshape(-1, 8, lanes)
+        higher = jnp.maximum(top, jnp.max(scores, axis=0))
+        shrink = jnp.exp(top - higher)
+        prob = jnp.exp(scores - higher[None])
+        norm = norm * shrink + jnp.sum(prob, axis=0)
+        delta = delta * shrink + jnp.sum(prob * dprob, axis=0)
+        return higher, norm, delta
+
+    zero = jnp.zeros((8, lanes), F32)
+    top, norm, delta = lax.fori_loop(0, kv_ref.shape[0] // chunk, one, (zero + MASKED, zero, zero))
+    highest = jnp.max(top, axis=0, keepdims=True)
+    shrink = jnp.exp(top - highest)
+    stats_ref[0:1, :] = highest
+    stats_ref[1:2, :] = jnp.sum(norm * shrink, axis=0, keepdims=True)
+    stats_ref[2:3, :] = jnp.sum(delta * shrink, axis=0, keepdims=True)
+    stats_ref[3:, :] = jnp.zeros((5, lanes), F32)
+
+
+def grads_body(
+    own, ctx_size, tokens, here_ref, q_ref, g_ref, kv_ref, stats_ref, far_ref, both_ref, dq_ref
+):
+    size = kv_ref.shape[1] // 2
+    lanes = q_ref.shape[0]
+    chunk = 8 * own
+    far = jnp.concatenate([far_ref[:, lanes // 2 :], far_ref[:, : lanes // 2]], axis=1)
+    near = stats_ref[...]
+    top = jnp.maximum(near[0:1], far[0:1])
+    shrink_near, shrink_far = jnp.exp(near[0:1] - top), jnp.exp(far[0:1] - top)
+    inverse = 1.0 / (near[1:2] * shrink_near + far[1:2] * shrink_far)
+    delta = (near[2:3] * shrink_near + far[2:3] * shrink_far) * inverse
+
+    def one(step, total):
+        rows = pl.ds(pl.multiple_of(step * chunk, chunk), chunk)
+        k = kv_ref[rows, :size]
+        scores = scores_of(step, own, ctx_size, tokens, here_ref, k, q_ref[...])
+        prob = jnp.exp(scores - top) * inverse
+        both_ref[rows, size:] = jnp.dot(
+            prob.astype(BF), g_ref[...], preferred_element_type=F32
+        ).astype(BF)
+        dprob = lax.dot_general(
+            kv_ref[rows, size:], g_ref[...], (((1,), (1,)), ((), ())), preferred_element_type=F32
+        )
+        dscore = (prob * (dprob - delta)).astype(BF)
+        both_ref[rows, :size] = jnp.dot(dscore, q_ref[...], preferred_element_type=F32).astype(BF)
+        return total + lax.dot_general(
+            k, dscore, (((0,), (0,)), ((), ())), preferred_element_type=F32
+        )
+
+    total = lax.fori_loop(0, kv_ref.shape[0] // chunk, one, jnp.zeros((size, lanes), F32))
+    dq_ref[...] = (total * size ** (-0.5)).T
+
+
+VMEM = pl.BlockSpec(memory_space=pltpu.VMEM)
+SMEM = pl.BlockSpec(memory_space=pltpu.SMEM)
+
+
+def here():
+    return jnp.stack([lax.axis_index("ctx"), lax.axis_index("exp") % X_LO]).astype(jnp.int32)
+
+
+def attention_stats(own, tokens, queries, grads, flat):
+    keys, lanes = flat.shape[0], queries.shape[0]
+    return pl.pallas_call(
+        functools.partial(stats_body, own, lax.axis_size("ctx"), tokens),
+        out_shape=jax.ShapeDtypeStruct((8, lanes), F32),
+        in_specs=[SMEM, VMEM, VMEM, VMEM],
+        out_specs=VMEM,
+        compiler_params=pltpu.CompilerParams(vmem_limit_bytes=24 * 2**20),
+        cost_estimate=pl.CostEstimate(
+            flops=4 * keys * lanes * flat.shape[1] // 2,
+            bytes_accessed=2 * flat.size,
+            transcendentals=keys * lanes,
+        ),
+        name="attention_stats",
+    )(here(), queries, grads, flat)
+
+
+def attention_grads(own, tokens, queries, grads, flat, stats, far):
+    keys, lanes = flat.shape[0], queries.shape[0]
+    size = flat.shape[1] // 2
+    return pl.pallas_call(
+        functools.partial(grads_body, own, lax.axis_size("ctx"), tokens),
+        out_shape=(
+            jax.ShapeDtypeStruct((keys, 2 * size), BF),
+            jax.ShapeDtypeStruct((lanes, size), F32),
+        ),
+        in_specs=[SMEM] + [VMEM] * 5,
+        out_specs=(VMEM, VMEM),
+        compiler_params=pltpu.CompilerParams(vmem_limit_bytes=24 * 2**20),
+        cost_estimate=pl.CostEstimate(
+            flops=10 * keys * lanes * size,
+            bytes_accessed=4 * flat.size,
+            transcendentals=keys * lanes,
+        ),
+        name="attention_grads",
+    )(here(), queries, grads, flat, stats, far)
+
+
+def by_head(rows):
+    return jnp.swapaxes(rows, 0, 1).reshape(-1, rows.shape[2])
+
+
+def ctx_sum(both, masks):
+    for mask in reversed(masks):
         half = both.shape[0] // 2
         sent = both[half:].astype(BF if half >= both.shape[1] // 2 else F32)
         both = both[:half] + swap(sent, mask).astype(F32)
+    return both
+
+
+def own_grads(both):
+    head_dim = both.shape[1] // 2
     grad_key = (both[:, :head_dim] * head_dim ** (-0.5)).astype(BF)[:, None, :]
     grad_value = both[:, head_dim:].astype(BF)[:, None, :]
     return grad_key, grad_value
@@ -202,14 +317,13 @@
 
 def act_block(total):
     units = total.shape[1] // 3
-    total = total + opposite(total.astype(BF)).astype(F32)
     hidden, d_gate, d_up = activate(
         total[:, :units], total[:, units : 2 * units], total[:, 2 * units :]
     )
     return jnp.concatenate([hidden, d_gate, d_up], axis=1)
 
 
-def finish(full, input_rows, grad_rows, gate_mat, up_mat, placed_low):
+def finish(full, input_rows, grad_rows, gate_mat, up_mat, placed_low, sums):
     exp_size, head_size = lax.axis_size("exp"), lax.axis_size("head")
     ring = lax.axis_size("ctx") // X_HI
     at = lax.axis_index("ctx") % ring
@@ -223,6 +337,8 @@
     other = lax.dynamic_slice_in_dim(contrib, (1 - half) * columns, columns, 1).astype(BF)
     mine = (mine + lax.ppermute(other, "head", [(0, 1), (1, 0)]).astype(F32)).astype(BF)
     mine = turn(mine.reshape(ring, -1, columns), (ring - at) % ring).reshape(exp_size, CAP, columns)
+    input_rows, grad_rows = after(input_rows, mine), after(grad_rows, mine)
+    sums = ctx_sum(after(sums, mine), MASKS[:2])
     back_rows = lax.all_to_all(mine, "exp", 0, 0, tiled=True)
     grad_input = jnp.dot(
         placed_low, back_rows.reshape(-1, columns), preferred_element_type=F32
@@ -230,7 +346,7 @@
     grad_gate = jnp.einsum("rd,rf->df", input_rows, d_gate, preferred_element_type=F32).astype(BF)
     grad_up = jnp.einsum("rd,rf->df", input_rows, d_up, preferred_element_type=F32).astype(BF)
     grad_down = jnp.einsum("rf,rd->fd", hidden, grad_rows, preferred_element_type=F32).astype(BF)
-    return grad_input, grad_gate[None], grad_up[None], grad_down[None]
+    return grad_input, grad_gate[None], grad_up[None], grad_down[None], sums
 
 
 def shards(
@@ -246,32 +362,43 @@
     up_weight,
     down_weight,
 ):
-    exp_size = lax.axis_size("exp")
-    near = ctx_gather(key_rows, value_vector_rows)
+    tokens, own = queries.shape[0], key_rows.shape[0]
+    rows = tokens * queries.shape[1]
+    size = queries.shape[2]
+    pair = jnp.concatenate([key_rows[:, 0, :], value_vector_rows[:, 0, :]], axis=1)
+    near = ctx_gather(pair, MASKS)
     placed_low, got = select(moe_input, moe_grad, expert_ids, router_weight)
-    flat = spread(after(near, got), "exp").reshape(-1, near.shape[1])
+    mine = jnp.concatenate([by_head(queries), by_head(grad_attn)], axis=0)
+    theirs = beside(mine)
+    flat = y_gather(after(near, got, theirs)).reshape(-1, near.shape[1])
+    queries = jnp.concatenate([mine[:rows], theirs[:rows]], axis=0)
+    grads = jnp.concatenate([mine[rows:], theirs[rows:]], axis=0)
     input_rows, grad_rows, gate_mat, up_mat, parts = project(
         got, gate_weight, up_weight, down_weight
     )
-    onward, back = sum_step(parts, 0, *sum_start(parts))
-    onward, back = sum_step(parts, 1, onward, back)
-    scores = masked_scores(queries, after(flat, onward, back))
-    onward, back = sum_step(parts, 2, onward, back)
-    probs_full, row_delta, value_grad = value_side(after(scores, onward, back), flat, grad_attn)
-    onward, back = sum_step(parts, 3, after(onward, scores), after(back, scores))
+    onward, back = sum_start(parts)
+    onward, back = after(onward, near), after(back, near)
+    for step in range(len(parts) // 2):
+        if step == 3:
+            onward, back = after(onward, flat), after(back, flat)
+        onward, back = sum_step(parts, step, onward, back)
     total = onward.astype(F32) + back.astype(F32) + parts[0].astype(F32)
-    dscore, key_grad = key_side(
-        probs_full, after(row_delta, total), queries, flat, grad_attn
-    )
-    block = act_block(after(total, value_grad))
-    grad_query = query_side(dscore, after(flat, block))
-    both = jnp.concatenate([key_grad, value_grad], axis=1)
-    blocks = ring_gather(block, {1: both, 2: grad_query})
-    both = gather_sum(both.reshape((exp_size, -1) + both.shape[1:]), "exp")
-    full = after(jnp.concatenate(blocks, axis=0), both)
-    of_experts = finish(full, input_rows, grad_rows, gate_mat, up_mat, placed_low)
-    grad_key, grad_value = to_owners(both)
-    return (grad_query, grad_key, grad_value) + of_experts
+    other = opposite(total.astype(BF))
+    stats = attention_stats(own, tokens, queries, grads, flat)
+    block = act_block(total + after(other, stats).astype(F32))
+    both, grad_query = attention_grads(
+        own, tokens, queries, grads, flat, stats, beside(stats)
+    )
+    sums = y_sum(both.reshape((-1,) + near.shape))
+    blocks = ring_gather(block, {2: both, 4: sums})
+    sums = ctx_sum(sums, MASKS[3:])
+    full = after(jnp.concatenate(blocks, axis=0), sums)
+    sums = ctx_sum(sums, MASKS[2:3])
+    of_experts = finish(full, input_rows, grad_rows, gate_mat, up_mat, placed_low, sums)
+    grad_query = grad_query[:rows] + beside(grad_query[rows:].astype(BF)).astype(F32)
+    grad_query = jnp.swapaxes(grad_query.astype(BF).reshape(-1, tokens, size), 0, 1)
+    grad_key, grad_value = own_grads(of_experts[-1])
+    return (grad_query, grad_key, grad_value) + of_experts[:-1]
 
 
 def solution(mesh):

time: 171 us -> 174 us (1.018)
  Pallas kernels: 0 us -> 14.7 us
  matrix products: 22.1 us -> 14.1 us
  waiting for transfers between devices: 47.7 us -> 54.1 us
  starting transfers between devices: 66.6 us -> 62.5 us
  other arithmetic: 19.3 us -> 16.5 us
  local copies, waits for them, and re-layouts: 12.4 us -> 9.86 us
    pallas_call x0 -> x2, Pallas kernels: none -> 14.7 us  [the longest x1 9.57 us: attention_grads(): pl.pallas_call(functools.partial(grads_body, own, lax.axis_size('ctx'), t...]
    dot_general x6 -> x0, matrix products: 13.5 us -> none  [the longest x1 3.25 us: query_side(): jnp.einsum('hpt,td->phd', dscore, flat[:, :head_dim], preferred_element_t...]
    ppermute x8, waiting for transfers between devices: 2.14 us -> 10.6 us  [left(): return lax.ppermute(block, 'ctx', z_shift(-1))]
    sub x1 -> x0, other arithmetic: 4.4 us -> none  [value_side(): probs_full = jax.nn.softmax(scores, axis=-1)]
    unnamed x37 -> x50, local copies, waits for them, and re-layouts: 8.01 us -> 3.66 us
    ppermute x8, waiting for transfers between devices: 14.9 us -> 18.6 us  [right(): return lax.ppermute(block, 'ctx', z_shift(1))]
    all_to_all x2, waiting for transfers between devices: 11.7 us -> 8.02 us  [the longest x1 8.01 us: y_gather(): lax.all_to_all(copies, 'exp', 0, 0, tiled=True, axis_index_groups=y_group...]
    ppermute x0 -> x3, starting transfers between devices: none -> 3.32 us  [beside(): lax.ppermute(block, 'exp', [(e, e ^ 1) for e in range(lax.axis_size('exp'...]
  transfers between devices with their start and end apart: 30 -> 33, of which waited for: 16 -> 15; matrix products, arithmetic and copies ran while one was open for 25% -> 20% of each run, Pallas kernels for 0% -> 8%
where the time goes in v5:
time: 174 us; the launch traced here: 173 us
  starting transfers between devices  62.5 us (36%)
  waiting for transfers between devices  54.1 us (31%)
  other arithmetic  16.5 us (9%)
  Pallas kernels  14.7 us (8%)
  matrix products  14.1 us (8%)
  local copies, waits for them, and re-layouts  9.86 us (6%)
    ppermute x8, waiting for transfers between devices, right(): return lax.ppermute(block, 'ctx', z_shift(1))  18.6 us
    ppermute x8, starting transfers between devices, left(): return lax.ppermute(block, 'ctx', z_shift(-1))  18 us
    ppermute x8, starting transfers between devices, swap(): lax.ppermute(block, 'ctx', [(c, c ^ mask) for c in range(lax.axis_size('c...  15.3 us
    ppermute x8, waiting for transfers between devices, swap(): lax.ppermute(block, 'ctx', [(c, c ^ mask) for c in range(lax.axis_size('c...  14.1 us
    ppermute x8, waiting for transfers between devices, left(): return lax.ppermute(block, 'ctx', z_shift(-1))  10.6 us
    pallas_call x1, Pallas kernels, attention_grads(): pl.pallas_call(functools.partial(grads_body, own, lax.axis_size('ctx'), t...  9.57 us
    all_to_all x1, waiting for transfers between devices, y_gather(): lax.all_to_all(copies, 'exp', 0, 0, tiled=True, axis_index_groups=y_group...  8.01 us
    all_to_all x1, starting transfers between devices, finish(): back_rows = lax.all_to_all(mine, 'exp', 0, 0, tiled=True)  6.31 us
  transfers between devices with their start and end apart: 33, of which 15 were waited for; matrix products, arithmetic and copies ran while one was open for 20% of the time, Pallas kernels for 8%

profile of v5, /device:TPU:2, one launch (start us, length us, event | category | flops | bytes accessed | tf_op | source)
XLA Modules:
  0.0 172.9 jit_solution(8884787496441464569)
XLA Ops:
  0.7 0.8 pad_maximum_fusion.13
  1.5 7.2 %collective-permute-start.1 = (bf16[32,256]{1,0:T(8,128)(2,1)S(1)}, bf16[32,256]{1,0:T(8,128)(2,1)S(1)}, u32[]{:S(2)}, u32[]{:S(2)}) collective-permute-start(bf16[32,256]{1,0:T(8,128)(2,1)S(1)} %get-tuple-element.58), channel_id=1, source_target_pairs={{0,64},{16,80},{32,96},{48,112},{64,0},{80,16},{96,32},{112,48},{1... | collective-permute-start | bytes 49160 | tf_op jit(solution)/shard_map/ppermute | solution.py:116
  8.7 0.7 convert_reduce_fusion.1
  9.5 1.1 reduce-window.6
  11.0 0.8 select_reduce_fusion.1
  12.3 1.4 fusion.8
  13.9 1.6 collective-permute-start.2
  15.5 0.8 pad_maximum_fusion
  16.3 6.1 %all-to-all-start = ((bf16[8,48,512]{2,1,0:T(8,128)(2,1)}), bf16[8,48,512]{2,1,0:T(8,128)(2,1)S(1)}, u32[]{:S(2)}, u32[]{:S(2)}) async-start(bf16[8,48,512]{2,1,0:T(8,128)(2,1)} %bitcast.14), calls=%async_computation | async-start | bytes 786432 | tf_op jit(solution)/shard_map/all_to_all | solution.py:296
  22.3 2.2 %collective-permute-start.3 = (bf16[128,256]{1,0:T(8,128)(2,1)S(1)}, bf16[128,256]{1,0:T(8,128)(2,1)S(1)}, u32[]{:S(2)}, u32[]{:S(2)}) collective-permute-start(bf16[128,256]{1,0:T(8,128)(2,1)S(1)} %pad_maximum_fusion.11), channel_id=1, source_target_pairs={{0,128},{16,144},{32,160},{48,176},{64,192},{80,208},{96,224},{112... | collective-permute-start | bytes 196616 | tf_op jit(solution)/shard_map/ppermute | solution.py:116
  24.5 5.3 %collective-permute-done.3 = bf16[128,256]{1,0:T(8,128)(2,1)S(1)} collective-permute-done((bf16[128,256]{1,0:T(8,128)(2,1)S(1)}, bf16[128,256]{1,0:T(8,128)(2,1)S(1)}, u32[]{:S(2)}, u32[]{:S(2)}) %collective-permute-start.3) | collective-permute-done | bytes 65568 | tf_op jit(solution)/shard_map/ppermute | solution.py:116
  29.8 1.1 collective-permute-start.4
  31.0 3.9 %collective-permute-done.4 = bf16[256,256]{1,0:T(8,128)(2,1)S(1)} collective-permute-done((bf16[256,256]{1,0:T(8,128)(2,1)S(1)}, bf16[256,256]{1,0:T(8,128)(2,1)S(1)}, u32[]{:S(2)}, u32[]{:S(2)}) %collective-permute-start.4) | collective-permute-done | bytes 131104 | tf_op jit(solution)/shard_map/ppermute | solution.py:116
  35.1 1.5 convolution_convert_fusion
  37.3 1.1 collective-permute-start.9
  38.4 2.2 %collective-permute-start.13 = (bf16[48,1152]{1,0:T(8,128)(2,1)S(1)}, bf16[48,1152]{1,0:T(8,128)(2,1)S(1)}, u32[]{:S(2)}, u32[]{:S(2)}) collective-permute-start(bf16[48,1152]{1,0:T(8,128)(2,1)S(1)} %get-tuple-element.28), channel_id=1, source_target_pairs={{0,112},{16,0},{32,16},{48,32},{64,48},{80,64},{96,80},{112,96},{1... | collective-permute-start | bytes 331784 | tf_op jit(solution)/shard_map/ppermute | solution.py:57
  40.6 2.7 %collective-permute-done.9 = bf16[48,1152]{1,0:T(8,128)(2,1)S(1)} collective-permute-done((bf16[48,1152]{1,0:T(8,128)(2,1)S(1)}, bf16[48,1152]{1,0:T(8,128)(2,1)S(1)}, u32[]{:S(2)}, u32[]{:S(2)}) %collective-permute-start.9) | collective-permute-done | bytes 110624 | tf_op jit(solution)/shard_map/ppermute | solution.py:53
  43.4 0.7 fusion.37
  44.2 0.8 collective-permute-start.10
  45.1 2.8 %collective-permute-start.14 = (bf16[48,2304]{1,0:T(8,128)(2,1)}, bf16[48,2304]{1,0:T(8,128)(2,1)}, u32[]{:S(2)}, u32[]{:S(2)}) collective-permute-start(bf16[48,2304]{1,0:T(8,128)(2,1)} %get-tuple-element.44), channel_id=1, source_target_pairs={{0,112},{16,0},{32,16},{48,32},{64,48},{80,64},{96,80},{112,96},{1... | collective-permute-start | bytes 663560 | tf_op jit(solution)/shard_map/ppermute | solution.py:57
  47.8 4.0 %collective-permute-done.10 = bf16[48,2304]{1,0:T(8,128)(2,1)S(1)} collective-permute-done((bf16[48,2304]{1,0:T(8,128)(2,1)S(1)}, bf16[48,2304]{1,0:T(8,128)(2,1)S(1)}, u32[]{:S(2)}, u32[]{:S(2)}) %collective-permute-start.10) | collective-permute-done | bytes 221216 | tf_op jit(solution)/shard_map/ppermute | solution.py:53
  51.9 0.7 add_convert_fusion.3
  53.5 6.9 %collective-permute-done.11 = bf16[48,2304]{1,0:T(8,128)(2,1)} collective-permute-done((bf16[48,2304]{1,0:T(8,128)(2,1)}, bf16[48,2304]{1,0:T(8,128)(2,1)}, u32[]{:S(2)}, u32[]{:S(2)}) %collective-permute-start.11) | collective-permute-done | bytes 221216 | tf_op jit(solution)/shard_map/ppermute | solution.py:53
  60.4 1.9 %add_convert_fusion.2 = (bf16[48,2304]{1,0:T(8,128)(2,1)}, bf16[48,2304]{1,0:T(8,128)(2,1)}) fusion(bf16[48,2304]{1,0:T(8,128)(2,1)} %collective-permute-done.11, bf16[384,768]{1,0:T(8,128)(2,1)S(1)} %convolution_convert_fusion, bf16[384,768]{1,0:T(8,128)(2,1)S(1)} %convolution_convert_fusion.1, bf16[384,768]{1,0:T(8,128)(2,1)S(1)} %convolution_convert_fusion.2, ...), kind=kLoop, calls=%fused_computation.36 | loop fusion | flops 1990656 | bytes 2654208 | tf_op jit(solution)/shard_map/convert_element_type | solution.py:70
  62.3 2.0 %collective-permute-start.15 = (bf16[48,2304]{1,0:T(8,128)(2,1)}, bf16[48,2304]{1,0:T(8,128)(2,1)}, u32[]{:S(2)}, u32[]{:S(2)}) collective-permute-start(bf16[48,2304]{1,0:T(8,128)(2,1)} %get-tuple-element.42), channel_id=1, source_target_pairs={{0,112},{16,0},{32,16},{48,32},{64,48},{80,64},{96,80},{112,96},{1... | collective-permute-start | bytes 663560 | tf_op jit(solution)/shard_map/ppermute | solution.py:57
  65.1 1.1 broadcast_in_dim.56
  66.1 4.5 %all-to-all-start.1 = ((bf16[4,512,256]{2,1,0:T(8,128)(2,1)}), bf16[4,512,256]{2,1,0:T(8,128)(2,1)S(1)}, u32[]{:S(2)}, u32[]{:S(2)}) async-start(bf16[4,512,256]{2,1,0:T(8,128)(2,1)} %broadcast_in_dim.56), calls=%async_computation.1 | async-start | bytes 2097152 | tf_op jit(solution)/shard_map/all_to_all | solution.py:35
  70.6 1.1 pad_maximum_fusion.2
  71.7 1.7 %add_convert_fusion = bf16[48,2304]{1,0:T(8,128)(2,1)} fusion(bf16[48,2304]{1,0:T(8,128)(2,1)} %collective-permute-done.15, bf16[384,768]{1,0:T(8,128)(2,1)S(1)} %convolution_convert_fusion, bf16[384,768]{1,0:T(8,128)(2,1)S(1)} %convolution_convert_fusion.1, bf16[384,768]{1,0:T(8,128)(2,1)} %copy-done.1), kind=kLoop, calls=%fused_computation.34 | loop fusion | flops 995328 | bytes 2211840 | tf_op jit(solution)/shard_map/convert_element_type | solution.py:70
  73.5 8.0 %all-to-all-done.1 = bf16[4,512,256]{2,1,0:T(8,128)(2,1)S(1)} async-done(((bf16[4,512,256]{2,1,0:T(8,128)(2,1)}), bf16[4,512,256]{2,1,0:T(8,128)(2,1)S(1)}, u32[]{:S(2)}, u32[]{:S(2)}) %all-to-all-start.1) | async-done | bytes 1048608 | tf_op jit(solution)/shard_map/all_to_all | solution.py:35
  81.5 2.0 %collective-permute-start.12 = (bf16[48,2304]{1,0:T(8,128)(2,1)}, bf16[48,2304]{1,0:T(8,128)(2,1)S(1)}, u32[]{:S(2)}, u32[]{:S(2)}) collective-permute-start(bf16[48,2304]{1,0:T(8,128)(2,1)} %get-tuple-element.27), channel_id=1, source_target_pairs={{0,16},{16,32},{32,48},{48,64},{64,80},{80,96},{96,112},{112,0},{1... | collective-permute-start | bytes 663560 | tf_op jit(solution)/shard_map/ppermute | solution.py:53
  83.5 1.8 %fusion.51 = (bf16[384,256]{1,0:T(8,128)(2,1)}, bf16[384,256]{1,0:T(8,128)(2,1)}) fusion(bf16[384,512]{1,0:T(8,128)(2,1)} %bitcast.67), kind=kLoop, calls=%fused_computation.129 | loop fusion | bytes 786432 | tf_op jit(solution)/shard_map/slice | solution.py:307
  85.3 5.1 %attention_stats.1.stats_ref = f32[8,1024]{1,0:T(8,128)S(1)} custom-call(s32[2]{0:T(128)S(1)} %pad_add_fusion.here_ref, bf16[1024,128]{1,0:T(8,128)(2,1)S(1)} %get-tuple-element.60.q_ref, bf16[1024,128]{1,0:T(8,128)(2,1)S(1)} %get-tuple-element.61.g_ref, bf16[2048,256]{1,0:T(8,128)(2,1)S(1)} %bitcast.62), custom_call_target="tpu_custom_call" | custom-call | flops 1073741824 | bytes 1048576 | tf_op jit(solution)/shard_map/attention_stats/pallas_call | solution.py:225
  90.4 1.3 collective-permute-start.5
  91.7 0.9 fusion.33
  92.8 1.5 collective-permute-done.5.far_ref
  94.4 9.6 %attention_grads.1 = (bf16[2048,256]{1,0:T(8,128)(2,1)}, f32[1024,128]{1,0:T(8,128)S(1)}) custom-call(s32[2]{0:T(128)S(1)} %pad_add_fusion.here_ref, bf16[1024,128]{1,0:T(8,128)(2,1)S(1)} %get-tuple-element.60.q_ref, bf16[1024,128]{1,0:T(8,128)(2,1)S(1)} %get-tuple-element.61.g_ref, bf16[2048,256]{1,0:T(8,128)(2,1)S(1)} %bitcast.63, ...), custom_call_target="tpu_custom_call" | custom-call | flops 2684354560 | bytes 2097152 | tf_op jit(solution)/shard_map/attention_grads/pallas_call | solution.py:243
  104.0 1.3 collective-permute-start.6
  105.3 3.5 %all-to-all-start.2 = ((bf16[4,512,256]{2,1,0:T(8,128)(2,1)}), bf16[4,512,256]{2,1,0:T(8,128)(2,1)S(1)}, u32[]{:S(2)}, u32[]{:S(2)}) async-start(bf16[4,512,256]{2,1,0:T(8,128)(2,1)} %bitcast.18), calls=%async_computation.2 | async-start | bytes 2097152 | tf_op jit(solution)/shard_map/all_to_all | solution.py:39
  108.9 1.0 convert_add_fusion
  110.0 0.7 pad_maximum_fusion.6
  110.7 1.2 collective-permute-start.18
  112.0 0.8 collective-permute-start.21
  112.8 0.8 copy.32
  113.6 4.4 %collective-permute-done.18 = bf16[48,2304]{1,0:T(8,128)(2,1)S(1)} collective-permute-done((bf16[48,2304]{1,0:T(8,128)(2,1)S(1)}, bf16[48,2304]{1,0:T(8,128)(2,1)S(1)}, u32[]{:S(2)}, u32[]{:S(2)}) %collective-permute-start.18) | collective-permute-done | bytes 221216 | tf_op jit(solution)/shard_map/ppermute | solution.py:57
  118.0 2.3 %collective-permute-start.19 = (bf16[48,2304]{1,0:T(8,128)(2,1)S(1)}, bf16[48,2304]{1,0:T(8,128)(2,1)S(1)}, u32[]{:S(2)}, u32[]{:S(2)}) collective-permute-start(bf16[48,2304]{1,0:T(8,128)(2,1)S(1)} %collective-permute-done.18), channel_id=1, source_target_pairs={{0,112},{16,0},{32,16},{48,32},{64,48},{80,64},{96,80},{112,96},{1... | collective-permute-start | bytes 663560 | tf_op jit(solution)/shard_map/ppermute | solution.py:57
  120.3 0.7 constant_dynamic-update-slice_fusion.10
  121.7 3.2 %collective-permute-done.19 = bf16[48,2304]{1,0:T(8,128)(2,1)S(1)} collective-permute-done((bf16[48,2304]{1,0:T(8,128)(2,1)S(1)}, bf16[48,2304]{1,0:T(8,128)(2,1)S(1)}, u32[]{:S(2)}, u32[]{:S(2)}) %collective-permute-start.19) | collective-permute-done | bytes 221216 | tf_op jit(solution)/shard_map/ppermute | solution.py:57
  125.0 3.7 %collective-permute-start.20 = (bf16[48,2304]{1,0:T(8,128)(2,1)S(1)}, bf16[48,2304]{1,0:T(8,128)(2,1)S(1)}, u32[]{:S(2)}, u32[]{:S(2)}) collective-permute-start(bf16[48,2304]{1,0:T(8,128)(2,1)S(1)} %collective-permute-done.19), channel_id=1, source_target_pairs={{0,112},{16,0},{32,16},{48,32},{64,48},{80,64},{96,80},{112,96},{1... | collective-permute-start | bytes 663560 | tf_op jit(solution)/shard_map/ppermute | solution.py:57
  130.0 2.1 %collective-permute-done.20 = bf16[48,2304]{1,0:T(8,128)(2,1)S(1)} collective-permute-done((bf16[48,2304]{1,0:T(8,128)(2,1)S(1)}, bf16[48,2304]{1,0:T(8,128)(2,1)S(1)}, u32[]{:S(2)}, u32[]{:S(2)}) %collective-permute-start.20) | collective-permute-done | bytes 221216 | tf_op jit(solution)/shard_map/ppermute | solution.py:57
  132.1 3.8 %collective-permute-start.25 = (bf16[48,1152]{1,0:T(8,128)(2,1)S(1)}, bf16[48,1152]{1,0:T(8,128)(2,1)S(1)}, u32[]{:S(2)}, u32[]{:S(2)}) collective-permute-start(bf16[48,1152]{1,0:T(8,128)(2,1)S(1)} %slice.174), channel_id=1, source_target_pairs={{0,112},{16,0},{32,16},{48,32},{64,48},{80,64},{96,80},{112,96},{1... | collective-permute-start | bytes 331784 | tf_op jit(solution)/shard_map/ppermute | solution.py:57
  137.3 0.9 collective-permute-done.25
  138.2 4.4 %collective-permute-done.24 = bf16[48,1152]{1,0:T(8,128)(2,1)S(1)} collective-permute-done((bf16[48,1152]{1,0:T(8,128)(2,1)S(1)}, bf16[48,1152]{1,0:T(8,128)(2,1)S(1)}, u32[]{:S(2)}, u32[]{:S(2)}) %collective-permute-start.24) | collective-permute-done | bytes 110624 | tf_op jit(solution)/shard_map/ppermute | solution.py:53
  144.0 0.7 constant_dynamic-update-slice_fusion.6
  145.4 1.4 fusion.15
  146.9 1.5 convolution_add_fusion
  148.7 1.3 collective-permute-done.26
  150.7 6.3 %all-to-all-start.3 = ((bf16[8,48,128]{2,1,0:T(8,128)(2,1)}), bf16[8,48,128]{2,1,0:T(8,128)(2,1)S(1)}, u32[]{:S(2)}, u32[]{:S(2)}) async-start(bf16[8,48,128]{2,1,0:T(8,128)(2,1)} %fusion.38), calls=%async_computation.3 | async-start | bytes 196608 | tf_op jit(solution)/shard_map/all_to_all | solution.py:342
  157.2 2.2 %fusion = bf16[1,256,768]{2,1,0:T(8,128)(2,1)} fusion(bf16[384,256]{1,0:T(8,128)(2,1)S(1)} %copy-done.4, bf16[384,2304]{1,0:T(8,128)(2,1)} %constant_dynamic-update-slice_fusion.5), kind=kOutput, calls=%fused_computation.7 | convolution fusion | flops 151191552 | bytes 1179648 | tf_op jit(solution)/shard_map/rd,rf->df/dot_general | solution.py:346
  159.4 2.2 %fusion.2 = bf16[1,768,256]{2,1,0:T(8,128)(2,1)} fusion(bf16[384,256]{1,0:T(8,128)(2,1)S(1)} %copy-done.14, bf16[384,2304]{1,0:T(8,128)(2,1)} %constant_dynamic-update-slice_fusion.5), kind=kOutput, calls=%fused_computation.9 | convolution fusion | flops 151191552 | bytes 1179648 | tf_op jit(solution)/shard_map/rf,rd->fd/dot_general | solution.py:348
  161.6 2.2 %fusion.1 = bf16[1,256,768]{2,1,0:T(8,128)(2,1)} fusion(bf16[384,256]{1,0:T(8,128)(2,1)S(1)} %copy-done.4, bf16[384,2304]{1,0:T(8,128)(2,1)} %constant_dynamic-update-slice_fusion.5), kind=kOutput, calls=%fused_computation.8 | convolution fusion | flops 151191552 | bytes 1179648 | tf_op jit(solution)/shard_map/rd,rf->df/dot_general | solution.py:347
  163.8 2.0 %collective-permute-start.28 = (f32[32,256]{1,0:T(8,128)S(1)}, f32[32,256]{1,0:T(8,128)S(1)}, u32[]{:S(2)}, u32[]{:S(2)}) collective-permute-start(f32[32,256]{1,0:T(8,128)S(1)} %slice.200), channel_id=1, source_target_pairs={{0,64},{16,80},{32,96},{48,112},{64,0},{80,16},{96,32},{112,48},{1... | collective-permute-start | bytes 98312 | tf_op jit(solution)/shard_map/ppermute | solution.py:116
  165.8 1.1 fusion.3
  166.9 4.9 %collective-permute-done.28 = f32[32,256]{1,0:T(8,128)S(1)} collective-permute-done((f32[32,256]{1,0:T(8,128)S(1)}, f32[32,256]{1,0:T(8,128)S(1)}, u32[]{:S(2)}, u32[]{:S(2)}) %collective-permute-start.28) | collective-permute-done | bytes 32800 | tf_op jit(solution)/shard_map/ppermute | solution.py:116
  (125 shorter events, 12.1 us)
Async XLA Ops:
  0.6 36.3 %copy-start = (bf16[1,256,1536]{2,1,0:T(8,128)(2,1)S(1)}, bf16[1,256,1536]{2,1,0:T(8,128)(2,1)}, u32[]{:S(2)}) copy-start(bf16[1,256,1536]{2,1,0:T(8,128)(2,1)} %param.19) | copy-start | bytes 2359300
  0.6 13.2 %copy-start.19 = (bf16[32,1,128]{2,0,1:T(8,128)(2,1)S(1)}, bf16[32,1,128]{2,0,1:T(8,128)(2,1)}, u32[]{:S(2)}) copy-start(bf16[32,1,128]{2,0,1:T(8,128)(2,1)} %param.13) | copy-start | bytes 24580
  0.7 13.2 %copy-start.20 = (bf16[32,1,128]{2,0,1:T(8,128)(2,1)S(1)}, bf16[32,1,128]{2,0,1:T(8,128)(2,1)}, u32[]{:S(2)}) copy-start(bf16[32,1,128]{2,0,1:T(8,128)(2,1)} %param.12) | copy-start | bytes 24580
  1.5 12.4 %collective-permute-start.1 = (bf16[32,256]{1,0:T(8,128)(2,1)S(1)}, bf16[32,256]{1,0:T(8,128)(2,1)S(1)}, u32[]{:S(2)}, u32[]{:S(2)}) collective-permute-start(bf16[32,256]{1,0:T(8,128)(2,1)S(1)} %get-tuple-element.58), channel_id=1, source_target_pairs={{0,64},{16,80},{32,96},{48,112},{64,0},{80,16},{96,32},{112,48},{1... | collective-permute-start | bytes 49160 | tf_op jit(solution)/shard_map/ppermute | solution.py:116
  11.0 5.3 %copy-start.15 = (s32[512,8]{0,1:T(8,128)}, s32[512,8]{0,1:T(8,128)S(1)}, u32[]{:S(2)}) copy-start(s32[512,8]{0,1:T(8,128)S(1)} %bitcast_subtract_fusion) | copy-start | bytes 49156
  13.9 8.4 %collective-permute-start.2 = (bf16[64,256]{1,0:T(8,128)(2,1)S(1)}, bf16[64,256]{1,0:T(8,128)(2,1)S(1)}, u32[]{:S(2)}, u32[]{:S(2)}) collective-permute-start(bf16[64,256]{1,0:T(8,128)(2,1)S(1)} %pad_maximum_fusion.12), channel_id=1, source_target_pairs={{0,32},{16,48},{32,0},{48,16},{64,96},{80,112},{96,64},{112,80},{1... | collective-permute-start | bytes 98312 | tf_op jit(solution)/shard_map/ppermute | solution.py:116
  16.2 20.4 %copy-start.12 = (bf16[1,256,1536]{2,1,0:T(8,128)(2,1)S(1)}, bf16[1,256,1536]{2,1,0:T(8,128)(2,1)}, u32[]{:S(2)}) copy-start(bf16[1,256,1536]{2,1,0:T(8,128)(2,1)} %param.20) | copy-start | bytes 2359300
  16.3 18.7 %all-to-all-start = ((bf16[8,48,512]{2,1,0:T(8,128)(2,1)}), bf16[8,48,512]{2,1,0:T(8,128)(2,1)S(1)}, u32[]{:S(2)}, u32[]{:S(2)}) async-start(bf16[8,48,512]{2,1,0:T(8,128)(2,1)} %bitcast.14), calls=%async_computation | async-start | bytes 786432 | tf_op jit(solution)/shard_map/all_to_all | solution.py:296
  22.3 7.5 %collective-permute-start.3 = (bf16[128,256]{1,0:T(8,128)(2,1)S(1)}, bf16[128,256]{1,0:T(8,128)(2,1)S(1)}, u32[]{:S(2)}, u32[]{:S(2)}) collective-permute-start(bf16[128,256]{1,0:T(8,128)(2,1)S(1)} %pad_maximum_fusion.11), channel_id=1, source_target_pairs={{0,128},{16,144},{32,160},{48,176},{64,192},{80,208},{96,224},{112... | collective-permute-start | bytes 196616 | tf_op jit(solution)/shard_map/ppermute | solution.py:116
  29.8 5.1 %collective-permute-start.4 = (bf16[256,256]{1,0:T(8,128)(2,1)S(1)}, bf16[256,256]{1,0:T(8,128)(2,1)S(1)}, u32[]{:S(2)}, u32[]{:S(2)}) collective-permute-start(bf16[256,256]{1,0:T(8,128)(2,1)S(1)} %pad_maximum_fusion.7), channel_id=1, source_target_pairs={{0,16},{16,0},{32,48},{48,32},{64,80},{80,64},{96,112},{112,96},{1... | collective-permute-start | bytes 393224 | tf_op jit(solution)/shard_map/ppermute | solution.py:116
  35.1 10.0 %copy-start.3 = (bf16[8,48,512]{2,1,0:T(8,128)(2,1)}, bf16[8,48,512]{2,1,0:T(8,128)(2,1)S(1)}, u32[]{:S(2)}) copy-start(bf16[8,48,512]{2,1,0:T(8,128)(2,1)S(1)} %fusion.19) | copy-start | bytes 1179652
  37.3 23.1 %copy-start.1 = (bf16[384,768]{1,0:T(8,128)(2,1)}, bf16[384,768]{1,0:T(8,128)(2,1)S(1)}, u32[]{:S(2)}) copy-start(bf16[384,768]{1,0:T(8,128)(2,1)S(1)} %convolution_convert_fusion.2) | copy-start | bytes 1769476
  37.3 6.0 %collective-permute-start.9 = (bf16[48,1152]{1,0:T(8,128)(2,1)S(1)}, bf16[48,1152]{1,0:T(8,128)(2,1)S(1)}, u32[]{:S(2)}, u32[]{:S(2)}) collective-permute-start(bf16[48,1152]{1,0:T(8,128)(2,1)S(1)} %get-tuple-element.26), channel_id=1, source_target_pairs={{0,16},{16,32},{32,48},{48,64},{64,80},{80,96},{96,112},{112,0},{1... | collective-permute-start | bytes 331784 | tf_op jit(solution)/shard_map/ppermute | solution.py:53
  38.4 4.9 %collective-permute-start.13 = (bf16[48,1152]{1,0:T(8,128)(2,1)S(1)}, bf16[48,1152]{1,0:T(8,128)(2,1)S(1)}, u32[]{:S(2)}, u32[]{:S(2)}) collective-permute-start(bf16[48,1152]{1,0:T(8,128)(2,1)S(1)} %get-tuple-element.28), channel_id=1, source_target_pairs={{0,112},{16,0},{32,16},{48,32},{64,48},{80,64},{96,80},{112,96},{1... | collective-permute-start | bytes 331784 | tf_op jit(solution)/shard_map/ppermute | solution.py:57
  43.4 1.5 copy-start.17
  43.4 1.6 copy-start.18
  44.2 7.7 %collective-permute-start.10 = (bf16[48,2304]{1,0:T(8,128)(2,1)S(1)}, bf16[48,2304]{1,0:T(8,128)(2,1)S(1)}, u32[]{:S(2)}, u32[]{:S(2)}) collective-permute-start(bf16[48,2304]{1,0:T(8,128)(2,1)S(1)} %get-tuple-element.43), channel_id=1, source_target_pairs={{0,16},{16,32},{32,48},{48,64},{64,80},{80,96},{96,112},{112,0},{1... | collective-permute-start | bytes 663560 | tf_op jit(solution)/shard_map/ppermute | solution.py:53
  45.0 7.8 %copy-start.5 = (bf16[2,256,128]{2,1,0:T(8,128)(2,1)}, bf16[2,256,128]{2,1,0:T(8,128)(2,1)S(1)}, u32[]{:S(2)}) copy-start(bf16[2,256,128]{2,1,0:T(8,128)(2,1)S(1)} %copy.28) | copy-start | bytes 393220
  45.1 7.7 %copy-start.6 = (bf16[2,256,128]{2,1,0:T(8,128)(2,1)}, bf16[2,256,128]{2,1,0:T(8,128)(2,1)S(1)}, u32[]{:S(2)}) copy-start(bf16[2,256,128]{2,1,0:T(8,128)(2,1)S(1)} %copy.29) | copy-start | bytes 393220
  45.1 8.5 %collective-permute-start.14 = (bf16[48,2304]{1,0:T(8,128)(2,1)}, bf16[48,2304]{1,0:T(8,128)(2,1)}, u32[]{:S(2)}, u32[]{:S(2)}) collective-permute-start(bf16[48,2304]{1,0:T(8,128)(2,1)} %get-tuple-element.44), channel_id=1, source_target_pairs={{0,112},{16,0},{32,16},{48,32},{64,48},{80,64},{96,80},{112,96},{1... | collective-permute-start | bytes 663560 | tf_op jit(solution)/shard_map/ppermute | solution.py:57
  52.6 7.8 %collective-permute-start.11 = (bf16[48,2304]{1,0:T(8,128)(2,1)}, bf16[48,2304]{1,0:T(8,128)(2,1)}, u32[]{:S(2)}, u32[]{:S(2)}) collective-permute-start(bf16[48,2304]{1,0:T(8,128)(2,1)} %add_convert_fusion.3), channel_id=1, source_target_pairs={{0,16},{16,32},{32,48},{48,64},{64,80},{80,96},{96,112},{112,0},{1... | collective-permute-start | bytes 663560 | tf_op jit(solution)/shard_map/ppermute | solution.py:53
  52.8 11.6 %collective-permute-start = (bf16[1024,128]{1,0:T(8,128)(2,1)S(1)}, bf16[1024,128]{1,0:T(8,128)(2,1)S(1)}, u32[]{:S(2)}, u32[]{:S(2)}) collective-permute-start(bf16[1024,128]{1,0:T(8,128)(2,1)S(1)} %pad_maximum_fusion.1), channel_id=1, source_target_pairs={{0,1},{1,0},{2,3},{3,2},{4,5},{5,4},{6,7},{7,6},{8,9},{9,8},{10,11... | collective-permute-start | bytes 786440 | tf_op jit(solution)/shard_map/ppermute | solution.py:44
  62.3 9.4 %collective-permute-start.15 = (bf16[48,2304]{1,0:T(8,128)(2,1)}, bf16[48,2304]{1,0:T(8,128)(2,1)}, u32[]{:S(2)}, u32[]{:S(2)}) collective-permute-start(bf16[48,2304]{1,0:T(8,128)(2,1)} %get-tuple-element.42), channel_id=1, source_target_pairs={{0,112},{16,0},{32,16},{48,32},{64,48},{80,64},{96,80},{112,96},{1... | collective-permute-start | bytes 663560 | tf_op jit(solution)/shard_map/ppermute | solution.py:57
  66.1 15.3 %all-to-all-start.1 = ((bf16[4,512,256]{2,1,0:T(8,128)(2,1)}), bf16[4,512,256]{2,1,0:T(8,128)(2,1)S(1)}, u32[]{:S(2)}, u32[]{:S(2)}) async-start(bf16[4,512,256]{2,1,0:T(8,128)(2,1)} %broadcast_in_dim.56), calls=%async_computation.1 | async-start | bytes 2097152 | tf_op jit(solution)/shard_map/all_to_all | solution.py:35
  81.5 10.2 %collective-permute-start.16 = (bf16[48,2304]{1,0:T(8,128)(2,1)}, bf16[48,2304]{1,0:T(8,128)(2,1)S(1)}, u32[]{:S(2)}, u32[]{:S(2)}) collective-permute-start(bf16[48,2304]{1,0:T(8,128)(2,1)} %add_convert_fusion), channel_id=1, source_target_pairs={{0,112},{16,0},{32,16},{48,32},{64,48},{80,64},{96,80},{112,96},{1... | collective-permute-start | bytes 663560 | tf_op jit(solution)/shard_map/ppermute | solution.py:57
  81.5 10.2 %collective-permute-start.12 = (bf16[48,2304]{1,0:T(8,128)(2,1)}, bf16[48,2304]{1,0:T(8,128)(2,1)S(1)}, u32[]{:S(2)}, u32[]{:S(2)}) collective-permute-start(bf16[48,2304]{1,0:T(8,128)(2,1)} %get-tuple-element.27), channel_id=1, source_target_pairs={{0,16},{16,32},{32,48},{48,64},{64,80},{80,96},{96,112},{112,0},{1... | collective-permute-start | bytes 663560 | tf_op jit(solution)/shard_map/ppermute | solution.py:53
  85.3 6.4 %copy-start.2 = (bf16[384,768]{1,0:T(8,128)(2,1)S(1)}, bf16[384,768]{1,0:T(8,128)(2,1)}, u32[]{:S(2)}) copy-start(bf16[384,768]{1,0:T(8,128)(2,1)} %copy-done.1) | copy-start | bytes 1769476
  90.4 4.0 %collective-permute-start.5 = (f32[8,1024]{1,0:T(8,128)S(1)}, f32[8,1024]{1,0:T(8,128)S(1)}, u32[]{:S(2)}, u32[]{:S(2)}) collective-permute-start(f32[8,1024]{1,0:T(8,128)S(1)} %attention_stats.1.stats_ref), channel_id=1, source_target_pairs={{0,1},{1,0},{2,3},{3,2},{4,5},{5,4},{6,7},{7,6},{8,9},{9,8},{10,11... | collective-permute-start | bytes 98312 | tf_op jit(solution)/shard_map/ppermute | solution.py:44
  91.7 1.1 copy-start.7
  91.7 1.1 copy-start.9
  92.6 16.2 %collective-permute-start.17 = (bf16[48,2304]{1,0:T(8,128)(2,1)}, bf16[48,2304]{1,0:T(8,128)(2,1)}, u32[]{:S(2)}, u32[]{:S(2)}) collective-permute-start(bf16[48,2304]{1,0:T(8,128)(2,1)} %get-tuple-element.39), channel_id=1, source_target_pairs={{0,128},{16,144},{32,160},{48,176},{64,192},{80,208},{96,224},{112... | collective-permute-start | bytes 663560 | tf_op jit(solution)/shard_map/ppermute | solution.py:62
  104.0 4.9 %copy-start.8 = (bf16[48,2304]{1,0:T(8,128)(2,1)S(1)}, bf16[48,2304]{1,0:T(8,128)(2,1)}, u32[]{:S(2)}) copy-start(bf16[48,2304]{1,0:T(8,128)(2,1)} %copy-done.7) | copy-start | bytes 663556
  104.0 4.9 %copy-start.10 = (bf16[48,2304]{1,0:T(8,128)(2,1)S(1)}, bf16[48,2304]{1,0:T(8,128)(2,1)}, u32[]{:S(2)}) copy-start(bf16[48,2304]{1,0:T(8,128)(2,1)} %copy-done.9) | copy-start | bytes 663556
  104.0 4.9 %copy-start.11 = (bf16[48,2304]{1,0:T(8,128)(2,1)S(1)}, bf16[48,2304]{1,0:T(8,128)(2,1)}, u32[]{:S(2)}) copy-start(bf16[48,2304]{1,0:T(8,128)(2,1)} %get-tuple-element.40) | copy-start | bytes 663556
  104.0 8.8 %collective-permute-start.6 = (bf16[512,128]{1,0:T(8,128)(2,1)S(1)}, bf16[512,128]{1,0:T(8,128)(2,1)S(1)}, u32[]{:S(2)}, u32[]{:S(2)}) collective-permute-start(bf16[512,128]{1,0:T(8,128)(2,1)S(1)} %slice.249), channel_id=1, source_target_pairs={{0,1},{1,0},{2,3},{3,2},{4,5},{5,4},{6,7},{7,6},{8,9},{9,8},{10,11... | collective-permute-start | bytes 393224 | tf_op jit(solution)/shard_map/ppermute | solution.py:44
  105.3 15.7 %all-to-all-start.2 = ((bf16[4,512,256]{2,1,0:T(8,128)(2,1)}), bf16[4,512,256]{2,1,0:T(8,128)(2,1)S(1)}, u32[]{:S(2)}, u32[]{:S(2)}) async-start(bf16[4,512,256]{2,1,0:T(8,128)(2,1)} %bitcast.18), calls=%async_computation.2 | async-start | bytes 2097152 | tf_op jit(solution)/shard_map/all_to_all | solution.py:39
  110.7 7.3 %collective-permute-start.18 = (bf16[48,2304]{1,0:T(8,128)(2,1)S(1)}, bf16[48,2304]{1,0:T(8,128)(2,1)S(1)}, u32[]{:S(2)}, u32[]{:S(2)}) collective-permute-start(bf16[48,2304]{1,0:T(8,128)(2,1)S(1)} %get-tuple-element.56), channel_id=1, source_target_pairs={{0,112},{16,0},{32,16},{48,32},{64,48},{80,64},{96,80},{112,96},{1... | collective-permute-start | bytes 663560 | tf_op jit(solution)/shard_map/ppermute | solution.py:57
  112.0 8.4 %collective-permute-start.21 = (bf16[48,2304]{1,0:T(8,128)(2,1)S(1)}, bf16[48,2304]{1,0:T(8,128)(2,1)S(1)}, u32[]{:S(2)}, u32[]{:S(2)}) collective-permute-start(bf16[48,2304]{1,0:T(8,128)(2,1)S(1)} %get-tuple-element.56), channel_id=1, source_target_pairs={{0,16},{16,32},{32,48},{48,64},{64,80},{80,96},{96,112},{112,0},{1... | collective-permute-start | bytes 663560 | tf_op jit(solution)/shard_map/ppermute | solution.py:53
  118.0 7.0 %collective-permute-start.19 = (bf16[48,2304]{1,0:T(8,128)(2,1)S(1)}, bf16[48,2304]{1,0:T(8,128)(2,1)S(1)}, u32[]{:S(2)}, u32[]{:S(2)}) collective-permute-start(bf16[48,2304]{1,0:T(8,128)(2,1)S(1)} %collective-permute-done.18), channel_id=1, source_target_pairs={{0,112},{16,0},{32,16},{48,32},{64,48},{80,64},{96,80},{112,96},{1... | collective-permute-start | bytes 663560 | tf_op jit(solution)/shard_map/ppermute | solution.py:57
  120.3 9.0 %collective-permute-start.22 = (bf16[48,2304]{1,0:T(8,128)(2,1)S(1)}, bf16[48,2304]{1,0:T(8,128)(2,1)S(1)}, u32[]{:S(2)}, u32[]{:S(2)}) collective-permute-start(bf16[48,2304]{1,0:T(8,128)(2,1)S(1)} %collective-permute-done.21), channel_id=1, source_target_pairs={{0,16},{16,32},{32,48},{48,64},{64,80},{80,96},{96,112},{112,0},{1... | collective-permute-start | bytes 663560 | tf_op jit(solution)/shard_map/ppermute | solution.py:53
  121.2 8.2 %collective-permute-start.7 = (bf16[256,256]{1,0:T(8,128)(2,1)S(1)}, bf16[256,256]{1,0:T(8,128)(2,1)S(1)}, u32[]{:S(2)}, u32[]{:S(2)}) collective-permute-start(bf16[256,256]{1,0:T(8,128)(2,1)S(1)} %slice.248), channel_id=1, source_target_pairs={{0,16},{16,0},{32,48},{48,32},{64,80},{80,64},{96,112},{112,96},{1... | collective-permute-start | bytes 393224 | tf_op jit(solution)/shard_map/ppermute | solution.py:116
  125.0 7.1 %collective-permute-start.20 = (bf16[48,2304]{1,0:T(8,128)(2,1)S(1)}, bf16[48,2304]{1,0:T(8,128)(2,1)S(1)}, u32[]{:S(2)}, u32[]{:S(2)}) collective-permute-start(bf16[48,2304]{1,0:T(8,128)(2,1)S(1)} %collective-permute-done.19), channel_id=1, source_target_pairs={{0,112},{16,0},{32,16},{48,32},{64,48},{80,64},{96,80},{112,96},{1... | collective-permute-start | bytes 663560 | tf_op jit(solution)/shard_map/ppermute | solution.py:57
  129.4 7.1 %collective-permute-start.23 = (bf16[48,2304]{1,0:T(8,128)(2,1)S(1)}, bf16[48,2304]{1,0:T(8,128)(2,1)S(1)}, u32[]{:S(2)}, u32[]{:S(2)}) collective-permute-start(bf16[48,2304]{1,0:T(8,128)(2,1)S(1)} %collective-permute-done.22), channel_id=1, source_target_pairs={{0,16},{16,32},{32,48},{48,64},{64,80},{80,96},{96,112},{112,0},{1... | collective-permute-start | bytes 663560 | tf_op jit(solution)/shard_map/ppermute | solution.py:53
  129.4 19.3 %collective-permute-start.8 = (bf16[128,256]{1,0:T(8,128)(2,1)S(1)}, bf16[128,256]{1,0:T(8,128)(2,1)S(1)}, u32[]{:S(2)}, u32[]{:S(2)}) collective-permute-start(bf16[128,256]{1,0:T(8,128)(2,1)S(1)} %slice.250), channel_id=1, source_target_pairs={{0,128},{16,144},{32,160},{48,176},{64,192},{80,208},{96,224},{112... | collective-permute-start | bytes 196616 | tf_op jit(solution)/shard_map/ppermute | solution.py:116
  132.1 6.1 %collective-permute-start.25 = (bf16[48,1152]{1,0:T(8,128)(2,1)S(1)}, bf16[48,1152]{1,0:T(8,128)(2,1)S(1)}, u32[]{:S(2)}, u32[]{:S(2)}) collective-permute-start(bf16[48,1152]{1,0:T(8,128)(2,1)S(1)} %slice.174), channel_id=1, source_target_pairs={{0,112},{16,0},{32,16},{48,32},{64,48},{80,64},{96,80},{112,96},{1... | collective-permute-start | bytes 331784 | tf_op jit(solution)/shard_map/ppermute | solution.py:57
  136.5 10.3 %copy-start.13 = (bf16[1,256,1536]{2,1,0:T(8,128)(2,1)S(1)}, bf16[1,256,1536]{2,1,0:T(8,128)(2,1)}, u32[]{:S(2)}) copy-start(bf16[1,256,1536]{2,1,0:T(8,128)(2,1)} %param.20) | copy-start | bytes 2359300
  136.5 6.0 %collective-permute-start.24 = (bf16[48,1152]{1,0:T(8,128)(2,1)S(1)}, bf16[48,1152]{1,0:T(8,128)(2,1)S(1)}, u32[]{:S(2)}, u32[]{:S(2)}) collective-permute-start(bf16[48,1152]{1,0:T(8,128)(2,1)S(1)} %slice.173), channel_id=1, source_target_pairs={{0,16},{16,32},{32,48},{48,64},{64,80},{80,96},{96,112},{112,0},{1... | collective-permute-start | bytes 331784 | tf_op jit(solution)/shard_map/ppermute | solution.py:53
  146.8 10.3 %copy-start.4 = (bf16[384,256]{1,0:T(8,128)(2,1)S(1)}, bf16[384,256]{1,0:T(8,128)(2,1)}, u32[]{:S(2)}) copy-start(bf16[384,256]{1,0:T(8,128)(2,1)} %get-tuple-element.37) | copy-start | bytes 589828
  146.8 12.5 %copy-start.14 = (bf16[384,256]{1,0:T(8,128)(2,1)S(1)}, bf16[384,256]{1,0:T(8,128)(2,1)}, u32[]{:S(2)}) copy-start(bf16[384,256]{1,0:T(8,128)(2,1)} %get-tuple-element.38) | copy-start | bytes 589828
  148.4 1.6 collective-permute-start.26
  150.7 15.1 %all-to-all-start.3 = ((bf16[8,48,128]{2,1,0:T(8,128)(2,1)}), bf16[8,48,128]{2,1,0:T(8,128)(2,1)S(1)}, u32[]{:S(2)}, u32[]{:S(2)}) async-start(bf16[8,48,128]{2,1,0:T(8,128)(2,1)} %fusion.38), calls=%async_computation.3 | async-start | bytes 196608 | tf_op jit(solution)/shard_map/all_to_all | solution.py:342
  157.0 6.8 %collective-permute-start.27 = (f32[64,256]{1,0:T(8,128)S(1)}, f32[64,256]{1,0:T(8,128)S(1)}, u32[]{:S(2)}, u32[]{:S(2)}) collective-permute-start(f32[64,256]{1,0:T(8,128)S(1)} %slice.178), channel_id=1, source_target_pairs={{0,32},{16,48},{32,0},{48,16},{64,96},{80,112},{96,64},{112,80},{1... | collective-permute-start | bytes 196616 | tf_op jit(solution)/shard_map/ppermute | solution.py:116
  157.1 8.7 %copy-start.16 = (s32[512,8]{0,1:T(8,128)S(1)}, s32[512,8]{0,1:T(8,128)}, u32[]{:S(2)}) copy-start(s32[512,8]{0,1:T(8,128)} %copy-done.15) | copy-start | bytes 49156
  163.8 7.9 %collective-permute-start.28 = (f32[32,256]{1,0:T(8,128)S(1)}, f32[32,256]{1,0:T(8,128)S(1)}, u32[]{:S(2)}, u32[]{:S(2)}) collective-permute-start(f32[32,256]{1,0:T(8,128)S(1)} %slice.200), channel_id=1, source_target_pairs={{0,64},{16,80},{32,96},{48,112},{64,0},{80,16},{96,32},{112,48},{1... | collective-permute-start | bytes 98312 | tf_op jit(solution)/shard_map/ppermute | solution.py:116

commit v6 on v5

--- a/solution.py
+++ b/solution.py
@@ -103,7 +103,7 @@
         blocks[n - step], blocks[step] = onward, back
     if far in waits:
         onward, back = after(onward, waits[far]), after(back, waits[far])
-    blocks[far] = jnp.concatenate([right(onward[:, :cut]), left(back[:, cut:])], axis=1)
+    blocks[far : far + 1] = [right(onward[:, :cut]), left(back[:, cut:])]
     return blocks
 
 
@@ -323,30 +323,102 @@
     return jnp.concatenate([hidden, d_gate, d_up], axis=1)
 
 
-def finish(full, input_rows, grad_rows, gate_mat, up_mat, placed_low, sums):
-    exp_size, head_size = lax.axis_size("exp"), lax.axis_size("head")
+def contrib_body(width, half_ref, gate_ref, up_ref, *refs):
+    blocks, (mine_ref, other_ref, full_ref) = refs[:-3], refs[-3:]
+    height = blocks[0].shape[0]
+    units = full_ref.shape[1] // 3
+    row = 0
+    halves = [block for block in blocks if block.shape[1] < full_ref.shape[1]]
+    for block in blocks:
+        if block is halves[0]:
+            cut = block.shape[1]
+            full_ref[row : row + height, :cut] = block[...]
+            continue
+        if block is halves[1]:
+            full_ref[row : row + height, cut:] = block[...]
+        else:
+            full_ref[row : row + height, :] = block[...]
+        row += height
+    across = (((1,), (1,)), ((), ()))
+    found = lax.dot_general(
+        full_ref[:, units : 2 * units], gate_ref[...], across, preferred_element_type=F32
+    ) + lax.dot_general(full_ref[:, 2 * units :], up_ref[...], across, preferred_element_type=F32)
+    first = half_ref[0] == 0
+    mine_ref[...] = jnp.where(first, found[:, :width], found[:, width:])
+    other_ref[...] = jnp.where(first, found[:, width:], found[:, :width]).astype(BF)
+
+
+def weights_body(full_ref, input_ref, grad_ref, gate_ref, up_ref, down_ref):
+    units = full_ref.shape[1] // 3
+    down = (((0,), (0,)), ((), ()))
+
+    def product(a, b):
+        return lax.dot_general(a, b, down, preferred_element_type=F32).astype(BF)
+
+    gate_ref[0] = product(input_ref[...], full_ref[:, units : 2 * units])
+    up_ref[0] = product(input_ref[...], full_ref[:, 2 * units :])
+    down_ref[0] = product(full_ref[:, :units], grad_ref[...])
+
+
+def contributions(blocks, gate_mat, up_mat):
+    rows = len(blocks) // 2 * 2 * blocks[0].shape[0]
+    columns = gate_mat.shape[0] // lax.axis_size("head")
+    whole = blocks[0].shape[1]
+    return pl.pallas_call(
+        functools.partial(contrib_body, columns),
+        out_shape=(
+            jax.ShapeDtypeStruct((rows, columns), F32),
+            jax.ShapeDtypeStruct((rows, columns), BF),
+            jax.ShapeDtypeStruct((rows, whole), BF),
+        ),
+        in_specs=[SMEM] + [VMEM] * (2 + len(blocks)),
+        out_specs=(VMEM,) * 3,
+        compiler_params=pltpu.CompilerParams(vmem_limit_bytes=24 * 2**20),
+        cost_estimate=pl.CostEstimate(
+            flops=4 * rows * whole // 3 * gate_mat.shape[0],
+            bytes_accessed=4 * rows * whole,
+            transcendentals=0,
+        ),
+        name="expert_contrib",
+    )(lax.axis_index("head").astype(jnp.int32).reshape(1), gate_mat, up_mat, *blocks)
+
+
+def weight_grads(full, input_rows, grad_rows):
+    units, width = full.shape[1] // 3, input_rows.shape[1]
+    return pl.pallas_call(
+        weights_body,
+        out_shape=(
+            jax.ShapeDtypeStruct((1, width, units), BF),
+            jax.ShapeDtypeStruct((1, width, units), BF),
+            jax.ShapeDtypeStruct((1, units, width), BF),
+        ),
+        in_specs=[VMEM] * 3,
+        out_specs=(VMEM,) * 3,
+        compiler_params=pltpu.CompilerParams(vmem_limit_bytes=24 * 2**20),
+        cost_estimate=pl.CostEstimate(
+            flops=6 * full.shape[0] * units * width,
+            bytes_accessed=4 * full.size,
+            transcendentals=0,
+        ),
+        name="expert_weight_grads",
+    )(full, input_rows, grad_rows)
+
+
+def finish(blocks, input_rows, grad_rows, gate_mat, up_mat, placed_low, sums):
+    exp_size = lax.axis_size("exp")
     ring = lax.axis_size("ctx") // X_HI
     at = lax.axis_index("ctx") % ring
-    half = lax.axis_index("head")
-    units = full.shape[1] // 3
-    columns = input_rows.shape[1] // head_size
-    hidden, d_gate, d_up = full[:, :units], full[:, units : 2 * units], full[:, 2 * units :]
-    contrib = jnp.einsum("rf,df->rd", d_gate, gate_mat, preferred_element_type=F32)
-    contrib = contrib + jnp.einsum("rf,df->rd", d_up, up_mat, preferred_element_type=F32)
-    mine = lax.dynamic_slice_in_dim(contrib, half * columns, columns, 1)
-    other = lax.dynamic_slice_in_dim(contrib, (1 - half) * columns, columns, 1).astype(BF)
+    mine, other, full = contributions(blocks, gate_mat, up_mat)
+    columns = mine.shape[1]
     mine = (mine + lax.ppermute(other, "head", [(0, 1), (1, 0)]).astype(F32)).astype(BF)
     mine = turn(mine.reshape(ring, -1, columns), (ring - at) % ring).reshape(exp_size, CAP, columns)
-    input_rows, grad_rows = after(input_rows, mine), after(grad_rows, mine)
-    sums = ctx_sum(after(sums, mine), MASKS[:2])
+    mine = after(mine, sums)
     back_rows = lax.all_to_all(mine, "exp", 0, 0, tiled=True)
     grad_input = jnp.dot(
         placed_low, back_rows.reshape(-1, columns), preferred_element_type=F32
     ).astype(BF)
-    grad_gate = jnp.einsum("rd,rf->df", input_rows, d_gate, preferred_element_type=F32).astype(BF)
-    grad_up = jnp.einsum("rd,rf->df", input_rows, d_up, preferred_element_type=F32).astype(BF)
-    grad_down = jnp.einsum("rf,rd->fd", hidden, grad_rows, preferred_element_type=F32).astype(BF)
-    return grad_input, grad_gate[None], grad_up[None], grad_down[None], sums
+    sums = ctx_sum(after(sums, mine), MASKS[:1])
+    return (grad_input,) + tuple(weight_grads(after(full, mine), input_rows, grad_rows)) + (sums,)
 
 
 def shards(
@@ -370,31 +442,32 @@
     placed_low, got = select(moe_input, moe_grad, expert_ids, router_weight)
     mine = jnp.concatenate([by_head(queries), by_head(grad_attn)], axis=0)
     theirs = beside(mine)
-    flat = y_gather(after(near, got, theirs)).reshape(-1, near.shape[1])
+    flat = y_gather(after(near, got)).reshape(-1, near.shape[1])
     queries = jnp.concatenate([mine[:rows], theirs[:rows]], axis=0)
     grads = jnp.concatenate([mine[rows:], theirs[rows:]], axis=0)
     input_rows, grad_rows, gate_mat, up_mat, parts = project(
         got, gate_weight, up_weight, down_weight
     )
     onward, back = sum_start(parts)
-    onward, back = after(onward, near), after(back, near)
-    for step in range(len(parts) // 2):
-        if step == 3:
-            onward, back = after(onward, flat), after(back, flat)
-        onward, back = sum_step(parts, step, onward, back)
+    onward, back = after(onward, near, theirs), after(back, near, theirs)
+    onward, back = sum_step(parts, 0, onward, back)
+    onward, back = sum_step(parts, 1, onward, back)
+    onward, back = after(onward, flat), after(back, flat)
+    stats = attention_stats(own, tokens, queries, grads, flat)
+    onward, back = sum_step(parts, 2, onward, back)
+    onward, back = sum_step(parts, 3, after(onward, stats), after(back, stats))
     total = onward.astype(F32) + back.astype(F32) + parts[0].astype(F32)
     other = opposite(total.astype(BF))
-    stats = attention_stats(own, tokens, queries, grads, flat)
-    block = act_block(total + after(other, stats).astype(F32))
     both, grad_query = attention_grads(
-        own, tokens, queries, grads, flat, stats, beside(stats)
-    )
+        own, tokens, queries, grads, after(flat, total), stats, beside(stats)
+    )
+    block = act_block(total + after(other, both).astype(F32))
     sums = y_sum(both.reshape((-1,) + near.shape))
-    blocks = ring_gather(block, {2: both, 4: sums})
-    sums = ctx_sum(sums, MASKS[3:])
-    full = after(jnp.concatenate(blocks, axis=0), sums)
-    sums = ctx_sum(sums, MASKS[2:3])
-    of_experts = finish(full, input_rows, grad_rows, gate_mat, up_mat, placed_low, sums)
+    blocks = ring_gather(block, {3: sums})
+    sums = ctx_sum(sums, MASKS[2:])
+    blocks[0] = after(block, sums)
+    sums = ctx_sum(sums, MASKS[1:2])
+    of_experts = finish(blocks, input_rows, grad_rows, gate_mat, up_mat, placed_low, sums)
     grad_query = grad_query[:rows] + beside(grad_query[rows:].astype(BF)).astype(F32)
     grad_query = jnp.swapaxes(grad_query.astype(BF).reshape(-1, tokens, size), 0, 1)
     grad_key, grad_value = own_grads(of_experts[-1])

time: 174 us -> 165 us (0.948)
  matrix products: 14.1 us -> 3.36 us
  starting transfers between devices: 62.5 us -> 66.7 us
  waiting for transfers between devices: 54.1 us -> 51.2 us
  other arithmetic: 16.5 us -> 14.1 us
  local copies, waits for them, and re-layouts: 9.86 us -> 11.6 us
    ppermute x8, waiting for transfers between devices: 10.6 us -> 0.02 us  [left(): return lax.ppermute(block, 'ctx', z_shift(-1))]
    dot_general x5 -> x0, matrix products: 9.51 us -> none  [the longest x1 2.22 us: finish(): jnp.einsum('rf,rd->fd', hidden, grad_rows, preferred_element_type=F32)]
    all_to_all x1, waiting for transfers between devices: 0.01 us -> 6.16 us  [y_sum(): lax.all_to_all(parts, 'exp', 0, 0, tiled=True, axis_index_groups=y_groups())]
    ppermute x8, starting transfers between devices: 18 us -> 24.1 us  [left(): return lax.ppermute(block, 'ctx', z_shift(-1))]
    ppermute x8, waiting for transfers between devices: 18.6 us -> 22.2 us  [right(): return lax.ppermute(block, 'ctx', z_shift(1))]
    ppermute x1, starting transfers between devices: 0.22 us -> 2.39 us  [opposite(): lax.ppermute(block, 'ctx', [(c, (c + n // X_HI) % n) for c in range(n)])]
    pallas_call x0 -> x2, Pallas kernels: none -> 2.07 us  [the longest x1 1.55 us: weight_grads(): pl.pallas_call(weights_body, out_shape=(jax.ShapeDtypeStruct((1, width, u...]
    all_to_all x1, starting transfers between devices: 6.31 us -> 4.38 us  [finish(): back_rows = lax.all_to_all(mine, 'exp', 0, 0, tiled=True)]
  transfers between devices with their start and end apart: 33 -> 33, of which waited for: 15 -> 13; matrix products, arithmetic and copies ran while one was open for 20% -> 12% of each run, Pallas kernels for 8% -> 10%
where the time goes in v6:
time: 165 us; the launch traced here: 164 us
  starting transfers between devices  66.7 us (40%)
  waiting for transfers between devices  51.2 us (31%)
  Pallas kernels  16 us (10%)
  other arithmetic  14.1 us (9%)
  local copies, waits for them, and re-layouts  11.6 us (7%)
  matrix products  3.36 us (2%)
    ppermute x8, starting transfers between devices, left(): return lax.ppermute(block, 'ctx', z_shift(-1))  24.1 us
    ppermute x8, waiting for transfers between devices, right(): return lax.ppermute(block, 'ctx', z_shift(1))  22.2 us
    ppermute x8, waiting for transfers between devices, swap(): lax.ppermute(block, 'ctx', [(c, c ^ mask) for c in range(lax.axis_size('c...  15.3 us
    ppermute x8, starting transfers between devices, swap(): lax.ppermute(block, 'ctx', [(c, c ^ mask) for c in range(lax.axis_size('c...  14.5 us
    pallas_call x1, Pallas kernels, attention_grads(): pl.pallas_call(functools.partial(grads_body, own, lax.axis_size('ctx'), t...  8.83 us
    all_to_all x1, waiting for transfers between devices, y_gather(): lax.all_to_all(copies, 'exp', 0, 0, tiled=True, axis_index_groups=y_group...  6.25 us
    all_to_all x1, waiting for transfers between devices, y_sum(): lax.all_to_all(parts, 'exp', 0, 0, tiled=True, axis_index_groups=y_groups())  6.16 us
    all_to_all x1, starting transfers between devices, select(): lax.all_to_all(sent.reshape(exp_size, CAP, 2 * width), 'exp', 0, 0, tiled...  5.96 us
  transfers between devices with their start and end apart: 33, of which 13 were waited for; matrix products, arithmetic and copies ran while one was open for 12% of the time, Pallas kernels for 10%

profile of v6, /device:TPU:2, one launch (start us, length us, event | category | flops | bytes accessed | tf_op | source)
XLA Modules:
  0.0 164.2 jit_solution(12818285173837144947)
XLA Ops:
  0.7 1.0 copy.28
  1.7 0.9 copy.29
  2.6 2.4 %collective-permute-start = (bf16[1024,128]{1,0:T(8,128)(2,1)S(1)}, bf16[1024,128]{1,0:T(8,128)(2,1)S(1)}, u32[]{:S(2)}, u32[]{:S(2)}) collective-permute-start(bf16[1024,128]{1,0:T(8,128)(2,1)S(1)} %pad_maximum_fusion.1), channel_id=1, source_target_pairs={{0,1},{1,0},{2,3},{3,2},{4,5},{5,4},{6,7},{7,6},{8,9},{9,8},{10,11... | collective-permute-start | bytes 786440 | tf_op jit(solution)/shard_map/ppermute | solution.py:44
  5.0 0.7 pad_maximum_fusion.13
  5.7 5.5 %collective-permute-start.1 = (bf16[32,256]{1,0:T(8,128)(2,1)S(1)}, bf16[32,256]{1,0:T(8,128)(2,1)S(1)}, u32[]{:S(2)}, u32[]{:S(2)}) collective-permute-start(bf16[32,256]{1,0:T(8,128)(2,1)S(1)} %get-tuple-element.70), channel_id=1, source_target_pairs={{0,64},{16,80},{32,96},{48,112},{64,0},{80,16},{96,32},{112,48},{1... | collective-permute-start | bytes 49160 | tf_op jit(solution)/shard_map/ppermute | solution.py:116
  11.3 0.7 convert_reduce_fusion.1
  12.0 1.1 reduce-window.6
  14.1 1.3 fusion.4
  15.6 0.8 pad_maximum_fusion
  16.4 6.0 %all-to-all-start = ((bf16[8,48,512]{2,1,0:T(8,128)(2,1)}), bf16[8,48,512]{2,1,0:T(8,128)(2,1)S(1)}, u32[]{:S(2)}, u32[]{:S(2)}) async-start(bf16[8,48,512]{2,1,0:T(8,128)(2,1)} %bitcast.14), calls=%async_computation | async-start | bytes 786432 | tf_op jit(solution)/shard_map/all_to_all | solution.py:296
  22.4 1.6 collective-permute-start.2
  24.0 1.2 dynamic-slice_bitcast_fusion
  25.1 2.2 %collective-permute-done.2 = bf16[64,256]{1,0:T(8,128)(2,1)S(1)} collective-permute-done((bf16[64,256]{1,0:T(8,128)(2,1)S(1)}, bf16[64,256]{1,0:T(8,128)(2,1)S(1)}, u32[]{:S(2)}, u32[]{:S(2)}) %collective-permute-start.2) | collective-permute-done | bytes 32800 | tf_op jit(solution)/shard_map/ppermute | solution.py:116
  27.3 2.4 %collective-permute-start.3 = (bf16[128,256]{1,0:T(8,128)(2,1)S(1)}, bf16[128,256]{1,0:T(8,128)(2,1)S(1)}, u32[]{:S(2)}, u32[]{:S(2)}) collective-permute-start(bf16[128,256]{1,0:T(8,128)(2,1)S(1)} %pad_maximum_fusion.11), channel_id=1, source_target_pairs={{0,128},{16,144},{32,160},{48,176},{64,192},{80,208},{96,224},{112... | collective-permute-start | bytes 196616 | tf_op jit(solution)/shard_map/ppermute | solution.py:116
  29.7 3.4 %collective-permute-done.3 = bf16[128,256]{1,0:T(8,128)(2,1)S(1)} collective-permute-done((bf16[128,256]{1,0:T(8,128)(2,1)S(1)}, bf16[128,256]{1,0:T(8,128)(2,1)S(1)}, u32[]{:S(2)}, u32[]{:S(2)}) %collective-permute-start.3) | collective-permute-done | bytes 65568 | tf_op jit(solution)/shard_map/ppermute | solution.py:116
  33.1 1.1 collective-permute-start.4
  34.2 3.9 %collective-permute-done.4 = bf16[256,256]{1,0:T(8,128)(2,1)S(1)} collective-permute-done((bf16[256,256]{1,0:T(8,128)(2,1)S(1)}, bf16[256,256]{1,0:T(8,128)(2,1)S(1)}, u32[]{:S(2)}, u32[]{:S(2)}) %collective-permute-start.4) | collective-permute-done | bytes 131104 | tf_op jit(solution)/shard_map/ppermute | solution.py:116
  39.5 1.8 %collective-permute-start.5 = (bf16[48,1152]{1,0:T(8,128)(2,1)S(1)}, bf16[48,1152]{1,0:T(8,128)(2,1)S(1)}, u32[]{:S(2)}, u32[]{:S(2)}) collective-permute-start(bf16[48,1152]{1,0:T(8,128)(2,1)S(1)} %get-tuple-element.31), channel_id=1, source_target_pairs={{0,16},{16,32},{32,48},{48,64},{64,80},{80,96},{96,112},{112,0},{1... | collective-permute-start | bytes 331784 | tf_op jit(solution)/shard_map/ppermute | solution.py:53
  41.3 1.5 collective-permute-start.9
  42.8 3.9 %collective-permute-done.5 = bf16[48,1152]{1,0:T(8,128)(2,1)S(1)} collective-permute-done((bf16[48,1152]{1,0:T(8,128)(2,1)S(1)}, bf16[48,1152]{1,0:T(8,128)(2,1)S(1)}, u32[]{:S(2)}, u32[]{:S(2)}) %collective-permute-start.5) | collective-permute-done | bytes 110624 | tf_op jit(solution)/shard_map/ppermute | solution.py:53
  46.8 0.7 fusion.19
  48.1 1.1 broadcast_in_dim.47
  49.2 4.2 %all-to-all-start.1 = ((bf16[4,512,256]{2,1,0:T(8,128)(2,1)}), bf16[4,512,256]{2,1,0:T(8,128)(2,1)S(1)}, u32[]{:S(2)}, u32[]{:S(2)}) async-start(bf16[4,512,256]{2,1,0:T(8,128)(2,1)} %broadcast_in_dim.47), calls=%async_computation.1 | async-start | bytes 2097152 | tf_op jit(solution)/shard_map/all_to_all | solution.py:35
  53.5 2.8 %collective-permute-start.10 = (bf16[48,2304]{1,0:T(8,128)(2,1)}, bf16[48,2304]{1,0:T(8,128)(2,1)}, u32[]{:S(2)}, u32[]{:S(2)}) collective-permute-start(bf16[48,2304]{1,0:T(8,128)(2,1)} %get-tuple-element.58), channel_id=1, source_target_pairs={{0,112},{16,0},{32,16},{48,32},{64,48},{80,64},{96,80},{112,96},{1... | collective-permute-start | bytes 663560 | tf_op jit(solution)/shard_map/ppermute | solution.py:57
  56.2 1.8 %add_convert_fusion.3 = bf16[48,2304]{1,0:T(8,128)(2,1)} fusion(bf16[48,2304]{1,0:T(8,128)(2,1)} %collective-permute-done.6, bf16[384,768]{1,0:T(8,128)(2,1)} %copy-done.13, bf16[384,768]{1,0:T(8,128)(2,1)} %copy-done.9, bf16[384,768]{1,0:T(8,128)(2,1)} %copy-done.11), kind=kLoop, calls=%fused_computation.24 | loop fusion | flops 995328 | bytes 2211840 | tf_op jit(solution)/shard_map/convert_element_type | solution.py:70
  58.0 6.2 %all-to-all-done.1 = bf16[4,512,256]{2,1,0:T(8,128)(2,1)S(1)} async-done(((bf16[4,512,256]{2,1,0:T(8,128)(2,1)}), bf16[4,512,256]{2,1,0:T(8,128)(2,1)S(1)}, u32[]{:S(2)}, u32[]{:S(2)}) %all-to-all-start.1) | async-done | bytes 1048608 | tf_op jit(solution)/shard_map/all_to_all | solution.py:35
  64.3 0.9 collective-permute-start.7
  65.2 6.4 %collective-permute-done.7 = bf16[48,2304]{1,0:T(8,128)(2,1)S(1)} collective-permute-done((bf16[48,2304]{1,0:T(8,128)(2,1)}, bf16[48,2304]{1,0:T(8,128)(2,1)S(1)}, u32[]{:S(2)}, u32[]{:S(2)}) %collective-permute-start.7) | collective-permute-done | bytes 221216 | tf_op jit(solution)/shard_map/ppermute | solution.py:53
  71.6 1.3 add_convert_fusion.2
  72.9 1.6 collective-permute-start.11
  74.6 5.1 %attention_stats.1.stats_ref = f32[8,1024]{1,0:T(8,128)S(1)} custom-call(s32[2]{0:T(128)S(1)} %pad_add_fusion.here_ref, bf16[1024,128]{1,0:T(8,128)(2,1)S(1)} %get-tuple-element.72.q_ref, bf16[1024,128]{1,0:T(8,128)(2,1)S(1)} %get-tuple-element.73.g_ref, bf16[2048,256]{1,0:T(8,128)(2,1)S(1)} %bitcast.50), custom_call_target="tpu_custom_call" | custom-call | flops 1073741824 | bytes 1048576 | tf_op jit(solution)/shard_map/attention_stats/pallas_call | solution.py:225
  80.3 3.0 %collective-permute-start.12 = (bf16[48,2304]{1,0:T(8,128)(2,1)S(1)}, bf16[48,2304]{1,0:T(8,128)(2,1)S(1)}, u32[]{:S(2)}, u32[]{:S(2)}) collective-permute-start(bf16[48,2304]{1,0:T(8,128)(2,1)S(1)} %add_convert_fusion), channel_id=1, source_target_pairs={{0,112},{16,0},{32,16},{48,32},{64,48},{80,64},{96,80},{112,96},{1... | collective-permute-start | bytes 663560 | tf_op jit(solution)/shard_map/ppermute | solution.py:57
  83.5 3.4 %collective-permute-done.8 = bf16[48,2304]{1,0:T(8,128)(2,1)S(1)} collective-permute-done((bf16[48,2304]{1,0:T(8,128)(2,1)S(1)}, bf16[48,2304]{1,0:T(8,128)(2,1)S(1)}, u32[]{:S(2)}, u32[]{:S(2)}) %collective-permute-start.8) | collective-permute-done | bytes 221216 | tf_op jit(solution)/shard_map/ppermute | solution.py:53
  86.9 0.9 fusion.29
  87.8 2.4 %collective-permute-start.18 = (bf16[48,2304]{1,0:T(8,128)(2,1)S(1)}, bf16[48,2304]{1,0:T(8,128)(2,1)}, u32[]{:S(2)}, u32[]{:S(2)}) collective-permute-start(bf16[48,2304]{1,0:T(8,128)(2,1)S(1)} %get-tuple-element.53), channel_id=1, source_target_pairs={{0,128},{16,144},{32,160},{48,176},{64,192},{80,208},{96,224},{112... | collective-permute-start | bytes 663560 | tf_op jit(solution)/shard_map/ppermute | solution.py:62
  90.2 8.8 %attention_grads.1 = (bf16[2048,256]{1,0:T(8,128)(2,1)S(1)}, f32[1024,128]{1,0:T(8,128)S(1)}) custom-call(s32[2]{0:T(128)S(1)} %pad_add_fusion.here_ref, bf16[1024,128]{1,0:T(8,128)(2,1)S(1)} %get-tuple-element.72.q_ref, bf16[1024,128]{1,0:T(8,128)(2,1)S(1)} %get-tuple-element.73.g_ref, bf16[2048,256]{1,0:T(8,128)(2,1)S(1)} %bitcast.51, ...), custom_call_target="tpu_custom_call" | custom-call | flops 2684354560 | bytes 2097152 | tf_op jit(solution)/shard_map/attention_grads/pallas_call | solution.py:243
  99.0 1.0 copy-done.1
  100.0 4.4 %all-to-all-start.2 = ((bf16[4,512,256]{2,1,0:T(8,128)(2,1)}), bf16[4,512,256]{2,1,0:T(8,128)(2,1)}, u32[]{:S(2)}, u32[]{:S(2)}) async-start(bf16[4,512,256]{2,1,0:T(8,128)(2,1)} %bitcast.52), calls=%async_computation.2 | async-start | bytes 2097152 | tf_op jit(solution)/shard_map/all_to_all | solution.py:39
  104.4 1.0 convert_add_fusion
  105.5 3.7 %collective-permute-start.19 = (bf16[48,2304]{1,0:T(8,128)(2,1)S(1)}, bf16[48,2304]{1,0:T(8,128)(2,1)S(1)}, u32[]{:S(2)}, u32[]{:S(2)}) collective-permute-start(bf16[48,2304]{1,0:T(8,128)(2,1)S(1)} %pad_maximum_fusion.6.refs_0_), channel_id=1, source_target_pairs={{0,112},{16,0},{32,16},{48,32},{64,48},{80,64},{96,80},{112,96},{1... | collective-permute-start | bytes 663560 | tf_op jit(solution)/shard_map/ppermute | solution.py:57
  109.1 6.2 %all-to-all-done.2 = bf16[4,512,256]{2,1,0:T(8,128)(2,1)} async-done(((bf16[4,512,256]{2,1,0:T(8,128)(2,1)}), bf16[4,512,256]{2,1,0:T(8,128)(2,1)}, u32[]{:S(2)}, u32[]{:S(2)}) %all-to-all-start.2) | async-done | bytes 1048608 | tf_op jit(solution)/shard_map/all_to_all | solution.py:39
  115.3 1.4 convert_reduce_fusion
  116.7 0.8 copy-done.17
  117.7 3.7 %collective-permute-start.20 = (bf16[48,2304]{1,0:T(8,128)(2,1)S(1)}, bf16[48,2304]{1,0:T(8,128)(2,1)S(1)}, u32[]{:S(2)}, u32[]{:S(2)}) collective-permute-start(bf16[48,2304]{1,0:T(8,128)(2,1)S(1)} %collective-permute-done.19.refs_1_), channel_id=1, source_target_pairs={{0,112},{16,0},{32,16},{48,32},{64,48},{80,64},{96,80},{112,96},{1... | collective-permute-start | bytes 663560 | tf_op jit(solution)/shard_map/ppermute | solution.py:57
  121.3 1.2 collective-permute-done.15
  122.6 1.0 slice_add_fusion
  123.6 1.9 %collective-permute-start.16 = (bf16[128,256]{1,0:T(8,128)(2,1)S(1)}, bf16[128,256]{1,0:T(8,128)(2,1)S(1)}, u32[]{:S(2)}, u32[]{:S(2)}) collective-permute-start(bf16[128,256]{1,0:T(8,128)(2,1)S(1)} %slice.230), channel_id=1, source_target_pairs={{0,128},{16,144},{32,160},{48,176},{64,192},{80,208},{96,224},{112... | collective-permute-start | bytes 196616 | tf_op jit(solution)/shard_map/ppermute | solution.py:116
  125.5 1.7 %fusion.30 = (bf16[384,256]{1,0:T(8,128)(2,1)S(1)}, bf16[384,256]{1,0:T(8,128)(2,1)}) fusion(bf16[384,512]{1,0:T(8,128)(2,1)} %bitcast.56), kind=kLoop, calls=%fused_computation.97 | loop fusion | bytes 786432 | tf_op jit(solution)/shard_map/slice | solution.py:307
  127.4 4.4 %collective-permute-start.21 = (bf16[48,2304]{1,0:T(8,128)(2,1)S(1)}, bf16[48,2304]{1,0:T(8,128)(2,1)S(1)}, u32[]{:S(2)}, u32[]{:S(2)}) collective-permute-start(bf16[48,2304]{1,0:T(8,128)(2,1)S(1)} %collective-permute-done.20.refs_2_), channel_id=1, source_target_pairs={{0,112},{16,0},{32,16},{48,32},{64,48},{80,64},{96,80},{112,96},{1... | collective-permute-start | bytes 663560 | tf_op jit(solution)/shard_map/ppermute | solution.py:57
  132.0 7.0 %collective-permute-done.24.refs_6_ = bf16[48,2304]{1,0:T(8,128)(2,1)S(1)} collective-permute-done((bf16[48,2304]{1,0:T(8,128)(2,1)S(1)}, bf16[48,2304]{1,0:T(8,128)(2,1)S(1)}, u32[]{:S(2)}, u32[]{:S(2)}) %collective-permute-start.24) | collective-permute-done | bytes 221216 | tf_op jit(solution)/shard_map/ppermute | solution.py:53
  139.1 3.5 %collective-permute-start.26 = (bf16[48,1152]{1,0:T(8,128)(2,1)S(1)}, bf16[48,1152]{1,0:T(8,128)(2,1)S(1)}, u32[]{:S(2)}, u32[]{:S(2)}) collective-permute-start(bf16[48,1152]{1,0:T(8,128)(2,1)S(1)} %slice.190), channel_id=1, source_target_pairs={{0,112},{16,0},{32,16},{48,32},{64,48},{80,64},{96,80},{112,96},{1... | collective-permute-start | bytes 331784 | tf_op jit(solution)/shard_map/ppermute | solution.py:57
  142.7 0.8 copy.32
  143.5 1.6 collective-permute-done.25.refs_4_
  145.1 0.9 copy-done.6
  146.0 0.9 copy-done.8
  147.6 1.3 collective-permute-done.27
  148.9 0.7 fusion.20
  149.6 4.4 %all-to-all-start.3 = ((bf16[8,48,128]{2,1,0:T(8,128)(2,1)}), bf16[8,48,128]{2,1,0:T(8,128)(2,1)S(1)}, u32[]{:S(2)}, u32[]{:S(2)}) async-start(bf16[8,48,128]{2,1,0:T(8,128)(2,1)} %fusion.20), calls=%async_computation.3 | async-start | bytes 196608 | tf_op jit(solution)/shard_map/all_to_all | solution.py:416
  154.0 1.9 %collective-permute-start.28 = (f32[32,256]{1,0:T(8,128)S(1)}, f32[32,256]{1,0:T(8,128)S(1)}, u32[]{:S(2)}, u32[]{:S(2)}) collective-permute-start(f32[32,256]{1,0:T(8,128)S(1)} %slice.169), channel_id=1, source_target_pairs={{0,64},{16,80},{32,96},{48,112},{64,0},{80,16},{96,32},{112,48},{1... | collective-permute-start | bytes 98312 | tf_op jit(solution)/shard_map/ppermute | solution.py:116
  155.8 1.5 expert_weight_grads.1
  157.4 4.5 %collective-permute-done.28 = f32[32,256]{1,0:T(8,128)S(1)} collective-permute-done((f32[32,256]{1,0:T(8,128)S(1)}, f32[32,256]{1,0:T(8,128)S(1)}, u32[]{:S(2)}, u32[]{:S(2)}) %collective-permute-start.28) | collective-permute-done | bytes 32800 | tf_op jit(solution)/shard_map/ppermute | solution.py:116
  161.9 0.6 fusion.22
  162.5 0.6 fusion.23
  163.1 1.1 fusion
  (123 shorter events, 5.5 us)
Async XLA Ops:
  0.6 38.5 %copy-start = (bf16[1,1536,256]{2,1,0:T(8,128)(2,1)S(1)}, bf16[1,1536,256]{2,1,0:T(8,128)(2,1)}, u32[]{:S(2)}) copy-start(bf16[1,1536,256]{2,1,0:T(8,128)(2,1)} %param.21) | copy-start | bytes 2359300
  0.6 12.9 %copy-start.21 = (s32[512,8]{0,1:T(8,128)S(1)}, s32[512,8]{0,1:T(8,128)}, u32[]{:S(2)}) copy-start(s32[512,8]{0,1:T(8,128)} %param.17) | copy-start | bytes 49156
  0.7 12.9 %copy-start.24 = (f32[512,8]{0,1:T(8,128)S(1)}, f32[512,8]{0,1:T(8,128)}, u32[]{:S(2)}) copy-start(f32[512,8]{0,1:T(8,128)} %param.18) | copy-start | bytes 49156
  0.7 13.4 %copy-start.18 = (bf16[512,256]{1,0:T(8,128)(2,1)S(1)}, bf16[512,256]{1,0:T(8,128)(2,1)}, u32[]{:S(2)}) copy-start(bf16[512,256]{1,0:T(8,128)(2,1)} %param.16) | copy-start | bytes 786436
  2.6 36.8 %collective-permute-start = (bf16[1024,128]{1,0:T(8,128)(2,1)S(1)}, bf16[1024,128]{1,0:T(8,128)(2,1)S(1)}, u32[]{:S(2)}, u32[]{:S(2)}) collective-permute-start(bf16[1024,128]{1,0:T(8,128)(2,1)S(1)} %pad_maximum_fusion.1), channel_id=1, source_target_pairs={{0,1},{1,0},{2,3},{3,2},{4,5},{5,4},{6,7},{7,6},{8,9},{9,8},{10,11... | collective-permute-start | bytes 786440 | tf_op jit(solution)/shard_map/ppermute | solution.py:44
  5.7 16.6 %collective-permute-start.1 = (bf16[32,256]{1,0:T(8,128)(2,1)S(1)}, bf16[32,256]{1,0:T(8,128)(2,1)S(1)}, u32[]{:S(2)}, u32[]{:S(2)}) collective-permute-start(bf16[32,256]{1,0:T(8,128)(2,1)S(1)} %get-tuple-element.70), channel_id=1, source_target_pairs={{0,64},{16,80},{32,96},{48,112},{64,0},{80,16},{96,32},{112,48},{1... | collective-permute-start | bytes 49160 | tf_op jit(solution)/shard_map/ppermute | solution.py:116
  12.0 3.6 %copy-start.22 = (pred[512,8]{0,1:T(8,128)(4,1)}, pred[512,8]{0,1:T(8,128)(4,1)S(1)}, u32[]{:S(2)}) copy-start(pred[512,8]{0,1:T(8,128)(4,1)S(1)} %broadcast_compare_fusion) | copy-start | bytes 12292
  15.5 6.9 %copy-start.19 = (bf16[32,1,128]{2,0,1:T(8,128)(2,1)S(1)}, bf16[32,1,128]{2,0,1:T(8,128)(2,1)}, u32[]{:S(2)}) copy-start(bf16[32,1,128]{2,0,1:T(8,128)(2,1)} %param.13) | copy-start | bytes 24580
  15.5 6.9 %copy-start.20 = (bf16[32,1,128]{2,0,1:T(8,128)(2,1)S(1)}, bf16[32,1,128]{2,0,1:T(8,128)(2,1)}, u32[]{:S(2)}) copy-start(bf16[32,1,128]{2,0,1:T(8,128)(2,1)} %param.12) | copy-start | bytes 24580
  16.4 21.8 %all-to-all-start = ((bf16[8,48,512]{2,1,0:T(8,128)(2,1)}), bf16[8,48,512]{2,1,0:T(8,128)(2,1)S(1)}, u32[]{:S(2)}, u32[]{:S(2)}) async-start(bf16[8,48,512]{2,1,0:T(8,128)(2,1)} %bitcast.14), calls=%async_computation | async-start | bytes 786432 | tf_op jit(solution)/shard_map/all_to_all | solution.py:296
  22.4 4.9 %collective-permute-start.2 = (bf16[64,256]{1,0:T(8,128)(2,1)S(1)}, bf16[64,256]{1,0:T(8,128)(2,1)S(1)}, u32[]{:S(2)}, u32[]{:S(2)}) collective-permute-start(bf16[64,256]{1,0:T(8,128)(2,1)S(1)} %pad_maximum_fusion.12), channel_id=1, source_target_pairs={{0,32},{16,48},{32,0},{48,16},{64,96},{80,112},{96,64},{112,80},{1... | collective-permute-start | bytes 98312 | tf_op jit(solution)/shard_map/ppermute | solution.py:116
  27.3 5.8 %collective-permute-start.3 = (bf16[128,256]{1,0:T(8,128)(2,1)S(1)}, bf16[128,256]{1,0:T(8,128)(2,1)S(1)}, u32[]{:S(2)}, u32[]{:S(2)}) collective-permute-start(bf16[128,256]{1,0:T(8,128)(2,1)S(1)} %pad_maximum_fusion.11), channel_id=1, source_target_pairs={{0,128},{16,144},{32,160},{48,176},{64,192},{80,208},{96,224},{112... | collective-permute-start | bytes 196616 | tf_op jit(solution)/shard_map/ppermute | solution.py:116
  33.1 5.1 %collective-permute-start.4 = (bf16[256,256]{1,0:T(8,128)(2,1)S(1)}, bf16[256,256]{1,0:T(8,128)(2,1)S(1)}, u32[]{:S(2)}, u32[]{:S(2)}) collective-permute-start(bf16[256,256]{1,0:T(8,128)(2,1)S(1)} %pad_maximum_fusion.7), channel_id=1, source_target_pairs={{0,16},{16,0},{32,48},{48,32},{64,80},{80,64},{96,112},{112,96},{1... | collective-permute-start | bytes 393224 | tf_op jit(solution)/shard_map/ppermute | solution.py:116
  38.3 0.7 copy-start.15
  38.7 8.8 %copy-start.9 = (bf16[384,768]{1,0:T(8,128)(2,1)}, bf16[384,768]{1,0:T(8,128)(2,1)S(1)}, u32[]{:S(2)}) copy-start(bf16[384,768]{1,0:T(8,128)(2,1)S(1)} %convolution_convert_fusion.1) | copy-start | bytes 1769476
  39.1 8.4 %copy-start.11 = (bf16[384,768]{1,0:T(8,128)(2,1)}, bf16[384,768]{1,0:T(8,128)(2,1)S(1)}, u32[]{:S(2)}) copy-start(bf16[384,768]{1,0:T(8,128)(2,1)S(1)} %convolution_convert_fusion.2) | copy-start | bytes 1769476
  39.4 8.1 %copy-start.13 = (bf16[384,768]{1,0:T(8,128)(2,1)}, bf16[384,768]{1,0:T(8,128)(2,1)S(1)}, u32[]{:S(2)}) copy-start(bf16[384,768]{1,0:T(8,128)(2,1)S(1)} %convolution_convert_fusion) | copy-start | bytes 1769476
  39.5 7.2 %collective-permute-start.5 = (bf16[48,1152]{1,0:T(8,128)(2,1)S(1)}, bf16[48,1152]{1,0:T(8,128)(2,1)S(1)}, u32[]{:S(2)}, u32[]{:S(2)}) collective-permute-start(bf16[48,1152]{1,0:T(8,128)(2,1)S(1)} %get-tuple-element.31), channel_id=1, source_target_pairs={{0,16},{16,32},{32,48},{48,64},{64,80},{80,96},{96,112},{112,0},{1... | collective-permute-start | bytes 331784 | tf_op jit(solution)/shard_map/ppermute | solution.py:53
  41.3 5.4 %collective-permute-start.9 = (bf16[48,1152]{1,0:T(8,128)(2,1)S(1)}, bf16[48,1152]{1,0:T(8,128)(2,1)S(1)}, u32[]{:S(2)}, u32[]{:S(2)}) collective-permute-start(bf16[48,1152]{1,0:T(8,128)(2,1)S(1)} %get-tuple-element.34), channel_id=1, source_target_pairs={{0,112},{16,0},{32,16},{48,32},{64,48},{80,64},{96,80},{112,96},{1... | collective-permute-start | bytes 331784 | tf_op jit(solution)/shard_map/ppermute | solution.py:57
  47.5 8.7 %collective-permute-start.6 = (bf16[48,2304]{1,0:T(8,128)(2,1)S(1)}, bf16[48,2304]{1,0:T(8,128)(2,1)}, u32[]{:S(2)}, u32[]{:S(2)}) collective-permute-start(bf16[48,2304]{1,0:T(8,128)(2,1)S(1)} %get-tuple-element.57), channel_id=1, source_target_pairs={{0,16},{16,32},{32,48},{48,64},{64,80},{80,96},{96,112},{112,0},{1... | collective-permute-start | bytes 663560 | tf_op jit(solution)/shard_map/ppermute | solution.py:53
  49.2 15.1 %all-to-all-start.1 = ((bf16[4,512,256]{2,1,0:T(8,128)(2,1)}), bf16[4,512,256]{2,1,0:T(8,128)(2,1)S(1)}, u32[]{:S(2)}, u32[]{:S(2)}) async-start(bf16[4,512,256]{2,1,0:T(8,128)(2,1)} %broadcast_in_dim.47), calls=%async_computation.1 | async-start | bytes 2097152 | tf_op jit(solution)/shard_map/all_to_all | solution.py:35
  53.5 11.8 %collective-permute-start.10 = (bf16[48,2304]{1,0:T(8,128)(2,1)}, bf16[48,2304]{1,0:T(8,128)(2,1)}, u32[]{:S(2)}, u32[]{:S(2)}) collective-permute-start(bf16[48,2304]{1,0:T(8,128)(2,1)} %get-tuple-element.58), channel_id=1, source_target_pairs={{0,112},{16,0},{32,16},{48,32},{64,48},{80,64},{96,80},{112,96},{1... | collective-permute-start | bytes 663560 | tf_op jit(solution)/shard_map/ppermute | solution.py:57
  64.3 7.4 %collective-permute-start.7 = (bf16[48,2304]{1,0:T(8,128)(2,1)}, bf16[48,2304]{1,0:T(8,128)(2,1)S(1)}, u32[]{:S(2)}, u32[]{:S(2)}) collective-permute-start(bf16[48,2304]{1,0:T(8,128)(2,1)} %add_convert_fusion.3), channel_id=1, source_target_pairs={{0,16},{16,32},{32,48},{48,64},{64,80},{80,96},{96,112},{112,0},{1... | collective-permute-start | bytes 663560 | tf_op jit(solution)/shard_map/ppermute | solution.py:53
  72.9 7.3 %collective-permute-start.11 = (bf16[48,2304]{1,0:T(8,128)(2,1)S(1)}, bf16[48,2304]{1,0:T(8,128)(2,1)S(1)}, u32[]{:S(2)}, u32[]{:S(2)}) collective-permute-start(bf16[48,2304]{1,0:T(8,128)(2,1)S(1)} %get-tuple-element.35), channel_id=1, source_target_pairs={{0,112},{16,0},{32,16},{48,32},{64,48},{80,64},{96,80},{112,96},{1... | collective-permute-start | bytes 663560 | tf_op jit(solution)/shard_map/ppermute | solution.py:57
  74.5 5.7 %copy-start.10 = (bf16[384,768]{1,0:T(8,128)(2,1)S(1)}, bf16[384,768]{1,0:T(8,128)(2,1)}, u32[]{:S(2)}) copy-start(bf16[384,768]{1,0:T(8,128)(2,1)} %copy-done.9) | copy-start | bytes 1769476
  74.6 5.7 %copy-start.12 = (bf16[384,768]{1,0:T(8,128)(2,1)S(1)}, bf16[384,768]{1,0:T(8,128)(2,1)}, u32[]{:S(2)}) copy-start(bf16[384,768]{1,0:T(8,128)(2,1)} %copy-done.11) | copy-start | bytes 1769476
  74.6 5.7 %copy-start.14 = (bf16[384,768]{1,0:T(8,128)(2,1)S(1)}, bf16[384,768]{1,0:T(8,128)(2,1)}, u32[]{:S(2)}) copy-start(bf16[384,768]{1,0:T(8,128)(2,1)} %copy-done.13) | copy-start | bytes 1769476
  79.7 7.2 %collective-permute-start.8 = (bf16[48,2304]{1,0:T(8,128)(2,1)S(1)}, bf16[48,2304]{1,0:T(8,128)(2,1)S(1)}, u32[]{:S(2)}, u32[]{:S(2)}) collective-permute-start(bf16[48,2304]{1,0:T(8,128)(2,1)S(1)} %get-tuple-element.33), channel_id=1, source_target_pairs={{0,16},{16,32},{32,48},{48,64},{64,80},{80,96},{96,112},{112,0},{1... | collective-permute-start | bytes 663560 | tf_op jit(solution)/shard_map/ppermute | solution.py:53
  80.3 6.6 %collective-permute-start.12 = (bf16[48,2304]{1,0:T(8,128)(2,1)S(1)}, bf16[48,2304]{1,0:T(8,128)(2,1)S(1)}, u32[]{:S(2)}, u32[]{:S(2)}) collective-permute-start(bf16[48,2304]{1,0:T(8,128)(2,1)S(1)} %add_convert_fusion), channel_id=1, source_target_pairs={{0,112},{16,0},{32,16},{48,32},{64,48},{80,64},{96,80},{112,96},{1... | collective-permute-start | bytes 663560 | tf_op jit(solution)/shard_map/ppermute | solution.py:57
  83.3 6.8 %collective-permute-start.13 = (f32[8,1024]{1,0:T(8,128)S(1)}, f32[8,1024]{1,0:T(8,128)S(1)}, u32[]{:S(2)}, u32[]{:S(2)}) collective-permute-start(f32[8,1024]{1,0:T(8,128)S(1)} %attention_stats.1.stats_ref), channel_id=1, source_target_pairs={{0,1},{1,0},{2,3},{3,2},{4,5},{5,4},{6,7},{7,6},{8,9},{9,8},{10,11... | collective-permute-start | bytes 98312 | tf_op jit(solution)/shard_map/ppermute | solution.py:44
  87.8 16.6 %collective-permute-start.18 = (bf16[48,2304]{1,0:T(8,128)(2,1)S(1)}, bf16[48,2304]{1,0:T(8,128)(2,1)}, u32[]{:S(2)}, u32[]{:S(2)}) collective-permute-start(bf16[48,2304]{1,0:T(8,128)(2,1)S(1)} %get-tuple-element.53), channel_id=1, source_target_pairs={{0,128},{16,144},{32,160},{48,176},{64,192},{80,208},{96,224},{112... | collective-permute-start | bytes 663560 | tf_op jit(solution)/shard_map/ppermute | solution.py:62
  99.0 1.0 copy-start.1
  100.0 4.4 %copy-start.16 = (f32[48,2304]{1,0:T(8,128)S(1)}, f32[48,2304]{1,0:T(8,128)}, u32[]{:S(2)}) copy-start(f32[48,2304]{1,0:T(8,128)} %get-tuple-element.54) | copy-start | bytes 1327108
  100.0 15.3 %all-to-all-start.2 = ((bf16[4,512,256]{2,1,0:T(8,128)(2,1)}), bf16[4,512,256]{2,1,0:T(8,128)(2,1)}, u32[]{:S(2)}, u32[]{:S(2)}) async-start(bf16[4,512,256]{2,1,0:T(8,128)(2,1)} %bitcast.52), calls=%async_computation.2 | async-start | bytes 2097152 | tf_op jit(solution)/shard_map/all_to_all | solution.py:39
  105.4 18.1 %copy-start.2 = (bf16[48,2304]{1,0:T(8,128)(2,1)}, bf16[48,2304]{1,0:T(8,128)(2,1)S(1)}, u32[]{:S(2)}) copy-start(bf16[48,2304]{1,0:T(8,128)(2,1)S(1)} %pad_maximum_fusion.6.refs_0_) | copy-start | bytes 663556
  105.5 12.2 %collective-permute-start.19 = (bf16[48,2304]{1,0:T(8,128)(2,1)S(1)}, bf16[48,2304]{1,0:T(8,128)(2,1)S(1)}, u32[]{:S(2)}, u32[]{:S(2)}) collective-permute-start(bf16[48,2304]{1,0:T(8,128)(2,1)S(1)} %pad_maximum_fusion.6.refs_0_), channel_id=1, source_target_pairs={{0,112},{16,0},{32,16},{48,32},{64,48},{80,64},{96,80},{112,96},{1... | collective-permute-start | bytes 663560 | tf_op jit(solution)/shard_map/ppermute | solution.py:57
  109.1 12.2 %collective-permute-start.22 = (bf16[48,2304]{1,0:T(8,128)(2,1)S(1)}, bf16[48,2304]{1,0:T(8,128)(2,1)S(1)}, u32[]{:S(2)}, u32[]{:S(2)}) collective-permute-start(bf16[48,2304]{1,0:T(8,128)(2,1)S(1)} %pad_maximum_fusion.6.refs_0_), channel_id=1, source_target_pairs={{0,16},{16,32},{32,48},{48,64},{64,80},{80,96},{96,112},{112,0},{1... | collective-permute-start | bytes 663560 | tf_op jit(solution)/shard_map/ppermute | solution.py:53
  116.7 0.8 copy-start.17
  117.5 5.1 %collective-permute-start.15 = (bf16[256,256]{1,0:T(8,128)(2,1)S(1)}, bf16[256,256]{1,0:T(8,128)(2,1)S(1)}, u32[]{:S(2)}, u32[]{:S(2)}) collective-permute-start(bf16[256,256]{1,0:T(8,128)(2,1)S(1)} %slice.228), channel_id=1, source_target_pairs={{0,16},{16,0},{32,48},{48,32},{64,80},{80,64},{96,112},{112,96},{1... | collective-permute-start | bytes 393224 | tf_op jit(solution)/shard_map/ppermute | solution.py:116
  117.7 21.3 %copy-start.5 = (bf16[48,2304]{1,0:T(8,128)(2,1)}, bf16[48,2304]{1,0:T(8,128)(2,1)S(1)}, u32[]{:S(2)}) copy-start(bf16[48,2304]{1,0:T(8,128)(2,1)S(1)} %collective-permute-done.19.refs_1_) | copy-start | bytes 663556
  117.7 9.7 %collective-permute-start.20 = (bf16[48,2304]{1,0:T(8,128)(2,1)S(1)}, bf16[48,2304]{1,0:T(8,128)(2,1)S(1)}, u32[]{:S(2)}, u32[]{:S(2)}) collective-permute-start(bf16[48,2304]{1,0:T(8,128)(2,1)S(1)} %collective-permute-done.19.refs_1_), channel_id=1, source_target_pairs={{0,112},{16,0},{32,16},{48,32},{64,48},{80,64},{96,80},{112,96},{1... | collective-permute-start | bytes 663560 | tf_op jit(solution)/shard_map/ppermute | solution.py:57
  121.3 17.7 %copy-start.7 = (bf16[48,2304]{1,0:T(8,128)(2,1)}, bf16[48,2304]{1,0:T(8,128)(2,1)S(1)}, u32[]{:S(2)}) copy-start(bf16[48,2304]{1,0:T(8,128)(2,1)S(1)} %collective-permute-done.22.refs_8_) | copy-start | bytes 663556
  121.3 10.5 %collective-permute-start.23 = (bf16[48,2304]{1,0:T(8,128)(2,1)S(1)}, bf16[48,2304]{1,0:T(8,128)(2,1)S(1)}, u32[]{:S(2)}, u32[]{:S(2)}) collective-permute-start(bf16[48,2304]{1,0:T(8,128)(2,1)S(1)} %collective-permute-done.22.refs_8_), channel_id=1, source_target_pairs={{0,16},{16,32},{32,48},{48,64},{64,80},{80,96},{96,112},{112,0},{1... | collective-permute-start | bytes 663560 | tf_op jit(solution)/shard_map/ppermute | solution.py:53
  123.6 21.5 %copy-start.3 = (bf16[48,2304]{1,0:T(8,128)(2,1)S(1)}, bf16[48,2304]{1,0:T(8,128)(2,1)}, u32[]{:S(2)}) copy-start(bf16[48,2304]{1,0:T(8,128)(2,1)} %copy-done.2) | copy-start | bytes 663556
  123.6 8.2 %collective-permute-start.16 = (bf16[128,256]{1,0:T(8,128)(2,1)S(1)}, bf16[128,256]{1,0:T(8,128)(2,1)S(1)}, u32[]{:S(2)}, u32[]{:S(2)}) collective-permute-start(bf16[128,256]{1,0:T(8,128)(2,1)S(1)} %slice.230), channel_id=1, source_target_pairs={{0,128},{16,144},{32,160},{48,176},{64,192},{80,208},{96,224},{112... | collective-permute-start | bytes 196616 | tf_op jit(solution)/shard_map/ppermute | solution.py:116
  127.3 15.4 %collective-permute-start.14 = (bf16[512,128]{1,0:T(8,128)(2,1)S(1)}, bf16[512,128]{1,0:T(8,128)(2,1)S(1)}, u32[]{:S(2)}, u32[]{:S(2)}) collective-permute-start(bf16[512,128]{1,0:T(8,128)(2,1)S(1)} %slice.229), channel_id=1, source_target_pairs={{0,1},{1,0},{2,3},{3,2},{4,5},{5,4},{6,7},{7,6},{8,9},{9,8},{10,11... | collective-permute-start | bytes 393224 | tf_op jit(solution)/shard_map/ppermute | solution.py:44
  127.4 11.7 %collective-permute-start.21 = (bf16[48,2304]{1,0:T(8,128)(2,1)S(1)}, bf16[48,2304]{1,0:T(8,128)(2,1)S(1)}, u32[]{:S(2)}, u32[]{:S(2)}) collective-permute-start(bf16[48,2304]{1,0:T(8,128)(2,1)S(1)} %collective-permute-done.20.refs_2_), channel_id=1, source_target_pairs={{0,112},{16,0},{32,16},{48,32},{64,48},{80,64},{96,80},{112,96},{1... | collective-permute-start | bytes 663560 | tf_op jit(solution)/shard_map/ppermute | solution.py:57
  131.8 7.1 %collective-permute-start.24 = (bf16[48,2304]{1,0:T(8,128)(2,1)S(1)}, bf16[48,2304]{1,0:T(8,128)(2,1)S(1)}, u32[]{:S(2)}, u32[]{:S(2)}) collective-permute-start(bf16[48,2304]{1,0:T(8,128)(2,1)S(1)} %collective-permute-done.23.refs_7_), channel_id=1, source_target_pairs={{0,16},{16,32},{32,48},{48,64},{64,80},{80,96},{96,112},{112,0},{1... | collective-permute-start | bytes 663560 | tf_op jit(solution)/shard_map/ppermute | solution.py:53
  131.9 15.7 %collective-permute-start.17 = (f32[64,256]{1,0:T(8,128)S(1)}, f32[64,256]{1,0:T(8,128)S(1)}, u32[]{:S(2)}, u32[]{:S(2)}) collective-permute-start(f32[64,256]{1,0:T(8,128)S(1)} %slice.185), channel_id=1, source_target_pairs={{0,32},{16,48},{32,0},{48,16},{64,96},{80,112},{96,64},{112,80},{1... | collective-permute-start | bytes 196616 | tf_op jit(solution)/shard_map/ppermute | solution.py:116
  139.0 6.0 %collective-permute-start.25 = (bf16[48,1152]{1,0:T(8,128)(2,1)S(1)}, bf16[48,1152]{1,0:T(8,128)(2,1)S(1)}, u32[]{:S(2)}, u32[]{:S(2)}) collective-permute-start(bf16[48,1152]{1,0:T(8,128)(2,1)S(1)} %slice.189), channel_id=1, source_target_pairs={{0,16},{16,32},{32,48},{48,64},{64,80},{80,96},{96,112},{112,0},{1... | collective-permute-start | bytes 331784 | tf_op jit(solution)/shard_map/ppermute | solution.py:53
  139.1 5.9 %collective-permute-start.26 = (bf16[48,1152]{1,0:T(8,128)(2,1)S(1)}, bf16[48,1152]{1,0:T(8,128)(2,1)S(1)}, u32[]{:S(2)}, u32[]{:S(2)}) collective-permute-start(bf16[48,1152]{1,0:T(8,128)(2,1)S(1)} %slice.190), channel_id=1, source_target_pairs={{0,112},{16,0},{32,16},{48,32},{64,48},{80,64},{96,80},{112,96},{1... | collective-permute-start | bytes 331784 | tf_op jit(solution)/shard_map/ppermute | solution.py:57
  145.1 0.9 copy-start.6
  146.0 0.9 copy-start.8
  147.5 8.4 %copy-start.4 = (bf16[384,256]{1,0:T(8,128)(2,1)S(1)}, bf16[384,256]{1,0:T(8,128)(2,1)}, u32[]{:S(2)}) copy-start(bf16[384,256]{1,0:T(8,128)(2,1)} %get-tuple-element.67.input_ref) | copy-start | bytes 589828
  147.5 1.4 collective-permute-start.27
  149.6 13.5 %all-to-all-start.3 = ((bf16[8,48,128]{2,1,0:T(8,128)(2,1)}), bf16[8,48,128]{2,1,0:T(8,128)(2,1)S(1)}, u32[]{:S(2)}, u32[]{:S(2)}) async-start(bf16[8,48,128]{2,1,0:T(8,128)(2,1)} %fusion.20), calls=%async_computation.3 | async-start | bytes 196608 | tf_op jit(solution)/shard_map/all_to_all | solution.py:416
  154.0 9.2 %copy-start.23 = (pred[512,8]{0,1:T(8,128)(4,1)S(1)}, pred[512,8]{0,1:T(8,128)(4,1)}, u32[]{:S(2)}) copy-start(pred[512,8]{0,1:T(8,128)(4,1)} %copy-done.22) | copy-start | bytes 12292
  154.0 7.9 %collective-permute-start.28 = (f32[32,256]{1,0:T(8,128)S(1)}, f32[32,256]{1,0:T(8,128)S(1)}, u32[]{:S(2)}, u32[]{:S(2)}) collective-permute-start(f32[32,256]{1,0:T(8,128)S(1)} %slice.169), channel_id=1, source_target_pairs={{0,64},{16,80},{32,96},{48,112},{64,0},{80,16},{96,32},{112,48},{1... | collective-permute-start | bytes 98312 | tf_op jit(solution)/shard_map/ppermute | solution.py:116

commit v7 on v6

--- a/solution.py
+++ b/solution.py
@@ -24,37 +24,44 @@
     return (hidden, d_gate, d_up)
 
 
-def y_groups():
-    n = lax.axis_size("exp")
-    return [list(range(x, n, X_LO)) for x in range(X_LO)]
-
-
-def y_gather(block):
-    n = lax.axis_size("exp") // X_LO
-    copies = jnp.broadcast_to(block[None], (n,) + block.shape)
-    return lax.all_to_all(copies, "exp", 0, 0, tiled=True, axis_index_groups=y_groups())
-
-
-def y_sum(parts):
-    got = lax.all_to_all(parts, "exp", 0, 0, tiled=True, axis_index_groups=y_groups())
-    return jnp.sum(got.astype(F32), axis=0)
+VMEM = pl.BlockSpec(memory_space=pltpu.VMEM)
+SMEM = pl.BlockSpec(memory_space=pltpu.SMEM)
+
+
+def stack_body(*refs):
+    row = 0
+    for ref in refs[:-1]:
+        refs[-1][row : row + ref.shape[0], :] = ref[...]
+        row += ref.shape[0]
+
+
+def stacked(*blocks):
+    rows = sum(block.shape[0] for block in blocks)
+    return pl.pallas_call(
+        stack_body,
+        out_shape=jax.ShapeDtypeStruct((rows,) + blocks[0].shape[1:], blocks[0].dtype),
+        in_specs=[VMEM] * len(blocks),
+        out_specs=VMEM,
+        cost_estimate=pl.CostEstimate(
+            flops=0, bytes_accessed=4 * rows * blocks[0].shape[1], transcendentals=0
+        ),
+        name="stack_rows",
+    )(*blocks)
 
 
 def beside(block):
     return lax.ppermute(block, "exp", [(e, e ^ 1) for e in range(lax.axis_size("exp"))])
 
 
-def z_shift(step):
+def z_move(block, step):
     n = lax.axis_size("ctx") // X_HI
-    return [(h * n + z, h * n + (z + step) % n) for h in range(X_HI) for z in range(n)]
-
-
-def right(block):
-    return lax.ppermute(block, "ctx", z_shift(1))
-
-
-def left(block):
-    return lax.ppermute(block, "ctx", z_shift(-1))
+    pairs = [(h * n + z, h * n + (z + step) % n) for h in range(X_HI) for z in range(n)]
+    return lax.ppermute(block, "ctx", pairs)
+
+
+def y_move(block, step):
+    n = lax.axis_size("exp")
+    return lax.ppermute(block, "exp", [(e, (e + step * X_LO) % n) for e in range(n)])
 
 
 def opposite(block):
@@ -76,35 +83,33 @@
     return parts[far][:, :cut], parts[far][:, cut:]
 
 
-def sum_step(parts, step, onward, back):
+def sum_step(move, parts, step, onward, back):
     n = len(parts)
     far = n // 2
     cut = parts[0].shape[1] // 2
-    onward, back = right(onward), left(back)
+    onward, back = move(onward, 1), move(back, -1)
     ahead, behind = parts[far - 1 - step], parts[(far + 1 + step) % n]
     if step == 0:
         onward = jnp.concatenate([add_low(onward, ahead[:, :cut]), ahead[:, cut:]], axis=1)
         back = jnp.concatenate([behind[:, :cut], add_low(back, behind[:, cut:])], axis=1)
     elif step < far - 1:
         onward, back = add_low(onward, ahead), add_low(back, behind)
+    else:
+        return onward.astype(F32) + back.astype(F32) + parts[0].astype(F32)
     return onward, back
 
 
-def ring_gather(block, waits):
-    n = lax.axis_size("ctx") // X_HI
-    far = n // 2
-    cut = block.shape[1] // 2
-    blocks = [block] + [None] * (n - 1)
-    onward = back = block
-    for step in range(1, far):
-        if step in waits:
-            onward, back = after(onward, waits[step]), after(back, waits[step])
-        onward, back = right(onward), left(back)
-        blocks[n - step], blocks[step] = onward, back
-    if far in waits:
-        onward, back = after(onward, waits[far]), after(back, waits[far])
-    blocks[far : far + 1] = [right(onward[:, :cut]), left(back[:, cut:])]
-    return blocks
+def ring_step(move, onward, back):
+    return move(onward, 1), move(back, -1)
+
+
+def ring_last(move, onward, back):
+    cut = onward.shape[1] // 2
+    return move(onward[:, :cut], 1), move(back[:, cut:], -1)
+
+
+def both_after(onward, back, *others):
+    return lax.optimization_barrier((onward, back) + others)[:2]
 
 
 def turn(blocks, places):
@@ -116,10 +121,22 @@
     return lax.ppermute(block, "ctx", [(c, c ^ mask) for c in range(lax.axis_size("ctx"))])
 
 
+def fours(masks):
+    return ((1, masks[0]), (2, masks[1]), (3, masks[0] ^ masks[1]))
+
+
 def ctx_gather(block, masks):
-    for mask in masks:
-        block = jnp.concatenate([block, swap(block, mask)], axis=0)
-    return block
+    return stacked(block, *[swap(block, mask) for _, mask in fours(masks)])
+
+
+def ctx_sum(both, masks):
+    quarter = both.shape[0] // 4
+    wire = BF if quarter >= both.shape[1] // 2 else F32
+    total = both[:quarter]
+    for place, mask in fours(masks):
+        sent = both[place * quarter : (place + 1) * quarter].astype(wire)
+        total = total + swap(sent, mask).astype(F32)
+    return total
 
 
 def mask_of(index):
@@ -132,12 +149,13 @@
     ahead = lax.broadcasted_iota(jnp.int32, (own, lanes), 1) % tokens - lax.broadcasted_iota(
         jnp.int32, (own, lanes), 0
     )
-    me, side = here_ref[0], here_ref[1]
+    me, side, row, rows = here_ref[0], here_ref[1], here_ref[2], here_ref[3]
     parts = k.shape[0] // own
     masked = []
     for part in range(parts):
         place = step * parts + part
-        start = (me ^ mask_of(place % ctx_size)) * tokens + (place // ctx_size * X_LO + side) * own
+        at = (row + place // ctx_size) % rows * X_LO + side
+        start = (me ^ mask_of(place % ctx_size)) * tokens + at * own
         masked.append(
             jnp.where(
                 ahead >= start - me * tokens,
@@ -212,12 +230,11 @@
     dq_ref[...] = (total * size ** (-0.5)).T
 
 
-VMEM = pl.BlockSpec(memory_space=pltpu.VMEM)
-SMEM = pl.BlockSpec(memory_space=pltpu.SMEM)
-
-
 def here():
-    return jnp.stack([lax.axis_index("ctx"), lax.axis_index("exp") % X_LO]).astype(jnp.int32)
+    exp, n = lax.axis_index("exp"), lax.axis_size("exp")
+    return jnp.stack(
+        [lax.axis_index("ctx"), exp % X_LO, exp // X_LO, jnp.int32(n // X_LO)]
+    ).astype(jnp.int32)
 
 
 def attention_stats(own, tokens, queries, grads, flat):
@@ -262,14 +279,6 @@
     return jnp.swapaxes(rows, 0, 1).reshape(-1, rows.shape[2])
 
 
-def ctx_sum(both, masks):
-    for mask in reversed(masks):
-        half = both.shape[0] // 2
-        sent = both[half:].astype(BF if half >= both.shape[1] // 2 else F32)
-        both = both[:half] + swap(sent, mask).astype(F32)
-    return both
-
-
 def own_grads(both):
     head_dim = both.shape[1] // 2
     grad_key = (both[:, :head_dim] * head_dim ** (-0.5)).astype(BF)[:, None, :]
@@ -277,7 +286,7 @@
     return grad_key, grad_value
 
 
-def select(moe_input, moe_grad, expert_ids, router_weight):
+def select(moe_input, moe_grad, expert_ids, router_weight, near):
     width = moe_input.shape[1]
     exp_size = lax.axis_size("exp")
     matches = expert_ids[:, :, None] == jnp.arange(exp_size)[None, None, :]
@@ -293,17 +302,18 @@
     picked = jnp.einsum("bs,bd->sd", placed_low, rows, preferred_element_type=F32)
     scaled = picked[:, width:] * slot_weight.reshape(-1, 1)
     sent = jnp.concatenate([picked[:, :width].astype(BF), scaled.astype(BF)], axis=1)
+    sent = after(sent, near)
     got = lax.all_to_all(sent.reshape(exp_size, CAP, 2 * width), "exp", 0, 0, tiled=True)
     return placed_low, got
 
 
 def project(got, gate_weight, up_weight, down_weight):
-    ring = lax.axis_size("ctx") // X_HI
-    at = lax.axis_index("ctx") % ring
+    ctx_size = lax.axis_size("ctx")
     half = lax.axis_index("head")
     units = gate_weight.shape[2] // lax.axis_size("head")
     width = got.shape[2] // 2
-    got = turn(got.reshape(ring, -1, 2 * width), at).reshape(-1, 2 * width)
+    got = jnp.swapaxes(got.reshape(ctx_size // X_HI, X_HI, -1, 2 * width), 0, 1)
+    got = got.reshape(-1, 2 * width)
     input_rows, grad_rows = got[:, :width], got[:, width:]
     gate_mat = lax.dynamic_slice_in_dim(gate_weight[0], half * units, units, 1)
     up_mat = lax.dynamic_slice_in_dim(up_weight[0], half * units, units, 1)
@@ -311,8 +321,8 @@
     gate_part = jnp.dot(input_rows, gate_mat, preferred_element_type=F32).astype(BF)
     up_part = jnp.dot(input_rows, up_mat, preferred_element_type=F32).astype(BF)
     back_part = jnp.einsum("rd,fd->rf", grad_rows, down_mat, preferred_element_type=F32).astype(BF)
-    parts = jnp.concatenate([gate_part, up_part, back_part], axis=1).reshape(ring, -1, 3 * units)
-    return input_rows, grad_rows, gate_mat, up_mat, [parts[j] for j in range(ring)]
+    parts = jnp.concatenate([gate_part, up_part, back_part], axis=1)
+    return gate_mat, up_mat, parts.reshape(ctx_size, -1, 3 * units)
 
 
 def act_block(total):
@@ -404,7 +414,7 @@
     )(full, input_rows, grad_rows)
 
 
-def finish(blocks, input_rows, grad_rows, gate_mat, up_mat, placed_low, sums):
+def finish(blocks, input_rows, grad_rows, gate_mat, up_mat, placed_low):
     exp_size = lax.axis_size("exp")
     ring = lax.axis_size("ctx") // X_HI
     at = lax.axis_index("ctx") % ring
@@ -412,13 +422,11 @@
     columns = mine.shape[1]
     mine = (mine + lax.ppermute(other, "head", [(0, 1), (1, 0)]).astype(F32)).astype(BF)
     mine = turn(mine.reshape(ring, -1, columns), (ring - at) % ring).reshape(exp_size, CAP, columns)
-    mine = after(mine, sums)
     back_rows = lax.all_to_all(mine, "exp", 0, 0, tiled=True)
     grad_input = jnp.dot(
         placed_low, back_rows.reshape(-1, columns), preferred_element_type=F32
     ).astype(BF)
-    sums = ctx_sum(after(sums, mine), MASKS[:1])
-    return (grad_input,) + tuple(weight_grads(after(full, mine), input_rows, grad_rows)) + (sums,)
+    return (grad_input,) + tuple(weight_grads(after(full, mine), input_rows, grad_rows))
 
 
 def shards(
@@ -438,40 +446,53 @@
     rows = tokens * queries.shape[1]
     size = queries.shape[2]
     pair = jnp.concatenate([key_rows[:, 0, :], value_vector_rows[:, 0, :]], axis=1)
-    near = ctx_gather(pair, MASKS)
-    placed_low, got = select(moe_input, moe_grad, expert_ids, router_weight)
+    near = ctx_gather(pair, MASKS[:2])
+    placed_low, got = select(moe_input, moe_grad, expert_ids, router_weight, near)
+    near = ctx_gather(near, MASKS[2:])
     mine = jnp.concatenate([by_head(queries), by_head(grad_attn)], axis=0)
     theirs = beside(mine)
-    flat = y_gather(after(near, got)).reshape(-1, near.shape[1])
     queries = jnp.concatenate([mine[:rows], theirs[:rows]], axis=0)
     grads = jnp.concatenate([mine[rows:], theirs[rows:]], axis=0)
-    input_rows, grad_rows, gate_mat, up_mat, parts = project(
-        got, gate_weight, up_weight, down_weight
-    )
-    onward, back = sum_start(parts)
-    onward, back = after(onward, near, theirs), after(back, near, theirs)
-    onward, back = sum_step(parts, 0, onward, back)
-    onward, back = sum_step(parts, 1, onward, back)
-    onward, back = after(onward, flat), after(back, flat)
+    above, below = ring_step(y_move, near, near)
+    gate_mat, up_mat, parts = project(
+        after(got, above, below, theirs), gate_weight, up_weight, down_weight
+    )
+    total = lax.all_to_all(parts, "ctx", 0, 0, tiled=True)
+    above, below = both_after(above, below, parts)
+    cut = near.shape[0] // 2
+    far = stacked(y_move(above[:cut], 1), y_move(below[cut:], -1))
+    flat = stacked(near, below, far, above)
     stats = attention_stats(own, tokens, queries, grads, flat)
-    onward, back = sum_step(parts, 2, onward, back)
-    onward, back = sum_step(parts, 3, after(onward, stats), after(back, stats))
-    total = onward.astype(F32) + back.astype(F32) + parts[0].astype(F32)
-    other = opposite(total.astype(BF))
     both, grad_query = attention_grads(
-        own, tokens, queries, grads, after(flat, total), stats, beside(stats)
-    )
-    block = act_block(total + after(other, both).astype(F32))
-    sums = y_sum(both.reshape((-1,) + near.shape))
-    blocks = ring_gather(block, {3: sums})
+        own, tokens, queries, grads, flat, stats, beside(stats)
+    )
+    terms = [both[j * near.shape[0] : (j + 1) * near.shape[0]] for j in range(4)]
+    up, down = sum_step(y_move, terms, 0, *sum_start(terms))
+    sums = sum_step(y_move, terms, 1, up, down)
+    block = act_block(jnp.sum(after(total, sums).astype(F32), axis=0))
+    partner = opposite(block)
+    first = lax.axis_index("ctx") // (lax.axis_size("ctx") // X_HI) == 0
+    block = jnp.concatenate(
+        [jnp.where(first, block, partner), jnp.where(first, partner, block)], axis=0
+    )
     sums = ctx_sum(sums, MASKS[2:])
-    blocks[0] = after(block, sums)
-    sums = ctx_sum(sums, MASKS[1:2])
-    of_experts = finish(blocks, input_rows, grad_rows, gate_mat, up_mat, placed_low, sums)
+    block = after(block, sums)
+    blocks = [block] + [None] * 8
+    blocks[8], blocks[1] = ring_step(z_move, block, block)
+    blocks[7], blocks[2] = ring_step(z_move, blocks[8], blocks[1])
+    sums = ctx_sum(sums, MASKS[:2])
+    blocks[6], blocks[3] = ring_step(z_move, blocks[7], blocks[2])
+    onward, back = both_after(blocks[6], blocks[3], sums)
+    blocks[4], blocks[5] = ring_last(z_move, onward, back)
+    ring = lax.axis_size("ctx") // X_HI
+    width = moe_input.shape[1]
+    got = turn(got.reshape(ring, -1, 2 * width), lax.axis_index("ctx") % ring)
+    got = got.reshape(-1, 2 * width)
+    input_rows, grad_rows = got[:, :width], got[:, width:]
+    of_experts = finish(blocks, input_rows, grad_rows, gate_mat, up_mat, placed_low)
     grad_query = grad_query[:rows] + beside(grad_query[rows:].astype(BF)).astype(F32)
     grad_query = jnp.swapaxes(grad_query.astype(BF).reshape(-1, tokens, size), 0, 1)
-    grad_key, grad_value = own_grads(of_experts[-1])
-    return (grad_query, grad_key, grad_value) + of_experts[:-1]
+    return (grad_query,) + own_grads(sums) + of_experts
 
 
 def solution(mesh):

time: 165 us -> 172 us (1.042); the launches traced: 164 us -> 169 us
  waiting for transfers between devices: 51.2 us -> 37.4 us
  starting transfers between devices: 66.7 us -> 77.8 us
  Pallas kernels: 16 us -> 23.3 us
    all_to_all x2 -> x1, waiting for transfers between devices: 12.4 us -> 0.01 us  [shards(): total = lax.all_to_all(parts, 'ctx', 0, 0, tiled=True)]
    ppermute x8 -> x12, waiting for transfers between devices: 15.3 us -> 3.76 us  [swap(): lax.ppermute(block, 'ctx', [(c, c ^ mask) for c in range(lax.axis_size('c...]
    ppermute x8 -> x12, starting transfers between devices: 14.5 us -> 25.9 us  [swap(): lax.ppermute(block, 'ctx', [(c, c ^ mask) for c in range(lax.axis_size('c...]
    pallas_call x0 -> x4, Pallas kernels: none -> 7 us  [stacked(): pl.pallas_call(stack_body, out_shape=jax.ShapeDtypeStruct((rows,) + block...]
    ppermute x16, starting transfers between devices: 28.1 us -> 23.2 us  [the longest x8 12 us: y_move(): lax.ppermute(block, 'exp', [(e, (e + step * X_LO) % n) for e in range(n)])]
    ppermute x16, waiting for transfers between devices: 22.3 us -> 26.8 us  [the longest x8 16.7 us: y_move(): lax.ppermute(block, 'exp', [(e, (e + step * X_LO) % n) for e in range(n)])]
    ppermute x3, waiting for transfers between devices: 0.01 us -> 4.07 us  [beside(): lax.ppermute(block, 'exp', [(e, e ^ 1) for e in range(lax.axis_size('exp'...]
    convert_element_type x4 -> x1, other arithmetic: 3.18 us -> 0.08 us  [add_low(): return (a.astype(F32) + b.astype(F32)).astype(BF)]
  transfers between devices with their start and end apart: 33 -> 36, of which waited for: 13 -> 17; matrix products, arithmetic and copies ran while one was open for 12% -> 11% of each run, Pallas kernels for 10% -> 13%
where the time goes in v7:
time: 172 us; the launch traced here: 169 us
  starting transfers between devices  77.8 us (45%)
  waiting for transfers between devices  37.4 us (22%)
  Pallas kernels  23.3 us (14%)
  other arithmetic  15 us (9%)
  local copies, waits for them, and re-layouts  10.9 us (6%)
  matrix products  3.48 us (2%)
    ppermute x12, starting transfers between devices, swap(): lax.ppermute(block, 'ctx', [(c, c ^ mask) for c in range(lax.axis_size('c...  25.9 us
    ppermute x8, waiting for transfers between devices, y_move(): lax.ppermute(block, 'exp', [(e, (e + step * X_LO) % n) for e in range(n)])  16.7 us
    ppermute x8, starting transfers between devices, y_move(): lax.ppermute(block, 'exp', [(e, (e + step * X_LO) % n) for e in range(n)])  12 us
    ppermute x8, starting transfers between devices, z_move(): return lax.ppermute(block, 'ctx', pairs)  11.2 us
    ppermute x8, waiting for transfers between devices, z_move(): return lax.ppermute(block, 'ctx', pairs)  10.1 us
    pallas_call x1, Pallas kernels, attention_grads(): pl.pallas_call(functools.partial(grads_body, own, lax.axis_size('ctx'), t...  8.96 us
    all_to_all x1, starting transfers between devices, shards(): total = lax.all_to_all(parts, 'ctx', 0, 0, tiled=True)  7.99 us
    pallas_call x4, Pallas kernels, stacked(): pl.pallas_call(stack_body, out_shape=jax.ShapeDtypeStruct((rows,) + block...  7 us
  transfers between devices with their start and end apart: 36, of which 17 were waited for; matrix products, arithmetic and copies ran while one was open for 11% of the time, Pallas kernels for 13%

profile of v7, /device:TPU:2, one launch (start us, length us, event | category | flops | bytes accessed | tf_op | source)
XLA Modules:
  0.0 169.1 jit_solution(8265505698619898690)
XLA Ops:
  0.6 0.8 pad_maximum_fusion.9.refs_0_
  1.4 7.2 %collective-permute-start.1 = (bf16[32,256]{1,0:T(8,128)(2,1)S(1)}, bf16[32,256]{1,0:T(8,128)(2,1)S(1)}, u32[]{:S(2)}, u32[]{:S(2)}) collective-permute-start(bf16[32,256]{1,0:T(8,128)(2,1)S(1)} %pad_maximum_fusion.9.refs_0_), channel_id=1, source_target_pairs={{0,64},{16,80},{32,96},{48,112},{64,0},{80,16},{96,32},{112,48},{1... | collective-permute-start | bytes 49160 | tf_op jit(solution)/shard_map/ppermute | solution.py:121
  8.6 1.5 collective-permute-start.2
  10.1 0.7 convert_reduce_fusion.1
  10.9 1.1 reduce-window.6
  12.4 0.8 select_reduce_fusion.1
  13.8 1.4 fusion.4
  15.4 0.8 pad_maximum_fusion.1
  17.5 1.4 stack_rows.4.refs_0_
  18.9 2.1 %collective-permute-start.4 = (bf16[128,256]{1,0:T(8,128)(2,1)}, bf16[128,256]{1,0:T(8,128)(2,1)S(1)}, u32[]{:S(2)}, u32[]{:S(2)}) collective-permute-start(bf16[128,256]{1,0:T(8,128)(2,1)} %stack_rows.4.refs_0_), channel_id=1, source_target_pairs={{0,128},{16,144},{32,160},{48,176},{64,192},{80,208},{96,224},{112... | collective-permute-start | bytes 196616 | tf_op jit(solution)/shard_map/ppermute | solution.py:121
  21.0 1.0 collective-permute-start.5
  22.0 1.8 %collective-permute-start.6 = (bf16[128,256]{1,0:T(8,128)(2,1)}, bf16[128,256]{1,0:T(8,128)(2,1)S(1)}, u32[]{:S(2)}, u32[]{:S(2)}) collective-permute-start(bf16[128,256]{1,0:T(8,128)(2,1)} %stack_rows.4.refs_0_), channel_id=1, source_target_pairs={{0,144},{16,128},{32,176},{48,160},{64,208},{80,192},{96,240},{112... | collective-permute-start | bytes 196616 | tf_op jit(solution)/shard_map/ppermute | solution.py:121
  23.9 5.9 %all-to-all-start = ((bf16[8,48,512]{2,1,0:T(8,128)(2,1)}), bf16[8,48,512]{2,1,0:T(8,128)(2,1)S(1)}, u32[]{:S(2)}, u32[]{:S(2)}) async-start(bf16[8,48,512]{2,1,0:T(8,128)(2,1)} %bitcast.15), calls=%async_computation | async-start | bytes 786432 | tf_op jit(solution)/shard_map/all_to_all | solution.py:306
  31.2 1.7 stack_rows.5.refs_0_
  32.9 2.0 %collective-permute-start.7 = (bf16[512,256]{1,0:T(8,128)(2,1)}, bf16[512,256]{1,0:T(8,128)(2,1)S(1)}, u32[]{:S(2)}, u32[]{:S(2)}) collective-permute-start(bf16[512,256]{1,0:T(8,128)(2,1)} %stack_rows.5.refs_0_), channel_id=1, source_target_pairs={{0,2},{1,3},{2,4},{3,5},{4,6},{5,7},{6,0},{7,1},{8,10},{9,11},{10,... | collective-permute-start | bytes 786440 | tf_op jit(solution)/shard_map/ppermute | solution.py:64
  34.9 1.2 collective-permute-start.8
  36.1 1.2 dynamic-slice_bitcast_fusion
  37.3 1.6 collective-permute-done
  38.9 3.1 %collective-permute-done.7.refs_3_ = bf16[512,256]{1,0:T(8,128)(2,1)S(1)} collective-permute-done((bf16[512,256]{1,0:T(8,128)(2,1)}, bf16[512,256]{1,0:T(8,128)(2,1)S(1)}, u32[]{:S(2)}, u32[]{:S(2)}) %collective-permute-start.7) | collective-permute-done | bytes 262176 | tf_op jit(solution)/shard_map/ppermute | solution.py:64
  43.1 1.3 pad_maximum_fusion
  44.4 8.0 %all-to-all-start.1 = ((bf16[16,24,2304]{2,1,0:T(8,128)(2,1)}), bf16[16,24,2304]{2,1,0:T(8,128)(2,1)}, u32[]{:S(2)}, u32[]{:S(2)}) async-start(bf16[16,24,2304]{2,1,0:T(8,128)(2,1)} %bitcast.22), calls=%async_computation.1 | async-start | bytes 3538944 | tf_op jit(solution)/shard_map/all_to_all | solution.py:460
  52.5 2.0 %collective-permute-start.10 = (bf16[256,256]{1,0:T(8,128)(2,1)S(1)}, bf16[256,256]{1,0:T(8,128)(2,1)S(1)}, u32[]{:S(2)}, u32[]{:S(2)}) collective-permute-start(bf16[256,256]{1,0:T(8,128)(2,1)S(1)} %slice.132), channel_id=1, source_target_pairs={{0,6},{1,7},{2,0},{3,1},{4,2},{5,3},{6,4},{7,5},{8,14},{9,15},{10,... | collective-permute-start | bytes 393224 | tf_op jit(solution)/shard_map/ppermute | solution.py:64
  54.8 2.8 %collective-permute-done.10.refs_1_ = bf16[256,256]{1,0:T(8,128)(2,1)S(1)} collective-permute-done((bf16[256,256]{1,0:T(8,128)(2,1)S(1)}, bf16[256,256]{1,0:T(8,128)(2,1)S(1)}, u32[]{:S(2)}, u32[]{:S(2)}) %collective-permute-start.10) | collective-permute-done | bytes 131104 | tf_op jit(solution)/shard_map/ppermute | solution.py:64
  57.6 3.2 %collective-permute-done.9.refs_0_ = bf16[256,256]{1,0:T(8,128)(2,1)S(1)} collective-permute-done((bf16[256,256]{1,0:T(8,128)(2,1)S(1)}, bf16[256,256]{1,0:T(8,128)(2,1)S(1)}, u32[]{:S(2)}, u32[]{:S(2)}) %collective-permute-start.9) | collective-permute-done | bytes 131104 | tf_op jit(solution)/shard_map/ppermute | solution.py:64
  61.5 1.7 %stack_rows.6.refs_2_ = bf16[512,256]{1,0:T(8,128)(2,1)} custom-call(bf16[256,256]{1,0:T(8,128)(2,1)} %copy-done.13, bf16[256,256]{1,0:T(8,128)(2,1)} %copy-done.12), custom_call_target="tpu_custom_call" | custom-call | bytes 524288 | tf_op jit(solution)/shard_map/stack_rows/pallas_call | solution.py:40
  63.2 2.2 %stack_rows.7.kv_ref = bf16[2048,256]{1,0:T(8,128)(2,1)} custom-call(bf16[512,256]{1,0:T(8,128)(2,1)} %stack_rows.5.refs_0_, bf16[512,256]{1,0:T(8,128)(2,1)} %copy-done.9, bf16[512,256]{1,0:T(8,128)(2,1)} %stack_rows.6.refs_2_, bf16[512,256]{1,0:T(8,128)(2,1)} %copy-done.8), custom_call_target="tpu_custom_call" | custom-call | bytes 2097152 | tf_op jit(solution)/shard_map/stack_rows/pallas_call | solution.py:40
  65.4 1.2 copy-done.1
  66.6 5.3 %attention_stats.1.stats_ref = f32[8,1024]{1,0:T(8,128)S(1)} custom-call(s32[4]{0:T(128)S(1)} %pad_add_fusion.here_ref, bf16[1024,128]{1,0:T(8,128)(2,1)S(1)} %get-tuple-element.64.q_ref, bf16[1024,128]{1,0:T(8,128)(2,1)S(1)} %get-tuple-element.65.g_ref, bf16[2048,256]{1,0:T(8,128)(2,1)S(1)} %copy-done.1), custom_call_target="tpu_custom_call" | custom-call | flops 1073741824 | bytes 1048576 | tf_op jit(solution)/shard_map/attention_stats/pallas_call | solution.py:242
  71.9 2.9 %collective-permute-start.11 = (f32[8,1024]{1,0:T(8,128)S(1)}, f32[8,1024]{1,0:T(8,128)S(1)}, u32[]{:S(2)}, u32[]{:S(2)}) collective-permute-start(f32[8,1024]{1,0:T(8,128)S(1)} %attention_stats.1.stats_ref), channel_id=1, source_target_pairs={{0,1},{1,0},{2,3},{3,2},{4,5},{5,4},{6,7},{7,6},{8,9},{9,8},{10,11... | collective-permute-start | bytes 98312 | tf_op jit(solution)/shard_map/ppermute | solution.py:53
  74.8 2.5 %collective-permute-done.11.far_ref = f32[8,1024]{1,0:T(8,128)S(1)} collective-permute-done((f32[8,1024]{1,0:T(8,128)S(1)}, f32[8,1024]{1,0:T(8,128)S(1)}, u32[]{:S(2)}, u32[]{:S(2)}) %collective-permute-start.11) | collective-permute-done | bytes 32800 | tf_op jit(solution)/shard_map/ppermute | solution.py:53
  77.3 0.9 copy-done.4
  78.2 9.0 %attention_grads.1 = (bf16[2048,256]{1,0:T(8,128)(2,1)S(1)}, f32[1024,128]{1,0:T(8,128)S(1)}) custom-call(s32[4]{0:T(128)S(1)} %pad_add_fusion.here_ref, bf16[1024,128]{1,0:T(8,128)(2,1)S(1)} %get-tuple-element.64.q_ref, bf16[1024,128]{1,0:T(8,128)(2,1)S(1)} %copy-done.4, bf16[2048,256]{1,0:T(8,128)(2,1)S(1)} %copy-done.1, ...), custom_call_target="tpu_custom_call" | custom-call | flops 2684354560 | bytes 2097152 | tf_op jit(solution)/shard_map/attention_grads/pallas_call | solution.py:260
  87.4 3.2 %collective-permute-start.15 = (bf16[512,128]{1,0:T(8,128)(2,1)S(1)}, bf16[512,128]{1,0:T(8,128)(2,1)S(1)}, u32[]{:S(2)}, u32[]{:S(2)}) collective-permute-start(bf16[512,128]{1,0:T(8,128)(2,1)S(1)} %get-tuple-element.46), channel_id=1, source_target_pairs={{0,6},{1,7},{2,0},{3,1},{4,2},{5,3},{6,4},{7,5},{8,14},{9,15},{10,... | collective-permute-start | bytes 393224 | tf_op jit(solution)/shard_map/ppermute | solution.py:64
  90.6 4.3 %collective-permute-done.13 = bf16[512,128]{1,0:T(8,128)(2,1)S(1)} collective-permute-done((bf16[512,128]{1,0:T(8,128)(2,1)S(1)}, bf16[512,128]{1,0:T(8,128)(2,1)S(1)}, u32[]{:S(2)}, u32[]{:S(2)}) %collective-permute-start.13) | collective-permute-done | bytes 131104 | tf_op jit(solution)/shard_map/ppermute | solution.py:64
  95.0 0.7 pad_maximum_fusion.5
  95.7 0.7 pad_maximum_fusion.6
  96.5 3.3 %collective-permute-start.16 = (bf16[512,256]{1,0:T(8,128)(2,1)}, bf16[512,256]{1,0:T(8,128)(2,1)}, u32[]{:S(2)}, u32[]{:S(2)}) collective-permute-start(bf16[512,256]{1,0:T(8,128)(2,1)} %pad_maximum_fusion.6), channel_id=1, source_target_pairs={{0,6},{1,7},{2,0},{3,1},{4,2},{5,3},{6,4},{7,5},{8,14},{9,15},{10,... | collective-permute-start | bytes 786440 | tf_op jit(solution)/shard_map/ppermute | solution.py:64
  99.8 0.9 fusion.8
  100.7 3.0 %collective-permute-done.14 = bf16[512,256]{1,0:T(8,128)(2,1)} collective-permute-done((bf16[512,256]{1,0:T(8,128)(2,1)}, bf16[512,256]{1,0:T(8,128)(2,1)}, u32[]{:S(2)}, u32[]{:S(2)}) %collective-permute-start.14) | collective-permute-done | bytes 262176 | tf_op jit(solution)/shard_map/ppermute | solution.py:64
  104.0 1.9 %fusion.27 = (bf16[512,256]{1,0:T(8,128)(2,1)S(1)}, f32[512,256]{1,0:T(8,128)}) fusion(bf16[2048,256]{1,0:T(8,128)(2,1)S(1)} %get-tuple-element.29, bf16[512,256]{1,0:T(8,128)(2,1)} %collective-permute-done.16, bf16[512,256]{1,0:T(8,128)(2,1)} %collective-permute-done.14), kind=kLoop, calls=%fused_computation.76 | loop fusion | flops 786432 | bytes 1572864 | tf_op jit(solution)/shard_map/convert.3
  105.9 3.1 %collective-permute-start.17 = (bf16[128,256]{1,0:T(8,128)(2,1)S(1)}, bf16[128,256]{1,0:T(8,128)(2,1)S(1)}, u32[]{:S(2)}, u32[]{:S(2)}) collective-permute-start(bf16[128,256]{1,0:T(8,128)(2,1)S(1)} %get-tuple-element.51), channel_id=1, source_target_pairs={{0,128},{16,144},{32,160},{48,176},{64,192},{80,208},{96,224},{112... | collective-permute-start | bytes 196616 | tf_op jit(solution)/shard_map/ppermute | solution.py:121
  109.0 2.5 %collective-permute-start.18 = (bf16[128,256]{1,0:T(8,128)(2,1)S(1)}, bf16[128,256]{1,0:T(8,128)(2,1)S(1)}, u32[]{:S(2)}, u32[]{:S(2)}) collective-permute-start(bf16[128,256]{1,0:T(8,128)(2,1)S(1)} %get-tuple-element.53), channel_id=1, source_target_pairs={{0,16},{16,0},{32,48},{48,32},{64,80},{80,64},{96,112},{112,96},{1... | collective-permute-start | bytes 196616 | tf_op jit(solution)/shard_map/ppermute | solution.py:121
  111.6 1.8 %convert_reduce_fusion = f32[24,2304]{1,0:T(8,128)S(1)} fusion(bf16[16,24,2304]{2,1,0:T(8,128)(2,1)} %all-to-all-done.1), kind=kLoop, calls=%fused_computation | loop fusion | flops 1714176 | bytes 1990656 | tf_op jit(solution)/shard_map/reduce_sum | solution.py:472
  113.5 3.0 %collective-permute-start.23 = (bf16[24,2304]{1,0:T(8,128)(2,1)S(1)}, bf16[24,2304]{1,0:T(8,128)(2,1)S(1)}, u32[]{:S(2)}, u32[]{:S(2)}) collective-permute-start(bf16[24,2304]{1,0:T(8,128)(2,1)S(1)} %pad_maximum_fusion.8), channel_id=1, source_target_pairs={{0,128},{16,144},{32,160},{48,176},{64,192},{80,208},{96,224},{112... | collective-permute-start | bytes 331784 | tf_op jit(solution)/shard_map/ppermute | solution.py:69
  116.5 1.7 %collective-permute-done.19 = bf16[128,256]{1,0:T(8,128)(2,1)S(1)} collective-permute-done((bf16[128,256]{1,0:T(8,128)(2,1)S(1)}, bf16[128,256]{1,0:T(8,128)(2,1)S(1)}, u32[]{:S(2)}, u32[]{:S(2)}) %collective-permute-start.19) | collective-permute-done | bytes 65568 | tf_op jit(solution)/shard_map/ppermute | solution.py:121
  118.2 0.9 fusion.18
  119.9 1.9 %collective-permute-start.24 = (bf16[48,2304]{1,0:T(8,128)(2,1)S(1)}, bf16[48,2304]{1,0:T(8,128)(2,1)S(1)}, u32[]{:S(2)}, u32[]{:S(2)}) collective-permute-start(bf16[48,2304]{1,0:T(8,128)(2,1)S(1)} %pad_maximum_fusion.7.refs_0_), channel_id=1, source_target_pairs={{0,112},{16,0},{32,16},{48,32},{64,48},{80,64},{96,80},{112,96},{1... | collective-permute-start | bytes 663560 | tf_op jit(solution)/shard_map/ppermute | solution.py:59
  122.1 5.8 %collective-permute-start.20 = (f32[32,256]{1,0:T(8,128)S(1)}, f32[32,256]{1,0:T(8,128)S(1)}, u32[]{:S(2)}, u32[]{:S(2)}) collective-permute-start(f32[32,256]{1,0:T(8,128)S(1)} %get-tuple-element.61), channel_id=1, source_target_pairs={{0,64},{16,80},{32,96},{48,112},{64,0},{80,16},{96,32},{112,48},{1... | collective-permute-start | bytes 98312 | tf_op jit(solution)/shard_map/ppermute | solution.py:121
  128.7 3.0 %collective-permute-start.25 = (bf16[48,2304]{1,0:T(8,128)(2,1)S(1)}, bf16[48,2304]{1,0:T(8,128)(2,1)S(1)}, u32[]{:S(2)}, u32[]{:S(2)}) collective-permute-start(bf16[48,2304]{1,0:T(8,128)(2,1)S(1)} %collective-permute-done.24.refs_1_), channel_id=1, source_target_pairs={{0,112},{16,0},{32,16},{48,32},{64,48},{80,64},{96,80},{112,96},{1... | collective-permute-start | bytes 663560 | tf_op jit(solution)/shard_map/ppermute | solution.py:59
  132.4 2.0 %collective-permute-done.20 = f32[32,256]{1,0:T(8,128)S(1)} collective-permute-done((f32[32,256]{1,0:T(8,128)S(1)}, f32[32,256]{1,0:T(8,128)S(1)}, u32[]{:S(2)}, u32[]{:S(2)}) %collective-permute-start.20) | collective-permute-done | bytes 32800 | tf_op jit(solution)/shard_map/ppermute | solution.py:121
  134.4 1.8 %collective-permute-start.12 = (bf16[512,128]{1,0:T(8,128)(2,1)S(1)}, bf16[512,128]{1,0:T(8,128)(2,1)S(1)}, u32[]{:S(2)}, u32[]{:S(2)}) collective-permute-start(bf16[512,128]{1,0:T(8,128)(2,1)S(1)} %slice.224), channel_id=1, source_target_pairs={{0,1},{1,0},{2,3},{3,2},{4,5},{5,4},{6,7},{7,6},{8,9},{9,8},{10,11... | collective-permute-start | bytes 393224 | tf_op jit(solution)/shard_map/ppermute | solution.py:53
  136.2 2.6 %collective-permute-start.26 = (bf16[48,2304]{1,0:T(8,128)(2,1)S(1)}, bf16[48,2304]{1,0:T(8,128)(2,1)S(1)}, u32[]{:S(2)}, u32[]{:S(2)}) collective-permute-start(bf16[48,2304]{1,0:T(8,128)(2,1)S(1)} %collective-permute-done.25.refs_2_), channel_id=1, source_target_pairs={{0,112},{16,0},{32,16},{48,32},{64,48},{80,64},{96,80},{112,96},{1... | collective-permute-start | bytes 663560 | tf_op jit(solution)/shard_map/ppermute | solution.py:59
  138.8 1.2 collective-permute-done.28.refs_7_
  140.0 2.2 %collective-permute-done.26.refs_3_ = bf16[48,2304]{1,0:T(8,128)(2,1)S(1)} collective-permute-done((bf16[48,2304]{1,0:T(8,128)(2,1)S(1)}, bf16[48,2304]{1,0:T(8,128)(2,1)S(1)}, u32[]{:S(2)}, u32[]{:S(2)}) %collective-permute-start.26) | collective-permute-done | bytes 221216 | tf_op jit(solution)/shard_map/ppermute | solution.py:59
  142.3 4.9 %collective-permute-done.29.refs_6_ = bf16[48,2304]{1,0:T(8,128)(2,1)S(1)} collective-permute-done((bf16[48,2304]{1,0:T(8,128)(2,1)S(1)}, bf16[48,2304]{1,0:T(8,128)(2,1)S(1)}, u32[]{:S(2)}, u32[]{:S(2)}) %collective-permute-start.29) | collective-permute-done | bytes 221216 | tf_op jit(solution)/shard_map/ppermute | solution.py:59
  147.3 3.3 %collective-permute-start.31 = (bf16[48,1152]{1,0:T(8,128)(2,1)S(1)}, bf16[48,1152]{1,0:T(8,128)(2,1)S(1)}, u32[]{:S(2)}, u32[]{:S(2)}) collective-permute-start(bf16[48,1152]{1,0:T(8,128)(2,1)S(1)} %slice.156), channel_id=1, source_target_pairs={{0,112},{16,0},{32,16},{48,32},{64,48},{80,64},{96,80},{112,96},{1... | collective-permute-start | bytes 331784 | tf_op jit(solution)/shard_map/ppermute | solution.py:59
  150.6 0.8 copy.39
  151.4 1.8 %collective-permute-done.30.refs_4_ = bf16[48,1152]{1,0:T(8,128)(2,1)S(1)} collective-permute-done((bf16[48,1152]{1,0:T(8,128)(2,1)S(1)}, bf16[48,1152]{1,0:T(8,128)(2,1)S(1)}, u32[]{:S(2)}, u32[]{:S(2)}) %collective-permute-start.30) | collective-permute-done | bytes 110624 | tf_op jit(solution)/shard_map/ppermute | solution.py:59
  155.9 6.9 %all-to-all-start.2 = ((bf16[8,48,128]{2,1,0:T(8,128)(2,1)}), bf16[8,48,128]{2,1,0:T(8,128)(2,1)S(1)}, u32[]{:S(2)}, u32[]{:S(2)}) async-start(bf16[8,48,128]{2,1,0:T(8,128)(2,1)} %fusion.19), calls=%async_computation.2 | async-start | bytes 196608 | tf_op jit(solution)/shard_map/all_to_all | solution.py:425
  162.8 1.3 fusion.24
  164.1 0.9 copy-done.2
  165.0 1.5 expert_weight_grads.1
  166.6 1.4 all-to-all-done.2
  168.0 1.1 fusion
  (122 shorter events, 11.7 us)
Async XLA Ops:
  0.6 42.0 %copy-start = (bf16[1,1536,256]{2,1,0:T(8,128)(2,1)S(1)}, bf16[1,1536,256]{2,1,0:T(8,128)(2,1)}, u32[]{:S(2)}) copy-start(bf16[1,1536,256]{2,1,0:T(8,128)(2,1)} %param.21) | copy-start | bytes 2359300
  1.4 14.7 %copy-start.15 = (bf16[32,256]{1,0:T(8,128)(2,1)}, bf16[32,256]{1,0:T(8,128)(2,1)S(1)}, u32[]{:S(2)}) copy-start(bf16[32,256]{1,0:T(8,128)(2,1)S(1)} %pad_maximum_fusion.9.refs_0_) | copy-start | bytes 49156
  1.4 14.8 %collective-permute-start.1 = (bf16[32,256]{1,0:T(8,128)(2,1)S(1)}, bf16[32,256]{1,0:T(8,128)(2,1)S(1)}, u32[]{:S(2)}, u32[]{:S(2)}) collective-permute-start(bf16[32,256]{1,0:T(8,128)(2,1)S(1)} %pad_maximum_fusion.9.refs_0_), channel_id=1, source_target_pairs={{0,64},{16,80},{32,96},{48,112},{64,0},{80,16},{96,32},{112,48},{1... | collective-permute-start | bytes 49160 | tf_op jit(solution)/shard_map/ppermute | solution.py:121
  8.6 7.6 %collective-permute-start.2 = (bf16[32,256]{1,0:T(8,128)(2,1)S(1)}, bf16[32,256]{1,0:T(8,128)(2,1)S(1)}, u32[]{:S(2)}, u32[]{:S(2)}) collective-permute-start(bf16[32,256]{1,0:T(8,128)(2,1)S(1)} %pad_maximum_fusion.9.refs_0_), channel_id=1, source_target_pairs={{0,32},{16,48},{32,0},{48,16},{64,96},{80,112},{96,64},{112,80},{1... | collective-permute-start | bytes 49160 | tf_op jit(solution)/shard_map/ppermute | solution.py:121
  10.1 6.2 %collective-permute-start.3 = (bf16[32,256]{1,0:T(8,128)(2,1)S(1)}, bf16[32,256]{1,0:T(8,128)(2,1)S(1)}, u32[]{:S(2)}, u32[]{:S(2)}) collective-permute-start(bf16[32,256]{1,0:T(8,128)(2,1)S(1)} %pad_maximum_fusion.9.refs_0_), channel_id=1, source_target_pairs={{0,96},{16,112},{32,64},{48,80},{64,32},{80,48},{96,0},{112,16},{1... | collective-permute-start | bytes 49160 | tf_op jit(solution)/shard_map/ppermute | solution.py:121
  10.9 2.8 %copy-start.19 = (pred[512,8]{0,1:T(8,128)(4,1)}, pred[512,8]{0,1:T(8,128)(4,1)S(1)}, u32[]{:S(2)}) copy-start(pred[512,8]{0,1:T(8,128)(4,1)S(1)} %broadcast_compare_fusion) | copy-start | bytes 12292
  13.2 3.0 %copy-start.10 = (bf16[256,2,128]{2,1,0:T(2,128)(2,1)S(1)}, bf16[256,2,128]{2,1,0:T(2,128)(2,1)}, u32[]{:S(2)}) copy-start(bf16[256,2,128]{2,1,0:T(2,128)(2,1)} %param.11) | copy-start | bytes 393220
  13.8 2.4 %copy-start.11 = (bf16[256,2,128]{2,1,0:T(2,128)(2,1)S(1)}, bf16[256,2,128]{2,1,0:T(2,128)(2,1)}, u32[]{:S(2)}) copy-start(bf16[256,2,128]{2,1,0:T(2,128)(2,1)} %param.14) | copy-start | bytes 393220
  16.2 0.6 copy-start.21
  16.3 0.6 copy-start.22
  16.9 0.6 copy-start.23
  18.9 11.0 %collective-permute-start.4 = (bf16[128,256]{1,0:T(8,128)(2,1)}, bf16[128,256]{1,0:T(8,128)(2,1)S(1)}, u32[]{:S(2)}, u32[]{:S(2)}) collective-permute-start(bf16[128,256]{1,0:T(8,128)(2,1)} %stack_rows.4.refs_0_), channel_id=1, source_target_pairs={{0,128},{16,144},{32,160},{48,176},{64,192},{80,208},{96,224},{112... | collective-permute-start | bytes 196616 | tf_op jit(solution)/shard_map/ppermute | solution.py:121
  21.0 8.9 %collective-permute-start.5 = (bf16[128,256]{1,0:T(8,128)(2,1)}, bf16[128,256]{1,0:T(8,128)(2,1)S(1)}, u32[]{:S(2)}, u32[]{:S(2)}) collective-permute-start(bf16[128,256]{1,0:T(8,128)(2,1)} %stack_rows.4.refs_0_), channel_id=1, source_target_pairs={{0,16},{16,0},{32,48},{48,32},{64,80},{80,64},{96,112},{112,96},{1... | collective-permute-start | bytes 196616 | tf_op jit(solution)/shard_map/ppermute | solution.py:121
  22.0 7.9 %collective-permute-start.6 = (bf16[128,256]{1,0:T(8,128)(2,1)}, bf16[128,256]{1,0:T(8,128)(2,1)S(1)}, u32[]{:S(2)}, u32[]{:S(2)}) collective-permute-start(bf16[128,256]{1,0:T(8,128)(2,1)} %stack_rows.4.refs_0_), channel_id=1, source_target_pairs={{0,144},{16,128},{32,176},{48,160},{64,208},{80,192},{96,240},{112... | collective-permute-start | bytes 196616 | tf_op jit(solution)/shard_map/ppermute | solution.py:121
  23.9 18.1 %all-to-all-start = ((bf16[8,48,512]{2,1,0:T(8,128)(2,1)}), bf16[8,48,512]{2,1,0:T(8,128)(2,1)S(1)}, u32[]{:S(2)}, u32[]{:S(2)}) async-start(bf16[8,48,512]{2,1,0:T(8,128)(2,1)} %bitcast.15), calls=%async_computation | async-start | bytes 786432 | tf_op jit(solution)/shard_map/all_to_all | solution.py:306
  29.8 9.1 %collective-permute-start = (bf16[1024,128]{1,0:T(8,128)(2,1)S(1)}, bf16[1024,128]{1,0:T(8,128)(2,1)S(1)}, u32[]{:S(2)}, u32[]{:S(2)}) collective-permute-start(bf16[1024,128]{1,0:T(8,128)(2,1)S(1)} %pad_maximum_fusion.2), channel_id=1, source_target_pairs={{0,1},{1,0},{2,3},{3,2},{4,5},{5,4},{6,7},{7,6},{8,9},{9,8},{10,11... | collective-permute-start | bytes 786440 | tf_op jit(solution)/shard_map/ppermute | solution.py:53
  29.9 0.6 copy-start.16
  30.0 0.6 copy-start.17
  30.6 0.6 copy-start.18
  32.9 9.1 %collective-permute-start.7 = (bf16[512,256]{1,0:T(8,128)(2,1)}, bf16[512,256]{1,0:T(8,128)(2,1)S(1)}, u32[]{:S(2)}, u32[]{:S(2)}) collective-permute-start(bf16[512,256]{1,0:T(8,128)(2,1)} %stack_rows.5.refs_0_), channel_id=1, source_target_pairs={{0,2},{1,3},{2,4},{3,5},{4,6},{5,7},{6,0},{7,1},{8,10},{9,11},{10,... | collective-permute-start | bytes 786440 | tf_op jit(solution)/shard_map/ppermute | solution.py:64
  34.9 7.1 %collective-permute-start.8 = (bf16[512,256]{1,0:T(8,128)(2,1)}, bf16[512,256]{1,0:T(8,128)(2,1)S(1)}, u32[]{:S(2)}, u32[]{:S(2)}) collective-permute-start(bf16[512,256]{1,0:T(8,128)(2,1)} %stack_rows.5.refs_0_), channel_id=1, source_target_pairs={{0,6},{1,7},{2,0},{3,1},{4,2},{5,3},{6,4},{7,5},{8,14},{9,15},{10,... | collective-permute-start | bytes 786440 | tf_op jit(solution)/shard_map/ppermute | solution.py:64
  42.0 12.6 %copy-start.8 = (bf16[512,256]{1,0:T(8,128)(2,1)}, bf16[512,256]{1,0:T(8,128)(2,1)S(1)}, u32[]{:S(2)}) copy-start(bf16[512,256]{1,0:T(8,128)(2,1)S(1)} %collective-permute-done.7.refs_3_) | copy-start | bytes 786436
  42.0 10.5 %copy-start.9 = (bf16[512,256]{1,0:T(8,128)(2,1)}, bf16[512,256]{1,0:T(8,128)(2,1)S(1)}, u32[]{:S(2)}) copy-start(bf16[512,256]{1,0:T(8,128)(2,1)S(1)} %collective-permute-done.8.refs_1_) | copy-start | bytes 786436
  42.0 1.1 copy-start.5
  44.4 67.2 %all-to-all-start.1 = ((bf16[16,24,2304]{2,1,0:T(8,128)(2,1)}), bf16[16,24,2304]{2,1,0:T(8,128)(2,1)}, u32[]{:S(2)}, u32[]{:S(2)}) async-start(bf16[16,24,2304]{2,1,0:T(8,128)(2,1)} %bitcast.22), calls=%async_computation.1 | async-start | bytes 3538944 | tf_op jit(solution)/shard_map/all_to_all | solution.py:460
  52.5 5.0 %collective-permute-start.10 = (bf16[256,256]{1,0:T(8,128)(2,1)S(1)}, bf16[256,256]{1,0:T(8,128)(2,1)S(1)}, u32[]{:S(2)}, u32[]{:S(2)}) collective-permute-start(bf16[256,256]{1,0:T(8,128)(2,1)S(1)} %slice.132), channel_id=1, source_target_pairs={{0,6},{1,7},{2,0},{3,1},{4,2},{5,3},{6,4},{7,5},{8,14},{9,15},{10,... | collective-permute-start | bytes 393224 | tf_op jit(solution)/shard_map/ppermute | solution.py:64
  54.5 6.3 %collective-permute-start.9 = (bf16[256,256]{1,0:T(8,128)(2,1)S(1)}, bf16[256,256]{1,0:T(8,128)(2,1)S(1)}, u32[]{:S(2)}, u32[]{:S(2)}) collective-permute-start(bf16[256,256]{1,0:T(8,128)(2,1)S(1)} %slice.131), channel_id=1, source_target_pairs={{0,2},{1,3},{2,4},{3,5},{4,6},{5,7},{6,0},{7,1},{8,10},{9,11},{10,... | collective-permute-start | bytes 393224 | tf_op jit(solution)/shard_map/ppermute | solution.py:64
  54.8 17.2 %copy-start.3 = (bf16[1024,128]{1,0:T(8,128)(2,1)}, bf16[1024,128]{1,0:T(8,128)(2,1)S(1)}, u32[]{:S(2)}) copy-start(bf16[1024,128]{1,0:T(8,128)(2,1)S(1)} %get-tuple-element.65.g_ref) | copy-start | bytes 786436
  57.6 3.2 %copy-start.12 = (bf16[256,256]{1,0:T(8,128)(2,1)}, bf16[256,256]{1,0:T(8,128)(2,1)S(1)}, u32[]{:S(2)}) copy-start(bf16[256,256]{1,0:T(8,128)(2,1)S(1)} %collective-permute-done.10.refs_1_) | copy-start | bytes 393220
  60.8 0.7 copy-start.13
  65.4 1.2 copy-start.1
  71.9 5.3 %collective-permute-start.11 = (f32[8,1024]{1,0:T(8,128)S(1)}, f32[8,1024]{1,0:T(8,128)S(1)}, u32[]{:S(2)}, u32[]{:S(2)}) collective-permute-start(f32[8,1024]{1,0:T(8,128)S(1)} %attention_stats.1.stats_ref), channel_id=1, source_target_pairs={{0,1},{1,0},{2,3},{3,2},{4,5},{5,4},{6,7},{7,6},{8,9},{9,8},{10,11... | collective-permute-start | bytes 98312 | tf_op jit(solution)/shard_map/ppermute | solution.py:53
  77.3 1.0 copy-start.4
  87.2 12.6 %copy-start.6 = (bf16[8,48,512]{2,1,0:T(8,128)(2,1)S(1)}, bf16[8,48,512]{2,1,0:T(8,128)(2,1)}, u32[]{:S(2)}) copy-start(bf16[8,48,512]{2,1,0:T(8,128)(2,1)} %copy-done.5) | copy-start | bytes 1179652
  87.3 7.6 %collective-permute-start.13 = (bf16[512,128]{1,0:T(8,128)(2,1)S(1)}, bf16[512,128]{1,0:T(8,128)(2,1)S(1)}, u32[]{:S(2)}, u32[]{:S(2)}) collective-permute-start(bf16[512,128]{1,0:T(8,128)(2,1)S(1)} %get-tuple-element.45), channel_id=1, source_target_pairs={{0,2},{1,3},{2,4},{3,5},{4,6},{5,7},{6,0},{7,1},{8,10},{9,11},{10,... | collective-permute-start | bytes 393224 | tf_op jit(solution)/shard_map/ppermute | solution.py:64
  87.4 7.5 %collective-permute-start.15 = (bf16[512,128]{1,0:T(8,128)(2,1)S(1)}, bf16[512,128]{1,0:T(8,128)(2,1)S(1)}, u32[]{:S(2)}, u32[]{:S(2)}) collective-permute-start(bf16[512,128]{1,0:T(8,128)(2,1)S(1)} %get-tuple-element.46), channel_id=1, source_target_pairs={{0,6},{1,7},{2,0},{3,1},{4,2},{5,3},{6,4},{7,5},{8,14},{9,15},{10,... | collective-permute-start | bytes 393224 | tf_op jit(solution)/shard_map/ppermute | solution.py:64
  95.7 8.0 %collective-permute-start.14 = (bf16[512,256]{1,0:T(8,128)(2,1)}, bf16[512,256]{1,0:T(8,128)(2,1)}, u32[]{:S(2)}, u32[]{:S(2)}) collective-permute-start(bf16[512,256]{1,0:T(8,128)(2,1)} %pad_maximum_fusion.5), channel_id=1, source_target_pairs={{0,2},{1,3},{2,4},{3,5},{4,6},{5,7},{6,0},{7,1},{8,10},{9,11},{10,... | collective-permute-start | bytes 786440 | tf_op jit(solution)/shard_map/ppermute | solution.py:64
  96.5 7.5 %collective-permute-start.16 = (bf16[512,256]{1,0:T(8,128)(2,1)}, bf16[512,256]{1,0:T(8,128)(2,1)}, u32[]{:S(2)}, u32[]{:S(2)}) collective-permute-start(bf16[512,256]{1,0:T(8,128)(2,1)} %pad_maximum_fusion.6), channel_id=1, source_target_pairs={{0,6},{1,7},{2,0},{3,1},{4,2},{5,3},{6,4},{7,5},{8,14},{9,15},{10,... | collective-permute-start | bytes 786440 | tf_op jit(solution)/shard_map/ppermute | solution.py:64
  105.9 10.6 %collective-permute-start.17 = (bf16[128,256]{1,0:T(8,128)(2,1)S(1)}, bf16[128,256]{1,0:T(8,128)(2,1)S(1)}, u32[]{:S(2)}, u32[]{:S(2)}) collective-permute-start(bf16[128,256]{1,0:T(8,128)(2,1)S(1)} %get-tuple-element.51), channel_id=1, source_target_pairs={{0,128},{16,144},{32,160},{48,176},{64,192},{80,208},{96,224},{112... | collective-permute-start | bytes 196616 | tf_op jit(solution)/shard_map/ppermute | solution.py:121
  109.0 7.4 %collective-permute-start.18 = (bf16[128,256]{1,0:T(8,128)(2,1)S(1)}, bf16[128,256]{1,0:T(8,128)(2,1)S(1)}, u32[]{:S(2)}, u32[]{:S(2)}) collective-permute-start(bf16[128,256]{1,0:T(8,128)(2,1)S(1)} %get-tuple-element.53), channel_id=1, source_target_pairs={{0,16},{16,0},{32,48},{48,32},{64,80},{80,64},{96,112},{112,96},{1... | collective-permute-start | bytes 196616 | tf_op jit(solution)/shard_map/ppermute | solution.py:121
  111.5 6.7 %collective-permute-start.19 = (bf16[128,256]{1,0:T(8,128)(2,1)S(1)}, bf16[128,256]{1,0:T(8,128)(2,1)S(1)}, u32[]{:S(2)}, u32[]{:S(2)}) collective-permute-start(bf16[128,256]{1,0:T(8,128)(2,1)S(1)} %get-tuple-element.52), channel_id=1, source_target_pairs={{0,144},{16,128},{32,176},{48,160},{64,208},{80,192},{96,240},{112... | collective-permute-start | bytes 196616 | tf_op jit(solution)/shard_map/ppermute | solution.py:121
  111.6 20.1 %copy-start.7 = (bf16[8,48,512]{2,1,0:T(8,128)(2,1)S(1)}, bf16[8,48,512]{2,1,0:T(8,128)(2,1)}, u32[]{:S(2)}) copy-start(bf16[8,48,512]{2,1,0:T(8,128)(2,1)} %fusion.8) | copy-start | bytes 1179652
  113.5 6.3 %collective-permute-start.23 = (bf16[24,2304]{1,0:T(8,128)(2,1)S(1)}, bf16[24,2304]{1,0:T(8,128)(2,1)S(1)}, u32[]{:S(2)}, u32[]{:S(2)}) collective-permute-start(bf16[24,2304]{1,0:T(8,128)(2,1)S(1)} %pad_maximum_fusion.8), channel_id=1, source_target_pairs={{0,128},{16,144},{32,160},{48,176},{64,192},{80,208},{96,224},{112... | collective-permute-start | bytes 331784 | tf_op jit(solution)/shard_map/ppermute | solution.py:69
  119.9 8.8 %collective-permute-start.24 = (bf16[48,2304]{1,0:T(8,128)(2,1)S(1)}, bf16[48,2304]{1,0:T(8,128)(2,1)S(1)}, u32[]{:S(2)}, u32[]{:S(2)}) collective-permute-start(bf16[48,2304]{1,0:T(8,128)(2,1)S(1)} %pad_maximum_fusion.7.refs_0_), channel_id=1, source_target_pairs={{0,112},{16,0},{32,16},{48,32},{64,48},{80,64},{96,80},{112,96},{1... | collective-permute-start | bytes 663560 | tf_op jit(solution)/shard_map/ppermute | solution.py:59
  121.8 9.8 %collective-permute-start.27 = (bf16[48,2304]{1,0:T(8,128)(2,1)S(1)}, bf16[48,2304]{1,0:T(8,128)(2,1)S(1)}, u32[]{:S(2)}, u32[]{:S(2)}) collective-permute-start(bf16[48,2304]{1,0:T(8,128)(2,1)S(1)} %pad_maximum_fusion.7.refs_0_), channel_id=1, source_target_pairs={{0,16},{16,32},{32,48},{48,64},{64,80},{80,96},{96,112},{112,0},{1... | collective-permute-start | bytes 663560 | tf_op jit(solution)/shard_map/ppermute | solution.py:59
  122.1 12.3 %collective-permute-start.20 = (f32[32,256]{1,0:T(8,128)S(1)}, f32[32,256]{1,0:T(8,128)S(1)}, u32[]{:S(2)}, u32[]{:S(2)}) collective-permute-start(f32[32,256]{1,0:T(8,128)S(1)} %get-tuple-element.61), channel_id=1, source_target_pairs={{0,64},{16,80},{32,96},{48,112},{64,0},{80,16},{96,32},{112,48},{1... | collective-permute-start | bytes 98312 | tf_op jit(solution)/shard_map/ppermute | solution.py:121
  127.9 12.1 %collective-permute-start.21 = (f32[32,256]{1,0:T(8,128)S(1)}, f32[32,256]{1,0:T(8,128)S(1)}, u32[]{:S(2)}, u32[]{:S(2)}) collective-permute-start(f32[32,256]{1,0:T(8,128)S(1)} %get-tuple-element.63), channel_id=1, source_target_pairs={{0,32},{16,48},{32,0},{48,16},{64,96},{80,112},{96,64},{112,80},{1... | collective-permute-start | bytes 98312 | tf_op jit(solution)/shard_map/ppermute | solution.py:121
  128.0 12.0 %collective-permute-start.22 = (f32[32,256]{1,0:T(8,128)S(1)}, f32[32,256]{1,0:T(8,128)S(1)}, u32[]{:S(2)}, u32[]{:S(2)}) collective-permute-start(f32[32,256]{1,0:T(8,128)S(1)} %get-tuple-element.62), channel_id=1, source_target_pairs={{0,96},{16,112},{32,64},{48,80},{64,32},{80,48},{96,0},{112,16},{1... | collective-permute-start | bytes 98312 | tf_op jit(solution)/shard_map/ppermute | solution.py:121
  128.7 7.5 %collective-permute-start.25 = (bf16[48,2304]{1,0:T(8,128)(2,1)S(1)}, bf16[48,2304]{1,0:T(8,128)(2,1)S(1)}, u32[]{:S(2)}, u32[]{:S(2)}) collective-permute-start(bf16[48,2304]{1,0:T(8,128)(2,1)S(1)} %collective-permute-done.24.refs_1_), channel_id=1, source_target_pairs={{0,112},{16,0},{32,16},{48,32},{64,48},{80,64},{96,80},{112,96},{1... | collective-permute-start | bytes 663560 | tf_op jit(solution)/shard_map/ppermute | solution.py:59
  131.7 8.3 %collective-permute-start.28 = (bf16[48,2304]{1,0:T(8,128)(2,1)S(1)}, bf16[48,2304]{1,0:T(8,128)(2,1)S(1)}, u32[]{:S(2)}, u32[]{:S(2)}) collective-permute-start(bf16[48,2304]{1,0:T(8,128)(2,1)S(1)} %collective-permute-done.27.refs_8_), channel_id=1, source_target_pairs={{0,16},{16,32},{32,48},{48,64},{64,80},{80,96},{96,112},{112,0},{1... | collective-permute-start | bytes 663560 | tf_op jit(solution)/shard_map/ppermute | solution.py:59
  134.4 16.2 %collective-permute-start.12 = (bf16[512,128]{1,0:T(8,128)(2,1)S(1)}, bf16[512,128]{1,0:T(8,128)(2,1)S(1)}, u32[]{:S(2)}, u32[]{:S(2)}) collective-permute-start(bf16[512,128]{1,0:T(8,128)(2,1)S(1)} %slice.224), channel_id=1, source_target_pairs={{0,1},{1,0},{2,3},{3,2},{4,5},{5,4},{6,7},{7,6},{8,9},{9,8},{10,11... | collective-permute-start | bytes 393224 | tf_op jit(solution)/shard_map/ppermute | solution.py:53
  136.2 6.1 %collective-permute-start.26 = (bf16[48,2304]{1,0:T(8,128)(2,1)S(1)}, bf16[48,2304]{1,0:T(8,128)(2,1)S(1)}, u32[]{:S(2)}, u32[]{:S(2)}) collective-permute-start(bf16[48,2304]{1,0:T(8,128)(2,1)S(1)} %collective-permute-done.25.refs_2_), channel_id=1, source_target_pairs={{0,112},{16,0},{32,16},{48,32},{64,48},{80,64},{96,80},{112,96},{1... | collective-permute-start | bytes 663560 | tf_op jit(solution)/shard_map/ppermute | solution.py:59
  140.0 7.1 %collective-permute-start.29 = (bf16[48,2304]{1,0:T(8,128)(2,1)S(1)}, bf16[48,2304]{1,0:T(8,128)(2,1)S(1)}, u32[]{:S(2)}, u32[]{:S(2)}) collective-permute-start(bf16[48,2304]{1,0:T(8,128)(2,1)S(1)} %collective-permute-done.28.refs_7_), channel_id=1, source_target_pairs={{0,16},{16,32},{32,48},{48,64},{64,80},{80,96},{96,112},{112,0},{1... | collective-permute-start | bytes 663560 | tf_op jit(solution)/shard_map/ppermute | solution.py:59
  140.0 13.8 %copy-start.14 = (f32[32,256]{1,0:T(8,128)}, f32[32,256]{1,0:T(8,128)S(1)}, u32[]{:S(2)}) copy-start(f32[32,256]{1,0:T(8,128)S(1)} %fusion.21) | copy-start | bytes 98308
  147.2 6.0 %collective-permute-start.30 = (bf16[48,1152]{1,0:T(8,128)(2,1)S(1)}, bf16[48,1152]{1,0:T(8,128)(2,1)S(1)}, u32[]{:S(2)}, u32[]{:S(2)}) collective-permute-start(bf16[48,1152]{1,0:T(8,128)(2,1)S(1)} %slice.155), channel_id=1, source_target_pairs={{0,16},{16,32},{32,48},{48,64},{64,80},{80,96},{96,112},{112,0},{1... | collective-permute-start | bytes 331784 | tf_op jit(solution)/shard_map/ppermute | solution.py:59
  147.3 5.9 %collective-permute-start.31 = (bf16[48,1152]{1,0:T(8,128)(2,1)S(1)}, bf16[48,1152]{1,0:T(8,128)(2,1)S(1)}, u32[]{:S(2)}, u32[]{:S(2)}) collective-permute-start(bf16[48,1152]{1,0:T(8,128)(2,1)S(1)} %slice.156), channel_id=1, source_target_pairs={{0,112},{16,0},{32,16},{48,32},{64,48},{80,64},{96,80},{112,96},{1... | collective-permute-start | bytes 331784 | tf_op jit(solution)/shard_map/ppermute | solution.py:59
  153.7 14.3 %copy-start.20 = (pred[512,8]{0,1:T(8,128)(4,1)S(1)}, pred[512,8]{0,1:T(8,128)(4,1)}, u32[]{:S(2)}) copy-start(pred[512,8]{0,1:T(8,128)(4,1)} %copy-done.19) | copy-start | bytes 12292
  153.7 1.4 collective-permute-start.32
  155.9 12.1 %all-to-all-start.2 = ((bf16[8,48,128]{2,1,0:T(8,128)(2,1)}), bf16[8,48,128]{2,1,0:T(8,128)(2,1)S(1)}, u32[]{:S(2)}, u32[]{:S(2)}) async-start(bf16[8,48,128]{2,1,0:T(8,128)(2,1)} %fusion.19), calls=%async_computation.2 | async-start | bytes 196608 | tf_op jit(solution)/shard_map/all_to_all | solution.py:425
  164.1 0.9 copy-start.2

commit v8 on v7

--- a/solution.py
+++ b/solution.py
@@ -11,7 +11,6 @@
 X_HI = 2
 X_LO = 2
 MASKED = -1e30
-MASKS = (4, 2, 8, 1)
 BF = jnp.bfloat16
 F32 = jnp.float32
 
@@ -24,31 +23,6 @@
     return (hidden, d_gate, d_up)
 
 
-VMEM = pl.BlockSpec(memory_space=pltpu.VMEM)
-SMEM = pl.BlockSpec(memory_space=pltpu.SMEM)
-
-
-def stack_body(*refs):
-    row = 0
-    for ref in refs[:-1]:
-        refs[-1][row : row + ref.shape[0], :] = ref[...]
-        row += ref.shape[0]
-
-
-def stacked(*blocks):
-    rows = sum(block.shape[0] for block in blocks)
-    return pl.pallas_call(
-        stack_body,
-        out_shape=jax.ShapeDtypeStruct((rows,) + blocks[0].shape[1:], blocks[0].dtype),
-        in_specs=[VMEM] * len(blocks),
-        out_specs=VMEM,
-        cost_estimate=pl.CostEstimate(
-            flops=0, bytes_accessed=4 * rows * blocks[0].shape[1], transcendentals=0
-        ),
-        name="stack_rows",
-    )(*blocks)
-
-
 def beside(block):
     return lax.ppermute(block, "exp", [(e, e ^ 1) for e in range(lax.axis_size("exp"))])
 
@@ -59,9 +33,40 @@
     return lax.ppermute(block, "ctx", pairs)
 
 
-def y_move(block, step):
-    n = lax.axis_size("exp")
-    return lax.ppermute(block, "exp", [(e, (e + step * X_LO) % n) for e in range(n)])
+def key_groups():
+    exps = lax.axis_size("exp")
+    pairs = lax.axis_size("ctx") * exps
+    return [[i for i in range(pairs) if i % X_LO == x] for x in range(X_LO)]
+
+
+def key_gather(block):
+    copies = jnp.broadcast_to(block[None], (len(key_groups()[0]),) + block.shape)
+    got = lax.all_to_all(
+        copies, ("ctx", "exp"), 0, 0, tiled=True, axis_index_groups=key_groups()
+    )
+    return got.reshape(-1, block.shape[1])
+
+
+def key_sum(both):
+    parts = both.reshape(len(key_groups()[0]), -1, both.shape[1])
+    got = lax.all_to_all(parts, ("ctx", "exp"), 0, 0, tiled=True, axis_index_groups=key_groups())
+    return jnp.sum(got.astype(F32), axis=0)
+
+
+def partner(block, mask):
+    return lax.ppermute(block, "exp", [(e, e ^ mask) for e in range(lax.axis_size("exp"))])
+
+
+def exchange(blocks, waits=None):
+    shape = blocks.shape
+    bits = shape[0].bit_length() - 1
+    for bit in range(bits):
+        if waits is not None and bit == bits - 1:
+            blocks = after(blocks, waits)
+        blocks = blocks.reshape((2**bit, 2, -1) + shape[1:])
+        got = partner(blocks[:, 1], 2 ** (bits - 1 - bit))
+        blocks = jnp.stack([blocks[:, 0], got], axis=1)
+    return blocks.reshape(shape)
 
 
 def opposite(block):
@@ -117,45 +122,18 @@
     return lax.dynamic_slice_in_dim(twice, places, blocks.shape[0], 0)
 
 
-def swap(block, mask):
-    return lax.ppermute(block, "ctx", [(c, c ^ mask) for c in range(lax.axis_size("ctx"))])
-
-
-def fours(masks):
-    return ((1, masks[0]), (2, masks[1]), (3, masks[0] ^ masks[1]))
-
-
-def ctx_gather(block, masks):
-    return stacked(block, *[swap(block, mask) for _, mask in fours(masks)])
-
-
-def ctx_sum(both, masks):
-    quarter = both.shape[0] // 4
-    wire = BF if quarter >= both.shape[1] // 2 else F32
-    total = both[:quarter]
-    for place, mask in fours(masks):
-        sent = both[place * quarter : (place + 1) * quarter].astype(wire)
-        total = total + swap(sent, mask).astype(F32)
-    return total
-
-
-def mask_of(index):
-    return sum((index >> bit) % 2 * mask for bit, mask in enumerate(MASKS))
-
-
-def scores_of(step, own, ctx_size, tokens, here_ref, k, q):
+def scores_of(step, own, rows, tokens, here_ref, k, q):
     lanes = q.shape[0]
     found = lax.dot_general(k, q, (((1,), (1,)), ((), ())), preferred_element_type=F32)
     ahead = lax.broadcasted_iota(jnp.int32, (own, lanes), 1) % tokens - lax.broadcasted_iota(
         jnp.int32, (own, lanes), 0
     )
-    me, side, row, rows = here_ref[0], here_ref[1], here_ref[2], here_ref[3]
+    me, side = here_ref[0], here_ref[1]
     parts = k.shape[0] // own
     masked = []
     for part in range(parts):
         place = step * parts + part
-        at = (row + place // ctx_size) % rows * X_LO + side
-        start = (me ^ mask_of(place % ctx_size)) * tokens + at * own
+        start = place // rows * tokens + (place % rows * X_LO + side) * own
         masked.append(
             jnp.where(
                 ahead >= start - me * tokens,
@@ -166,17 +144,17 @@
     return jnp.concatenate(masked, axis=0)
 
 
-def stats_body(own, ctx_size, tokens, here_ref, q_ref, g_ref, kv_ref, stats_ref):
+def stats_body(own, rows, tokens, here_ref, q_ref, g_ref, kv_ref, stats_ref):
     size = kv_ref.shape[1] // 2
     lanes = q_ref.shape[0]
     chunk = 8 * own
 
     def one(step, held):
         top, norm, delta = held
-        rows = pl.ds(pl.multiple_of(step * chunk, chunk), chunk)
-        scores = scores_of(step, own, ctx_size, tokens, here_ref, kv_ref[rows, :size], q_ref[...])
+        at = pl.ds(pl.multiple_of(step * chunk, chunk), chunk)
+        scores = scores_of(step, own, rows, tokens, here_ref, kv_ref[at, :size], q_ref[...])
         dprob = lax.dot_general(
-            kv_ref[rows, size:], g_ref[...], (((1,), (1,)), ((), ())), preferred_element_type=F32
+            kv_ref[at, size:], g_ref[...], (((1,), (1,)), ((), ())), preferred_element_type=F32
         )
         scores, dprob = scores.reshape(-1, 8, lanes), dprob.reshape(-1, 8, lanes)
         higher = jnp.maximum(top, jnp.max(scores, axis=0))
@@ -197,7 +175,7 @@
 
 
 def grads_body(
-    own, ctx_size, tokens, here_ref, q_ref, g_ref, kv_ref, stats_ref, far_ref, both_ref, dq_ref
+    own, rows, tokens, here_ref, q_ref, g_ref, kv_ref, stats_ref, far_ref, both_ref, dq_ref
 ):
     size = kv_ref.shape[1] // 2
     lanes = q_ref.shape[0]
@@ -210,18 +188,18 @@
     delta = (near[2:3] * shrink_near + far[2:3] * shrink_far) * inverse
 
     def one(step, total):
-        rows = pl.ds(pl.multiple_of(step * chunk, chunk), chunk)
-        k = kv_ref[rows, :size]
-        scores = scores_of(step, own, ctx_size, tokens, here_ref, k, q_ref[...])
+        at = pl.ds(pl.multiple_of(step * chunk, chunk), chunk)
+        k = kv_ref[at, :size]
+        scores = scores_of(step, own, rows, tokens, here_ref, k, q_ref[...])
         prob = jnp.exp(scores - top) * inverse
-        both_ref[rows, size:] = jnp.dot(
+        both_ref[at, size:] = jnp.dot(
             prob.astype(BF), g_ref[...], preferred_element_type=F32
         ).astype(BF)
         dprob = lax.dot_general(
-            kv_ref[rows, size:], g_ref[...], (((1,), (1,)), ((), ())), preferred_element_type=F32
+            kv_ref[at, size:], g_ref[...], (((1,), (1,)), ((), ())), preferred_element_type=F32
         )
         dscore = (prob * (dprob - delta)).astype(BF)
-        both_ref[rows, :size] = jnp.dot(dscore, q_ref[...], preferred_element_type=F32).astype(BF)
+        both_ref[at, :size] = jnp.dot(dscore, q_ref[...], preferred_element_type=F32).astype(BF)
         return total + lax.dot_general(
             k, dscore, (((0,), (0,)), ((), ())), preferred_element_type=F32
         )
@@ -230,17 +208,18 @@
     dq_ref[...] = (total * size ** (-0.5)).T
 
 
+VMEM = pl.BlockSpec(memory_space=pltpu.VMEM)
+SMEM = pl.BlockSpec(memory_space=pltpu.SMEM)
+
+
 def here():
-    exp, n = lax.axis_index("exp"), lax.axis_size("exp")
-    return jnp.stack(
-        [lax.axis_index("ctx"), exp % X_LO, exp // X_LO, jnp.int32(n // X_LO)]
-    ).astype(jnp.int32)
+    return jnp.stack([lax.axis_index("ctx"), lax.axis_index("exp") % X_LO]).astype(jnp.int32)
 
 
 def attention_stats(own, tokens, queries, grads, flat):
     keys, lanes = flat.shape[0], queries.shape[0]
     return pl.pallas_call(
-        functools.partial(stats_body, own, lax.axis_size("ctx"), tokens),
+        functools.partial(stats_body, own, lax.axis_size("exp") // X_LO, tokens),
         out_shape=jax.ShapeDtypeStruct((8, lanes), F32),
         in_specs=[SMEM, VMEM, VMEM, VMEM],
         out_specs=VMEM,
@@ -258,7 +237,7 @@
     keys, lanes = flat.shape[0], queries.shape[0]
     size = flat.shape[1] // 2
     return pl.pallas_call(
-        functools.partial(grads_body, own, lax.axis_size("ctx"), tokens),
+        functools.partial(grads_body, own, lax.axis_size("exp") // X_LO, tokens),
         out_shape=(
             jax.ShapeDtypeStruct((keys, 2 * size), BF),
             jax.ShapeDtypeStruct((lanes, size), F32),
@@ -286,10 +265,11 @@
     return grad_key, grad_value
 
 
-def select(moe_input, moe_grad, expert_ids, router_weight, near):
+def select(moe_input, moe_grad, expert_ids, router_weight, flat):
     width = moe_input.shape[1]
     exp_size = lax.axis_size("exp")
-    matches = expert_ids[:, :, None] == jnp.arange(exp_size)[None, None, :]
+    labels = lax.axis_index("exp") ^ jnp.arange(exp_size)
+    matches = expert_ids[:, :, None] == labels[None, None, :]
     member = jnp.sum(matches.astype(jnp.int32), axis=1)
     weight_row = jnp.sum(jnp.where(matches, router_weight[:, :, None], 0.0), axis=1)
     slot_rank = jnp.cumsum(member, axis=0) - member
@@ -302,18 +282,17 @@
     picked = jnp.einsum("bs,bd->sd", placed_low, rows, preferred_element_type=F32)
     scaled = picked[:, width:] * slot_weight.reshape(-1, 1)
     sent = jnp.concatenate([picked[:, :width].astype(BF), scaled.astype(BF)], axis=1)
-    sent = after(sent, near)
-    got = lax.all_to_all(sent.reshape(exp_size, CAP, 2 * width), "exp", 0, 0, tiled=True)
+    got = exchange(sent.reshape(exp_size, CAP, 2 * width), flat)
     return placed_low, got
 
 
 def project(got, gate_weight, up_weight, down_weight):
-    ctx_size = lax.axis_size("ctx")
+    ring = lax.axis_size("ctx") // X_HI
+    at = lax.axis_index("ctx") % ring
     half = lax.axis_index("head")
     units = gate_weight.shape[2] // lax.axis_size("head")
     width = got.shape[2] // 2
-    got = jnp.swapaxes(got.reshape(ctx_size // X_HI, X_HI, -1, 2 * width), 0, 1)
-    got = got.reshape(-1, 2 * width)
+    got = turn(got.reshape(ring, -1, 2 * width), at).reshape(-1, 2 * width)
     input_rows, grad_rows = got[:, :width], got[:, width:]
     gate_mat = lax.dynamic_slice_in_dim(gate_weight[0], half * units, units, 1)
     up_mat = lax.dynamic_slice_in_dim(up_weight[0], half * units, units, 1)
@@ -321,8 +300,8 @@
     gate_part = jnp.dot(input_rows, gate_mat, preferred_element_type=F32).astype(BF)
     up_part = jnp.dot(input_rows, up_mat, preferred_element_type=F32).astype(BF)
     back_part = jnp.einsum("rd,fd->rf", grad_rows, down_mat, preferred_element_type=F32).astype(BF)
-    parts = jnp.concatenate([gate_part, up_part, back_part], axis=1)
-    return gate_mat, up_mat, parts.reshape(ctx_size, -1, 3 * units)
+    parts = jnp.concatenate([gate_part, up_part, back_part], axis=1).reshape(ring, -1, 3 * units)
+    return input_rows, grad_rows, gate_mat, up_mat, [parts[j] for j in range(ring)]
 
 
 def act_block(total):
@@ -422,7 +401,7 @@
     columns = mine.shape[1]
     mine = (mine + lax.ppermute(other, "head", [(0, 1), (1, 0)]).astype(F32)).astype(BF)
     mine = turn(mine.reshape(ring, -1, columns), (ring - at) % ring).reshape(exp_size, CAP, columns)
-    back_rows = lax.all_to_all(mine, "exp", 0, 0, tiled=True)
+    back_rows = exchange(mine)
     grad_input = jnp.dot(
         placed_low, back_rows.reshape(-1, columns), preferred_element_type=F32
     ).astype(BF)
@@ -446,49 +425,37 @@
     rows = tokens * queries.shape[1]
     size = queries.shape[2]
     pair = jnp.concatenate([key_rows[:, 0, :], value_vector_rows[:, 0, :]], axis=1)
-    near = ctx_gather(pair, MASKS[:2])
-    placed_low, got = select(moe_input, moe_grad, expert_ids, router_weight, near)
-    near = ctx_gather(near, MASKS[2:])
+    flat = key_gather(pair)
+    placed_low, got = select(moe_input, moe_grad, expert_ids, router_weight, flat)
     mine = jnp.concatenate([by_head(queries), by_head(grad_attn)], axis=0)
     theirs = beside(mine)
     queries = jnp.concatenate([mine[:rows], theirs[:rows]], axis=0)
     grads = jnp.concatenate([mine[rows:], theirs[rows:]], axis=0)
-    above, below = ring_step(y_move, near, near)
-    gate_mat, up_mat, parts = project(
-        after(got, above, below, theirs), gate_weight, up_weight, down_weight
-    )
-    total = lax.all_to_all(parts, "ctx", 0, 0, tiled=True)
-    above, below = both_after(above, below, parts)
-    cut = near.shape[0] // 2
-    far = stacked(y_move(above[:cut], 1), y_move(below[cut:], -1))
-    flat = stacked(near, below, far, above)
-    stats = attention_stats(own, tokens, queries, grads, flat)
+    input_rows, grad_rows, gate_mat, up_mat, parts = project(
+        got, gate_weight, up_weight, down_weight
+    )
+    onward, back = both_after(*sum_start(parts), theirs)
+    stats = attention_stats(own, tokens, queries, grads, after(flat, onward, back))
+    onward, back = sum_step(z_move, parts, 0, onward, back)
+    onward, back = both_after(onward, back, stats)
+    far_stats = beside(stats)
+    onward, back = sum_step(z_move, parts, 1, onward, back)
+    onward, back = both_after(onward, back, far_stats)
     both, grad_query = attention_grads(
-        own, tokens, queries, grads, flat, stats, beside(stats)
-    )
-    terms = [both[j * near.shape[0] : (j + 1) * near.shape[0]] for j in range(4)]
-    up, down = sum_step(y_move, terms, 0, *sum_start(terms))
-    sums = sum_step(y_move, terms, 1, up, down)
-    block = act_block(jnp.sum(after(total, sums).astype(F32), axis=0))
-    partner = opposite(block)
-    first = lax.axis_index("ctx") // (lax.axis_size("ctx") // X_HI) == 0
-    block = jnp.concatenate(
-        [jnp.where(first, block, partner), jnp.where(first, partner, block)], axis=0
-    )
-    sums = ctx_sum(sums, MASKS[2:])
-    block = after(block, sums)
+        own, tokens, queries, grads, after(flat, onward, back), stats, far_stats
+    )
+    onward, back = sum_step(z_move, parts, 2, onward, back)
+    onward, back = both_after(onward, back, both)
+    total = sum_step(z_move, parts, 3, onward, back)
+    sums = key_sum(both)
+    other = opposite(total.astype(BF))
+    block = act_block(total + other.astype(F32))
     blocks = [block] + [None] * 8
     blocks[8], blocks[1] = ring_step(z_move, block, block)
     blocks[7], blocks[2] = ring_step(z_move, blocks[8], blocks[1])
-    sums = ctx_sum(sums, MASKS[:2])
     blocks[6], blocks[3] = ring_step(z_move, blocks[7], blocks[2])
     onward, back = both_after(blocks[6], blocks[3], sums)
     blocks[4], blocks[5] = ring_last(z_move, onward, back)
-    ring = lax.axis_size("ctx") // X_HI
-    width = moe_input.shape[1]
-    got = turn(got.reshape(ring, -1, 2 * width), lax.axis_index("ctx") % ring)
-    got = got.reshape(-1, 2 * width)
-    input_rows, grad_rows = got[:, :width], got[:, width:]
     of_experts = finish(blocks, input_rows, grad_rows, gate_mat, up_mat, placed_low)
     grad_query = grad_query[:rows] + beside(grad_query[rows:].astype(BF)).astype(F32)
     grad_query = jnp.swapaxes(grad_query.astype(BF).reshape(-1, tokens, size), 0, 1)

time: 172 us -> 163 us (0.948)
  waiting for transfers between devices: 37.4 us -> 61.6 us
  starting transfers between devices: 77.8 us -> 64.2 us
  Pallas kernels: 23.3 us -> 16.5 us
  other arithmetic: 15 us -> 9.36 us
  local copies, waits for them, and re-layouts: 10.9 us -> 5.72 us
    ppermute x20 -> x6, starting transfers between devices: 38 us -> 11.4 us  [partner(): lax.ppermute(block, 'exp', [(e, e ^ mask) for e in range(lax.axis_size('e...]
    ppermute x8 -> x16, starting transfers between devices: 11.2 us -> 27.9 us  [z_move(): return lax.ppermute(block, 'ctx', pairs)]
    ppermute x8 -> x16, waiting for transfers between devices: 10.1 us -> 24.6 us  [z_move(): return lax.ppermute(block, 'ctx', pairs)]
    ppermute x1, waiting for transfers between devices: 0.66 us -> 9.17 us  [opposite(): lax.ppermute(block, 'ctx', [(c, (c + n // X_HI) % n) for c in range(n)])]
    pallas_call x6 -> x2, Pallas kernels: 21.3 us -> 13.3 us  [the longest x1 8.56 us: attention_grads(): pl.pallas_call(functools.partial(grads_body, own, lax.axis_size('exp') //...]
    unnamed x48 -> x35, local copies, waits for them, and re-layouts: 6.27 us -> 0.11 us
    all_to_all x3 -> x2, waiting for transfers between devices: 1.45 us -> 5.89 us  [the longest x1 5.89 us: key_gather(): lax.all_to_all(copies, ('ctx', 'exp'), 0, 0, tiled=True, axis_index_group...]
    ppermute x1, starting transfers between devices: 3 us -> 0.09 us  [opposite(): lax.ppermute(block, 'ctx', [(c, (c + n // X_HI) % n) for c in range(n)])]
  transfers between devices with their start and end apart: 36 -> 29, of which waited for: 17 -> 18; matrix products, arithmetic and copies ran while one was open for 11% -> 7% of each run, Pallas kernels for 13% -> 9%
where the time goes in v8:
time: 163 us; the launch traced here: 161 us
  starting transfers between devices  64.2 us (39%)
  waiting for transfers between devices  61.6 us (38%)
  Pallas kernels  16.5 us (10%)
  other arithmetic  9.36 us (6%)
  local copies, waits for them, and re-layouts  5.72 us (4%)
  matrix products  2.4 us (1%)
    ppermute x16, starting transfers between devices, z_move(): return lax.ppermute(block, 'ctx', pairs)  27.9 us
    ppermute x16, waiting for transfers between devices, z_move(): return lax.ppermute(block, 'ctx', pairs)  24.6 us
    ppermute x6, waiting for transfers between devices, partner(): lax.ppermute(block, 'exp', [(e, e ^ mask) for e in range(lax.axis_size('e...  20.4 us
    all_to_all x1, starting transfers between devices, key_gather(): lax.all_to_all(copies, ('ctx', 'exp'), 0, 0, tiled=True, axis_index_group...  13.8 us
    ppermute x6, starting transfers between devices, partner(): lax.ppermute(block, 'exp', [(e, e ^ mask) for e in range(lax.axis_size('e...  11.4 us
    ppermute x1, waiting for transfers between devices, opposite(): lax.ppermute(block, 'ctx', [(c, (c + n // X_HI) % n) for c in range(n)])  9.17 us
    pallas_call x1, Pallas kernels, attention_grads(): pl.pallas_call(functools.partial(grads_body, own, lax.axis_size('exp') //...  8.56 us
    all_to_all x1, starting transfers between devices, key_sum(): lax.all_to_all(parts, ('ctx', 'exp'), 0, 0, tiled=True, axis_index_groups...  6.19 us
  transfers between devices with their start and end apart: 29, of which 18 were waited for; matrix products, arithmetic and copies ran while one was open for 7% of the time, Pallas kernels for 9%

profile of v8, /device:TPU:2, one launch (start us, length us, event | category | flops | bytes accessed | tf_op | source)
XLA Modules:
  0.0 161.0 jit_solution(13381993194633125862)
XLA Ops:
  0.6 0.8 pad_maximum_fusion.16
  1.4 1.1 broadcast_in_dim.43
  2.6 13.8 %all-to-all-start = ((bf16[64,32,256]{2,1,0:T(8,128)(2,1)}), bf16[64,32,256]{2,1,0:T(8,128)(2,1)S(1)}, u32[]{:S(2)}, u32[]{:S(2)}) async-start(bf16[64,32,256]{2,1,0:T(8,128)(2,1)} %broadcast_in_dim.43), calls=%async_computation | async-start | bytes 2097152 | tf_op jit(solution)/shard_map/all_to_all | solution.py:44
  16.5 1.1 reduce-window.6
  18.1 0.3 select_reduce_fusion
  18.8 0.4 fusion.2
  19.4 3.2 %collective-permute-start.1 = (bf16[1,4,48,512]{3,2,1,0:T(8,128)(2,1)S(1)}, bf16[1,4,48,512]{3,2,1,0:T(8,128)(2,1)S(1)}, u32[]{:S(2)}, u32[]{:S(2)}) collective-permute-start(bf16[1,4,48,512]{3,2,1,0:T(8,128)(2,1)S(1)} %get-tuple-element.73), channel_id=1, source_target_pairs={{0,4},{1,5},{2,6},{3,7},{4,0},{5,1},{6,2},{7,3},{8,12},{9,13},{10,... | collective-permute-start | bytes 589832 | tf_op jit(solution)/shard_map/ppermute | solution.py:57
  22.6 0.7 pad_maximum_fusion.3
  23.4 1.4 collective-permute-start
  24.8 6.5 %collective-permute-done.1 = bf16[1,4,48,512]{3,2,1,0:T(8,128)(2,1)S(1)} collective-permute-done((bf16[1,4,48,512]{3,2,1,0:T(8,128)(2,1)S(1)}, bf16[1,4,48,512]{3,2,1,0:T(8,128)(2,1)S(1)}, u32[]{:S(2)}, u32[]{:S(2)}) %collective-permute-start.1) | collective-permute-done | bytes 196640 | tf_op jit(solution)/shard_map/ppermute | solution.py:57
  31.4 1.0 collective-permute-start.2
  32.4 1.2 dynamic-slice_bitcast_fusion
  33.6 6.5 %collective-permute-done.2 = bf16[2,2,48,512]{3,2,1,0:T(8,128)(2,1)S(1)} collective-permute-done((bf16[2,2,48,512]{3,2,1,0:T(8,128)(2,1)S(1)}, bf16[2,2,48,512]{3,2,1,0:T(8,128)(2,1)S(1)}, u32[]{:S(2)}, u32[]{:S(2)}) %collective-permute-start.2) | collective-permute-done | bytes 196640 | tf_op jit(solution)/shard_map/ppermute | solution.py:57
  40.1 5.9 %all-to-all-done = bf16[64,32,256]{2,1,0:T(8,128)(2,1)S(1)} async-done(((bf16[64,32,256]{2,1,0:T(8,128)(2,1)}), bf16[64,32,256]{2,1,0:T(8,128)(2,1)S(1)}, u32[]{:S(2)}, u32[]{:S(2)}) %all-to-all-start) | async-done | bytes 1048608 | tf_op jit(solution)/shard_map/all_to_all | solution.py:44
  46.1 1.5 collective-permute-start.3
  47.6 4.2 %collective-permute-done.3 = bf16[4,1,48,512]{3,2,0,1:T(8,128)(2,1)S(1)} collective-permute-done((bf16[4,1,48,512]{3,2,0,1:T(8,128)(2,1)S(1)}, bf16[4,1,48,512]{3,2,0,1:T(8,128)(2,1)S(1)}, u32[]{:S(2)}, u32[]{:S(2)}) %collective-permute-start.3) | collective-permute-done | bytes 196640 | tf_op jit(solution)/shard_map/ppermute | solution.py:57
  52.1 0.3 convolution_convert_fusion.2
  52.4 0.4 convolution_convert_fusion
  52.8 0.3 convolution_convert_fusion.1
  53.2 2.2 %collective-permute-start.4 = (bf16[48,1152]{1,0:T(8,128)(2,1)S(1)}, bf16[48,1152]{1,0:T(8,128)(2,1)S(1)}, u32[]{:S(2)}, u32[]{:S(2)}) collective-permute-start(bf16[48,1152]{1,0:T(8,128)(2,1)S(1)} %get-tuple-element.30), channel_id=1, source_target_pairs={{0,16},{16,32},{32,48},{48,64},{64,80},{80,96},{96,112},{112,0},{1... | collective-permute-start | bytes 331784 | tf_op jit(solution)/shard_map/ppermute | solution.py:33
  55.4 1.1 collective-permute-start.5
  56.5 4.8 %attention_stats.1.stats_ref = f32[8,1024]{1,0:T(8,128)S(1)} custom-call(s32[2]{0:T(128)S(1)} %pad_add_fusion.here_ref, bf16[1024,128]{1,0:T(8,128)(2,1)S(1)} %get-tuple-element.82.q_ref, bf16[1024,128]{1,0:T(8,128)(2,1)S(1)} %get-tuple-element.83.g_ref, bf16[2048,256]{1,0:T(8,128)(2,1)S(1)} %bitcast.81), custom_call_target="tpu_custom_call" | custom-call | flops 1073741824 | bytes 1048576 | tf_op jit(solution)/shard_map/attention_stats/pallas_call | solution.py:221
  61.4 1.0 collective-permute-start.6
  62.5 2.3 %collective-permute-start.7 = (bf16[48,2304]{1,0:T(8,128)(2,1)S(1)}, bf16[48,2304]{1,0:T(8,128)(2,1)S(1)}, u32[]{:S(2)}, u32[]{:S(2)}) collective-permute-start(bf16[48,2304]{1,0:T(8,128)(2,1)S(1)} %get-tuple-element.34), channel_id=1, source_target_pairs={{0,112},{16,0},{32,16},{48,32},{64,48},{80,64},{96,80},{112,96},{1... | collective-permute-start | bytes 663560 | tf_op jit(solution)/shard_map/ppermute | solution.py:33
  64.8 1.4 collective-permute-start.8
  66.2 3.1 %collective-permute-done.6 = bf16[48,2304]{1,0:T(8,128)(2,1)S(1)} collective-permute-done((bf16[48,2304]{1,0:T(8,128)(2,1)S(1)}, bf16[48,2304]{1,0:T(8,128)(2,1)S(1)}, u32[]{:S(2)}, u32[]{:S(2)}) %collective-permute-start.6) | collective-permute-done | bytes 221216 | tf_op jit(solution)/shard_map/ppermute | solution.py:33
  69.2 0.4 collective-permute-done.7
  69.8 0.6 collective-permute-start.10
  70.4 2.8 %collective-permute-start.11 = (bf16[48,2304]{1,0:T(8,128)(2,1)S(1)}, bf16[48,2304]{1,0:T(8,128)(2,1)S(1)}, u32[]{:S(2)}, u32[]{:S(2)}) collective-permute-start(bf16[48,2304]{1,0:T(8,128)(2,1)S(1)} %get-tuple-element.36), channel_id=1, source_target_pairs={{0,112},{16,0},{32,16},{48,32},{64,48},{80,64},{96,80},{112,96},{1... | collective-permute-start | bytes 663560 | tf_op jit(solution)/shard_map/ppermute | solution.py:33
  73.1 8.6 %attention_grads.1 = (bf16[2048,256]{1,0:T(8,128)(2,1)S(1)}, f32[1024,128]{1,0:T(8,128)S(1)}) custom-call(s32[2]{0:T(128)S(1)} %pad_add_fusion.here_ref, bf16[1024,128]{1,0:T(8,128)(2,1)S(1)} %get-tuple-element.82.q_ref, bf16[1024,128]{1,0:T(8,128)(2,1)S(1)} %get-tuple-element.83.g_ref, bf16[2048,256]{1,0:T(8,128)(2,1)S(1)} %bitcast.82, ...), custom_call_target="tpu_custom_call" | custom-call | flops 2684354560 | bytes 2097152 | tf_op jit(solution)/shard_map/attention_grads/pallas_call | solution.py:239
  81.7 1.0 add_convert_fusion
  82.7 3.2 %collective-permute-start.13 = (bf16[48,2304]{1,0:T(8,128)(2,1)S(1)}, bf16[48,2304]{1,0:T(8,128)(2,1)S(1)}, u32[]{:S(2)}, u32[]{:S(2)}) collective-permute-start(bf16[48,2304]{1,0:T(8,128)(2,1)S(1)} %get-tuple-element.41), channel_id=1, source_target_pairs={{0,112},{16,0},{32,16},{48,32},{64,48},{80,64},{96,80},{112,96},{1... | collective-permute-start | bytes 663560 | tf_op jit(solution)/shard_map/ppermute | solution.py:33
  86.0 6.2 %all-to-all-start.1 = ((bf16[64,32,256]{2,1,0:T(8,128)(2,1)}), bf16[64,32,256]{2,1,0:T(8,128)(2,1)}, u32[]{:S(2)}, u32[]{:S(2)}) async-start(bf16[64,32,256]{2,1,0:T(8,128)(2,1)} %bitcast.83), calls=%async_computation.1 | async-start | bytes 2097152 | tf_op jit(solution)/shard_map/all_to_all | solution.py:52
  92.2 5.0 %collective-permute-done.13 = bf16[48,2304]{1,0:T(8,128)(2,1)S(1)} collective-permute-done((bf16[48,2304]{1,0:T(8,128)(2,1)S(1)}, bf16[48,2304]{1,0:T(8,128)(2,1)S(1)}, u32[]{:S(2)}, u32[]{:S(2)}) %collective-permute-start.13) | collective-permute-done | bytes 221216 | tf_op jit(solution)/shard_map/ppermute | solution.py:33
  97.2 1.0 fusion.12
  98.3 9.2 %collective-permute-done.14 = bf16[48,2304]{1,0:T(8,128)(2,1)S(1)} collective-permute-done((bf16[48,2304]{1,0:T(8,128)(2,1)S(1)}, bf16[48,2304]{1,0:T(8,128)(2,1)S(1)}, u32[]{:S(2)}, u32[]{:S(2)}) %collective-permute-start.14) | collective-permute-done | bytes 221216 | tf_op jit(solution)/shard_map/ppermute | solution.py:74
  107.7 4.0 %collective-permute-start.15 = (bf16[48,2304]{1,0:T(8,128)(2,1)S(1)}, bf16[48,2304]{1,0:T(8,128)(2,1)S(1)}, u32[]{:S(2)}, u32[]{:S(2)}) collective-permute-start(bf16[48,2304]{1,0:T(8,128)(2,1)S(1)} %pad_maximum_fusion.8.refs_0_), channel_id=1, source_target_pairs={{0,112},{16,0},{32,16},{48,32},{64,48},{80,64},{96,80},{112,96},{1... | collective-permute-start | bytes 663560 | tf_op jit(solution)/shard_map/ppermute | solution.py:33
  111.7 4.9 %collective-permute-done.15.refs_1_ = bf16[48,2304]{1,0:T(8,128)(2,1)S(1)} collective-permute-done((bf16[48,2304]{1,0:T(8,128)(2,1)S(1)}, bf16[48,2304]{1,0:T(8,128)(2,1)S(1)}, u32[]{:S(2)}, u32[]{:S(2)}) %collective-permute-start.15) | collective-permute-done | bytes 221216 | tf_op jit(solution)/shard_map/ppermute | solution.py:33
  116.6 3.7 %collective-permute-start.16 = (bf16[48,2304]{1,0:T(8,128)(2,1)S(1)}, bf16[48,2304]{1,0:T(8,128)(2,1)}, u32[]{:S(2)}, u32[]{:S(2)}) collective-permute-start(bf16[48,2304]{1,0:T(8,128)(2,1)S(1)} %collective-permute-done.15.refs_1_), channel_id=1, source_target_pairs={{0,112},{16,0},{32,16},{48,32},{64,48},{80,64},{96,80},{112,96},{1... | collective-permute-start | bytes 663560 | tf_op jit(solution)/shard_map/ppermute | solution.py:33
  120.3 3.4 %collective-permute-done.16.refs_2_ = bf16[48,2304]{1,0:T(8,128)(2,1)} collective-permute-done((bf16[48,2304]{1,0:T(8,128)(2,1)S(1)}, bf16[48,2304]{1,0:T(8,128)(2,1)}, u32[]{:S(2)}, u32[]{:S(2)}) %collective-permute-start.16) | collective-permute-done | bytes 221216 | tf_op jit(solution)/shard_map/ppermute | solution.py:33
  123.8 3.8 %collective-permute-start.17 = (bf16[48,2304]{1,0:T(8,128)(2,1)}, bf16[48,2304]{1,0:T(8,128)(2,1)S(1)}, u32[]{:S(2)}, u32[]{:S(2)}) collective-permute-start(bf16[48,2304]{1,0:T(8,128)(2,1)} %collective-permute-done.16.refs_2_), channel_id=1, source_target_pairs={{0,112},{16,0},{32,16},{48,32},{64,48},{80,64},{96,80},{112,96},{1... | collective-permute-start | bytes 663560 | tf_op jit(solution)/shard_map/ppermute | solution.py:33
  127.6 1.4 convert_reduce_fusion
  129.0 2.4 %collective-permute-done.17.refs_3_ = bf16[48,2304]{1,0:T(8,128)(2,1)S(1)} collective-permute-done((bf16[48,2304]{1,0:T(8,128)(2,1)}, bf16[48,2304]{1,0:T(8,128)(2,1)S(1)}, u32[]{:S(2)}, u32[]{:S(2)}) %collective-permute-start.17) | collective-permute-done | bytes 221216 | tf_op jit(solution)/shard_map/ppermute | solution.py:33
  131.3 3.6 %collective-permute-done.20.refs_6_ = bf16[48,2304]{1,0:T(8,128)(2,1)S(1)} collective-permute-done((bf16[48,2304]{1,0:T(8,128)(2,1)}, bf16[48,2304]{1,0:T(8,128)(2,1)S(1)}, u32[]{:S(2)}, u32[]{:S(2)}) %collective-permute-start.20) | collective-permute-done | bytes 221216 | tf_op jit(solution)/shard_map/ppermute | solution.py:33
  134.9 0.7 slice.178
  135.6 0.7 slice.179
  136.2 3.2 %collective-permute-start.22 = (bf16[48,1152]{1,0:T(8,128)(2,1)}, bf16[48,1152]{1,0:T(8,128)(2,1)S(1)}, u32[]{:S(2)}, u32[]{:S(2)}) collective-permute-start(bf16[48,1152]{1,0:T(8,128)(2,1)} %slice.179), channel_id=1, source_target_pairs={{0,112},{16,0},{32,16},{48,32},{64,48},{80,64},{96,80},{112,96},{1... | collective-permute-start | bytes 331784 | tf_op jit(solution)/shard_map/ppermute | solution.py:33
  139.5 0.8 fusion
  140.3 1.5 collective-permute-done.21.refs_4_
  141.7 0.4 collective-permute-done.22.refs_5_
  142.1 1.6 %expert_contrib.1 = (f32[384,128]{1,0:T(8,128)S(1)}, bf16[384,128]{1,0:T(8,128)(2,1)S(1)}, bf16[384,2304]{1,0:T(8,128)(2,1)S(1)}) custom-call(s32[1]{0:T(128)} %bitcast.36.half_ref, bf16[256,768]{1,0:T(8,128)(2,1)S(1)} %get-tuple-element.85.gate_ref, bf16[256,768]{1,0:T(8,128)(2,1)S(1)} %get-tuple-element.84.up_ref, ...), custom_call_target="tpu_custom_call" | custom-call | flops 301989888 | bytes 3538944 | tf_op jit(solution)/shard_map/expert_contrib/pallas_call | solution.py:356
  143.9 1.7 %collective-permute-start.9 = (bf16[512,128]{1,0:T(8,128)(2,1)S(1)}, bf16[512,128]{1,0:T(8,128)(2,1)S(1)}, u32[]{:S(2)}, u32[]{:S(2)}) collective-permute-start(bf16[512,128]{1,0:T(8,128)(2,1)S(1)} %slice.262), channel_id=1, source_target_pairs={{0,1},{1,0},{2,3},{3,2},{4,5},{5,4},{6,7},{7,6},{8,9},{9,8},{10,11... | collective-permute-start | bytes 393224 | tf_op jit(solution)/shard_map/ppermute | solution.py:27
  145.8 2.8 %collective-permute-start.24 = (bf16[1,4,48,128]{3,2,1,0:T(8,128)(2,1)S(1)}, bf16[1,4,48,128]{3,2,1,0:T(8,128)(2,1)S(1)}, u32[]{:S(2)}, u32[]{:S(2)}) collective-permute-start(bf16[1,4,48,128]{3,2,1,0:T(8,128)(2,1)S(1)} %get-tuple-element.81), channel_id=1, source_target_pairs={{0,4},{1,5},{2,6},{3,7},{4,0},{5,1},{6,2},{7,3},{8,12},{9,13},{10,... | collective-permute-start | bytes 147464 | tf_op jit(solution)/shard_map/ppermute | solution.py:57
  148.6 1.5 collective-permute-done.9
  150.2 0.8 copy.51
  151.0 0.5 collective-permute-done.24
  151.5 2.0 %collective-permute-start.25 = (bf16[2,2,48,128]{3,2,1,0:T(8,128)(2,1)S(1)}, bf16[2,2,48,128]{3,2,1,0:T(8,128)(2,1)S(1)}, u32[]{:S(2)}, u32[]{:S(2)}) collective-permute-start(bf16[2,2,48,128]{3,2,1,0:T(8,128)(2,1)S(1)} %get-tuple-element.79), channel_id=1, source_target_pairs={{0,2},{1,3},{2,0},{3,1},{4,6},{5,7},{6,4},{7,5},{8,10},{9,11},{10,... | collective-permute-start | bytes 147464 | tf_op jit(solution)/shard_map/ppermute | solution.py:57
  153.5 0.6 fusion.27
  154.1 1.6 collective-permute-done.25
  155.7 1.0 collective-permute-start.26
  156.7 0.6 fusion.28
  157.3 1.5 expert_weight_grads.1
  158.9 1.0 collective-permute-done.26
  159.9 1.1 convolution_convert_fusion.3
  (97 shorter events, 2.6 us)
Async XLA Ops:
  0.6 51.8 %copy-start = (bf16[1,1536,256]{2,1,0:T(8,128)(2,1)S(1)}, bf16[1,1536,256]{2,1,0:T(8,128)(2,1)}, u32[]{:S(2)}) copy-start(bf16[1,1536,256]{2,1,0:T(8,128)(2,1)} %param.21) | copy-start | bytes 2359300
  2.6 13.8 %copy-start.15 = (s32[512,8]{0,1:T(8,128)S(1)}, s32[512,8]{0,1:T(8,128)}, u32[]{:S(2)}) copy-start(s32[512,8]{0,1:T(8,128)} %param.17) | copy-start | bytes 49156
  2.6 15.3 %copy-start.16 = (f32[512,8]{0,1:T(8,128)S(1)}, f32[512,8]{0,1:T(8,128)}, u32[]{:S(2)}) copy-start(f32[512,8]{0,1:T(8,128)} %param.18) | copy-start | bytes 49156
  2.6 16.2 %copy-start.8 = (bf16[512,256]{1,0:T(8,128)(2,1)S(1)}, bf16[512,256]{1,0:T(8,128)(2,1)}, u32[]{:S(2)}) copy-start(bf16[512,256]{1,0:T(8,128)(2,1)} %param.16) | copy-start | bytes 786436
  2.6 16.2 %copy-start.9 = (bf16[512,256]{1,0:T(8,128)(2,1)S(1)}, bf16[512,256]{1,0:T(8,128)(2,1)}, u32[]{:S(2)}) copy-start(bf16[512,256]{1,0:T(8,128)(2,1)} %param.15) | copy-start | bytes 786436
  2.6 43.4 %all-to-all-start = ((bf16[64,32,256]{2,1,0:T(8,128)(2,1)}), bf16[64,32,256]{2,1,0:T(8,128)(2,1)S(1)}, u32[]{:S(2)}, u32[]{:S(2)}) async-start(bf16[64,32,256]{2,1,0:T(8,128)(2,1)} %broadcast_in_dim.43), calls=%async_computation | async-start | bytes 2097152 | tf_op jit(solution)/shard_map/all_to_all | solution.py:44
  18.1 1.2 copy-start.10
  19.2 3.4 %copy-start.13 = (bf16[256,2,128]{2,1,0:T(2,128)(2,1)S(1)}, bf16[256,2,128]{2,1,0:T(2,128)(2,1)}, u32[]{:S(2)}) copy-start(bf16[256,2,128]{2,1,0:T(2,128)(2,1)} %param.11) | copy-start | bytes 393220
  19.2 3.4 %copy-start.14 = (bf16[256,2,128]{2,1,0:T(2,128)(2,1)S(1)}, bf16[256,2,128]{2,1,0:T(2,128)(2,1)}, u32[]{:S(2)}) copy-start(bf16[256,2,128]{2,1,0:T(2,128)(2,1)} %param.14) | copy-start | bytes 393220
  19.4 11.9 %collective-permute-start.1 = (bf16[1,4,48,512]{3,2,1,0:T(8,128)(2,1)S(1)}, bf16[1,4,48,512]{3,2,1,0:T(8,128)(2,1)S(1)}, u32[]{:S(2)}, u32[]{:S(2)}) collective-permute-start(bf16[1,4,48,512]{3,2,1,0:T(8,128)(2,1)S(1)} %get-tuple-element.73), channel_id=1, source_target_pairs={{0,4},{1,5},{2,6},{3,7},{4,0},{5,1},{6,2},{7,3},{8,12},{9,13},{10,... | collective-permute-start | bytes 589832 | tf_op jit(solution)/shard_map/ppermute | solution.py:57
  23.4 24.2 %collective-permute-start = (bf16[1024,128]{1,0:T(8,128)(2,1)}, bf16[1024,128]{1,0:T(8,128)(2,1)S(1)}, u32[]{:S(2)}, u32[]{:S(2)}) collective-permute-start(bf16[1024,128]{1,0:T(8,128)(2,1)} %pad_maximum_fusion.3), channel_id=1, source_target_pairs={{0,1},{1,0},{2,3},{3,2},{4,5},{5,4},{6,7},{7,6},{8,9},{9,8},{10,11... | collective-permute-start | bytes 786440 | tf_op jit(solution)/shard_map/ppermute | solution.py:27
  31.4 8.7 %collective-permute-start.2 = (bf16[2,2,48,512]{3,2,1,0:T(8,128)(2,1)S(1)}, bf16[2,2,48,512]{3,2,1,0:T(8,128)(2,1)S(1)}, u32[]{:S(2)}, u32[]{:S(2)}) collective-permute-start(bf16[2,2,48,512]{3,2,1,0:T(8,128)(2,1)S(1)} %get-tuple-element.71), channel_id=1, source_target_pairs={{0,2},{1,3},{2,0},{3,1},{4,6},{5,7},{6,4},{7,5},{8,10},{9,11},{10,... | collective-permute-start | bytes 589832 | tf_op jit(solution)/shard_map/ppermute | solution.py:57
  46.1 5.8 %collective-permute-start.3 = (bf16[4,1,48,512]{3,2,0,1:T(8,128)(2,1)S(1)}, bf16[4,1,48,512]{3,2,0,1:T(8,128)(2,1)S(1)}, u32[]{:S(2)}, u32[]{:S(2)}) collective-permute-start(bf16[4,1,48,512]{3,2,0,1:T(8,128)(2,1)S(1)} %get-tuple-element.69), channel_id=1, source_target_pairs={{0,1},{1,0},{2,3},{3,2},{4,5},{5,4},{6,7},{7,6},{8,9},{9,8},{10,11... | collective-permute-start | bytes 589832 | tf_op jit(solution)/shard_map/ppermute | solution.py:57
  52.1 0.7 copy-start.6
  52.4 29.3 %copy-start.2 = (bf16[384,768]{1,0:T(8,128)(2,1)}, bf16[384,768]{1,0:T(8,128)(2,1)S(1)}, u32[]{:S(2)}) copy-start(bf16[384,768]{1,0:T(8,128)(2,1)S(1)} %convolution_convert_fusion.2) | copy-start | bytes 1769476
  52.8 28.9 %copy-start.4 = (bf16[384,768]{1,0:T(8,128)(2,1)}, bf16[384,768]{1,0:T(8,128)(2,1)S(1)}, u32[]{:S(2)}) copy-start(bf16[384,768]{1,0:T(8,128)(2,1)S(1)} %convolution_convert_fusion) | copy-start | bytes 1769476
  53.1 28.6 %copy-start.5 = (bf16[384,768]{1,0:T(8,128)(2,1)}, bf16[384,768]{1,0:T(8,128)(2,1)S(1)}, u32[]{:S(2)}) copy-start(bf16[384,768]{1,0:T(8,128)(2,1)S(1)} %convolution_convert_fusion.1) | copy-start | bytes 1769476
  53.2 8.1 %collective-permute-start.4 = (bf16[48,1152]{1,0:T(8,128)(2,1)S(1)}, bf16[48,1152]{1,0:T(8,128)(2,1)S(1)}, u32[]{:S(2)}, u32[]{:S(2)}) collective-permute-start(bf16[48,1152]{1,0:T(8,128)(2,1)S(1)} %get-tuple-element.30), channel_id=1, source_target_pairs={{0,16},{16,32},{32,48},{48,64},{64,80},{80,96},{96,112},{112,0},{1... | collective-permute-start | bytes 331784 | tf_op jit(solution)/shard_map/ppermute | solution.py:33
  55.4 5.9 %collective-permute-start.5 = (bf16[48,1152]{1,0:T(8,128)(2,1)S(1)}, bf16[48,1152]{1,0:T(8,128)(2,1)S(1)}, u32[]{:S(2)}, u32[]{:S(2)}) collective-permute-start(bf16[48,1152]{1,0:T(8,128)(2,1)S(1)} %get-tuple-element.31), channel_id=1, source_target_pairs={{0,112},{16,0},{32,16},{48,32},{64,48},{80,64},{96,80},{112,96},{1... | collective-permute-start | bytes 331784 | tf_op jit(solution)/shard_map/ppermute | solution.py:33
  61.4 7.8 %collective-permute-start.6 = (bf16[48,2304]{1,0:T(8,128)(2,1)S(1)}, bf16[48,2304]{1,0:T(8,128)(2,1)S(1)}, u32[]{:S(2)}, u32[]{:S(2)}) collective-permute-start(bf16[48,2304]{1,0:T(8,128)(2,1)S(1)} %get-tuple-element.33), channel_id=1, source_target_pairs={{0,16},{16,32},{32,48},{48,64},{64,80},{80,96},{96,112},{112,0},{1... | collective-permute-start | bytes 663560 | tf_op jit(solution)/shard_map/ppermute | solution.py:33
  62.5 7.2 %collective-permute-start.7 = (bf16[48,2304]{1,0:T(8,128)(2,1)S(1)}, bf16[48,2304]{1,0:T(8,128)(2,1)S(1)}, u32[]{:S(2)}, u32[]{:S(2)}) collective-permute-start(bf16[48,2304]{1,0:T(8,128)(2,1)S(1)} %get-tuple-element.34), channel_id=1, source_target_pairs={{0,112},{16,0},{32,16},{48,32},{64,48},{80,64},{96,80},{112,96},{1... | collective-permute-start | bytes 663560 | tf_op jit(solution)/shard_map/ppermute | solution.py:33
  64.8 5.0 %collective-permute-start.8 = (f32[8,1024]{1,0:T(8,128)S(1)}, f32[8,1024]{1,0:T(8,128)S(1)}, u32[]{:S(2)}, u32[]{:S(2)}) collective-permute-start(f32[8,1024]{1,0:T(8,128)S(1)} %attention_stats.1.stats_ref), channel_id=1, source_target_pairs={{0,1},{1,0},{2,3},{3,2},{4,5},{5,4},{6,7},{7,6},{8,9},{9,8},{10,11... | collective-permute-start | bytes 98312 | tf_op jit(solution)/shard_map/ppermute | solution.py:27
  69.8 11.9 %collective-permute-start.10 = (bf16[48,2304]{1,0:T(8,128)(2,1)S(1)}, bf16[48,2304]{1,0:T(8,128)(2,1)S(1)}, u32[]{:S(2)}, u32[]{:S(2)}) collective-permute-start(bf16[48,2304]{1,0:T(8,128)(2,1)S(1)} %get-tuple-element.35), channel_id=1, source_target_pairs={{0,16},{16,32},{32,48},{48,64},{64,80},{80,96},{96,112},{112,0},{1... | collective-permute-start | bytes 663560 | tf_op jit(solution)/shard_map/ppermute | solution.py:33
  70.4 11.3 %collective-permute-start.11 = (bf16[48,2304]{1,0:T(8,128)(2,1)S(1)}, bf16[48,2304]{1,0:T(8,128)(2,1)S(1)}, u32[]{:S(2)}, u32[]{:S(2)}) collective-permute-start(bf16[48,2304]{1,0:T(8,128)(2,1)S(1)} %get-tuple-element.36), channel_id=1, source_target_pairs={{0,112},{16,0},{32,16},{48,32},{64,48},{80,64},{96,80},{112,96},{1... | collective-permute-start | bytes 663560 | tf_op jit(solution)/shard_map/ppermute | solution.py:33
  81.7 1.0 copy-start.1
  82.7 14.4 %copy-start.3 = (bf16[384,768]{1,0:T(8,128)(2,1)S(1)}, bf16[384,768]{1,0:T(8,128)(2,1)}, u32[]{:S(2)}) copy-start(bf16[384,768]{1,0:T(8,128)(2,1)} %copy-done.2) | copy-start | bytes 1769476
  82.7 9.4 %collective-permute-start.12 = (bf16[48,2304]{1,0:T(8,128)(2,1)}, bf16[48,2304]{1,0:T(8,128)(2,1)S(1)}, u32[]{:S(2)}, u32[]{:S(2)}) collective-permute-start(bf16[48,2304]{1,0:T(8,128)(2,1)} %get-tuple-element.40), channel_id=1, source_target_pairs={{0,16},{16,32},{32,48},{48,64},{64,80},{80,96},{96,112},{112,0},{1... | collective-permute-start | bytes 663560 | tf_op jit(solution)/shard_map/ppermute | solution.py:33
  82.7 14.4 %collective-permute-start.13 = (bf16[48,2304]{1,0:T(8,128)(2,1)S(1)}, bf16[48,2304]{1,0:T(8,128)(2,1)S(1)}, u32[]{:S(2)}, u32[]{:S(2)}) collective-permute-start(bf16[48,2304]{1,0:T(8,128)(2,1)S(1)} %get-tuple-element.41), channel_id=1, source_target_pairs={{0,112},{16,0},{32,16},{48,32},{64,48},{80,64},{96,80},{112,96},{1... | collective-permute-start | bytes 663560 | tf_op jit(solution)/shard_map/ppermute | solution.py:33
  86.0 41.6 %all-to-all-start.1 = ((bf16[64,32,256]{2,1,0:T(8,128)(2,1)}), bf16[64,32,256]{2,1,0:T(8,128)(2,1)}, u32[]{:S(2)}, u32[]{:S(2)}) async-start(bf16[64,32,256]{2,1,0:T(8,128)(2,1)} %bitcast.83), calls=%async_computation.1 | async-start | bytes 2097152 | tf_op jit(solution)/shard_map/all_to_all | solution.py:52
  98.2 9.3 %collective-permute-start.14 = (bf16[48,2304]{1,0:T(8,128)(2,1)S(1)}, bf16[48,2304]{1,0:T(8,128)(2,1)S(1)}, u32[]{:S(2)}, u32[]{:S(2)}) collective-permute-start(bf16[48,2304]{1,0:T(8,128)(2,1)S(1)} %get-tuple-element.51), channel_id=1, source_target_pairs={{0,128},{16,144},{32,160},{48,176},{64,192},{80,208},{96,224},{112... | collective-permute-start | bytes 663560 | tf_op jit(solution)/shard_map/ppermute | solution.py:74
  107.6 31.9 %copy-start.11 = (s32[512,8]{0,1:T(8,128)S(1)}, s32[512,8]{0,1:T(8,128)}, u32[]{:S(2)}) copy-start(s32[512,8]{0,1:T(8,128)} %copy-done.10) | copy-start | bytes 49156
  107.7 8.9 %collective-permute-start.15 = (bf16[48,2304]{1,0:T(8,128)(2,1)S(1)}, bf16[48,2304]{1,0:T(8,128)(2,1)S(1)}, u32[]{:S(2)}, u32[]{:S(2)}) collective-permute-start(bf16[48,2304]{1,0:T(8,128)(2,1)S(1)} %pad_maximum_fusion.8.refs_0_), channel_id=1, source_target_pairs={{0,112},{16,0},{32,16},{48,32},{64,48},{80,64},{96,80},{112,96},{1... | collective-permute-start | bytes 663560 | tf_op jit(solution)/shard_map/ppermute | solution.py:33
  111.7 8.6 %collective-permute-start.18 = (bf16[48,2304]{1,0:T(8,128)(2,1)S(1)}, bf16[48,2304]{1,0:T(8,128)(2,1)S(1)}, u32[]{:S(2)}, u32[]{:S(2)}) collective-permute-start(bf16[48,2304]{1,0:T(8,128)(2,1)S(1)} %pad_maximum_fusion.8.refs_0_), channel_id=1, source_target_pairs={{0,16},{16,32},{32,48},{48,64},{64,80},{80,96},{96,112},{112,0},{1... | collective-permute-start | bytes 663560 | tf_op jit(solution)/shard_map/ppermute | solution.py:33
  116.6 7.1 %collective-permute-start.16 = (bf16[48,2304]{1,0:T(8,128)(2,1)S(1)}, bf16[48,2304]{1,0:T(8,128)(2,1)}, u32[]{:S(2)}, u32[]{:S(2)}) collective-permute-start(bf16[48,2304]{1,0:T(8,128)(2,1)S(1)} %collective-permute-done.15.refs_1_), channel_id=1, source_target_pairs={{0,112},{16,0},{32,16},{48,32},{64,48},{80,64},{96,80},{112,96},{1... | collective-permute-start | bytes 663560 | tf_op jit(solution)/shard_map/ppermute | solution.py:33
  120.3 7.2 %collective-permute-start.19 = (bf16[48,2304]{1,0:T(8,128)(2,1)S(1)}, bf16[48,2304]{1,0:T(8,128)(2,1)}, u32[]{:S(2)}, u32[]{:S(2)}) collective-permute-start(bf16[48,2304]{1,0:T(8,128)(2,1)S(1)} %collective-permute-done.18.refs_8_), channel_id=1, source_target_pairs={{0,16},{16,32},{32,48},{48,64},{64,80},{80,96},{96,112},{112,0},{1... | collective-permute-start | bytes 663560 | tf_op jit(solution)/shard_map/ppermute | solution.py:33
  123.8 7.6 %collective-permute-start.17 = (bf16[48,2304]{1,0:T(8,128)(2,1)}, bf16[48,2304]{1,0:T(8,128)(2,1)S(1)}, u32[]{:S(2)}, u32[]{:S(2)}) collective-permute-start(bf16[48,2304]{1,0:T(8,128)(2,1)} %collective-permute-done.16.refs_2_), channel_id=1, source_target_pairs={{0,112},{16,0},{32,16},{48,32},{64,48},{80,64},{96,80},{112,96},{1... | collective-permute-start | bytes 663560 | tf_op jit(solution)/shard_map/ppermute | solution.py:33
  127.6 7.4 %collective-permute-start.20 = (bf16[48,2304]{1,0:T(8,128)(2,1)}, bf16[48,2304]{1,0:T(8,128)(2,1)S(1)}, u32[]{:S(2)}, u32[]{:S(2)}) collective-permute-start(bf16[48,2304]{1,0:T(8,128)(2,1)} %collective-permute-done.19.refs_7_), channel_id=1, source_target_pairs={{0,16},{16,32},{32,48},{48,64},{64,80},{80,96},{96,112},{112,0},{1... | collective-permute-start | bytes 663560 | tf_op jit(solution)/shard_map/ppermute | solution.py:33
  135.6 6.2 %collective-permute-start.21 = (bf16[48,1152]{1,0:T(8,128)(2,1)}, bf16[48,1152]{1,0:T(8,128)(2,1)S(1)}, u32[]{:S(2)}, u32[]{:S(2)}) collective-permute-start(bf16[48,1152]{1,0:T(8,128)(2,1)} %slice.178), channel_id=1, source_target_pairs={{0,16},{16,32},{32,48},{48,64},{64,80},{80,96},{96,112},{112,0},{1... | collective-permute-start | bytes 331784 | tf_op jit(solution)/shard_map/ppermute | solution.py:33
  136.2 5.9 %collective-permute-start.22 = (bf16[48,1152]{1,0:T(8,128)(2,1)}, bf16[48,1152]{1,0:T(8,128)(2,1)S(1)}, u32[]{:S(2)}, u32[]{:S(2)}) collective-permute-start(bf16[48,1152]{1,0:T(8,128)(2,1)} %slice.179), channel_id=1, source_target_pairs={{0,112},{16,0},{32,16},{48,32},{64,48},{80,64},{96,80},{112,96},{1... | collective-permute-start | bytes 331784 | tf_op jit(solution)/shard_map/ppermute | solution.py:33
  142.1 1.8 %copy-start.7 = (bf16[8,48,512]{2,1,0:T(8,128)(2,1)S(1)}, bf16[8,48,512]{2,1,0:T(8,128)(2,1)}, u32[]{:S(2)}) copy-start(bf16[8,48,512]{2,1,0:T(8,128)(2,1)} %copy-done.6) | copy-start | bytes 1179652
  143.8 1.9 %collective-permute-start.23 = (bf16[384,128]{1,0:T(8,128)(2,1)S(1)}, bf16[384,128]{1,0:T(8,128)(2,1)S(1)}, u32[]{:S(2)}, u32[]{:S(2)}) collective-permute-start(bf16[384,128]{1,0:T(8,128)(2,1)S(1)} %get-tuple-element.45), channel_id=1, source_target_pairs={{0,8},{8,0},{1,9},{9,1},{2,10},{10,2},{3,11},{11,3},{4,12},{12,4},... | collective-permute-start | bytes 294920 | tf_op jit(solution)/shard_map/ppermute | solution.py:402
  143.9 6.2 %collective-permute-start.9 = (bf16[512,128]{1,0:T(8,128)(2,1)S(1)}, bf16[512,128]{1,0:T(8,128)(2,1)S(1)}, u32[]{:S(2)}, u32[]{:S(2)}) collective-permute-start(bf16[512,128]{1,0:T(8,128)(2,1)S(1)} %slice.262), channel_id=1, source_target_pairs={{0,1},{1,0},{2,3},{3,2},{4,5},{5,4},{6,7},{7,6},{8,9},{9,8},{10,11... | collective-permute-start | bytes 393224 | tf_op jit(solution)/shard_map/ppermute | solution.py:27
  145.8 5.7 %collective-permute-start.24 = (bf16[1,4,48,128]{3,2,1,0:T(8,128)(2,1)S(1)}, bf16[1,4,48,128]{3,2,1,0:T(8,128)(2,1)S(1)}, u32[]{:S(2)}, u32[]{:S(2)}) collective-permute-start(bf16[1,4,48,128]{3,2,1,0:T(8,128)(2,1)S(1)} %get-tuple-element.81), channel_id=1, source_target_pairs={{0,4},{1,5},{2,6},{3,7},{4,0},{5,1},{6,2},{7,3},{8,12},{9,13},{10,... | collective-permute-start | bytes 147464 | tf_op jit(solution)/shard_map/ppermute | solution.py:57
  151.5 4.2 %collective-permute-start.25 = (bf16[2,2,48,128]{3,2,1,0:T(8,128)(2,1)S(1)}, bf16[2,2,48,128]{3,2,1,0:T(8,128)(2,1)S(1)}, u32[]{:S(2)}, u32[]{:S(2)}) collective-permute-start(bf16[2,2,48,128]{3,2,1,0:T(8,128)(2,1)S(1)} %get-tuple-element.79), channel_id=1, source_target_pairs={{0,2},{1,3},{2,0},{3,1},{4,6},{5,7},{6,4},{7,5},{8,10},{9,11},{10,... | collective-permute-start | bytes 147464 | tf_op jit(solution)/shard_map/ppermute | solution.py:57
  155.7 4.2 %collective-permute-start.26 = (bf16[4,1,48,128]{3,2,0,1:T(8,128)(2,1)S(1)}, bf16[4,1,48,128]{3,2,0,1:T(8,128)(2,1)S(1)}, u32[]{:S(2)}, u32[]{:S(2)}) collective-permute-start(bf16[4,1,48,128]{3,2,0,1:T(8,128)(2,1)S(1)} %get-tuple-element.77), channel_id=1, source_target_pairs={{0,1},{1,0},{2,3},{3,2},{4,5},{5,4},{6,7},{7,6},{8,9},{9,8},{10,11... | collective-permute-start | bytes 147464 | tf_op jit(solution)/shard_map/ppermute | solution.py:57
  157.3 2.6 %copy-start.12 = (pred[512,8,48]{0,2,1:T(8,128)(4,1)S(1)}, pred[512,8,48]{0,2,1:T(8,128)(4,1)}, u32[]{:S(2)}) copy-start(pred[512,8,48]{0,2,1:T(8,128)(4,1)} %fusion) | copy-start | bytes 589828

commit v9 on v8

--- a/solution.py
+++ b/solution.py
@@ -11,6 +11,7 @@
 X_HI = 2
 X_LO = 2
 MASKED = -1e30
+MASKS = (4, 2, 8, 1)
 BF = jnp.bfloat16
 F32 = jnp.float32
 
@@ -47,22 +48,34 @@
     return got.reshape(-1, block.shape[1])
 
 
-def key_sum(both):
-    parts = both.reshape(len(key_groups()[0]), -1, both.shape[1])
-    got = lax.all_to_all(parts, ("ctx", "exp"), 0, 0, tiled=True, axis_index_groups=key_groups())
-    return jnp.sum(got.astype(F32), axis=0)
+def y_parts(both):
+    n = lax.axis_size("exp")
+    groups = [list(range(x, n, X_LO)) for x in range(X_LO)]
+    parts = both.reshape(n // X_LO, -1, both.shape[1])
+    return lax.all_to_all(parts, "exp", 0, 0, tiled=True, axis_index_groups=groups)
+
+
+def ctx_sum(both, masks):
+    for mask in reversed(masks):
+        half = both.shape[0] // 2
+        sent = both[half:].astype(BF if half >= both.shape[1] // 2 else F32)
+        pairs = [(c, c ^ mask) for c in range(lax.axis_size("ctx"))]
+        both = both[:half] + lax.ppermute(sent, "ctx", pairs).astype(F32)
+    return both
+
+
+def place_of(apart):
+    return sum(apart // mask % 2 * 2**bit for bit, mask in enumerate(MASKS))
 
 
 def partner(block, mask):
     return lax.ppermute(block, "exp", [(e, e ^ mask) for e in range(lax.axis_size("exp"))])
 
 
-def exchange(blocks, waits=None):
+def exchange(blocks):
     shape = blocks.shape
     bits = shape[0].bit_length() - 1
     for bit in range(bits):
-        if waits is not None and bit == bits - 1:
-            blocks = after(blocks, waits)
         blocks = blocks.reshape((2**bit, 2, -1) + shape[1:])
         got = partner(blocks[:, 1], 2 ** (bits - 1 - bit))
         blocks = jnp.stack([blocks[:, 0], got], axis=1)
@@ -133,7 +146,7 @@
     masked = []
     for part in range(parts):
         place = step * parts + part
-        start = place // rows * tokens + (place % rows * X_LO + side) * own
+        start = (here_ref[2] + place // rows) * tokens + (place % rows * X_LO + side) * own
         masked.append(
             jnp.where(
                 ahead >= start - me * tokens,
@@ -175,8 +188,10 @@
 
 
 def grads_body(
-    own, rows, tokens, here_ref, q_ref, g_ref, kv_ref, stats_ref, far_ref, both_ref, dq_ref
+    own, rows, tokens, here_ref, q_ref, g_ref, kv_ref, stats_ref, far_ref, *refs
 ):
+    before, (both_ref, dq_ref) = refs[:-2], refs[-2:]
+    both_ref[...] = before[0][...] if before else jnp.zeros_like(both_ref)
     size = kv_ref.shape[1] // 2
     lanes = q_ref.shape[0]
     chunk = 8 * own
@@ -192,28 +207,34 @@
         k = kv_ref[at, :size]
         scores = scores_of(step, own, rows, tokens, here_ref, k, q_ref[...])
         prob = jnp.exp(scores - top) * inverse
-        both_ref[at, size:] = jnp.dot(
-            prob.astype(BF), g_ref[...], preferred_element_type=F32
-        ).astype(BF)
+        value = jnp.dot(prob.astype(BF), g_ref[...], preferred_element_type=F32).astype(BF)
         dprob = lax.dot_general(
             kv_ref[at, size:], g_ref[...], (((1,), (1,)), ((), ())), preferred_element_type=F32
         )
         dscore = (prob * (dprob - delta)).astype(BF)
-        both_ref[at, :size] = jnp.dot(dscore, q_ref[...], preferred_element_type=F32).astype(BF)
+        key = jnp.dot(dscore, q_ref[...], preferred_element_type=F32).astype(BF)
+        for part in range(8):
+            place = step * 8 + part
+            i = place_of((here_ref[2] + place // rows) ^ here_ref[0])
+            piece = slice(part * own, (part + 1) * own)
+            both_ref[place % rows, i, :, :size] = key[piece]
+            both_ref[place % rows, i, :, size:] = value[piece]
         return total + lax.dot_general(
             k, dscore, (((0,), (0,)), ((), ())), preferred_element_type=F32
         )
 
     total = lax.fori_loop(0, kv_ref.shape[0] // chunk, one, jnp.zeros((size, lanes), F32))
-    dq_ref[...] = (total * size ** (-0.5)).T
+    total = (total * size ** (-0.5)).T
+    dq_ref[...] = total + before[1][...] if before else total
 
 
 VMEM = pl.BlockSpec(memory_space=pltpu.VMEM)
 SMEM = pl.BlockSpec(memory_space=pltpu.SMEM)
 
 
-def here():
-    return jnp.stack([lax.axis_index("ctx"), lax.axis_index("exp") % X_LO]).astype(jnp.int32)
+def here(first):
+    side = lax.axis_index("exp") % X_LO
+    return jnp.stack([lax.axis_index("ctx"), side, jnp.int32(first)]).astype(jnp.int32)
 
 
 def attention_stats(own, tokens, queries, grads, flat):
@@ -230,19 +251,20 @@
             transcendentals=keys * lanes,
         ),
         name="attention_stats",
-    )(here(), queries, grads, flat)
-
-
-def attention_grads(own, tokens, queries, grads, flat, stats, far):
+    )(here(0), queries, grads, flat)
+
+
+def attention_grads(own, tokens, first, queries, grads, flat, stats, far, before=()):
     keys, lanes = flat.shape[0], queries.shape[0]
     size = flat.shape[1] // 2
+    rows = lax.axis_size("exp") // X_LO
     return pl.pallas_call(
-        functools.partial(grads_body, own, lax.axis_size("exp") // X_LO, tokens),
+        functools.partial(grads_body, own, rows, tokens),
         out_shape=(
-            jax.ShapeDtypeStruct((keys, 2 * size), BF),
+            jax.ShapeDtypeStruct((rows, lax.axis_size("ctx"), own, 2 * size), BF),
             jax.ShapeDtypeStruct((lanes, size), F32),
         ),
-        in_specs=[SMEM] + [VMEM] * 5,
+        in_specs=[SMEM] + [VMEM] * (5 + len(before)),
         out_specs=(VMEM, VMEM),
         compiler_params=pltpu.CompilerParams(vmem_limit_bytes=24 * 2**20),
         cost_estimate=pl.CostEstimate(
@@ -251,7 +273,7 @@
             transcendentals=keys * lanes,
         ),
         name="attention_grads",
-    )(here(), queries, grads, flat, stats, far)
+    )(here(first), queries, grads, flat, stats, far, *before)
 
 
 def by_head(rows):
@@ -265,7 +287,7 @@
     return grad_key, grad_value
 
 
-def select(moe_input, moe_grad, expert_ids, router_weight, flat):
+def select(moe_input, moe_grad, expert_ids, router_weight):
     width = moe_input.shape[1]
     exp_size = lax.axis_size("exp")
     labels = lax.axis_index("exp") ^ jnp.arange(exp_size)
@@ -282,7 +304,7 @@
     picked = jnp.einsum("bs,bd->sd", placed_low, rows, preferred_element_type=F32)
     scaled = picked[:, width:] * slot_weight.reshape(-1, 1)
     sent = jnp.concatenate([picked[:, :width].astype(BF), scaled.astype(BF)], axis=1)
-    got = exchange(sent.reshape(exp_size, CAP, 2 * width), flat)
+    got = exchange(sent.reshape(exp_size, CAP, 2 * width))
     return placed_low, got
 
 
@@ -426,7 +448,7 @@
     size = queries.shape[2]
     pair = jnp.concatenate([key_rows[:, 0, :], value_vector_rows[:, 0, :]], axis=1)
     flat = key_gather(pair)
-    placed_low, got = select(moe_input, moe_grad, expert_ids, router_weight, flat)
+    placed_low, got = select(moe_input, moe_grad, expert_ids, router_weight)
     mine = jnp.concatenate([by_head(queries), by_head(grad_attn)], axis=0)
     theirs = beside(mine)
     queries = jnp.concatenate([mine[:rows], theirs[:rows]], axis=0)
@@ -441,24 +463,38 @@
     far_stats = beside(stats)
     onward, back = sum_step(z_move, parts, 1, onward, back)
     onward, back = both_after(onward, back, far_stats)
+    half = flat.shape[0] // 2
+    middle = lax.axis_size("ctx") // 2
+    lower = attention_grads(
+        own, tokens, 0, queries, grads, after(flat[:half], onward, back), stats, far_stats
+    )
+    onward, back = sum_step(z_move, parts, 2, onward, back)
+    onward, back = both_after(onward, back, *lower)
     both, grad_query = attention_grads(
-        own, tokens, queries, grads, after(flat, onward, back), stats, far_stats
-    )
-    onward, back = sum_step(z_move, parts, 2, onward, back)
-    onward, back = both_after(onward, back, both)
-    total = sum_step(z_move, parts, 3, onward, back)
-    sums = key_sum(both)
+        own, tokens, middle, queries, grads, after(flat[half:], onward, back), stats, far_stats, lower
+    )
+    total = after(sum_step(z_move, parts, 3, onward, back), both)
+    terms = y_parts(both.reshape(-1, pair.shape[1]))
     other = opposite(total.astype(BF))
     block = act_block(total + other.astype(F32))
+    far_query = beside(grad_query[rows:].astype(BF))
+    grad_query = (grad_query[:rows] + far_query.astype(F32)).astype(BF)
     blocks = [block] + [None] * 8
     blocks[8], blocks[1] = ring_step(z_move, block, block)
-    blocks[7], blocks[2] = ring_step(z_move, blocks[8], blocks[1])
-    blocks[6], blocks[3] = ring_step(z_move, blocks[7], blocks[2])
+    sums = jnp.sum(after(terms, blocks[8], blocks[1]).astype(F32), axis=0)
+    onward, back = both_after(blocks[8], blocks[1], far_query)
+    blocks[7], blocks[2] = ring_step(z_move, onward, back)
+    sums = ctx_sum(sums, MASKS[3:])
+    onward, back = both_after(blocks[7], blocks[2], sums)
+    blocks[6], blocks[3] = ring_step(z_move, onward, back)
+    sums = ctx_sum(sums, MASKS[2:3])
     onward, back = both_after(blocks[6], blocks[3], sums)
     blocks[4], blocks[5] = ring_last(z_move, onward, back)
+    sums = ctx_sum(sums, MASKS[1:2])
+    blocks[0] = after(block, sums)
+    sums = ctx_sum(sums, MASKS[:1])
     of_experts = finish(blocks, input_rows, grad_rows, gate_mat, up_mat, placed_low)
-    grad_query = grad_query[:rows] + beside(grad_query[rows:].astype(BF)).astype(F32)
-    grad_query = jnp.swapaxes(grad_query.astype(BF).reshape(-1, tokens, size), 0, 1)
+    grad_query = jnp.swapaxes(grad_query.reshape(-1, tokens, size), 0, 1)
     return (grad_query,) + own_grads(sums) + of_experts
 
 

time: 163 us -> 154 us (0.945)
  waiting for transfers between devices: 61.6 us -> 47.6 us
  starting transfers between devices: 64.2 us -> 66.8 us
    ppermute x0 -> x4, starting transfers between devices: none -> 9.93 us  [ctx_sum(): both = both[:half] + lax.ppermute(sent, 'ctx', pairs).astype(F32)]
    ppermute x6, waiting for transfers between devices: 20.4 us -> 14.7 us  [partner(): lax.ppermute(block, 'exp', [(e, e ^ mask) for e in range(lax.axis_size('e...]
    ppermute x1, waiting for transfers between devices: 9.17 us -> 3.91 us  [opposite(): lax.ppermute(block, 'ctx', [(c, (c + n // X_HI) % n) for c in range(n)])]
    all_to_all x1, waiting for transfers between devices: 5.89 us -> 0.98 us  [key_gather(): lax.all_to_all(copies, ('ctx', 'exp'), 0, 0, tiled=True, axis_index_group...]
    ppermute x0 -> x4, waiting for transfers between devices: none -> 4.52 us  [ctx_sum(): both = both[:half] + lax.ppermute(sent, 'ctx', pairs).astype(F32)]
    ppermute x16, starting transfers between devices: 27.9 us -> 24 us  [z_move(): return lax.ppermute(block, 'ctx', pairs)]
    all_to_all x1, starting transfers between devices: 13.8 us -> 11.8 us  [key_gather(): lax.all_to_all(copies, ('ctx', 'exp'), 0, 0, tiled=True, axis_index_group...]
    all_to_all x1, starting transfers between devices: 6.19 us -> 4.25 us  [y_parts(): lax.all_to_all(parts, 'exp', 0, 0, tiled=True, axis_index_groups=groups)]
  transfers between devices with their start and end apart: 29 -> 33, of which waited for: 18 -> 19; matrix products, arithmetic and copies ran while one was open for 7% -> 9% of each run, Pallas kernels for 9% -> 8%
where the time goes in v9:
time: 154 us; the launch traced here: 153 us
  starting transfers between devices  66.8 us (43%)
  waiting for transfers between devices  47.6 us (31%)
  Pallas kernels  17 us (11%)
  other arithmetic  10.1 us (7%)
  local copies, waits for them, and re-layouts  7.16 us (5%)
  matrix products  3.44 us (2%)
    ppermute x16, starting transfers between devices, z_move(): return lax.ppermute(block, 'ctx', pairs)  24 us
    ppermute x16, waiting for transfers between devices, z_move(): return lax.ppermute(block, 'ctx', pairs)  23.5 us
    ppermute x6, waiting for transfers between devices, partner(): lax.ppermute(block, 'exp', [(e, e ^ mask) for e in range(lax.axis_size('e...  14.7 us
    ppermute x6, starting transfers between devices, partner(): lax.ppermute(block, 'exp', [(e, e ^ mask) for e in range(lax.axis_size('e...  12.2 us
    all_to_all x1, starting transfers between devices, key_gather(): lax.all_to_all(copies, ('ctx', 'exp'), 0, 0, tiled=True, axis_index_group...  11.8 us
    pallas_call x2, Pallas kernels, attention_grads(): pl.pallas_call(functools.partial(grads_body, own, rows, tokens), out_shap...  10.2 us
    ppermute x4, starting transfers between devices, ctx_sum(): both = both[:half] + lax.ppermute(sent, 'ctx', pairs).astype(F32)  9.93 us
    pallas_call x1, Pallas kernels, attention_stats(): pl.pallas_call(functools.partial(stats_body, own, lax.axis_size('exp') //...  4.79 us
  transfers between devices with their start and end apart: 33, of which 19 were waited for; matrix products, arithmetic and copies ran while one was open for 9% of the time, Pallas kernels for 8%

profile of v9, /device:TPU:2, one launch (start us, length us, event | category | flops | bytes accessed | tf_op | source)
XLA Modules:
  0.0 153.4 jit_solution(2024607636684039513)
XLA Ops:
  0.7 0.9 fusion.19
  1.6 1.1 reduce-window.6
  3.0 0.8 fusion.20
  4.5 1.4 fusion.2
  6.2 3.3 %collective-permute-start.1 = (bf16[1,4,48,512]{3,2,1,0:T(8,128)(2,1)S(1)}, bf16[1,4,48,512]{3,2,1,0:T(8,128)(2,1)S(1)}, u32[]{:S(2)}, u32[]{:S(2)}) collective-permute-start(bf16[1,4,48,512]{3,2,1,0:T(8,128)(2,1)S(1)} %get-tuple-element.91), channel_id=1, source_target_pairs={{0,4},{1,5},{2,6},{3,7},{4,0},{5,1},{6,2},{7,3},{8,12},{9,13},{10,... | collective-permute-start | bytes 589832 | tf_op jit(solution)/shard_map/ppermute | solution.py:72
  9.5 0.7 pad_maximum_fusion.3
  10.8 1.1 broadcast_in_dim.43
  11.9 11.8 %all-to-all-start = ((bf16[64,32,256]{2,1,0:T(8,128)(2,1)}), bf16[64,32,256]{2,1,0:T(8,128)(2,1)S(1)}, u32[]{:S(2)}, u32[]{:S(2)}) async-start(bf16[64,32,256]{2,1,0:T(8,128)(2,1)} %broadcast_in_dim.43), calls=%async_computation | async-start | bytes 2097152 | tf_op jit(solution)/shard_map/all_to_all | solution.py:45
  23.9 1.7 %collective-permute-start.2 = (bf16[2,2,48,512]{3,2,1,0:T(8,128)(2,1)S(1)}, bf16[2,2,48,512]{3,2,1,0:T(8,128)(2,1)S(1)}, u32[]{:S(2)}, u32[]{:S(2)}) collective-permute-start(bf16[2,2,48,512]{3,2,1,0:T(8,128)(2,1)S(1)} %get-tuple-element.89), channel_id=1, source_target_pairs={{0,2},{1,3},{2,0},{3,1},{4,6},{5,7},{6,4},{7,5},{8,10},{9,11},{10,... | collective-permute-start | bytes 589832 | tf_op jit(solution)/shard_map/ppermute | solution.py:72
  25.6 1.2 dynamic-slice_bitcast_fusion
  26.8 6.4 %collective-permute-done.2 = bf16[2,2,48,512]{3,2,1,0:T(8,128)(2,1)S(1)} collective-permute-done((bf16[2,2,48,512]{3,2,1,0:T(8,128)(2,1)S(1)}, bf16[2,2,48,512]{3,2,1,0:T(8,128)(2,1)S(1)}, u32[]{:S(2)}, u32[]{:S(2)}) %collective-permute-start.2) | collective-permute-done | bytes 196640 | tf_op jit(solution)/shard_map/ppermute | solution.py:72
  33.3 1.9 %collective-permute-start.3 = (bf16[4,1,48,512]{3,2,0,1:T(8,128)(2,1)S(1)}, bf16[4,1,48,512]{3,2,0,1:T(8,128)(2,1)S(1)}, u32[]{:S(2)}, u32[]{:S(2)}) collective-permute-start(bf16[4,1,48,512]{3,2,0,1:T(8,128)(2,1)S(1)} %get-tuple-element.87), channel_id=1, source_target_pairs={{0,1},{1,0},{2,3},{3,2},{4,5},{5,4},{6,7},{7,6},{8,9},{9,8},{10,11... | collective-permute-start | bytes 589832 | tf_op jit(solution)/shard_map/ppermute | solution.py:72
  35.2 1.0 fusion.36
  36.2 3.7 %collective-permute-done.3 = bf16[4,1,48,512]{3,2,0,1:T(8,128)(2,1)S(1)} collective-permute-done((bf16[4,1,48,512]{3,2,0,1:T(8,128)(2,1)S(1)}, bf16[4,1,48,512]{3,2,0,1:T(8,128)(2,1)S(1)}, u32[]{:S(2)}, u32[]{:S(2)}) %collective-permute-start.3) | collective-permute-done | bytes 196640 | tf_op jit(solution)/shard_map/ppermute | solution.py:72
  41.2 3.0 %collective-permute-start.4 = (bf16[48,1152]{1,0:T(8,128)(2,1)S(1)}, bf16[48,1152]{1,0:T(8,128)(2,1)S(1)}, u32[]{:S(2)}, u32[]{:S(2)}) collective-permute-start(bf16[48,1152]{1,0:T(8,128)(2,1)S(1)} %get-tuple-element.38), channel_id=1, source_target_pairs={{0,16},{16,32},{32,48},{48,64},{64,80},{80,96},{96,112},{112,0},{1... | collective-permute-start | bytes 331784 | tf_op jit(solution)/shard_map/ppermute | solution.py:34
  44.2 1.5 collective-permute-start.5
  45.8 5.1 %collective-permute-done.4 = bf16[48,1152]{1,0:T(8,128)(2,1)S(1)} collective-permute-done((bf16[48,1152]{1,0:T(8,128)(2,1)S(1)}, bf16[48,1152]{1,0:T(8,128)(2,1)S(1)}, u32[]{:S(2)}, u32[]{:S(2)}) %collective-permute-start.4) | collective-permute-done | bytes 110624 | tf_op jit(solution)/shard_map/ppermute | solution.py:34
  51.0 0.7 fusion.13
  51.7 1.0 all-to-all-done
  52.7 4.8 %attention_stats.1.stats_ref = f32[8,1024]{1,0:T(8,128)S(1)} custom-call(s32[3]{0:T(128)S(1)} %pad_add_fusion.2.here_ref, bf16[1024,128]{1,0:T(8,128)(2,1)S(1)} %get-tuple-element.100.q_ref, bf16[1024,128]{1,0:T(8,128)(2,1)S(1)} %get-tuple-element.101.g_ref, bf16[2048,256]{1,0:T(8,128)(2,1)S(1)} %bitcast.83), custom_call_target="tpu_custom_call" | custom-call | flops 1073741824 | bytes 1048576 | tf_op jit(solution)/shard_map/attention_stats/pallas_call | solution.py:242
  57.5 3.3 %collective-permute-start.6 = (bf16[48,2304]{1,0:T(8,128)(2,1)S(1)}, bf16[48,2304]{1,0:T(8,128)(2,1)S(1)}, u32[]{:S(2)}, u32[]{:S(2)}) collective-permute-start(bf16[48,2304]{1,0:T(8,128)(2,1)S(1)} %copy-done.12), channel_id=1, source_target_pairs={{0,16},{16,32},{32,48},{48,64},{64,80},{80,96},{96,112},{112,0},{1... | collective-permute-start | bytes 663560 | tf_op jit(solution)/shard_map/ppermute | solution.py:34
  60.8 1.8 %collective-permute-start.8 = (f32[8,1024]{1,0:T(8,128)S(1)}, f32[8,1024]{1,0:T(8,128)S(1)}, u32[]{:S(2)}, u32[]{:S(2)}) collective-permute-start(f32[8,1024]{1,0:T(8,128)S(1)} %attention_stats.1.stats_ref), channel_id=1, source_target_pairs={{0,1},{1,0},{2,3},{3,2},{4,5},{5,4},{6,7},{7,6},{8,9},{9,8},{10,11... | collective-permute-start | bytes 98312 | tf_op jit(solution)/shard_map/ppermute | solution.py:28
  62.6 2.1 %collective-permute-done.6 = bf16[48,2304]{1,0:T(8,128)(2,1)S(1)} collective-permute-done((bf16[48,2304]{1,0:T(8,128)(2,1)S(1)}, bf16[48,2304]{1,0:T(8,128)(2,1)S(1)}, u32[]{:S(2)}, u32[]{:S(2)}) %collective-permute-start.6) | collective-permute-done | bytes 221216 | tf_op jit(solution)/shard_map/ppermute | solution.py:34
  64.7 4.2 %collective-permute-done.7 = bf16[48,2304]{1,0:T(8,128)(2,1)S(1)} collective-permute-done((bf16[48,2304]{1,0:T(8,128)(2,1)S(1)}, bf16[48,2304]{1,0:T(8,128)(2,1)S(1)}, u32[]{:S(2)}, u32[]{:S(2)}) %collective-permute-start.7) | collective-permute-done | bytes 221216 | tf_op jit(solution)/shard_map/ppermute | solution.py:34
  69.2 2.0 %collective-permute-start.9 = (bf16[48,2304]{1,0:T(8,128)(2,1)S(1)}, bf16[48,2304]{1,0:T(8,128)(2,1)S(1)}, u32[]{:S(2)}, u32[]{:S(2)}) collective-permute-start(bf16[48,2304]{1,0:T(8,128)(2,1)S(1)} %get-tuple-element.43), channel_id=1, source_target_pairs={{0,16},{16,32},{32,48},{48,64},{64,80},{80,96},{96,112},{112,0},{1... | collective-permute-start | bytes 663560 | tf_op jit(solution)/shard_map/ppermute | solution.py:34
  71.3 4.7 %attention_grads.2 = (bf16[4,16,32,256]{3,2,1,0:T(8,128)(2,1)S(1)}, f32[1024,128]{1,0:T(8,128)S(1)}) custom-call(s32[3]{0:T(128)S(1)} %pad_add_fusion.2.here_ref, bf16[1024,128]{1,0:T(8,128)(2,1)S(1)} %get-tuple-element.100.q_ref, bf16[1024,128]{1,0:T(8,128)(2,1)S(1)} %get-tuple-element.101.g_ref, bf16[1024,256]{1,0:T(8,128)(2,1)S(1)} %bitcast.85, ...), custom_call_target="tpu_custom_call" | custom-call | flops 1342177280 | bytes 1048576 | tf_op jit(solution)/shard_map/attention_grads/pallas_call | solution.py:261
  76.0 1.3 collective-permute-done.10
  77.4 1.3 collective-permute-done.9
  78.9 3.2 %collective-permute-start.13 = (bf16[48,2304]{1,0:T(8,128)(2,1)S(1)}, bf16[48,2304]{1,0:T(8,128)(2,1)S(1)}, u32[]{:S(2)}, u32[]{:S(2)}) collective-permute-start(bf16[48,2304]{1,0:T(8,128)(2,1)S(1)} %get-tuple-element.49), channel_id=1, source_target_pairs={{0,112},{16,0},{32,16},{48,32},{64,48},{80,64},{96,80},{112,96},{1... | collective-permute-start | bytes 663560 | tf_op jit(solution)/shard_map/ppermute | solution.py:34
  82.2 5.4 %attention_grads.3 = (bf16[4,16,32,256]{3,2,1,0:T(8,128)(2,1)}, f32[1024,128]{1,0:T(8,128)S(1)}) custom-call(s32[3]{0:T(128)S(1)} %pad_add_fusion.here_ref, bf16[1024,128]{1,0:T(8,128)(2,1)S(1)} %get-tuple-element.100.q_ref, bf16[1024,128]{1,0:T(8,128)(2,1)S(1)} %copy-done.2, bf16[1024,256]{1,0:T(8,128)(2,1)S(1)} %bitcast.84, ...), custom_call_target="tpu_custom_call" | custom-call | flops 1342177280 | bytes 1048576 | tf_op jit(solution)/shard_map/attention_grads/pallas_call | solution.py:261
  87.7 0.8 collective-permute-start.14
  88.5 4.2 %all-to-all-start.1 = ((bf16[4,512,256]{2,1,0:T(8,128)(2,1)}), bf16[4,512,256]{2,1,0:T(8,128)(2,1)}, u32[]{:S(2)}, u32[]{:S(2)}) async-start(bf16[4,512,256]{2,1,0:T(8,128)(2,1)} %bitcast.34), calls=%async_computation.1 | async-start | bytes 2097152 | tf_op jit(solution)/shard_map/all_to_all | solution.py:55
  92.7 3.9 %collective-permute-done.14 = bf16[48,2304]{1,0:T(8,128)(2,1)S(1)} collective-permute-done((bf16[48,2304]{1,0:T(8,128)(2,1)S(1)}, bf16[48,2304]{1,0:T(8,128)(2,1)S(1)}, u32[]{:S(2)}, u32[]{:S(2)}) %collective-permute-start.14) | collective-permute-done | bytes 221216 | tf_op jit(solution)/shard_map/ppermute | solution.py:87
  96.9 3.2 %collective-permute-start.16 = (bf16[48,2304]{1,0:T(8,128)(2,1)S(1)}, bf16[48,2304]{1,0:T(8,128)(2,1)S(1)}, u32[]{:S(2)}, u32[]{:S(2)}) collective-permute-start(bf16[48,2304]{1,0:T(8,128)(2,1)S(1)} %pad_maximum_fusion.8.refs_0_), channel_id=1, source_target_pairs={{0,112},{16,0},{32,16},{48,32},{64,48},{80,64},{96,80},{112,96},{1... | collective-permute-start | bytes 663560 | tf_op jit(solution)/shard_map/ppermute | solution.py:34
  100.2 1.4 collective-permute-start.11
  101.6 3.8 %collective-permute-done.15.refs_8_ = bf16[48,2304]{1,0:T(8,128)(2,1)S(1)} collective-permute-done((bf16[48,2304]{1,0:T(8,128)(2,1)S(1)}, bf16[48,2304]{1,0:T(8,128)(2,1)S(1)}, u32[]{:S(2)}, u32[]{:S(2)}) %collective-permute-start.15) | collective-permute-done | bytes 221216 | tf_op jit(solution)/shard_map/ppermute | solution.py:34
  105.4 1.5 convert_reduce_fusion
  106.9 1.4 collective-permute-start.17
  108.3 1.5 collective-permute-start.21
  110.3 2.6 %collective-permute-done.17 = bf16[256,256]{1,0:T(8,128)(2,1)S(1)} collective-permute-done((bf16[256,256]{1,0:T(8,128)(2,1)S(1)}, bf16[256,256]{1,0:T(8,128)(2,1)S(1)}, u32[]{:S(2)}, u32[]{:S(2)}) %collective-permute-start.17) | collective-permute-done | bytes 131104 | tf_op jit(solution)/shard_map/ppermute | solution.py:63
  112.9 0.6 slice.330
  113.6 1.9 %collective-permute-start.18 = (bf16[128,256]{1,0:T(8,128)(2,1)}, bf16[128,256]{1,0:T(8,128)(2,1)S(1)}, u32[]{:S(2)}, u32[]{:S(2)}) collective-permute-start(bf16[128,256]{1,0:T(8,128)(2,1)} %slice.330), channel_id=1, source_target_pairs={{0,128},{16,144},{32,160},{48,176},{64,192},{80,208},{96,224},{112... | collective-permute-start | bytes 196616 | tf_op jit(solution)/shard_map/ppermute | solution.py:63
  115.5 0.8 fusion
  116.3 0.6 collective-permute-done.22.refs_7_
  116.9 1.5 collective-permute-start.23
  118.9 0.6 collective-permute-done.18
  119.6 2.5 %collective-permute-start.19 = (f32[64,256]{1,0:T(8,128)S(1)}, f32[64,256]{1,0:T(8,128)S(1)}, u32[]{:S(2)}, u32[]{:S(2)}) collective-permute-start(f32[64,256]{1,0:T(8,128)S(1)} %slice.260), channel_id=1, source_target_pairs={{0,32},{16,48},{32,0},{48,16},{64,96},{80,112},{96,64},{112,80},{1... | collective-permute-start | bytes 196616 | tf_op jit(solution)/shard_map/ppermute | solution.py:63
  122.0 1.0 fusion.34
  123.1 2.5 %collective-permute-done.24.refs_6_ = bf16[48,2304]{1,0:T(8,128)(2,1)S(1)} collective-permute-done((bf16[48,2304]{1,0:T(8,128)(2,1)S(1)}, bf16[48,2304]{1,0:T(8,128)(2,1)S(1)}, u32[]{:S(2)}, u32[]{:S(2)}) %collective-permute-start.24) | collective-permute-done | bytes 221216 | tf_op jit(solution)/shard_map/ppermute | solution.py:34
  125.7 3.3 %collective-permute-start.26 = (bf16[48,1152]{1,0:T(8,128)(2,1)S(1)}, bf16[48,1152]{1,0:T(8,128)(2,1)S(1)}, u32[]{:S(2)}, u32[]{:S(2)}) collective-permute-start(bf16[48,1152]{1,0:T(8,128)(2,1)S(1)} %slice.229), channel_id=1, source_target_pairs={{0,112},{16,0},{32,16},{48,32},{64,48},{80,64},{96,80},{112,96},{1... | collective-permute-start | bytes 331784 | tf_op jit(solution)/shard_map/ppermute | solution.py:34
  129.0 2.6 %collective-permute-done.25.refs_4_ = bf16[48,1152]{1,0:T(8,128)(2,1)S(1)} collective-permute-done((bf16[48,1152]{1,0:T(8,128)(2,1)S(1)}, bf16[48,1152]{1,0:T(8,128)(2,1)S(1)}, u32[]{:S(2)}, u32[]{:S(2)}) %collective-permute-start.25) | collective-permute-done | bytes 110624 | tf_op jit(solution)/shard_map/ppermute | solution.py:34
  132.3 0.9 add_convert_fusion.4
  133.2 0.8 copy.51
  134.0 4.1 %collective-permute-start.20 = (f32[32,256]{1,0:T(8,128)S(1)}, f32[32,256]{1,0:T(8,128)S(1)}, u32[]{:S(2)}, u32[]{:S(2)}) collective-permute-start(f32[32,256]{1,0:T(8,128)S(1)} %slice.262), channel_id=1, source_target_pairs={{0,64},{16,80},{32,96},{48,112},{64,0},{80,16},{96,32},{112,48},{1... | collective-permute-start | bytes 98312 | tf_op jit(solution)/shard_map/ppermute | solution.py:63
  138.3 2.2 %collective-permute-start.28 = (bf16[1,4,48,128]{3,2,1,0:T(8,128)(2,1)S(1)}, bf16[1,4,48,128]{3,2,1,0:T(8,128)(2,1)S(1)}, u32[]{:S(2)}, u32[]{:S(2)}) collective-permute-start(bf16[1,4,48,128]{3,2,1,0:T(8,128)(2,1)S(1)} %get-tuple-element.99), channel_id=1, source_target_pairs={{0,4},{1,5},{2,6},{3,7},{4,0},{5,1},{6,2},{7,3},{8,12},{9,13},{10,... | collective-permute-start | bytes 147464 | tf_op jit(solution)/shard_map/ppermute | solution.py:72
  140.5 1.3 collective-permute-done.20
  141.8 2.1 %collective-permute-done.28 = bf16[1,4,48,128]{3,2,1,0:T(8,128)(2,1)S(1)} collective-permute-done((bf16[1,4,48,128]{3,2,1,0:T(8,128)(2,1)S(1)}, bf16[1,4,48,128]{3,2,1,0:T(8,128)(2,1)S(1)}, u32[]{:S(2)}, u32[]{:S(2)}) %collective-permute-start.28) | collective-permute-done | bytes 49184 | tf_op jit(solution)/shard_map/ppermute | solution.py:72
  144.0 1.3 collective-permute-start.29
  145.3 0.6 fusion.26
  145.9 2.2 %collective-permute-done.29 = bf16[2,2,48,128]{3,2,1,0:T(8,128)(2,1)S(1)} collective-permute-done((bf16[2,2,48,128]{3,2,1,0:T(8,128)(2,1)S(1)}, bf16[2,2,48,128]{3,2,1,0:T(8,128)(2,1)S(1)}, u32[]{:S(2)}, u32[]{:S(2)}) %collective-permute-start.29) | collective-permute-done | bytes 49184 | tf_op jit(solution)/shard_map/ppermute | solution.py:72
  148.2 1.8 %collective-permute-start.30 = (bf16[4,1,48,128]{3,2,0,1:T(8,128)(2,1)S(1)}, bf16[4,1,48,128]{3,2,0,1:T(8,128)(2,1)S(1)}, u32[]{:S(2)}, u32[]{:S(2)}) collective-permute-start(bf16[4,1,48,128]{3,2,0,1:T(8,128)(2,1)S(1)} %get-tuple-element.95), channel_id=1, source_target_pairs={{0,1},{1,0},{2,3},{3,2},{4,5},{5,4},{6,7},{7,6},{8,9},{9,8},{10,11... | collective-permute-start | bytes 147464 | tf_op jit(solution)/shard_map/ppermute | solution.py:72
  150.0 0.6 fusion.27
  150.6 1.5 %expert_weight_grads.1 = (bf16[1,256,768]{2,1,0:T(8,128)(2,1)}, bf16[1,256,768]{2,1,0:T(8,128)(2,1)}, bf16[1,768,256]{2,1,0:T(8,128)(2,1)}) custom-call(bf16[384,2304]{1,0:T(8,128)(2,1)S(1)} %get-tuple-element.65.full_ref, bf16[384,256]{1,0:T(8,128)(2,1)S(1)} %get-tuple-element.85.input_ref, bf16[384,256]{1,0:T(8,128)(2,1)S(1)} %get-tuple-element.84.grad_ref), custom_call_target="tpu_custom_call" | custom-call | flops 452984832 | bytes 3538944 | tf_op jit(solution)/shard_map/expert_weight_grads/pallas_call | solution.py:399
  152.4 1.0 convolution_convert_fusion.3
  (119 shorter events, 6.6 us)
Async XLA Ops:
  0.6 39.5 %copy-start = (bf16[1,1536,256]{2,1,0:T(8,128)(2,1)S(1)}, bf16[1,1536,256]{2,1,0:T(8,128)(2,1)}, u32[]{:S(2)}) copy-start(bf16[1,1536,256]{2,1,0:T(8,128)(2,1)} %param.21) | copy-start | bytes 2359300
  6.0 3.5 %copy-start.14 = (bf16[256,2,128]{2,1,0:T(2,128)(2,1)S(1)}, bf16[256,2,128]{2,1,0:T(2,128)(2,1)}, u32[]{:S(2)}) copy-start(bf16[256,2,128]{2,1,0:T(2,128)(2,1)} %param.11) | copy-start | bytes 393220
  6.0 3.5 %copy-start.15 = (bf16[256,2,128]{2,1,0:T(2,128)(2,1)S(1)}, bf16[256,2,128]{2,1,0:T(2,128)(2,1)}, u32[]{:S(2)}) copy-start(bf16[256,2,128]{2,1,0:T(2,128)(2,1)} %param.14) | copy-start | bytes 393220
  6.1 4.7 %copy-start.16 = (bf16[32,1,128]{2,0,1:T(8,128)(2,1)S(1)}, bf16[32,1,128]{2,0,1:T(8,128)(2,1)}, u32[]{:S(2)}) copy-start(bf16[32,1,128]{2,0,1:T(8,128)(2,1)} %param.13) | copy-start | bytes 24580
  6.1 4.7 %copy-start.17 = (bf16[32,1,128]{2,0,1:T(8,128)(2,1)S(1)}, bf16[32,1,128]{2,0,1:T(8,128)(2,1)}, u32[]{:S(2)}) copy-start(bf16[32,1,128]{2,0,1:T(8,128)(2,1)} %param.12) | copy-start | bytes 24580
  6.2 17.6 %collective-permute-start.1 = (bf16[1,4,48,512]{3,2,1,0:T(8,128)(2,1)S(1)}, bf16[1,4,48,512]{3,2,1,0:T(8,128)(2,1)S(1)}, u32[]{:S(2)}, u32[]{:S(2)}) collective-permute-start(bf16[1,4,48,512]{3,2,1,0:T(8,128)(2,1)S(1)} %get-tuple-element.91), channel_id=1, source_target_pairs={{0,4},{1,5},{2,6},{3,7},{4,0},{5,1},{6,2},{7,3},{8,12},{9,13},{10,... | collective-permute-start | bytes 589832 | tf_op jit(solution)/shard_map/ppermute | solution.py:72
  10.3 24.9 %collective-permute-start = (bf16[1024,128]{1,0:T(8,128)(2,1)}, bf16[1024,128]{1,0:T(8,128)(2,1)}, u32[]{:S(2)}, u32[]{:S(2)}) collective-permute-start(bf16[1024,128]{1,0:T(8,128)(2,1)} %pad_maximum_fusion.3), channel_id=1, source_target_pairs={{0,1},{1,0},{2,3},{3,2},{4,5},{5,4},{6,7},{7,6},{8,9},{9,8},{10,11... | collective-permute-start | bytes 786440 | tf_op jit(solution)/shard_map/ppermute | solution.py:28
  11.9 40.7 %all-to-all-start = ((bf16[64,32,256]{2,1,0:T(8,128)(2,1)}), bf16[64,32,256]{2,1,0:T(8,128)(2,1)S(1)}, u32[]{:S(2)}, u32[]{:S(2)}) async-start(bf16[64,32,256]{2,1,0:T(8,128)(2,1)} %broadcast_in_dim.43), calls=%async_computation | async-start | bytes 2097152 | tf_op jit(solution)/shard_map/all_to_all | solution.py:45
  23.9 9.3 %collective-permute-start.2 = (bf16[2,2,48,512]{3,2,1,0:T(8,128)(2,1)S(1)}, bf16[2,2,48,512]{3,2,1,0:T(8,128)(2,1)S(1)}, u32[]{:S(2)}, u32[]{:S(2)}) collective-permute-start(bf16[2,2,48,512]{3,2,1,0:T(8,128)(2,1)S(1)} %get-tuple-element.89), channel_id=1, source_target_pairs={{0,2},{1,3},{2,0},{3,1},{4,6},{5,7},{6,4},{7,5},{8,10},{9,11},{10,... | collective-permute-start | bytes 589832 | tf_op jit(solution)/shard_map/ppermute | solution.py:72
  33.3 6.6 %collective-permute-start.3 = (bf16[4,1,48,512]{3,2,0,1:T(8,128)(2,1)S(1)}, bf16[4,1,48,512]{3,2,0,1:T(8,128)(2,1)S(1)}, u32[]{:S(2)}, u32[]{:S(2)}) collective-permute-start(bf16[4,1,48,512]{3,2,0,1:T(8,128)(2,1)S(1)} %get-tuple-element.87), channel_id=1, source_target_pairs={{0,1},{1,0},{2,3},{3,2},{4,5},{5,4},{6,7},{7,6},{8,9},{9,8},{10,11... | collective-permute-start | bytes 589832 | tf_op jit(solution)/shard_map/ppermute | solution.py:72
  40.1 0.7 copy-start.11
  40.5 10.5 %copy-start.5 = (bf16[384,768]{1,0:T(8,128)(2,1)}, bf16[384,768]{1,0:T(8,128)(2,1)S(1)}, u32[]{:S(2)}) copy-start(bf16[384,768]{1,0:T(8,128)(2,1)S(1)} %convolution_convert_fusion) | copy-start | bytes 1769476
  40.8 10.2 %copy-start.7 = (bf16[384,768]{1,0:T(8,128)(2,1)}, bf16[384,768]{1,0:T(8,128)(2,1)S(1)}, u32[]{:S(2)}) copy-start(bf16[384,768]{1,0:T(8,128)(2,1)S(1)} %convolution_convert_fusion.2) | copy-start | bytes 1769476
  41.2 9.8 %copy-start.9 = (bf16[384,768]{1,0:T(8,128)(2,1)}, bf16[384,768]{1,0:T(8,128)(2,1)S(1)}, u32[]{:S(2)}) copy-start(bf16[384,768]{1,0:T(8,128)(2,1)S(1)} %convolution_convert_fusion.1) | copy-start | bytes 1769476
  41.2 9.7 %collective-permute-start.4 = (bf16[48,1152]{1,0:T(8,128)(2,1)S(1)}, bf16[48,1152]{1,0:T(8,128)(2,1)S(1)}, u32[]{:S(2)}, u32[]{:S(2)}) collective-permute-start(bf16[48,1152]{1,0:T(8,128)(2,1)S(1)} %get-tuple-element.38), channel_id=1, source_target_pairs={{0,16},{16,32},{32,48},{48,64},{64,80},{80,96},{96,112},{112,0},{1... | collective-permute-start | bytes 331784 | tf_op jit(solution)/shard_map/ppermute | solution.py:34
  44.2 6.6 %collective-permute-start.5 = (bf16[48,1152]{1,0:T(8,128)(2,1)S(1)}, bf16[48,1152]{1,0:T(8,128)(2,1)S(1)}, u32[]{:S(2)}, u32[]{:S(2)}) collective-permute-start(bf16[48,1152]{1,0:T(8,128)(2,1)S(1)} %get-tuple-element.39), channel_id=1, source_target_pairs={{0,112},{16,0},{32,16},{48,32},{64,48},{80,64},{96,80},{112,96},{1... | collective-permute-start | bytes 331784 | tf_op jit(solution)/shard_map/ppermute | solution.py:34
  45.8 25.5 %copy-start.1 = (bf16[1024,128]{1,0:T(8,128)(2,1)}, bf16[1024,128]{1,0:T(8,128)(2,1)S(1)}, u32[]{:S(2)}) copy-start(bf16[1024,128]{1,0:T(8,128)(2,1)S(1)} %get-tuple-element.101.g_ref) | copy-start | bytes 786436
  52.7 4.8 %copy-start.12 = (bf16[48,2304]{1,0:T(8,128)(2,1)S(1)}, bf16[48,2304]{1,0:T(8,128)(2,1)}, u32[]{:S(2)}) copy-start(bf16[48,2304]{1,0:T(8,128)(2,1)} %get-tuple-element.41) | copy-start | bytes 663556
  52.7 16.3 %copy-start.6 = (bf16[384,768]{1,0:T(8,128)(2,1)S(1)}, bf16[384,768]{1,0:T(8,128)(2,1)}, u32[]{:S(2)}) copy-start(bf16[384,768]{1,0:T(8,128)(2,1)} %copy-done.5) | copy-start | bytes 1769476
  52.7 16.3 %copy-start.8 = (bf16[384,768]{1,0:T(8,128)(2,1)S(1)}, bf16[384,768]{1,0:T(8,128)(2,1)}, u32[]{:S(2)}) copy-start(bf16[384,768]{1,0:T(8,128)(2,1)} %copy-done.7) | copy-start | bytes 1769476
  52.7 16.3 %copy-start.10 = (bf16[384,768]{1,0:T(8,128)(2,1)S(1)}, bf16[384,768]{1,0:T(8,128)(2,1)}, u32[]{:S(2)}) copy-start(bf16[384,768]{1,0:T(8,128)(2,1)} %copy-done.9) | copy-start | bytes 1769476
  57.5 7.2 %collective-permute-start.6 = (bf16[48,2304]{1,0:T(8,128)(2,1)S(1)}, bf16[48,2304]{1,0:T(8,128)(2,1)S(1)}, u32[]{:S(2)}, u32[]{:S(2)}) collective-permute-start(bf16[48,2304]{1,0:T(8,128)(2,1)S(1)} %copy-done.12), channel_id=1, source_target_pairs={{0,16},{16,32},{32,48},{48,64},{64,80},{80,96},{96,112},{112,0},{1... | collective-permute-start | bytes 663560 | tf_op jit(solution)/shard_map/ppermute | solution.py:34
  60.8 8.2 %collective-permute-start.7 = (bf16[48,2304]{1,0:T(8,128)(2,1)S(1)}, bf16[48,2304]{1,0:T(8,128)(2,1)S(1)}, u32[]{:S(2)}, u32[]{:S(2)}) collective-permute-start(bf16[48,2304]{1,0:T(8,128)(2,1)S(1)} %get-tuple-element.42), channel_id=1, source_target_pairs={{0,112},{16,0},{32,16},{48,32},{64,48},{80,64},{96,80},{112,96},{1... | collective-permute-start | bytes 663560 | tf_op jit(solution)/shard_map/ppermute | solution.py:34
  60.8 8.3 %collective-permute-start.8 = (f32[8,1024]{1,0:T(8,128)S(1)}, f32[8,1024]{1,0:T(8,128)S(1)}, u32[]{:S(2)}, u32[]{:S(2)}) collective-permute-start(f32[8,1024]{1,0:T(8,128)S(1)} %attention_stats.1.stats_ref), channel_id=1, source_target_pairs={{0,1},{1,0},{2,3},{3,2},{4,5},{5,4},{6,7},{7,6},{8,9},{9,8},{10,11... | collective-permute-start | bytes 98312 | tf_op jit(solution)/shard_map/ppermute | solution.py:28
  69.1 8.3 %collective-permute-start.10 = (bf16[48,2304]{1,0:T(8,128)(2,1)S(1)}, bf16[48,2304]{1,0:T(8,128)(2,1)S(1)}, u32[]{:S(2)}, u32[]{:S(2)}) collective-permute-start(bf16[48,2304]{1,0:T(8,128)(2,1)S(1)} %get-tuple-element.44), channel_id=1, source_target_pairs={{0,112},{16,0},{32,16},{48,32},{64,48},{80,64},{96,80},{112,96},{1... | collective-permute-start | bytes 663560 | tf_op jit(solution)/shard_map/ppermute | solution.py:34
  69.2 9.5 %collective-permute-start.9 = (bf16[48,2304]{1,0:T(8,128)(2,1)S(1)}, bf16[48,2304]{1,0:T(8,128)(2,1)S(1)}, u32[]{:S(2)}, u32[]{:S(2)}) collective-permute-start(bf16[48,2304]{1,0:T(8,128)(2,1)S(1)} %get-tuple-element.43), channel_id=1, source_target_pairs={{0,16},{16,32},{32,48},{48,64},{64,80},{80,96},{96,112},{112,0},{1... | collective-permute-start | bytes 663560 | tf_op jit(solution)/shard_map/ppermute | solution.py:34
  76.0 6.1 %copy-start.2 = (bf16[1024,128]{1,0:T(8,128)(2,1)S(1)}, bf16[1024,128]{1,0:T(8,128)(2,1)}, u32[]{:S(2)}) copy-start(bf16[1024,128]{1,0:T(8,128)(2,1)} %copy-done.1) | copy-start | bytes 786436
  78.8 8.8 %collective-permute-start.12 = (bf16[48,2304]{1,0:T(8,128)(2,1)S(1)}, bf16[48,2304]{1,0:T(8,128)(2,1)S(1)}, u32[]{:S(2)}, u32[]{:S(2)}) collective-permute-start(bf16[48,2304]{1,0:T(8,128)(2,1)S(1)} %get-tuple-element.48), channel_id=1, source_target_pairs={{0,16},{16,32},{32,48},{48,64},{64,80},{80,96},{96,112},{112,0},{1... | collective-permute-start | bytes 663560 | tf_op jit(solution)/shard_map/ppermute | solution.py:34
  78.9 8.7 %collective-permute-start.13 = (bf16[48,2304]{1,0:T(8,128)(2,1)S(1)}, bf16[48,2304]{1,0:T(8,128)(2,1)S(1)}, u32[]{:S(2)}, u32[]{:S(2)}) collective-permute-start(bf16[48,2304]{1,0:T(8,128)(2,1)S(1)} %get-tuple-element.49), channel_id=1, source_target_pairs={{0,112},{16,0},{32,16},{48,32},{64,48},{80,64},{96,80},{112,96},{1... | collective-permute-start | bytes 663560 | tf_op jit(solution)/shard_map/ppermute | solution.py:34
  87.7 8.9 %collective-permute-start.14 = (bf16[48,2304]{1,0:T(8,128)(2,1)S(1)}, bf16[48,2304]{1,0:T(8,128)(2,1)S(1)}, u32[]{:S(2)}, u32[]{:S(2)}) collective-permute-start(bf16[48,2304]{1,0:T(8,128)(2,1)S(1)} %convert_element_type.154), channel_id=1, source_target_pairs={{0,128},{16,144},{32,160},{48,176},{64,192},{80,208},{96,224},{112... | collective-permute-start | bytes 663560 | tf_op jit(solution)/shard_map/ppermute | solution.py:87
  88.5 16.9 %all-to-all-start.1 = ((bf16[4,512,256]{2,1,0:T(8,128)(2,1)}), bf16[4,512,256]{2,1,0:T(8,128)(2,1)}, u32[]{:S(2)}, u32[]{:S(2)}) async-start(bf16[4,512,256]{2,1,0:T(8,128)(2,1)} %bitcast.34), calls=%async_computation.1 | async-start | bytes 2097152 | tf_op jit(solution)/shard_map/all_to_all | solution.py:55
  96.8 8.6 %collective-permute-start.15 = (bf16[48,2304]{1,0:T(8,128)(2,1)S(1)}, bf16[48,2304]{1,0:T(8,128)(2,1)S(1)}, u32[]{:S(2)}, u32[]{:S(2)}) collective-permute-start(bf16[48,2304]{1,0:T(8,128)(2,1)S(1)} %pad_maximum_fusion.8.refs_0_), channel_id=1, source_target_pairs={{0,16},{16,32},{32,48},{48,64},{64,80},{80,96},{96,112},{112,0},{1... | collective-permute-start | bytes 663560 | tf_op jit(solution)/shard_map/ppermute | solution.py:34
  96.9 8.5 %collective-permute-start.16 = (bf16[48,2304]{1,0:T(8,128)(2,1)S(1)}, bf16[48,2304]{1,0:T(8,128)(2,1)S(1)}, u32[]{:S(2)}, u32[]{:S(2)}) collective-permute-start(bf16[48,2304]{1,0:T(8,128)(2,1)S(1)} %pad_maximum_fusion.8.refs_0_), channel_id=1, source_target_pairs={{0,112},{16,0},{32,16},{48,32},{64,48},{80,64},{96,80},{112,96},{1... | collective-permute-start | bytes 663560 | tf_op jit(solution)/shard_map/ppermute | solution.py:34
  100.2 8.1 %collective-permute-start.11 = (bf16[512,128]{1,0:T(8,128)(2,1)S(1)}, bf16[512,128]{1,0:T(8,128)(2,1)}, u32[]{:S(2)}, u32[]{:S(2)}) collective-permute-start(bf16[512,128]{1,0:T(8,128)(2,1)S(1)} %slice.329), channel_id=1, source_target_pairs={{0,1},{1,0},{2,3},{3,2},{4,5},{5,4},{6,7},{7,6},{8,9},{9,8},{10,11... | collective-permute-start | bytes 393224 | tf_op jit(solution)/shard_map/ppermute | solution.py:28
  105.4 7.5 %copy-start.3 = (bf16[48,2304]{1,0:T(8,128)(2,1)}, bf16[48,2304]{1,0:T(8,128)(2,1)S(1)}, u32[]{:S(2)}) copy-start(bf16[48,2304]{1,0:T(8,128)(2,1)S(1)} %collective-permute-done.16.refs_1_) | copy-start | bytes 663556
  106.9 6.0 %collective-permute-start.17 = (bf16[256,256]{1,0:T(8,128)(2,1)S(1)}, bf16[256,256]{1,0:T(8,128)(2,1)S(1)}, u32[]{:S(2)}, u32[]{:S(2)}) collective-permute-start(bf16[256,256]{1,0:T(8,128)(2,1)S(1)} %slice.328), channel_id=1, source_target_pairs={{0,16},{16,0},{32,48},{48,32},{64,80},{80,64},{96,112},{112,96},{1... | collective-permute-start | bytes 393224 | tf_op jit(solution)/shard_map/ppermute | solution.py:63
  108.3 8.0 %collective-permute-start.21 = (bf16[48,2304]{1,0:T(8,128)(2,1)S(1)}, bf16[48,2304]{1,0:T(8,128)(2,1)S(1)}, u32[]{:S(2)}, u32[]{:S(2)}) collective-permute-start(bf16[48,2304]{1,0:T(8,128)(2,1)S(1)} %collective-permute-done.16.refs_1_), channel_id=1, source_target_pairs={{0,112},{16,0},{32,16},{48,32},{64,48},{80,64},{96,80},{112,96},{1... | collective-permute-start | bytes 663560 | tf_op jit(solution)/shard_map/ppermute | solution.py:34
  109.8 7.1 %collective-permute-start.22 = (bf16[48,2304]{1,0:T(8,128)(2,1)S(1)}, bf16[48,2304]{1,0:T(8,128)(2,1)S(1)}, u32[]{:S(2)}, u32[]{:S(2)}) collective-permute-start(bf16[48,2304]{1,0:T(8,128)(2,1)S(1)} %collective-permute-done.15.refs_8_), channel_id=1, source_target_pairs={{0,16},{16,32},{32,48},{48,64},{64,80},{80,96},{96,112},{112,0},{1... | collective-permute-start | bytes 663560 | tf_op jit(solution)/shard_map/ppermute | solution.py:34
  113.6 6.0 %collective-permute-start.18 = (bf16[128,256]{1,0:T(8,128)(2,1)}, bf16[128,256]{1,0:T(8,128)(2,1)S(1)}, u32[]{:S(2)}, u32[]{:S(2)}) collective-permute-start(bf16[128,256]{1,0:T(8,128)(2,1)} %slice.330), channel_id=1, source_target_pairs={{0,128},{16,144},{32,160},{48,176},{64,192},{80,208},{96,224},{112... | collective-permute-start | bytes 196616 | tf_op jit(solution)/shard_map/ppermute | solution.py:63
  116.3 15.3 %copy-start.4 = (bf16[48,2304]{1,0:T(8,128)(2,1)S(1)}, bf16[48,2304]{1,0:T(8,128)(2,1)}, u32[]{:S(2)}) copy-start(bf16[48,2304]{1,0:T(8,128)(2,1)} %copy-done.3) | copy-start | bytes 663556
  116.9 6.2 %collective-permute-start.23 = (bf16[48,2304]{1,0:T(8,128)(2,1)S(1)}, bf16[48,2304]{1,0:T(8,128)(2,1)S(1)}, u32[]{:S(2)}, u32[]{:S(2)}) collective-permute-start(bf16[48,2304]{1,0:T(8,128)(2,1)S(1)} %collective-permute-done.21.refs_2_), channel_id=1, source_target_pairs={{0,112},{16,0},{32,16},{48,32},{64,48},{80,64},{96,80},{112,96},{1... | collective-permute-start | bytes 663560 | tf_op jit(solution)/shard_map/ppermute | solution.py:34
  118.4 7.1 %collective-permute-start.24 = (bf16[48,2304]{1,0:T(8,128)(2,1)S(1)}, bf16[48,2304]{1,0:T(8,128)(2,1)S(1)}, u32[]{:S(2)}, u32[]{:S(2)}) collective-permute-start(bf16[48,2304]{1,0:T(8,128)(2,1)S(1)} %collective-permute-done.22.refs_7_), channel_id=1, source_target_pairs={{0,16},{16,32},{32,48},{48,64},{64,80},{80,96},{96,112},{112,0},{1... | collective-permute-start | bytes 663560 | tf_op jit(solution)/shard_map/ppermute | solution.py:34
  119.6 9.4 %collective-permute-start.19 = (f32[64,256]{1,0:T(8,128)S(1)}, f32[64,256]{1,0:T(8,128)S(1)}, u32[]{:S(2)}, u32[]{:S(2)}) collective-permute-start(f32[64,256]{1,0:T(8,128)S(1)} %slice.260), channel_id=1, source_target_pairs={{0,32},{16,48},{32,0},{48,16},{64,96},{80,112},{96,64},{112,80},{1... | collective-permute-start | bytes 196616 | tf_op jit(solution)/shard_map/ppermute | solution.py:63
  125.6 6.0 %collective-permute-start.25 = (bf16[48,1152]{1,0:T(8,128)(2,1)S(1)}, bf16[48,1152]{1,0:T(8,128)(2,1)S(1)}, u32[]{:S(2)}, u32[]{:S(2)}) collective-permute-start(bf16[48,1152]{1,0:T(8,128)(2,1)S(1)} %slice.228), channel_id=1, source_target_pairs={{0,16},{16,32},{32,48},{48,64},{64,80},{80,96},{96,112},{112,0},{1... | collective-permute-start | bytes 331784 | tf_op jit(solution)/shard_map/ppermute | solution.py:34
  125.7 5.9 %collective-permute-start.26 = (bf16[48,1152]{1,0:T(8,128)(2,1)S(1)}, bf16[48,1152]{1,0:T(8,128)(2,1)S(1)}, u32[]{:S(2)}, u32[]{:S(2)}) collective-permute-start(bf16[48,1152]{1,0:T(8,128)(2,1)S(1)} %slice.229), channel_id=1, source_target_pairs={{0,112},{16,0},{32,16},{48,32},{64,48},{80,64},{96,80},{112,96},{1... | collective-permute-start | bytes 331784 | tf_op jit(solution)/shard_map/ppermute | solution.py:34
  132.2 6.0 %collective-permute-start.27 = (bf16[384,128]{1,0:T(8,128)(2,1)S(1)}, bf16[384,128]{1,0:T(8,128)(2,1)S(1)}, u32[]{:S(2)}, u32[]{:S(2)}) collective-permute-start(bf16[384,128]{1,0:T(8,128)(2,1)S(1)} %get-tuple-element.63), channel_id=1, source_target_pairs={{0,8},{8,0},{1,9},{9,1},{2,10},{10,2},{3,11},{11,3},{4,12},{12,4},... | collective-permute-start | bytes 294920 | tf_op jit(solution)/shard_map/ppermute | solution.py:424
  134.0 7.8 %collective-permute-start.20 = (f32[32,256]{1,0:T(8,128)S(1)}, f32[32,256]{1,0:T(8,128)S(1)}, u32[]{:S(2)}, u32[]{:S(2)}) collective-permute-start(f32[32,256]{1,0:T(8,128)S(1)} %slice.262), channel_id=1, source_target_pairs={{0,64},{16,80},{32,96},{48,112},{64,0},{80,16},{96,32},{112,48},{1... | collective-permute-start | bytes 98312 | tf_op jit(solution)/shard_map/ppermute | solution.py:63
  138.3 5.7 %collective-permute-start.28 = (bf16[1,4,48,128]{3,2,1,0:T(8,128)(2,1)S(1)}, bf16[1,4,48,128]{3,2,1,0:T(8,128)(2,1)S(1)}, u32[]{:S(2)}, u32[]{:S(2)}) collective-permute-start(bf16[1,4,48,128]{3,2,1,0:T(8,128)(2,1)S(1)} %get-tuple-element.99), channel_id=1, source_target_pairs={{0,4},{1,5},{2,6},{3,7},{4,0},{5,1},{6,2},{7,3},{8,12},{9,13},{10,... | collective-permute-start | bytes 147464 | tf_op jit(solution)/shard_map/ppermute | solution.py:72
  144.0 4.2 %collective-permute-start.29 = (bf16[2,2,48,128]{3,2,1,0:T(8,128)(2,1)S(1)}, bf16[2,2,48,128]{3,2,1,0:T(8,128)(2,1)S(1)}, u32[]{:S(2)}, u32[]{:S(2)}) collective-permute-start(bf16[2,2,48,128]{3,2,1,0:T(8,128)(2,1)S(1)} %get-tuple-element.97), channel_id=1, source_target_pairs={{0,2},{1,3},{2,0},{3,1},{4,6},{5,7},{6,4},{7,5},{8,10},{9,11},{10,... | collective-permute-start | bytes 147464 | tf_op jit(solution)/shard_map/ppermute | solution.py:72
  148.2 4.2 %collective-permute-start.30 = (bf16[4,1,48,128]{3,2,0,1:T(8,128)(2,1)S(1)}, bf16[4,1,48,128]{3,2,0,1:T(8,128)(2,1)S(1)}, u32[]{:S(2)}, u32[]{:S(2)}) collective-permute-start(bf16[4,1,48,128]{3,2,0,1:T(8,128)(2,1)S(1)} %get-tuple-element.95), channel_id=1, source_target_pairs={{0,1},{1,0},{2,3},{3,2},{4,5},{5,4},{6,7},{7,6},{8,9},{9,8},{10,11... | collective-permute-start | bytes 147464 | tf_op jit(solution)/shard_map/ppermute | solution.py:72
  150.6 1.8 %copy-start.13 = (pred[512,8,48]{0,2,1:T(8,128)(4,1)S(1)}, pred[512,8,48]{0,2,1:T(8,128)(4,1)}, u32[]{:S(2)}) copy-start(pred[512,8,48]{0,2,1:T(8,128)(4,1)} %fusion) | copy-start | bytes 589828

commit v10 on v9

--- a/solution.py
+++ b/solution.py
@@ -34,25 +34,25 @@
     return lax.ppermute(block, "ctx", pairs)
 
 
-def key_groups():
-    exps = lax.axis_size("exp")
-    pairs = lax.axis_size("ctx") * exps
-    return [[i for i in range(pairs) if i % X_LO == x] for x in range(X_LO)]
-
-
-def key_gather(block):
-    copies = jnp.broadcast_to(block[None], (len(key_groups()[0]),) + block.shape)
-    got = lax.all_to_all(
-        copies, ("ctx", "exp"), 0, 0, tiled=True, axis_index_groups=key_groups()
-    )
-    return got.reshape(-1, block.shape[1])
+def y_groups():
+    n = lax.axis_size("exp")
+    return [list(range(x, n, X_LO)) for x in range(X_LO)]
+
+
+def ctx_gather(block):
+    copies = jnp.broadcast_to(block[None], (lax.axis_size("ctx"),) + block.shape)
+    return lax.all_to_all(copies, "ctx", 0, 0, tiled=True)
+
+
+def y_gather(block):
+    copies = jnp.broadcast_to(block[None], (len(y_groups()[0]),) + block.shape)
+    got = lax.all_to_all(copies, "exp", 0, 0, tiled=True, axis_index_groups=y_groups())
+    return got.reshape(-1, block.shape[-1])
 
 
 def y_parts(both):
-    n = lax.axis_size("exp")
-    groups = [list(range(x, n, X_LO)) for x in range(X_LO)]
-    parts = both.reshape(n // X_LO, -1, both.shape[1])
-    return lax.all_to_all(parts, "exp", 0, 0, tiled=True, axis_index_groups=groups)
+    parts = both.reshape(len(y_groups()[0]), -1, both.shape[1])
+    return lax.all_to_all(parts, "exp", 0, 0, tiled=True, axis_index_groups=y_groups())
 
 
 def ctx_sum(both, masks):
@@ -72,10 +72,12 @@
     return lax.ppermute(block, "exp", [(e, e ^ mask) for e in range(lax.axis_size("exp"))])
 
 
-def exchange(blocks):
+def exchange(blocks, waits):
     shape = blocks.shape
     bits = shape[0].bit_length() - 1
     for bit in range(bits):
+        if bit == bits - 1:
+            blocks = after(blocks, waits)
         blocks = blocks.reshape((2**bit, 2, -1) + shape[1:])
         got = partner(blocks[:, 1], 2 ** (bits - 1 - bit))
         blocks = jnp.stack([blocks[:, 0], got], axis=1)
@@ -135,7 +137,7 @@
     return lax.dynamic_slice_in_dim(twice, places, blocks.shape[0], 0)
 
 
-def scores_of(step, own, rows, tokens, here_ref, k, q):
+def scores_of(step, own, ctx_size, tokens, here_ref, k, q):
     lanes = q.shape[0]
     found = lax.dot_general(k, q, (((1,), (1,)), ((), ())), preferred_element_type=F32)
     ahead = lax.broadcasted_iota(jnp.int32, (own, lanes), 1) % tokens - lax.broadcasted_iota(
@@ -146,7 +148,8 @@
     masked = []
     for part in range(parts):
         place = step * parts + part
-        start = (here_ref[2] + place // rows) * tokens + (place % rows * X_LO + side) * own
+        at = (here_ref[2] + place // ctx_size) * X_LO + side
+        start = place % ctx_size * tokens + at * own
         masked.append(
             jnp.where(
                 ahead >= start - me * tokens,
@@ -157,7 +160,7 @@
     return jnp.concatenate(masked, axis=0)
 
 
-def stats_body(own, rows, tokens, here_ref, q_ref, g_ref, kv_ref, stats_ref):
+def stats_body(own, ctx_size, tokens, here_ref, q_ref, g_ref, kv_ref, stats_ref):
     size = kv_ref.shape[1] // 2
     lanes = q_ref.shape[0]
     chunk = 8 * own
@@ -165,7 +168,7 @@
     def one(step, held):
         top, norm, delta = held
         at = pl.ds(pl.multiple_of(step * chunk, chunk), chunk)
-        scores = scores_of(step, own, rows, tokens, here_ref, kv_ref[at, :size], q_ref[...])
+        scores = scores_of(step, own, ctx_size, tokens, here_ref, kv_ref[at, :size], q_ref[...])
         dprob = lax.dot_general(
             kv_ref[at, size:], g_ref[...], (((1,), (1,)), ((), ())), preferred_element_type=F32
         )
@@ -188,7 +191,7 @@
 
 
 def grads_body(
-    own, rows, tokens, here_ref, q_ref, g_ref, kv_ref, stats_ref, far_ref, *refs
+    own, ctx_size, tokens, here_ref, q_ref, g_ref, kv_ref, stats_ref, far_ref, *refs
 ):
     before, (both_ref, dq_ref) = refs[:-2], refs[-2:]
     both_ref[...] = before[0][...] if before else jnp.zeros_like(both_ref)
@@ -205,7 +208,7 @@
     def one(step, total):
         at = pl.ds(pl.multiple_of(step * chunk, chunk), chunk)
         k = kv_ref[at, :size]
-        scores = scores_of(step, own, rows, tokens, here_ref, k, q_ref[...])
+        scores = scores_of(step, own, ctx_size, tokens, here_ref, k, q_ref[...])
         prob = jnp.exp(scores - top) * inverse
         value = jnp.dot(prob.astype(BF), g_ref[...], preferred_element_type=F32).astype(BF)
         dprob = lax.dot_general(
@@ -215,10 +218,11 @@
         key = jnp.dot(dscore, q_ref[...], preferred_element_type=F32).astype(BF)
         for part in range(8):
             place = step * 8 + part
-            i = place_of((here_ref[2] + place // rows) ^ here_ref[0])
+            y = here_ref[2] + place // ctx_size
+            i = place_of(place % ctx_size ^ here_ref[0])
             piece = slice(part * own, (part + 1) * own)
-            both_ref[place % rows, i, :, :size] = key[piece]
-            both_ref[place % rows, i, :, size:] = value[piece]
+            both_ref[y, i, :, :size] = key[piece]
+            both_ref[y, i, :, size:] = value[piece]
         return total + lax.dot_general(
             k, dscore, (((0,), (0,)), ((), ())), preferred_element_type=F32
         )
@@ -240,7 +244,7 @@
 def attention_stats(own, tokens, queries, grads, flat):
     keys, lanes = flat.shape[0], queries.shape[0]
     return pl.pallas_call(
-        functools.partial(stats_body, own, lax.axis_size("exp") // X_LO, tokens),
+        functools.partial(stats_body, own, lax.axis_size("ctx"), tokens),
         out_shape=jax.ShapeDtypeStruct((8, lanes), F32),
         in_specs=[SMEM, VMEM, VMEM, VMEM],
         out_specs=VMEM,
@@ -259,7 +263,7 @@
     size = flat.shape[1] // 2
     rows = lax.axis_size("exp") // X_LO
     return pl.pallas_call(
-        functools.partial(grads_body, own, rows, tokens),
+        functools.partial(grads_body, own, lax.axis_size("ctx"), tokens),
         out_shape=(
             jax.ShapeDtypeStruct((rows, lax.axis_size("ctx"), own, 2 * size), BF),
             jax.ShapeDtypeStruct((lanes, size), F32),
@@ -287,7 +291,7 @@
     return grad_key, grad_value
 
 
-def select(moe_input, moe_grad, expert_ids, router_weight):
+def select(moe_input, moe_grad, expert_ids, router_weight, near):
     width = moe_input.shape[1]
     exp_size = lax.axis_size("exp")
     labels = lax.axis_index("exp") ^ jnp.arange(exp_size)
@@ -304,7 +308,7 @@
     picked = jnp.einsum("bs,bd->sd", placed_low, rows, preferred_element_type=F32)
     scaled = picked[:, width:] * slot_weight.reshape(-1, 1)
     sent = jnp.concatenate([picked[:, :width].astype(BF), scaled.astype(BF)], axis=1)
-    got = exchange(sent.reshape(exp_size, CAP, 2 * width))
+    got = exchange(sent.reshape(exp_size, CAP, 2 * width), near)
     return placed_low, got
 
 
@@ -334,7 +338,7 @@
     return jnp.concatenate([hidden, d_gate, d_up], axis=1)
 
 
-def contrib_body(width, half_ref, gate_ref, up_ref, *refs):
+def contrib_body(width, here_ref, gate_ref, up_ref, *refs):
     blocks, (mine_ref, other_ref, full_ref) = refs[:-3], refs[-3:]
     height = blocks[0].shape[0]
     units = full_ref.shape[1] // 3
@@ -354,9 +358,34 @@
     found = lax.dot_general(
         full_ref[:, units : 2 * units], gate_ref[...], across, preferred_element_type=F32
     ) + lax.dot_general(full_ref[:, 2 * units :], up_ref[...], across, preferred_element_type=F32)
-    first = half_ref[0] == 0
-    mine_ref[...] = jnp.where(first, found[:, :width], found[:, width:])
-    other_ref[...] = jnp.where(first, found[:, width:], found[:, :width]).astype(BF)
+    first = here_ref[0] == 0
+    mine = jnp.where(first, found[:, :width], found[:, width:])
+    other = jnp.where(first, found[:, width:], found[:, :width]).astype(BF)
+    count = mine_ref.shape[0]
+    for j in range(count):
+        to = (j + here_ref[1]) % count ^ here_ref[2]
+        mine_ref[to] = mine[j * height : (j + 1) * height]
+        other_ref[to] = other[j * height : (j + 1) * height]
+
+
+def order_body(here_ref, back_ref, rows_ref):
+    count, height, _ = back_ref.shape
+    for j in range(count):
+        rows_ref[j * height : (j + 1) * height, :] = back_ref[j ^ here_ref[0]]
+
+
+def ordered(back_rows):
+    count, height, columns = back_rows.shape
+    return pl.pallas_call(
+        order_body,
+        out_shape=jax.ShapeDtypeStruct((count * height, columns), BF),
+        in_specs=[SMEM, VMEM],
+        out_specs=VMEM,
+        cost_estimate=pl.CostEstimate(
+            flops=0, bytes_accessed=4 * back_rows.size, transcendentals=0
+        ),
+        name="order_rows",
+    )(lax.axis_index("exp").astype(jnp.int32).reshape(1), back_rows)
 
 
 def weights_body(full_ref, input_ref, grad_ref, gate_ref, up_ref, down_ref):
@@ -375,11 +404,14 @@
     rows = len(blocks) // 2 * 2 * blocks[0].shape[0]
     columns = gate_mat.shape[0] // lax.axis_size("head")
     whole = blocks[0].shape[1]
+    count = len(blocks) // 2 * 2
+    at = lax.axis_index("ctx") % (lax.axis_size("ctx") // X_HI)
+    here = jnp.stack([lax.axis_index("head"), at, lax.axis_index("exp")])
     return pl.pallas_call(
         functools.partial(contrib_body, columns),
         out_shape=(
-            jax.ShapeDtypeStruct((rows, columns), F32),
-            jax.ShapeDtypeStruct((rows, columns), BF),
+            jax.ShapeDtypeStruct((count, rows // count, columns), F32),
+            jax.ShapeDtypeStruct((count, rows // count, columns), BF),
             jax.ShapeDtypeStruct((rows, whole), BF),
         ),
         in_specs=[SMEM] + [VMEM] * (2 + len(blocks)),
@@ -391,7 +423,7 @@
             transcendentals=0,
         ),
         name="expert_contrib",
-    )(lax.axis_index("head").astype(jnp.int32).reshape(1), gate_mat, up_mat, *blocks)
+    )(here.astype(jnp.int32), gate_mat, up_mat, *blocks)
 
 
 def weight_grads(full, input_rows, grad_rows):
@@ -416,17 +448,10 @@
 
 
 def finish(blocks, input_rows, grad_rows, gate_mat, up_mat, placed_low):
-    exp_size = lax.axis_size("exp")
-    ring = lax.axis_size("ctx") // X_HI
-    at = lax.axis_index("ctx") % ring
     mine, other, full = contributions(blocks, gate_mat, up_mat)
-    columns = mine.shape[1]
     mine = (mine + lax.ppermute(other, "head", [(0, 1), (1, 0)]).astype(F32)).astype(BF)
-    mine = turn(mine.reshape(ring, -1, columns), (ring - at) % ring).reshape(exp_size, CAP, columns)
-    back_rows = exchange(mine)
-    grad_input = jnp.dot(
-        placed_low, back_rows.reshape(-1, columns), preferred_element_type=F32
-    ).astype(BF)
+    back_rows = lax.all_to_all(mine, "exp", 0, 0, tiled=True)
+    grad_input = jnp.dot(placed_low, ordered(back_rows), preferred_element_type=F32).astype(BF)
     return (grad_input,) + tuple(weight_grads(after(full, mine), input_rows, grad_rows))
 
 
@@ -447,8 +472,9 @@
     rows = tokens * queries.shape[1]
     size = queries.shape[2]
     pair = jnp.concatenate([key_rows[:, 0, :], value_vector_rows[:, 0, :]], axis=1)
-    flat = key_gather(pair)
-    placed_low, got = select(moe_input, moe_grad, expert_ids, router_weight)
+    near = ctx_gather(pair)
+    placed_low, got = select(moe_input, moe_grad, expert_ids, router_weight, near)
+    flat = y_gather(near)
     mine = jnp.concatenate([by_head(queries), by_head(grad_attn)], axis=0)
     theirs = beside(mine)
     queries = jnp.concatenate([mine[:rows], theirs[:rows]], axis=0)
@@ -457,16 +483,16 @@
         got, gate_weight, up_weight, down_weight
     )
     onward, back = both_after(*sum_start(parts), theirs)
+    onward, back = sum_step(z_move, parts, 0, onward, back)
+    onward, back = both_after(onward, back, flat)
     stats = attention_stats(own, tokens, queries, grads, after(flat, onward, back))
-    onward, back = sum_step(z_move, parts, 0, onward, back)
+    onward, back = sum_step(z_move, parts, 1, onward, back)
     onward, back = both_after(onward, back, stats)
     far_stats = beside(stats)
-    onward, back = sum_step(z_move, parts, 1, onward, back)
-    onward, back = both_after(onward, back, far_stats)
     half = flat.shape[0] // 2
-    middle = lax.axis_size("ctx") // 2
+    middle = lax.axis_size("exp") // X_LO // 2
     lower = attention_grads(
-        own, tokens, 0, queries, grads, after(flat[:half], onward, back), stats, far_stats
+        own, tokens, 0, queries, grads, flat[:half], after(stats, onward, back), far_stats
     )
     onward, back = sum_step(z_move, parts, 2, onward, back)
     onward, back = both_after(onward, back, *lower)

time: 154 us -> 160 us (1.039); the launches traced: 153 us -> 157 us
  waiting for transfers between devices: 47.6 us -> 40.1 us
  starting transfers between devices: 66.8 us -> 70.9 us
  local copies, waits for them, and re-layouts: 7.16 us -> 10.3 us
  Pallas kernels: 17 us -> 19.1 us
    all_to_all x2 -> x4, waiting for transfers between devices: 0.98 us -> 17.7 us  [the longest x1 8.95 us: y_gather(): lax.all_to_all(copies, 'exp', 0, 0, tiled=True, axis_index_groups=y_group...]
    ppermute x16, waiting for transfers between devices: 23.5 us -> 9.89 us  [z_move(): return lax.ppermute(block, 'ctx', pairs)]
    ppermute x6 -> x3, waiting for transfers between devices: 14.7 us -> 6.13 us  [partner(): lax.ppermute(block, 'exp', [(e, e ^ mask) for e in range(lax.axis_size('e...]
    ppermute x6 -> x3, starting transfers between devices: 12.2 us -> 5.57 us  [partner(): lax.ppermute(block, 'exp', [(e, e ^ mask) for e in range(lax.axis_size('e...]
    all_to_all x2 -> x4, starting transfers between devices: 16.1 us -> 21.8 us  [the longest x1 10.1 us: ctx_gather(): return lax.all_to_all(copies, 'ctx', 0, 0, tiled=True)]
    unnamed x37 -> x42, local copies, waits for them, and re-layouts: 0.12 us -> 4.47 us
    ppermute x4, starting transfers between devices: 9.93 us -> 12.8 us  [ctx_sum(): both = both[:half] + lax.ppermute(sent, 'ctx', pairs).astype(F32)]
    ppermute x1, waiting for transfers between devices: 3.91 us -> 1.39 us  [opposite(): lax.ppermute(block, 'ctx', [(c, (c + n // X_HI) % n) for c in range(n)])]
  transfers between devices with their start and end apart: 33 -> 32, of which waited for: 19 -> 15; matrix products, arithmetic and copies ran while one was open for 9% -> 7% of each run, Pallas kernels for 8% -> 10%
where the time goes in v10:
time: 160 us; the launch traced here: 157 us
  starting transfers between devices  70.9 us (44%)
  waiting for transfers between devices  40.1 us (25%)
  Pallas kernels  19.1 us (12%)
  other arithmetic  11.2 us (7%)
  local copies, waits for them, and re-layouts  10.3 us (6%)
  matrix products  4.32 us (3%)
    ppermute x16, starting transfers between devices, z_move(): return lax.ppermute(block, 'ctx', pairs)  24.7 us
    ppermute x4, starting transfers between devices, ctx_sum(): both = both[:half] + lax.ppermute(sent, 'ctx', pairs).astype(F32)  12.8 us
    pallas_call x2, Pallas kernels, attention_grads(): pl.pallas_call(functools.partial(grads_body, own, lax.axis_size('ctx'), t...  10.2 us
    all_to_all x1, starting transfers between devices, ctx_gather(): return lax.all_to_all(copies, 'ctx', 0, 0, tiled=True)  10.1 us
    ppermute x16, waiting for transfers between devices, z_move(): return lax.ppermute(block, 'ctx', pairs)  9.89 us
    all_to_all x1, waiting for transfers between devices, y_gather(): lax.all_to_all(copies, 'exp', 0, 0, tiled=True, axis_index_groups=y_group...  8.95 us
    ppermute x3, waiting for transfers between devices, partner(): lax.ppermute(block, 'exp', [(e, e ^ mask) for e in range(lax.axis_size('e...  6.13 us
    ppermute x3, starting transfers between devices, partner(): lax.ppermute(block, 'exp', [(e, e ^ mask) for e in range(lax.axis_size('e...  5.57 us
  transfers between devices with their start and end apart: 32, of which 15 were waited for; matrix products, arithmetic and copies ran while one was open for 7% of the time, Pallas kernels for 10%

profile of v10, /device:TPU:2, one launch (start us, length us, event | category | flops | bytes accessed | tf_op | source)
XLA Modules:
  0.0 157.1 jit_solution(13479532802507357023)
XLA Ops:
  0.7 0.9 fusion.19
  1.6 1.1 reduce-window.6
  3.0 0.8 fusion.20
  4.5 1.4 fusion.2
  6.2 3.3 %collective-permute-start.1 = (bf16[1,4,48,512]{3,2,1,0:T(8,128)(2,1)S(1)}, bf16[1,4,48,512]{3,2,1,0:T(8,128)(2,1)S(1)}, u32[]{:S(2)}, u32[]{:S(2)}) collective-permute-start(bf16[1,4,48,512]{3,2,1,0:T(8,128)(2,1)S(1)} %get-tuple-element.93), channel_id=1, source_target_pairs={{0,4},{1,5},{2,6},{3,7},{4,0},{5,1},{6,2},{7,3},{8,12},{9,13},{10,... | collective-permute-start | bytes 589832 | tf_op jit(solution)/shard_map/ppermute | solution.py:72
  9.5 0.7 broadcast_in_dim.32
  10.2 10.1 %all-to-all-start = ((bf16[16,32,256]{2,1,0:T(8,128)(2,1)}), bf16[16,32,256]{2,1,0:T(8,128)(2,1)S(1)}, u32[]{:S(2)}, u32[]{:S(2)}) async-start(bf16[16,32,256]{2,1,0:T(8,128)(2,1)} %broadcast_in_dim.32), calls=%async_computation | async-start | bytes 524288 | tf_op jit(solution)/shard_map/all_to_all | solution.py:44
  20.4 0.8 collective-permute-start.2
  21.3 0.6 copy-done.15
  21.9 1.5 collective-permute-start
  23.5 3.1 %collective-permute-done.2 = bf16[2,2,48,512]{3,2,1,0:T(8,128)(2,1)S(1)} collective-permute-done((bf16[2,2,48,512]{3,2,1,0:T(8,128)(2,1)S(1)}, bf16[2,2,48,512]{3,2,1,0:T(8,128)(2,1)S(1)}, u32[]{:S(2)}, u32[]{:S(2)}) %collective-permute-start.2) | collective-permute-done | bytes 196640 | tf_op jit(solution)/shard_map/ppermute | solution.py:72
  26.6 5.0 %all-to-all-done = bf16[16,32,256]{2,1,0:T(8,128)(2,1)S(1)} async-done(((bf16[16,32,256]{2,1,0:T(8,128)(2,1)}), bf16[16,32,256]{2,1,0:T(8,128)(2,1)S(1)}, u32[]{:S(2)}, u32[]{:S(2)}) %all-to-all-start) | async-done | bytes 262176 | tf_op jit(solution)/shard_map/all_to_all | solution.py:44
  31.7 1.5 collective-permute-start.3
  33.3 1.2 dynamic-slice_bitcast_fusion
  34.5 3.0 %collective-permute-done.3 = bf16[4,1,48,512]{3,2,0,1:T(8,128)(2,1)S(1)} collective-permute-done((bf16[4,1,48,512]{3,2,0,1:T(8,128)(2,1)S(1)}, bf16[4,1,48,512]{3,2,0,1:T(8,128)(2,1)S(1)}, u32[]{:S(2)}, u32[]{:S(2)}) %collective-permute-start.3) | collective-permute-done | bytes 196640 | tf_op jit(solution)/shard_map/ppermute | solution.py:72
  38.8 0.8 pad_maximum_fusion.11
  39.6 2.1 %collective-permute-start.4 = (bf16[48,1152]{1,0:T(8,128)(2,1)}, bf16[48,1152]{1,0:T(8,128)(2,1)}, u32[]{:S(2)}, u32[]{:S(2)}) collective-permute-start(bf16[48,1152]{1,0:T(8,128)(2,1)} %get-tuple-element.40), channel_id=1, source_target_pairs={{0,16},{16,32},{32,48},{48,64},{64,80},{80,96},{96,112},{112,0},{1... | collective-permute-start | bytes 331784 | tf_op jit(solution)/shard_map/ppermute | solution.py:34
  41.8 1.1 collective-permute-start.5
  42.9 0.7 fusion.32
  43.6 1.1 broadcast_in_dim.50
  44.7 3.5 %all-to-all-start.1 = ((bf16[4,16,32,256]{3,2,1,0:T(8,128)(2,1)}), bf16[4,16,32,256]{3,2,1,0:T(8,128)(2,1)S(1)}, u32[]{:S(2)}, u32[]{:S(2)}) async-start(bf16[4,16,32,256]{3,2,1,0:T(8,128)(2,1)} %broadcast_in_dim.50), calls=%async_computation.1 | async-start | bytes 2097152 | tf_op jit(solution)/shard_map/all_to_all | solution.py:49
  48.3 1.2 add_convert_fusion.5
  49.7 0.8 fusion.13
  50.5 9.0 %all-to-all-done.1 = bf16[4,16,32,256]{3,2,1,0:T(8,128)(2,1)S(1)} async-done(((bf16[4,16,32,256]{3,2,1,0:T(8,128)(2,1)}), bf16[4,16,32,256]{3,2,1,0:T(8,128)(2,1)S(1)}, u32[]{:S(2)}, u32[]{:S(2)}) %all-to-all-start.1) | async-done | bytes 1048608 | tf_op jit(solution)/shard_map/all_to_all | solution.py:49
  59.4 1.2 collective-permute-start.6
  60.6 2.0 %collective-permute-start.7 = (bf16[48,2304]{1,0:T(8,128)(2,1)}, bf16[48,2304]{1,0:T(8,128)(2,1)S(1)}, u32[]{:S(2)}, u32[]{:S(2)}) collective-permute-start(bf16[48,2304]{1,0:T(8,128)(2,1)} %get-tuple-element.43), channel_id=1, source_target_pairs={{0,112},{16,0},{32,16},{48,32},{64,48},{80,64},{96,80},{112,96},{1... | collective-permute-start | bytes 663560 | tf_op jit(solution)/shard_map/ppermute | solution.py:34
  62.7 1.1 pad_maximum_fusion.4
  63.7 4.8 %attention_stats.1.stats_ref = f32[8,1024]{1,0:T(8,128)S(1)} custom-call(s32[3]{0:T(128)S(1)} %pad_add_fusion.2.here_ref, bf16[1024,128]{1,0:T(8,128)(2,1)S(1)} %get-tuple-element.96.q_ref, bf16[1024,128]{1,0:T(8,128)(2,1)S(1)} %get-tuple-element.97.g_ref, bf16[2048,256]{1,0:T(8,128)(2,1)S(1)} %bitcast.66), custom_call_target="tpu_custom_call" | custom-call | flops 1073741824 | bytes 1048576 | tf_op jit(solution)/shard_map/attention_stats/pallas_call | solution.py:246
  68.5 1.5 collective-permute-start.10
  70.3 3.2 %collective-permute-start.9 = (bf16[48,2304]{1,0:T(8,128)(2,1)S(1)}, bf16[48,2304]{1,0:T(8,128)(2,1)S(1)}, u32[]{:S(2)}, u32[]{:S(2)}) collective-permute-start(bf16[48,2304]{1,0:T(8,128)(2,1)S(1)} %get-tuple-element.46), channel_id=1, source_target_pairs={{0,112},{16,0},{32,16},{48,32},{64,48},{80,64},{96,80},{112,96},{1... | collective-permute-start | bytes 663560 | tf_op jit(solution)/shard_map/ppermute | solution.py:34
  73.6 4.7 %attention_grads.2 = (bf16[4,16,32,256]{3,2,1,0:T(8,128)(2,1)S(1)}, f32[1024,128]{1,0:T(8,128)S(1)}) custom-call(s32[3]{0:T(128)S(1)} %pad_add_fusion.2.here_ref, bf16[1024,128]{1,0:T(8,128)(2,1)S(1)} %get-tuple-element.96.q_ref, bf16[1024,128]{1,0:T(8,128)(2,1)S(1)} %get-tuple-element.97.g_ref, bf16[1024,256]{1,0:T(8,128)(2,1)S(1)} %bitcast.68, ...), custom_call_target="tpu_custom_call" | custom-call | flops 1342177280 | bytes 1048576 | tf_op jit(solution)/shard_map/attention_grads/pallas_call | solution.py:265
  78.3 1.1 collective-permute-done.8
  79.7 3.5 %collective-permute-start.13 = (bf16[48,2304]{1,0:T(8,128)(2,1)S(1)}, bf16[48,2304]{1,0:T(8,128)(2,1)S(1)}, u32[]{:S(2)}, u32[]{:S(2)}) collective-permute-start(bf16[48,2304]{1,0:T(8,128)(2,1)S(1)} %get-tuple-element.51), channel_id=1, source_target_pairs={{0,112},{16,0},{32,16},{48,32},{64,48},{80,64},{96,80},{112,96},{1... | collective-permute-start | bytes 663560 | tf_op jit(solution)/shard_map/ppermute | solution.py:34
  83.3 5.4 %attention_grads.3 = (bf16[4,16,32,256]{3,2,1,0:T(8,128)(2,1)}, f32[1024,128]{1,0:T(8,128)S(1)}) custom-call(s32[3]{0:T(128)S(1)} %pad_add_fusion.here_ref, bf16[1024,128]{1,0:T(8,128)(2,1)S(1)} %get-tuple-element.96.q_ref, bf16[1024,128]{1,0:T(8,128)(2,1)S(1)} %get-tuple-element.97.g_ref, bf16[1024,256]{1,0:T(8,128)(2,1)S(1)} %bitcast.67, ...), custom_call_target="tpu_custom_call" | custom-call | flops 1342177280 | bytes 1048576 | tf_op jit(solution)/shard_map/attention_grads/pallas_call | solution.py:265
  88.8 1.9 %collective-permute-start.14 = (bf16[48,2304]{1,0:T(8,128)(2,1)S(1)}, bf16[48,2304]{1,0:T(8,128)(2,1)S(1)}, u32[]{:S(2)}, u32[]{:S(2)}) collective-permute-start(bf16[48,2304]{1,0:T(8,128)(2,1)S(1)} %convert_element_type.154), channel_id=1, source_target_pairs={{0,128},{16,144},{32,160},{48,176},{64,192},{80,208},{96,224},{112... | collective-permute-start | bytes 663560 | tf_op jit(solution)/shard_map/ppermute | solution.py:89
  90.7 4.2 %all-to-all-start.2 = ((bf16[4,512,256]{2,1,0:T(8,128)(2,1)}), bf16[4,512,256]{2,1,0:T(8,128)(2,1)}, u32[]{:S(2)}, u32[]{:S(2)}) async-start(bf16[4,512,256]{2,1,0:T(8,128)(2,1)} %bitcast.34), calls=%async_computation.2 | async-start | bytes 2097152 | tf_op jit(solution)/shard_map/all_to_all | solution.py:55
  95.0 1.4 collective-permute-done.14
  96.7 3.2 %collective-permute-start.16 = (bf16[48,2304]{1,0:T(8,128)(2,1)S(1)}, bf16[48,2304]{1,0:T(8,128)(2,1)S(1)}, u32[]{:S(2)}, u32[]{:S(2)}) collective-permute-start(bf16[48,2304]{1,0:T(8,128)(2,1)S(1)} %pad_maximum_fusion.8.refs_0_), channel_id=1, source_target_pairs={{0,112},{16,0},{32,16},{48,32},{64,48},{80,64},{96,80},{112,96},{1... | collective-permute-start | bytes 663560 | tf_op jit(solution)/shard_map/ppermute | solution.py:34
  99.8 3.9 %collective-permute-done.15.refs_8_ = bf16[48,2304]{1,0:T(8,128)(2,1)S(1)} collective-permute-done((bf16[48,2304]{1,0:T(8,128)(2,1)S(1)}, bf16[48,2304]{1,0:T(8,128)(2,1)S(1)}, u32[]{:S(2)}, u32[]{:S(2)}) %collective-permute-start.15) | collective-permute-done | bytes 221216 | tf_op jit(solution)/shard_map/ppermute | solution.py:34
  103.8 2.2 %all-to-all-done.2 = bf16[4,512,256]{2,1,0:T(8,128)(2,1)} async-done(((bf16[4,512,256]{2,1,0:T(8,128)(2,1)}), bf16[4,512,256]{2,1,0:T(8,128)(2,1)}, u32[]{:S(2)}, u32[]{:S(2)}) %all-to-all-start.2) | async-done | bytes 1048608 | tf_op jit(solution)/shard_map/all_to_all | solution.py:55
  105.9 1.4 convert_reduce_fusion
  107.4 1.5 collective-permute-start.17
  108.9 1.2 collective-permute-start.11
  110.1 2.7 %collective-permute-done.17 = bf16[256,256]{1,0:T(8,128)(2,1)S(1)} collective-permute-done((bf16[256,256]{1,0:T(8,128)(2,1)S(1)}, bf16[256,256]{1,0:T(8,128)(2,1)S(1)}, u32[]{:S(2)}, u32[]{:S(2)}) %collective-permute-start.17) | collective-permute-done | bytes 131104 | tf_op jit(solution)/shard_map/ppermute | solution.py:63
  112.9 1.9 %collective-permute-start.18 = (bf16[128,256]{1,0:T(8,128)(2,1)S(1)}, bf16[128,256]{1,0:T(8,128)(2,1)S(1)}, u32[]{:S(2)}, u32[]{:S(2)}) collective-permute-start(bf16[128,256]{1,0:T(8,128)(2,1)S(1)} %slice.289), channel_id=1, source_target_pairs={{0,128},{16,144},{32,160},{48,176},{64,192},{80,208},{96,224},{112... | collective-permute-start | bytes 196616 | tf_op jit(solution)/shard_map/ppermute | solution.py:63
  114.9 2.6 %collective-permute-start.21 = (bf16[48,2304]{1,0:T(8,128)(2,1)S(1)}, bf16[48,2304]{1,0:T(8,128)(2,1)S(1)}, u32[]{:S(2)}, u32[]{:S(2)}) collective-permute-start(bf16[48,2304]{1,0:T(8,128)(2,1)S(1)} %collective-permute-done.16.refs_1_), channel_id=1, source_target_pairs={{0,112},{16,0},{32,16},{48,32},{64,48},{80,64},{96,80},{112,96},{1... | collective-permute-start | bytes 663560 | tf_op jit(solution)/shard_map/ppermute | solution.py:34
  117.5 1.2 collective-permute-done.18
  118.8 4.1 %collective-permute-start.19 = (f32[64,256]{1,0:T(8,128)S(1)}, f32[64,256]{1,0:T(8,128)S(1)}, u32[]{:S(2)}, u32[]{:S(2)}) collective-permute-start(f32[64,256]{1,0:T(8,128)S(1)} %slice.236), channel_id=1, source_target_pairs={{0,32},{16,48},{32,0},{48,16},{64,96},{80,112},{96,64},{112,80},{1... | collective-permute-start | bytes 196616 | tf_op jit(solution)/shard_map/ppermute | solution.py:63
  122.9 2.4 %collective-permute-done.22.refs_7_ = bf16[48,2304]{1,0:T(8,128)(2,1)S(1)} collective-permute-done((bf16[48,2304]{1,0:T(8,128)(2,1)S(1)}, bf16[48,2304]{1,0:T(8,128)(2,1)S(1)}, u32[]{:S(2)}, u32[]{:S(2)}) %collective-permute-start.22) | collective-permute-done | bytes 221216 | tf_op jit(solution)/shard_map/ppermute | solution.py:34
  125.8 1.6 %collective-permute-start.24 = (bf16[48,2304]{1,0:T(8,128)(2,1)S(1)}, bf16[48,2304]{1,0:T(8,128)(2,1)S(1)}, u32[]{:S(2)}, u32[]{:S(2)}) collective-permute-start(bf16[48,2304]{1,0:T(8,128)(2,1)S(1)} %collective-permute-done.22.refs_7_), channel_id=1, source_target_pairs={{0,16},{16,32},{32,48},{48,64},{64,80},{80,96},{96,112},{112,0},{1... | collective-permute-start | bytes 663560 | tf_op jit(solution)/shard_map/ppermute | solution.py:34
  127.4 5.2 %collective-permute-start.20 = (f32[32,256]{1,0:T(8,128)S(1)}, f32[32,256]{1,0:T(8,128)S(1)}, u32[]{:S(2)}, u32[]{:S(2)}) collective-permute-start(f32[32,256]{1,0:T(8,128)S(1)} %slice.238), channel_id=1, source_target_pairs={{0,64},{16,80},{32,96},{48,112},{64,0},{80,16},{96,32},{112,48},{1... | collective-permute-start | bytes 98312 | tf_op jit(solution)/shard_map/ppermute | solution.py:63
  132.7 0.8 copy.42
  133.6 3.3 %collective-permute-start.26 = (bf16[48,1152]{1,0:T(8,128)(2,1)S(1)}, bf16[48,1152]{1,0:T(8,128)(2,1)S(1)}, u32[]{:S(2)}, u32[]{:S(2)}) collective-permute-start(bf16[48,1152]{1,0:T(8,128)(2,1)S(1)} %slice.211), channel_id=1, source_target_pairs={{0,112},{16,0},{32,16},{48,32},{64,48},{80,64},{96,80},{112,96},{1... | collective-permute-start | bytes 331784 | tf_op jit(solution)/shard_map/ppermute | solution.py:34
  137.1 2.4 %collective-permute-done.25.refs_4_ = bf16[48,1152]{1,0:T(8,128)(2,1)S(1)} collective-permute-done((bf16[48,1152]{1,0:T(8,128)(2,1)S(1)}, bf16[48,1152]{1,0:T(8,128)(2,1)S(1)}, u32[]{:S(2)}, u32[]{:S(2)}) %collective-permute-start.25) | collective-permute-done | bytes 110624 | tf_op jit(solution)/shard_map/ppermute | solution.py:34
  139.5 1.1 expert_contrib.1
  140.6 1.2 copy-done.1
  142.5 0.7 collective-permute-done.27
  143.2 0.7 add_convert_fusion.7
  143.8 3.9 %all-to-all-start.3 = ((bf16[8,48,128]{2,1,0:T(8,128)(2,1)}), bf16[8,48,128]{2,1,0:T(8,128)(2,1)S(1)}, u32[]{:S(2)}, u32[]{:S(2)}) async-start(bf16[8,48,128]{2,1,0:T(8,128)(2,1)} %add_convert_fusion.7), calls=%async_computation.3 | async-start | bytes 196608 | tf_op jit(solution)/shard_map/all_to_all | solution.py:453
  148.3 1.5 copy-done.2
  149.8 1.5 expert_weight_grads.1
  151.4 1.6 %all-to-all-done.3.back_ref = bf16[8,48,128]{2,1,0:T(8,128)(2,1)S(1)} async-done(((bf16[8,48,128]{2,1,0:T(8,128)(2,1)}), bf16[8,48,128]{2,1,0:T(8,128)(2,1)S(1)}, u32[]{:S(2)}, u32[]{:S(2)}) %all-to-all-start.3) | async-done | bytes 98336 | tf_op jit(solution)/shard_map/all_to_all | solution.py:453
  153.6 1.5 order_rows.1
  155.2 1.9 %convolution_convert_fusion.3 = bf16[512,128]{1,0:T(8,128)(2,1)} fusion(pred[512,384]{0,1:T(32,128)(4,1)S(1)} %fusion.1, bf16[384,128]{1,0:T(8,128)(2,1)} %order_rows.1), kind=kOutput, calls=%fused_computation.4 | convolution fusion | flops 50397184 | bytes 425984 | tf_op jit(solution)/shard_map/dot_general | solution.py:454
  (118 shorter events, 6.9 us)
Async XLA Ops:
  0.6 37.8 %copy-start = (bf16[1,1536,256]{2,1,0:T(8,128)(2,1)S(1)}, bf16[1,1536,256]{2,1,0:T(8,128)(2,1)}, u32[]{:S(2)}) copy-start(bf16[1,1536,256]{2,1,0:T(8,128)(2,1)} %param.21) | copy-start | bytes 2359300
  6.0 3.5 %copy-start.19 = (bf16[32,1,128]{2,0,1:T(8,128)(2,1)S(1)}, bf16[32,1,128]{2,0,1:T(8,128)(2,1)}, u32[]{:S(2)}) copy-start(bf16[32,1,128]{2,0,1:T(8,128)(2,1)} %param.13) | copy-start | bytes 24580
  6.0 3.5 %copy-start.20 = (bf16[32,1,128]{2,0,1:T(8,128)(2,1)S(1)}, bf16[32,1,128]{2,0,1:T(8,128)(2,1)}, u32[]{:S(2)}) copy-start(bf16[32,1,128]{2,0,1:T(8,128)(2,1)} %param.12) | copy-start | bytes 24580
  6.1 15.0 %copy-start.17 = (bf16[256,2,128]{2,1,0:T(2,128)(2,1)S(1)}, bf16[256,2,128]{2,1,0:T(2,128)(2,1)}, u32[]{:S(2)}) copy-start(bf16[256,2,128]{2,1,0:T(2,128)(2,1)} %param.11) | copy-start | bytes 393220
  6.2 15.1 %copy-start.18 = (bf16[256,2,128]{2,1,0:T(2,128)(2,1)S(1)}, bf16[256,2,128]{2,1,0:T(2,128)(2,1)}, u32[]{:S(2)}) copy-start(bf16[256,2,128]{2,1,0:T(2,128)(2,1)} %param.14) | copy-start | bytes 393220
  6.2 14.2 %collective-permute-start.1 = (bf16[1,4,48,512]{3,2,1,0:T(8,128)(2,1)S(1)}, bf16[1,4,48,512]{3,2,1,0:T(8,128)(2,1)S(1)}, u32[]{:S(2)}, u32[]{:S(2)}) collective-permute-start(bf16[1,4,48,512]{3,2,1,0:T(8,128)(2,1)S(1)} %get-tuple-element.93), channel_id=1, source_target_pairs={{0,4},{1,5},{2,6},{3,7},{4,0},{5,1},{6,2},{7,3},{8,12},{9,13},{10,... | collective-permute-start | bytes 589832 | tf_op jit(solution)/shard_map/ppermute | solution.py:72
  10.2 21.4 %all-to-all-start = ((bf16[16,32,256]{2,1,0:T(8,128)(2,1)}), bf16[16,32,256]{2,1,0:T(8,128)(2,1)S(1)}, u32[]{:S(2)}, u32[]{:S(2)}) async-start(bf16[16,32,256]{2,1,0:T(8,128)(2,1)} %broadcast_in_dim.32), calls=%async_computation | async-start | bytes 524288 | tf_op jit(solution)/shard_map/all_to_all | solution.py:44
  20.4 6.2 %collective-permute-start.2 = (bf16[2,2,48,512]{3,2,1,0:T(8,128)(2,1)S(1)}, bf16[2,2,48,512]{3,2,1,0:T(8,128)(2,1)S(1)}, u32[]{:S(2)}, u32[]{:S(2)}) collective-permute-start(bf16[2,2,48,512]{3,2,1,0:T(8,128)(2,1)S(1)} %get-tuple-element.91), channel_id=1, source_target_pairs={{0,2},{1,3},{2,0},{3,1},{4,6},{5,7},{6,4},{7,5},{8,10},{9,11},{10,... | collective-permute-start | bytes 589832 | tf_op jit(solution)/shard_map/ppermute | solution.py:72
  21.2 0.7 copy-start.15
  21.9 17.6 %collective-permute-start = (bf16[1024,128]{1,0:T(8,128)(2,1)S(1)}, bf16[1024,128]{1,0:T(8,128)(2,1)S(1)}, u32[]{:S(2)}, u32[]{:S(2)}) collective-permute-start(bf16[1024,128]{1,0:T(8,128)(2,1)S(1)} %pad_maximum_fusion.3), channel_id=1, source_target_pairs={{0,1},{1,0},{2,3},{3,2},{4,5},{5,4},{6,7},{7,6},{8,9},{9,8},{10,11... | collective-permute-start | bytes 786440 | tf_op jit(solution)/shard_map/ppermute | solution.py:28
  31.7 5.8 %collective-permute-start.3 = (bf16[4,1,48,512]{3,2,0,1:T(8,128)(2,1)S(1)}, bf16[4,1,48,512]{3,2,0,1:T(8,128)(2,1)S(1)}, u32[]{:S(2)}, u32[]{:S(2)}) collective-permute-start(bf16[4,1,48,512]{3,2,0,1:T(8,128)(2,1)S(1)} %get-tuple-element.89), channel_id=1, source_target_pairs={{0,1},{1,0},{2,3},{3,2},{4,5},{5,4},{6,7},{7,6},{8,9},{9,8},{10,11... | collective-permute-start | bytes 589832 | tf_op jit(solution)/shard_map/ppermute | solution.py:72
  37.7 0.7 copy-start.13
  38.0 41.5 %copy-start.5 = (bf16[384,768]{1,0:T(8,128)(2,1)}, bf16[384,768]{1,0:T(8,128)(2,1)S(1)}, u32[]{:S(2)}) copy-start(bf16[384,768]{1,0:T(8,128)(2,1)S(1)} %convolution_convert_fusion.2) | copy-start | bytes 1769476
  38.4 1.1 copy-start.7
  38.8 0.9 copy-start.10
  39.6 8.6 %collective-permute-start.4 = (bf16[48,1152]{1,0:T(8,128)(2,1)}, bf16[48,1152]{1,0:T(8,128)(2,1)}, u32[]{:S(2)}, u32[]{:S(2)}) collective-permute-start(bf16[48,1152]{1,0:T(8,128)(2,1)} %get-tuple-element.40), channel_id=1, source_target_pairs={{0,16},{16,32},{32,48},{48,64},{64,80},{80,96},{96,112},{112,0},{1... | collective-permute-start | bytes 331784 | tf_op jit(solution)/shard_map/ppermute | solution.py:34
  41.8 6.5 %collective-permute-start.5 = (bf16[48,1152]{1,0:T(8,128)(2,1)}, bf16[48,1152]{1,0:T(8,128)(2,1)}, u32[]{:S(2)}, u32[]{:S(2)}) collective-permute-start(bf16[48,1152]{1,0:T(8,128)(2,1)} %get-tuple-element.41), channel_id=1, source_target_pairs={{0,112},{16,0},{32,16},{48,32},{64,48},{80,64},{96,80},{112,96},{1... | collective-permute-start | bytes 331784 | tf_op jit(solution)/shard_map/ppermute | solution.py:34
  44.7 14.7 %all-to-all-start.1 = ((bf16[4,16,32,256]{3,2,1,0:T(8,128)(2,1)}), bf16[4,16,32,256]{3,2,1,0:T(8,128)(2,1)S(1)}, u32[]{:S(2)}, u32[]{:S(2)}) async-start(bf16[4,16,32,256]{3,2,1,0:T(8,128)(2,1)} %broadcast_in_dim.50), calls=%async_computation.1 | async-start | bytes 2097152 | tf_op jit(solution)/shard_map/all_to_all | solution.py:49
  48.2 1.2 copy-start.8
  48.3 1.4 copy-start.11
  59.4 10.6 %collective-permute-start.6 = (bf16[48,2304]{1,0:T(8,128)(2,1)}, bf16[48,2304]{1,0:T(8,128)(2,1)S(1)}, u32[]{:S(2)}, u32[]{:S(2)}) collective-permute-start(bf16[48,2304]{1,0:T(8,128)(2,1)} %get-tuple-element.42), channel_id=1, source_target_pairs={{0,16},{16,32},{32,48},{48,64},{64,80},{80,96},{96,112},{112,0},{1... | collective-permute-start | bytes 663560 | tf_op jit(solution)/shard_map/ppermute | solution.py:34
  60.6 9.4 %collective-permute-start.7 = (bf16[48,2304]{1,0:T(8,128)(2,1)}, bf16[48,2304]{1,0:T(8,128)(2,1)S(1)}, u32[]{:S(2)}, u32[]{:S(2)}) collective-permute-start(bf16[48,2304]{1,0:T(8,128)(2,1)} %get-tuple-element.43), channel_id=1, source_target_pairs={{0,112},{16,0},{32,16},{48,32},{64,48},{80,64},{96,80},{112,96},{1... | collective-permute-start | bytes 663560 | tf_op jit(solution)/shard_map/ppermute | solution.py:34
  63.7 6.3 %copy-start.9 = (bf16[384,768]{1,0:T(8,128)(2,1)S(1)}, bf16[384,768]{1,0:T(8,128)(2,1)}, u32[]{:S(2)}) copy-start(bf16[384,768]{1,0:T(8,128)(2,1)} %copy-done.7) | copy-start | bytes 1769476
  63.7 6.3 %copy-start.12 = (bf16[384,768]{1,0:T(8,128)(2,1)S(1)}, bf16[384,768]{1,0:T(8,128)(2,1)}, u32[]{:S(2)}) copy-start(bf16[384,768]{1,0:T(8,128)(2,1)} %copy-done.10) | copy-start | bytes 1769476
  68.5 5.1 %collective-permute-start.10 = (f32[8,1024]{1,0:T(8,128)S(1)}, f32[8,1024]{1,0:T(8,128)S(1)}, u32[]{:S(2)}, u32[]{:S(2)}) collective-permute-start(f32[8,1024]{1,0:T(8,128)S(1)} %attention_stats.1.stats_ref), channel_id=1, source_target_pairs={{0,1},{1,0},{2,3},{3,2},{4,5},{5,4},{6,7},{7,6},{8,9},{9,8},{10,11... | collective-permute-start | bytes 98312 | tf_op jit(solution)/shard_map/ppermute | solution.py:28
  70.2 9.3 %collective-permute-start.8 = (bf16[48,2304]{1,0:T(8,128)(2,1)S(1)}, bf16[48,2304]{1,0:T(8,128)(2,1)S(1)}, u32[]{:S(2)}, u32[]{:S(2)}) collective-permute-start(bf16[48,2304]{1,0:T(8,128)(2,1)S(1)} %get-tuple-element.45), channel_id=1, source_target_pairs={{0,16},{16,32},{32,48},{48,64},{64,80},{80,96},{96,112},{112,0},{1... | collective-permute-start | bytes 663560 | tf_op jit(solution)/shard_map/ppermute | solution.py:34
  70.3 9.2 %collective-permute-start.9 = (bf16[48,2304]{1,0:T(8,128)(2,1)S(1)}, bf16[48,2304]{1,0:T(8,128)(2,1)S(1)}, u32[]{:S(2)}, u32[]{:S(2)}) collective-permute-start(bf16[48,2304]{1,0:T(8,128)(2,1)S(1)} %get-tuple-element.46), channel_id=1, source_target_pairs={{0,112},{16,0},{32,16},{48,32},{64,48},{80,64},{96,80},{112,96},{1... | collective-permute-start | bytes 663560 | tf_op jit(solution)/shard_map/ppermute | solution.py:34
  79.6 9.1 %collective-permute-start.12 = (bf16[48,2304]{1,0:T(8,128)(2,1)S(1)}, bf16[48,2304]{1,0:T(8,128)(2,1)S(1)}, u32[]{:S(2)}, u32[]{:S(2)}) collective-permute-start(bf16[48,2304]{1,0:T(8,128)(2,1)S(1)} %get-tuple-element.50), channel_id=1, source_target_pairs={{0,16},{16,32},{32,48},{48,64},{64,80},{80,96},{96,112},{112,0},{1... | collective-permute-start | bytes 663560 | tf_op jit(solution)/shard_map/ppermute | solution.py:34
  79.7 9.0 %collective-permute-start.13 = (bf16[48,2304]{1,0:T(8,128)(2,1)S(1)}, bf16[48,2304]{1,0:T(8,128)(2,1)S(1)}, u32[]{:S(2)}, u32[]{:S(2)}) collective-permute-start(bf16[48,2304]{1,0:T(8,128)(2,1)S(1)} %get-tuple-element.51), channel_id=1, source_target_pairs={{0,112},{16,0},{32,16},{48,32},{64,48},{80,64},{96,80},{112,96},{1... | collective-permute-start | bytes 663560 | tf_op jit(solution)/shard_map/ppermute | solution.py:34
  83.3 5.4 %copy-start.6 = (bf16[384,768]{1,0:T(8,128)(2,1)S(1)}, bf16[384,768]{1,0:T(8,128)(2,1)}, u32[]{:S(2)}) copy-start(bf16[384,768]{1,0:T(8,128)(2,1)} %copy-done.5) | copy-start | bytes 1769476
  88.8 7.5 %collective-permute-start.14 = (bf16[48,2304]{1,0:T(8,128)(2,1)S(1)}, bf16[48,2304]{1,0:T(8,128)(2,1)S(1)}, u32[]{:S(2)}, u32[]{:S(2)}) collective-permute-start(bf16[48,2304]{1,0:T(8,128)(2,1)S(1)} %convert_element_type.154), channel_id=1, source_target_pairs={{0,128},{16,144},{32,160},{48,176},{64,192},{80,208},{96,224},{112... | collective-permute-start | bytes 663560 | tf_op jit(solution)/shard_map/ppermute | solution.py:89
  90.7 15.2 %all-to-all-start.2 = ((bf16[4,512,256]{2,1,0:T(8,128)(2,1)}), bf16[4,512,256]{2,1,0:T(8,128)(2,1)}, u32[]{:S(2)}, u32[]{:S(2)}) async-start(bf16[4,512,256]{2,1,0:T(8,128)(2,1)} %bitcast.34), calls=%async_computation.2 | async-start | bytes 2097152 | tf_op jit(solution)/shard_map/all_to_all | solution.py:55
  96.5 7.2 %collective-permute-start.15 = (bf16[48,2304]{1,0:T(8,128)(2,1)S(1)}, bf16[48,2304]{1,0:T(8,128)(2,1)S(1)}, u32[]{:S(2)}, u32[]{:S(2)}) collective-permute-start(bf16[48,2304]{1,0:T(8,128)(2,1)S(1)} %pad_maximum_fusion.8.refs_0_), channel_id=1, source_target_pairs={{0,16},{16,32},{32,48},{48,64},{64,80},{80,96},{96,112},{112,0},{1... | collective-permute-start | bytes 663560 | tf_op jit(solution)/shard_map/ppermute | solution.py:34
  96.7 7.1 %collective-permute-start.16 = (bf16[48,2304]{1,0:T(8,128)(2,1)S(1)}, bf16[48,2304]{1,0:T(8,128)(2,1)S(1)}, u32[]{:S(2)}, u32[]{:S(2)}) collective-permute-start(bf16[48,2304]{1,0:T(8,128)(2,1)S(1)} %pad_maximum_fusion.8.refs_0_), channel_id=1, source_target_pairs={{0,112},{16,0},{32,16},{48,32},{64,48},{80,64},{96,80},{112,96},{1... | collective-permute-start | bytes 663560 | tf_op jit(solution)/shard_map/ppermute | solution.py:34
  103.8 11.1 %copy-start.3 = (bf16[48,2304]{1,0:T(8,128)(2,1)}, bf16[48,2304]{1,0:T(8,128)(2,1)S(1)}, u32[]{:S(2)}) copy-start(bf16[48,2304]{1,0:T(8,128)(2,1)S(1)} %collective-permute-done.16.refs_1_) | copy-start | bytes 663556
  107.3 15.5 %copy-start.14 = (bf16[8,48,512]{2,1,0:T(8,128)(2,1)S(1)}, bf16[8,48,512]{2,1,0:T(8,128)(2,1)}, u32[]{:S(2)}) copy-start(bf16[8,48,512]{2,1,0:T(8,128)(2,1)} %copy-done.13) | copy-start | bytes 1179652
  107.4 5.4 %collective-permute-start.17 = (bf16[256,256]{1,0:T(8,128)(2,1)S(1)}, bf16[256,256]{1,0:T(8,128)(2,1)S(1)}, u32[]{:S(2)}, u32[]{:S(2)}) collective-permute-start(bf16[256,256]{1,0:T(8,128)(2,1)S(1)} %slice.287), channel_id=1, source_target_pairs={{0,16},{16,0},{32,48},{48,32},{64,80},{80,64},{96,112},{112,96},{1... | collective-permute-start | bytes 393224 | tf_op jit(solution)/shard_map/ppermute | solution.py:63
  108.9 5.9 %collective-permute-start.11 = (bf16[512,128]{1,0:T(8,128)(2,1)S(1)}, bf16[512,128]{1,0:T(8,128)(2,1)S(1)}, u32[]{:S(2)}, u32[]{:S(2)}) collective-permute-start(bf16[512,128]{1,0:T(8,128)(2,1)S(1)} %slice.288), channel_id=1, source_target_pairs={{0,1},{1,0},{2,3},{3,2},{4,5},{5,4},{6,7},{7,6},{8,9},{9,8},{10,11... | collective-permute-start | bytes 393224 | tf_op jit(solution)/shard_map/ppermute | solution.py:28
  112.9 5.9 %collective-permute-start.18 = (bf16[128,256]{1,0:T(8,128)(2,1)S(1)}, bf16[128,256]{1,0:T(8,128)(2,1)S(1)}, u32[]{:S(2)}, u32[]{:S(2)}) collective-permute-start(bf16[128,256]{1,0:T(8,128)(2,1)S(1)} %slice.289), channel_id=1, source_target_pairs={{0,128},{16,144},{32,160},{48,176},{64,192},{80,208},{96,224},{112... | collective-permute-start | bytes 196616 | tf_op jit(solution)/shard_map/ppermute | solution.py:63
  114.9 8.0 %collective-permute-start.21 = (bf16[48,2304]{1,0:T(8,128)(2,1)S(1)}, bf16[48,2304]{1,0:T(8,128)(2,1)S(1)}, u32[]{:S(2)}, u32[]{:S(2)}) collective-permute-start(bf16[48,2304]{1,0:T(8,128)(2,1)S(1)} %collective-permute-done.16.refs_1_), channel_id=1, source_target_pairs={{0,112},{16,0},{32,16},{48,32},{64,48},{80,64},{96,80},{112,96},{1... | collective-permute-start | bytes 663560 | tf_op jit(solution)/shard_map/ppermute | solution.py:34
  117.5 7.8 %collective-permute-start.22 = (bf16[48,2304]{1,0:T(8,128)(2,1)S(1)}, bf16[48,2304]{1,0:T(8,128)(2,1)S(1)}, u32[]{:S(2)}, u32[]{:S(2)}) collective-permute-start(bf16[48,2304]{1,0:T(8,128)(2,1)S(1)} %collective-permute-done.15.refs_8_), channel_id=1, source_target_pairs={{0,16},{16,32},{32,48},{48,64},{64,80},{80,96},{96,112},{112,0},{1... | collective-permute-start | bytes 663560 | tf_op jit(solution)/shard_map/ppermute | solution.py:34
  118.8 20.8 %copy-start.4 = (bf16[48,2304]{1,0:T(8,128)(2,1)S(1)}, bf16[48,2304]{1,0:T(8,128)(2,1)}, u32[]{:S(2)}) copy-start(bf16[48,2304]{1,0:T(8,128)(2,1)} %copy-done.3) | copy-start | bytes 663556
  118.8 8.6 %collective-permute-start.19 = (f32[64,256]{1,0:T(8,128)S(1)}, f32[64,256]{1,0:T(8,128)S(1)}, u32[]{:S(2)}, u32[]{:S(2)}) collective-permute-start(f32[64,256]{1,0:T(8,128)S(1)} %slice.236), channel_id=1, source_target_pairs={{0,32},{16,48},{32,0},{48,16},{64,96},{80,112},{96,64},{112,80},{1... | collective-permute-start | bytes 196616 | tf_op jit(solution)/shard_map/ppermute | solution.py:63
  125.3 8.1 %collective-permute-start.23 = (bf16[48,2304]{1,0:T(8,128)(2,1)S(1)}, bf16[48,2304]{1,0:T(8,128)(2,1)S(1)}, u32[]{:S(2)}, u32[]{:S(2)}) collective-permute-start(bf16[48,2304]{1,0:T(8,128)(2,1)S(1)} %collective-permute-done.21.refs_2_), channel_id=1, source_target_pairs={{0,112},{16,0},{32,16},{48,32},{64,48},{80,64},{96,80},{112,96},{1... | collective-permute-start | bytes 663560 | tf_op jit(solution)/shard_map/ppermute | solution.py:34
  125.8 7.7 %collective-permute-start.24 = (bf16[48,2304]{1,0:T(8,128)(2,1)S(1)}, bf16[48,2304]{1,0:T(8,128)(2,1)S(1)}, u32[]{:S(2)}, u32[]{:S(2)}) collective-permute-start(bf16[48,2304]{1,0:T(8,128)(2,1)S(1)} %collective-permute-done.22.refs_7_), channel_id=1, source_target_pairs={{0,16},{16,32},{32,48},{48,64},{64,80},{80,96},{96,112},{112,0},{1... | collective-permute-start | bytes 663560 | tf_op jit(solution)/shard_map/ppermute | solution.py:34
  127.4 9.7 %collective-permute-start.20 = (f32[32,256]{1,0:T(8,128)S(1)}, f32[32,256]{1,0:T(8,128)S(1)}, u32[]{:S(2)}, u32[]{:S(2)}) collective-permute-start(f32[32,256]{1,0:T(8,128)S(1)} %slice.238), channel_id=1, source_target_pairs={{0,64},{16,80},{32,96},{48,112},{64,0},{80,16},{96,32},{112,48},{1... | collective-permute-start | bytes 98312 | tf_op jit(solution)/shard_map/ppermute | solution.py:63
  133.5 6.0 %collective-permute-start.25 = (bf16[48,1152]{1,0:T(8,128)(2,1)S(1)}, bf16[48,1152]{1,0:T(8,128)(2,1)S(1)}, u32[]{:S(2)}, u32[]{:S(2)}) collective-permute-start(bf16[48,1152]{1,0:T(8,128)(2,1)S(1)} %slice.210), channel_id=1, source_target_pairs={{0,16},{16,32},{32,48},{48,64},{64,80},{80,96},{96,112},{112,0},{1... | collective-permute-start | bytes 331784 | tf_op jit(solution)/shard_map/ppermute | solution.py:34
  133.6 5.9 %collective-permute-start.26 = (bf16[48,1152]{1,0:T(8,128)(2,1)S(1)}, bf16[48,1152]{1,0:T(8,128)(2,1)S(1)}, u32[]{:S(2)}, u32[]{:S(2)}) collective-permute-start(bf16[48,1152]{1,0:T(8,128)(2,1)S(1)} %slice.211), channel_id=1, source_target_pairs={{0,112},{16,0},{32,16},{48,32},{64,48},{80,64},{96,80},{112,96},{1... | collective-permute-start | bytes 331784 | tf_op jit(solution)/shard_map/ppermute | solution.py:34
  140.6 1.3 copy-start.1
  141.9 1.3 collective-permute-start.27
  143.8 9.1 %all-to-all-start.3 = ((bf16[8,48,128]{2,1,0:T(8,128)(2,1)}), bf16[8,48,128]{2,1,0:T(8,128)(2,1)S(1)}, u32[]{:S(2)}, u32[]{:S(2)}) async-start(bf16[8,48,128]{2,1,0:T(8,128)(2,1)} %add_convert_fusion.7), calls=%async_computation.3 | async-start | bytes 196608 | tf_op jit(solution)/shard_map/all_to_all | solution.py:453
  148.3 1.5 copy-start.2
  153.0 0.6 copy-start.16

commit v11 on v10

--- a/solution.py
+++ b/solution.py
@@ -39,15 +39,15 @@
     return [list(range(x, n, X_LO)) for x in range(X_LO)]
 
 
-def ctx_gather(block):
-    copies = jnp.broadcast_to(block[None], (lax.axis_size("ctx"),) + block.shape)
-    return lax.all_to_all(copies, "ctx", 0, 0, tiled=True)
-
-
-def y_gather(block):
-    copies = jnp.broadcast_to(block[None], (len(y_groups()[0]),) + block.shape)
-    got = lax.all_to_all(copies, "exp", 0, 0, tiled=True, axis_index_groups=y_groups())
-    return got.reshape(-1, block.shape[-1])
+def key_gather(block):
+    exps, ctxs = lax.axis_size("exp"), lax.axis_size("ctx")
+    groups = [
+        [c * exps + y * X_LO + x for y in range(exps // X_LO) for c in range(ctxs)]
+        for x in range(X_LO)
+    ]
+    copies = jnp.broadcast_to(block[None], (len(groups[0]),) + block.shape)
+    got = lax.all_to_all(copies, ("ctx", "exp"), 0, 0, tiled=True, axis_index_groups=groups)
+    return got.reshape(-1, block.shape[1])
 
 
 def y_parts(both):
@@ -72,12 +72,10 @@
     return lax.ppermute(block, "exp", [(e, e ^ mask) for e in range(lax.axis_size("exp"))])
 
 
-def exchange(blocks, waits):
+def exchange(blocks):
     shape = blocks.shape
     bits = shape[0].bit_length() - 1
     for bit in range(bits):
-        if bit == bits - 1:
-            blocks = after(blocks, waits)
         blocks = blocks.reshape((2**bit, 2, -1) + shape[1:])
         got = partner(blocks[:, 1], 2 ** (bits - 1 - bit))
         blocks = jnp.stack([blocks[:, 0], got], axis=1)
@@ -103,11 +101,12 @@
     return parts[far][:, :cut], parts[far][:, cut:]
 
 
-def sum_step(move, parts, step, onward, back):
+def sum_step(move, parts, step, onward, back, waits=()):
     n = len(parts)
     far = n // 2
     cut = parts[0].shape[1] // 2
     onward, back = move(onward, 1), move(back, -1)
+    onward, back = both_after(onward, back, *waits)
     ahead, behind = parts[far - 1 - step], parts[(far + 1 + step) % n]
     if step == 0:
         onward = jnp.concatenate([add_low(onward, ahead[:, :cut]), ahead[:, cut:]], axis=1)
@@ -291,7 +290,7 @@
     return grad_key, grad_value
 
 
-def select(moe_input, moe_grad, expert_ids, router_weight, near):
+def select(moe_input, moe_grad, expert_ids, router_weight):
     width = moe_input.shape[1]
     exp_size = lax.axis_size("exp")
     labels = lax.axis_index("exp") ^ jnp.arange(exp_size)
@@ -308,7 +307,7 @@
     picked = jnp.einsum("bs,bd->sd", placed_low, rows, preferred_element_type=F32)
     scaled = picked[:, width:] * slot_weight.reshape(-1, 1)
     sent = jnp.concatenate([picked[:, :width].astype(BF), scaled.astype(BF)], axis=1)
-    got = exchange(sent.reshape(exp_size, CAP, 2 * width), near)
+    got = exchange(sent.reshape(exp_size, CAP, 2 * width))
     return placed_low, got
 
 
@@ -472,9 +471,8 @@
     rows = tokens * queries.shape[1]
     size = queries.shape[2]
     pair = jnp.concatenate([key_rows[:, 0, :], value_vector_rows[:, 0, :]], axis=1)
-    near = ctx_gather(pair)
-    placed_low, got = select(moe_input, moe_grad, expert_ids, router_weight, near)
-    flat = y_gather(near)
+    flat = key_gather(pair)
+    placed_low, got = select(moe_input, moe_grad, expert_ids, router_weight)
     mine = jnp.concatenate([by_head(queries), by_head(grad_attn)], axis=0)
     theirs = beside(mine)
     queries = jnp.concatenate([mine[:rows], theirs[:rows]], axis=0)
@@ -483,12 +481,11 @@
         got, gate_weight, up_weight, down_weight
     )
     onward, back = both_after(*sum_start(parts), theirs)
-    onward, back = sum_step(z_move, parts, 0, onward, back)
-    onward, back = both_after(onward, back, flat)
     stats = attention_stats(own, tokens, queries, grads, after(flat, onward, back))
+    onward, back = sum_step(z_move, parts, 0, onward, back, (stats,))
+    far_stats = beside(stats)
     onward, back = sum_step(z_move, parts, 1, onward, back)
-    onward, back = both_after(onward, back, stats)
-    far_stats = beside(stats)
+    onward, back = both_after(onward, back, far_stats)
     half = flat.shape[0] // 2
     middle = lax.axis_size("exp") // X_LO // 2
     lower = attention_grads(

time: 160 us -> 159 us (level)
  waiting for transfers between devices: 40.1 us -> 47.9 us
  starting transfers between devices: 70.9 us -> 65.7 us
  local copies, waits for them, and re-layouts: 10.3 us -> 8.02 us
    ppermute x16, waiting for transfers between devices: 9.89 us -> 18.7 us  [z_move(): return lax.ppermute(block, 'ctx', pairs)]
    all_to_all x2 -> x1, waiting for transfers between devices: 13.9 us -> 5.29 us  [key_gather(): lax.all_to_all(copies, ('ctx', 'exp'), 0, 0, tiled=True, axis_index_group...]
    ppermute x3, waiting for transfers between devices: 6.13 us -> 13.2 us  [partner(): lax.ppermute(block, 'exp', [(e, e ^ mask) for e in range(lax.axis_size('e...]
    ppermute x4, starting transfers between devices: 12.8 us -> 8.66 us  [ctx_sum(): both = both[:half] + lax.ppermute(sent, 'ctx', pairs).astype(F32)]
    all_to_all x2 -> x1, starting transfers between devices: 13.6 us -> 11.8 us  [key_gather(): lax.all_to_all(copies, ('ctx', 'exp'), 0, 0, tiled=True, axis_index_group...]
    unnamed x42 -> x44, local copies, waits for them, and re-layouts: 4.47 us -> 3.61 us
  transfers between devices with their start and end apart: 32 -> 31, of which waited for: 15 -> 17; matrix products, arithmetic and copies ran while one was open for 7% -> 6% of each run, Pallas kernels for 10% -> 11%
where the time goes in v11:
time: 159 us; the launch traced here: 157 us
  starting transfers between devices  65.7 us (41%)
  waiting for transfers between devices  47.9 us (30%)
  Pallas kernels  19.1 us (12%)
  other arithmetic  10.8 us (7%)
  local copies, waits for them, and re-layouts  8.02 us (5%)
  matrix products  4.4 us (3%)
    ppermute x16, starting transfers between devices, z_move(): return lax.ppermute(block, 'ctx', pairs)  23.8 us
    ppermute x16, waiting for transfers between devices, z_move(): return lax.ppermute(block, 'ctx', pairs)  18.7 us
    ppermute x3, waiting for transfers between devices, partner(): lax.ppermute(block, 'exp', [(e, e ^ mask) for e in range(lax.axis_size('e...  13.2 us
    all_to_all x1, starting transfers between devices, key_gather(): lax.all_to_all(copies, ('ctx', 'exp'), 0, 0, tiled=True, axis_index_group...  11.8 us
    pallas_call x2, Pallas kernels, attention_grads(): pl.pallas_call(functools.partial(grads_body, own, lax.axis_size('ctx'), t...  10.2 us
    ppermute x4, starting transfers between devices, ctx_sum(): both = both[:half] + lax.ppermute(sent, 'ctx', pairs).astype(F32)  8.66 us
    ppermute x3, starting transfers between devices, partner(): lax.ppermute(block, 'exp', [(e, e ^ mask) for e in range(lax.axis_size('e...  6.84 us
    all_to_all x1, waiting for transfers between devices, key_gather(): lax.all_to_all(copies, ('ctx', 'exp'), 0, 0, tiled=True, axis_index_group...  5.29 us
  transfers between devices with their start and end apart: 31, of which 17 were waited for; matrix products, arithmetic and copies ran while one was open for 6% of the time, Pallas kernels for 11%

profile of v11, /device:TPU:2, one launch (start us, length us, event | category | flops | bytes accessed | tf_op | source)
XLA Modules:
  0.0 157.1 jit_solution(11264859417502722498)
XLA Ops:
  0.7 0.9 fusion.19
  1.6 1.1 reduce-window.6
  3.0 0.8 fusion.20
  4.5 1.5 fusion.2
  6.3 3.3 %collective-permute-start.1 = (bf16[1,4,48,512]{3,2,1,0:T(8,128)(2,1)S(1)}, bf16[1,4,48,512]{3,2,1,0:T(8,128)(2,1)S(1)}, u32[]{:S(2)}, u32[]{:S(2)}) collective-permute-start(bf16[1,4,48,512]{3,2,1,0:T(8,128)(2,1)S(1)} %get-tuple-element.103), channel_id=1, source_target_pairs={{0,4},{1,5},{2,6},{3,7},{4,0},{5,1},{6,2},{7,3},{8,12},{9,13},{10,... | collective-permute-start | bytes 589832 | tf_op jit(solution)/shard_map/ppermute | solution.py:72
  9.6 0.7 pad_maximum_fusion.3
  10.9 1.1 broadcast_in_dim.43
  12.0 11.8 %all-to-all-start = ((bf16[64,32,256]{2,1,0:T(8,128)(2,1)}), bf16[64,32,256]{2,1,0:T(8,128)(2,1)S(1)}, u32[]{:S(2)}, u32[]{:S(2)}) async-start(bf16[64,32,256]{2,1,0:T(8,128)(2,1)} %broadcast_in_dim.43), calls=%async_computation | async-start | bytes 2097152 | tf_op jit(solution)/shard_map/all_to_all | solution.py:49
  23.9 1.7 %collective-permute-start.2 = (bf16[2,2,48,512]{3,2,1,0:T(8,128)(2,1)S(1)}, bf16[2,2,48,512]{3,2,1,0:T(8,128)(2,1)}, u32[]{:S(2)}, u32[]{:S(2)}) collective-permute-start(bf16[2,2,48,512]{3,2,1,0:T(8,128)(2,1)S(1)} %get-tuple-element.101), channel_id=1, source_target_pairs={{0,2},{1,3},{2,0},{3,1},{4,6},{5,7},{6,4},{7,5},{8,10},{9,11},{10,... | collective-permute-start | bytes 589832 | tf_op jit(solution)/shard_map/ppermute | solution.py:72
  25.6 1.2 dynamic-slice_bitcast_fusion
  26.9 6.9 %collective-permute-done.2 = bf16[2,2,48,512]{3,2,1,0:T(8,128)(2,1)} collective-permute-done((bf16[2,2,48,512]{3,2,1,0:T(8,128)(2,1)S(1)}, bf16[2,2,48,512]{3,2,1,0:T(8,128)(2,1)}, u32[]{:S(2)}, u32[]{:S(2)}) %collective-permute-start.2) | collective-permute-done | bytes 196640 | tf_op jit(solution)/shard_map/ppermute | solution.py:72
  33.8 1.0 pad_maximum_fusion.1
  34.8 1.9 %collective-permute-start.3 = (bf16[4,1,48,512]{3,2,0,1:T(8,128)(2,1)S(1)}, bf16[4,1,48,512]{3,2,0,1:T(8,128)(2,1)S(1)}, u32[]{:S(2)}, u32[]{:S(2)}) collective-permute-start(bf16[4,1,48,512]{3,2,0,1:T(8,128)(2,1)S(1)} %get-tuple-element.99), channel_id=1, source_target_pairs={{0,1},{1,0},{2,3},{3,2},{4,5},{5,4},{6,7},{7,6},{8,9},{9,8},{10,11... | collective-permute-start | bytes 589832 | tf_op jit(solution)/shard_map/ppermute | solution.py:72
  36.7 6.2 %collective-permute-done.3 = bf16[4,1,48,512]{3,2,0,1:T(8,128)(2,1)S(1)} collective-permute-done((bf16[4,1,48,512]{3,2,0,1:T(8,128)(2,1)S(1)}, bf16[4,1,48,512]{3,2,0,1:T(8,128)(2,1)S(1)}, u32[]{:S(2)}, u32[]{:S(2)}) %collective-permute-start.3) | collective-permute-done | bytes 196640 | tf_op jit(solution)/shard_map/ppermute | solution.py:72
  44.4 0.8 pad_maximum_fusion.11
  45.1 0.6 collective-permute-start.4
  45.7 2.7 %collective-permute-start.5 = (bf16[48,1152]{1,0:T(8,128)(2,1)}, bf16[48,1152]{1,0:T(8,128)(2,1)}, u32[]{:S(2)}, u32[]{:S(2)}) collective-permute-start(bf16[48,1152]{1,0:T(8,128)(2,1)} %get-tuple-element.45), channel_id=1, source_target_pairs={{0,112},{16,0},{32,16},{48,32},{64,48},{80,64},{96,80},{112,96},{1... | collective-permute-start | bytes 331784 | tf_op jit(solution)/shard_map/ppermute | solution.py:34
  48.4 5.3 %all-to-all-done = bf16[64,32,256]{2,1,0:T(8,128)(2,1)S(1)} async-done(((bf16[64,32,256]{2,1,0:T(8,128)(2,1)}), bf16[64,32,256]{2,1,0:T(8,128)(2,1)S(1)}, u32[]{:S(2)}, u32[]{:S(2)}) %all-to-all-start) | async-done | bytes 1048608 | tf_op jit(solution)/shard_map/all_to_all | solution.py:49
  53.7 4.8 %attention_stats.1.stats_ref = f32[8,1024]{1,0:T(8,128)S(1)} custom-call(s32[3]{0:T(128)S(1)} %pad_add_fusion.2.here_ref, bf16[1024,128]{1,0:T(8,128)(2,1)S(1)} %get-tuple-element.106.q_ref, bf16[1024,128]{1,0:T(8,128)(2,1)S(1)} %get-tuple-element.107.g_ref, bf16[2048,256]{1,0:T(8,128)(2,1)S(1)} %bitcast.66), custom_call_target="tpu_custom_call" | custom-call | flops 1073741824 | bytes 1048576 | tf_op jit(solution)/shard_map/attention_stats/pallas_call | solution.py:245
  58.6 1.0 add_convert_fusion.5
  59.6 2.1 %collective-permute-start.6 = (bf16[48,2304]{1,0:T(8,128)(2,1)S(1)}, bf16[48,2304]{1,0:T(8,128)(2,1)S(1)}, u32[]{:S(2)}, u32[]{:S(2)}) collective-permute-start(bf16[48,2304]{1,0:T(8,128)(2,1)S(1)} %get-tuple-element.88), channel_id=1, source_target_pairs={{0,16},{16,32},{32,48},{48,64},{64,80},{80,96},{96,112},{112,0},{1... | collective-permute-start | bytes 663560 | tf_op jit(solution)/shard_map/ppermute | solution.py:34
  61.6 1.3 collective-permute-start.7
  62.9 1.8 %collective-permute-start.8 = (f32[8,1024]{1,0:T(8,128)S(1)}, f32[8,1024]{1,0:T(8,128)S(1)}, u32[]{:S(2)}, u32[]{:S(2)}) collective-permute-start(f32[8,1024]{1,0:T(8,128)S(1)} %attention_stats.1.stats_ref), channel_id=1, source_target_pairs={{0,1},{1,0},{2,3},{3,2},{4,5},{5,4},{6,7},{7,6},{8,9},{9,8},{10,11... | collective-permute-start | bytes 98312 | tf_op jit(solution)/shard_map/ppermute | solution.py:28
  64.7 2.1 %collective-permute-done.6 = bf16[48,2304]{1,0:T(8,128)(2,1)S(1)} collective-permute-done((bf16[48,2304]{1,0:T(8,128)(2,1)S(1)}, bf16[48,2304]{1,0:T(8,128)(2,1)S(1)}, u32[]{:S(2)}, u32[]{:S(2)}) %collective-permute-start.6) | collective-permute-done | bytes 221216 | tf_op jit(solution)/shard_map/ppermute | solution.py:34
  66.8 1.5 collective-permute-done.7
  68.4 3.1 %collective-permute-start.10 = (bf16[48,2304]{1,0:T(8,128)(2,1)S(1)}, bf16[48,2304]{1,0:T(8,128)(2,1)S(1)}, u32[]{:S(2)}, u32[]{:S(2)}) collective-permute-start(bf16[48,2304]{1,0:T(8,128)(2,1)S(1)} %get-tuple-element.52), channel_id=1, source_target_pairs={{0,112},{16,0},{32,16},{48,32},{64,48},{80,64},{96,80},{112,96},{1... | collective-permute-start | bytes 663560 | tf_op jit(solution)/shard_map/ppermute | solution.py:34
  71.7 4.8 %attention_grads.2 = (bf16[4,16,32,256]{3,2,1,0:T(8,128)(2,1)S(1)}, f32[1024,128]{1,0:T(8,128)S(1)}) custom-call(s32[3]{0:T(128)S(1)} %pad_add_fusion.2.here_ref, bf16[1024,128]{1,0:T(8,128)(2,1)S(1)} %get-tuple-element.106.q_ref, bf16[1024,128]{1,0:T(8,128)(2,1)S(1)} %get-tuple-element.107.g_ref, bf16[1024,256]{1,0:T(8,128)(2,1)S(1)} %bitcast.68, ...), custom_call_target="tpu_custom_call" | custom-call | flops 1342177280 | bytes 1048576 | tf_op jit(solution)/shard_map/attention_grads/pallas_call | solution.py:264
  76.4 3.0 %collective-permute-done.9 = bf16[48,2304]{1,0:T(8,128)(2,1)S(1)} collective-permute-done((bf16[48,2304]{1,0:T(8,128)(2,1)S(1)}, bf16[48,2304]{1,0:T(8,128)(2,1)S(1)}, u32[]{:S(2)}, u32[]{:S(2)}) %collective-permute-start.9) | collective-permute-done | bytes 221216 | tf_op jit(solution)/shard_map/ppermute | solution.py:34
  79.9 3.0 %collective-permute-start.13 = (bf16[48,2304]{1,0:T(8,128)(2,1)S(1)}, bf16[48,2304]{1,0:T(8,128)(2,1)S(1)}, u32[]{:S(2)}, u32[]{:S(2)}) collective-permute-start(bf16[48,2304]{1,0:T(8,128)(2,1)S(1)} %get-tuple-element.59), channel_id=1, source_target_pairs={{0,112},{16,0},{32,16},{48,32},{64,48},{80,64},{96,80},{112,96},{1... | collective-permute-start | bytes 663560 | tf_op jit(solution)/shard_map/ppermute | solution.py:34
  83.0 5.4 %attention_grads.3 = (bf16[4,16,32,256]{3,2,1,0:T(8,128)(2,1)}, f32[1024,128]{1,0:T(8,128)S(1)}) custom-call(s32[3]{0:T(128)S(1)} %pad_add_fusion.here_ref, bf16[1024,128]{1,0:T(8,128)(2,1)S(1)} %get-tuple-element.106.q_ref, bf16[1024,128]{1,0:T(8,128)(2,1)S(1)} %copy-done.4, bf16[1024,256]{1,0:T(8,128)(2,1)S(1)} %bitcast.67, ...), custom_call_target="tpu_custom_call" | custom-call | flops 1342177280 | bytes 1048576 | tf_op jit(solution)/shard_map/attention_grads/pallas_call | solution.py:264
  88.5 0.7 collective-permute-start.14
  89.2 4.6 %all-to-all-start.1 = ((bf16[4,512,256]{2,1,0:T(8,128)(2,1)}), bf16[4,512,256]{2,1,0:T(8,128)(2,1)}, u32[]{:S(2)}, u32[]{:S(2)}) async-start(bf16[4,512,256]{2,1,0:T(8,128)(2,1)} %bitcast.34), calls=%async_computation.1 | async-start | bytes 2097152 | tf_op jit(solution)/shard_map/all_to_all | solution.py:55
  93.8 2.3 %collective-permute-done.14 = bf16[48,2304]{1,0:T(8,128)(2,1)S(1)} collective-permute-done((bf16[48,2304]{1,0:T(8,128)(2,1)S(1)}, bf16[48,2304]{1,0:T(8,128)(2,1)S(1)}, u32[]{:S(2)}, u32[]{:S(2)}) %collective-permute-start.14) | collective-permute-done | bytes 221216 | tf_op jit(solution)/shard_map/ppermute | solution.py:87
  96.3 3.2 %collective-permute-start.16 = (bf16[48,2304]{1,0:T(8,128)(2,1)S(1)}, bf16[48,2304]{1,0:T(8,128)(2,1)S(1)}, u32[]{:S(2)}, u32[]{:S(2)}) collective-permute-start(bf16[48,2304]{1,0:T(8,128)(2,1)S(1)} %pad_maximum_fusion.8.refs_0_), channel_id=1, source_target_pairs={{0,112},{16,0},{32,16},{48,32},{64,48},{80,64},{96,80},{112,96},{1... | collective-permute-start | bytes 663560 | tf_op jit(solution)/shard_map/ppermute | solution.py:34
  99.5 3.9 %collective-permute-done.15.refs_8_ = bf16[48,2304]{1,0:T(8,128)(2,1)S(1)} collective-permute-done((bf16[48,2304]{1,0:T(8,128)(2,1)S(1)}, bf16[48,2304]{1,0:T(8,128)(2,1)S(1)}, u32[]{:S(2)}, u32[]{:S(2)}) %collective-permute-start.15) | collective-permute-done | bytes 221216 | tf_op jit(solution)/shard_map/ppermute | solution.py:34
  103.5 1.3 all-to-all-done.1
  104.8 1.4 convert_reduce_fusion
  106.3 1.9 %collective-permute-start.11 = (bf16[512,128]{1,0:T(8,128)(2,1)S(1)}, bf16[512,128]{1,0:T(8,128)(2,1)S(1)}, u32[]{:S(2)}, u32[]{:S(2)}) collective-permute-start(bf16[512,128]{1,0:T(8,128)(2,1)S(1)} %slice.288), channel_id=1, source_target_pairs={{0,1},{1,0},{2,3},{3,2},{4,5},{5,4},{6,7},{7,6},{8,9},{9,8},{10,11... | collective-permute-start | bytes 393224 | tf_op jit(solution)/shard_map/ppermute | solution.py:28
  108.3 3.7 %collective-permute-done.17 = bf16[256,256]{1,0:T(8,128)(2,1)S(1)} collective-permute-done((bf16[256,256]{1,0:T(8,128)(2,1)S(1)}, bf16[256,256]{1,0:T(8,128)(2,1)S(1)}, u32[]{:S(2)}, u32[]{:S(2)}) %collective-permute-start.17) | collective-permute-done | bytes 131104 | tf_op jit(solution)/shard_map/ppermute | solution.py:63
  112.0 2.6 %collective-permute-start.18 = (bf16[128,256]{1,0:T(8,128)(2,1)S(1)}, bf16[128,256]{1,0:T(8,128)(2,1)S(1)}, u32[]{:S(2)}, u32[]{:S(2)}) collective-permute-start(bf16[128,256]{1,0:T(8,128)(2,1)S(1)} %slice.289), channel_id=1, source_target_pairs={{0,128},{16,144},{32,160},{48,176},{64,192},{80,208},{96,224},{112... | collective-permute-start | bytes 196616 | tf_op jit(solution)/shard_map/ppermute | solution.py:63
  114.7 1.8 %collective-permute-start.21 = (bf16[48,2304]{1,0:T(8,128)(2,1)S(1)}, bf16[48,2304]{1,0:T(8,128)(2,1)S(1)}, u32[]{:S(2)}, u32[]{:S(2)}) collective-permute-start(bf16[48,2304]{1,0:T(8,128)(2,1)S(1)} %collective-permute-done.16.refs_1_), channel_id=1, source_target_pairs={{0,112},{16,0},{32,16},{48,32},{64,48},{80,64},{96,80},{112,96},{1... | collective-permute-start | bytes 663560 | tf_op jit(solution)/shard_map/ppermute | solution.py:34
  116.8 1.1 collective-permute-done.18
  117.9 2.5 %collective-permute-start.19 = (f32[64,256]{1,0:T(8,128)S(1)}, f32[64,256]{1,0:T(8,128)S(1)}, u32[]{:S(2)}, u32[]{:S(2)}) collective-permute-start(f32[64,256]{1,0:T(8,128)S(1)} %slice.236), channel_id=1, source_target_pairs={{0,32},{16,48},{32,0},{48,16},{64,96},{80,112},{96,64},{112,80},{1... | collective-permute-start | bytes 196616 | tf_op jit(solution)/shard_map/ppermute | solution.py:63
  120.5 0.9 collective-permute-done.21.refs_2_
  121.3 3.5 %collective-permute-done.22.refs_7_ = bf16[48,2304]{1,0:T(8,128)(2,1)S(1)} collective-permute-done((bf16[48,2304]{1,0:T(8,128)(2,1)S(1)}, bf16[48,2304]{1,0:T(8,128)(2,1)S(1)}, u32[]{:S(2)}, u32[]{:S(2)}) %collective-permute-start.22) | collective-permute-done | bytes 221216 | tf_op jit(solution)/shard_map/ppermute | solution.py:34
  124.8 2.0 %collective-permute-start.24 = (bf16[48,2304]{1,0:T(8,128)(2,1)S(1)}, bf16[48,2304]{1,0:T(8,128)(2,1)S(1)}, u32[]{:S(2)}, u32[]{:S(2)}) collective-permute-start(bf16[48,2304]{1,0:T(8,128)(2,1)S(1)} %collective-permute-done.22.refs_7_), channel_id=1, source_target_pairs={{0,16},{16,32},{32,48},{48,64},{64,80},{80,96},{96,112},{112,0},{1... | collective-permute-start | bytes 663560 | tf_op jit(solution)/shard_map/ppermute | solution.py:34
  126.9 3.5 %collective-permute-start.20 = (f32[32,256]{1,0:T(8,128)S(1)}, f32[32,256]{1,0:T(8,128)S(1)}, u32[]{:S(2)}, u32[]{:S(2)}) collective-permute-start(f32[32,256]{1,0:T(8,128)S(1)} %slice.238), channel_id=1, source_target_pairs={{0,64},{16,80},{32,96},{48,112},{64,0},{80,16},{96,32},{112,48},{1... | collective-permute-start | bytes 98312 | tf_op jit(solution)/shard_map/ppermute | solution.py:63
  130.4 0.8 copy.42
  131.2 1.1 collective-permute-done.24.refs_6_
  132.9 2.9 %collective-permute-start.26 = (bf16[48,1152]{1,0:T(8,128)(2,1)S(1)}, bf16[48,1152]{1,0:T(8,128)(2,1)S(1)}, u32[]{:S(2)}, u32[]{:S(2)}) collective-permute-start(bf16[48,1152]{1,0:T(8,128)(2,1)S(1)} %slice.211), channel_id=1, source_target_pairs={{0,112},{16,0},{32,16},{48,32},{64,48},{80,64},{96,80},{112,96},{1... | collective-permute-start | bytes 331784 | tf_op jit(solution)/shard_map/ppermute | solution.py:34
  135.7 2.6 %collective-permute-done.25.refs_4_ = bf16[48,1152]{1,0:T(8,128)(2,1)S(1)} collective-permute-done((bf16[48,1152]{1,0:T(8,128)(2,1)S(1)}, bf16[48,1152]{1,0:T(8,128)(2,1)S(1)}, u32[]{:S(2)}, u32[]{:S(2)}) %collective-permute-start.25) | collective-permute-done | bytes 110624 | tf_op jit(solution)/shard_map/ppermute | solution.py:34
  138.4 1.1 expert_contrib.1
  139.5 1.2 copy-done.1
  140.7 0.6 fusion.22
  141.3 0.7 collective-permute-done.27
  142.0 0.7 add_convert_fusion.7
  142.7 5.1 %all-to-all-start.2 = ((bf16[8,48,128]{2,1,0:T(8,128)(2,1)}), bf16[8,48,128]{2,1,0:T(8,128)(2,1)S(1)}, u32[]{:S(2)}, u32[]{:S(2)}) async-start(bf16[8,48,128]{2,1,0:T(8,128)(2,1)} %add_convert_fusion.7), calls=%async_computation.2 | async-start | bytes 196608 | tf_op jit(solution)/shard_map/all_to_all | solution.py:452
  147.7 0.6 fusion.23
  148.3 1.5 copy-done.2
  149.8 1.5 expert_weight_grads.1
  151.4 1.6 %all-to-all-done.2.back_ref = bf16[8,48,128]{2,1,0:T(8,128)(2,1)S(1)} async-done(((bf16[8,48,128]{2,1,0:T(8,128)(2,1)}), bf16[8,48,128]{2,1,0:T(8,128)(2,1)S(1)}, u32[]{:S(2)}, u32[]{:S(2)}) %all-to-all-start.2) | async-done | bytes 98336 | tf_op jit(solution)/shard_map/all_to_all | solution.py:452
  153.0 0.6 copy-done.17
  153.7 1.5 order_rows.1
  155.2 1.9 %convolution_convert_fusion.3 = bf16[512,128]{1,0:T(8,128)(2,1)} fusion(pred[512,384]{0,1:T(32,128)(4,1)S(1)} %copy-done.16, bf16[384,128]{1,0:T(8,128)(2,1)} %order_rows.1), kind=kOutput, calls=%fused_computation.4 | convolution fusion | flops 50397184 | bytes 425984 | tf_op jit(solution)/shard_map/dot_general | solution.py:453
  (117 shorter events, 5.7 us)
Async XLA Ops:
  0.6 42.6 %copy-start = (bf16[1,1536,256]{2,1,0:T(8,128)(2,1)S(1)}, bf16[1,1536,256]{2,1,0:T(8,128)(2,1)}, u32[]{:S(2)}) copy-start(bf16[1,1536,256]{2,1,0:T(8,128)(2,1)} %param.21) | copy-start | bytes 2359300
  4.5 1.7 %copy-start.15 = (pred[512,384]{0,1:T(32,128)(4,1)}, pred[512,384]{0,1:T(32,128)(4,1)S(1)}, u32[]{:S(2)}) copy-start(pred[512,384]{0,1:T(32,128)(4,1)S(1)} %fusion.1) | copy-start | bytes 589828
  6.0 3.5 %copy-start.18 = (bf16[256,2,128]{2,1,0:T(2,128)(2,1)S(1)}, bf16[256,2,128]{2,1,0:T(2,128)(2,1)}, u32[]{:S(2)}) copy-start(bf16[256,2,128]{2,1,0:T(2,128)(2,1)} %param.11) | copy-start | bytes 393220
  6.1 3.6 %copy-start.19 = (bf16[256,2,128]{2,1,0:T(2,128)(2,1)S(1)}, bf16[256,2,128]{2,1,0:T(2,128)(2,1)}, u32[]{:S(2)}) copy-start(bf16[256,2,128]{2,1,0:T(2,128)(2,1)} %param.14) | copy-start | bytes 393220
  6.2 4.7 %copy-start.20 = (bf16[32,1,128]{2,0,1:T(8,128)(2,1)S(1)}, bf16[32,1,128]{2,0,1:T(8,128)(2,1)}, u32[]{:S(2)}) copy-start(bf16[32,1,128]{2,0,1:T(8,128)(2,1)} %param.13) | copy-start | bytes 24580
  6.2 4.7 %copy-start.21 = (bf16[32,1,128]{2,0,1:T(8,128)(2,1)S(1)}, bf16[32,1,128]{2,0,1:T(8,128)(2,1)}, u32[]{:S(2)}) copy-start(bf16[32,1,128]{2,0,1:T(8,128)(2,1)} %param.12) | copy-start | bytes 24580
  6.3 17.6 %collective-permute-start.1 = (bf16[1,4,48,512]{3,2,1,0:T(8,128)(2,1)S(1)}, bf16[1,4,48,512]{3,2,1,0:T(8,128)(2,1)S(1)}, u32[]{:S(2)}, u32[]{:S(2)}) collective-permute-start(bf16[1,4,48,512]{3,2,1,0:T(8,128)(2,1)S(1)} %get-tuple-element.103), channel_id=1, source_target_pairs={{0,4},{1,5},{2,6},{3,7},{4,0},{5,1},{6,2},{7,3},{8,12},{9,13},{10,... | collective-permute-start | bytes 589832 | tf_op jit(solution)/shard_map/ppermute | solution.py:72
  10.4 26.3 %collective-permute-start = (bf16[1024,128]{1,0:T(8,128)(2,1)}, bf16[1024,128]{1,0:T(8,128)(2,1)S(1)}, u32[]{:S(2)}, u32[]{:S(2)}) collective-permute-start(bf16[1024,128]{1,0:T(8,128)(2,1)} %pad_maximum_fusion.3), channel_id=1, source_target_pairs={{0,1},{1,0},{2,3},{3,2},{4,5},{5,4},{6,7},{7,6},{8,9},{9,8},{10,11... | collective-permute-start | bytes 786440 | tf_op jit(solution)/shard_map/ppermute | solution.py:28
  12.0 41.7 %all-to-all-start = ((bf16[64,32,256]{2,1,0:T(8,128)(2,1)}), bf16[64,32,256]{2,1,0:T(8,128)(2,1)S(1)}, u32[]{:S(2)}, u32[]{:S(2)}) async-start(bf16[64,32,256]{2,1,0:T(8,128)(2,1)} %broadcast_in_dim.43), calls=%async_computation | async-start | bytes 2097152 | tf_op jit(solution)/shard_map/all_to_all | solution.py:49
  23.9 9.9 %collective-permute-start.2 = (bf16[2,2,48,512]{3,2,1,0:T(8,128)(2,1)S(1)}, bf16[2,2,48,512]{3,2,1,0:T(8,128)(2,1)}, u32[]{:S(2)}, u32[]{:S(2)}) collective-permute-start(bf16[2,2,48,512]{3,2,1,0:T(8,128)(2,1)S(1)} %get-tuple-element.101), channel_id=1, source_target_pairs={{0,2},{1,3},{2,0},{3,1},{4,6},{5,7},{6,4},{7,5},{8,10},{9,11},{10,... | collective-permute-start | bytes 589832 | tf_op jit(solution)/shard_map/ppermute | solution.py:72
  34.8 8.1 %collective-permute-start.3 = (bf16[4,1,48,512]{3,2,0,1:T(8,128)(2,1)S(1)}, bf16[4,1,48,512]{3,2,0,1:T(8,128)(2,1)S(1)}, u32[]{:S(2)}, u32[]{:S(2)}) collective-permute-start(bf16[4,1,48,512]{3,2,0,1:T(8,128)(2,1)S(1)} %get-tuple-element.99), channel_id=1, source_target_pairs={{0,1},{1,0},{2,3},{3,2},{4,5},{5,4},{6,7},{7,6},{8,9},{9,8},{10,11... | collective-permute-start | bytes 589832 | tf_op jit(solution)/shard_map/ppermute | solution.py:72
  43.2 0.7 copy-start.13
  43.6 0.8 copy-start.7
  43.9 1.2 copy-start.9
  44.4 4.0 %copy-start.11 = (bf16[384,768]{1,0:T(8,128)(2,1)}, bf16[384,768]{1,0:T(8,128)(2,1)S(1)}, u32[]{:S(2)}) copy-start(bf16[384,768]{1,0:T(8,128)(2,1)S(1)} %convolution_convert_fusion.1) | copy-start | bytes 1769476
  45.1 13.4 %collective-permute-start.4 = (bf16[48,1152]{1,0:T(8,128)(2,1)}, bf16[48,1152]{1,0:T(8,128)(2,1)S(1)}, u32[]{:S(2)}, u32[]{:S(2)}) collective-permute-start(bf16[48,1152]{1,0:T(8,128)(2,1)} %get-tuple-element.44), channel_id=1, source_target_pairs={{0,16},{16,32},{32,48},{48,64},{64,80},{80,96},{96,112},{112,0},{1... | collective-permute-start | bytes 331784 | tf_op jit(solution)/shard_map/ppermute | solution.py:34
  45.7 12.8 %collective-permute-start.5 = (bf16[48,1152]{1,0:T(8,128)(2,1)}, bf16[48,1152]{1,0:T(8,128)(2,1)}, u32[]{:S(2)}, u32[]{:S(2)}) collective-permute-start(bf16[48,1152]{1,0:T(8,128)(2,1)} %get-tuple-element.45), channel_id=1, source_target_pairs={{0,112},{16,0},{32,16},{48,32},{64,48},{80,64},{96,80},{112,96},{1... | collective-permute-start | bytes 331784 | tf_op jit(solution)/shard_map/ppermute | solution.py:34
  48.4 23.2 %copy-start.3 = (bf16[1024,128]{1,0:T(8,128)(2,1)}, bf16[1024,128]{1,0:T(8,128)(2,1)S(1)}, u32[]{:S(2)}) copy-start(bf16[1024,128]{1,0:T(8,128)(2,1)S(1)} %get-tuple-element.107.g_ref) | copy-start | bytes 786436
  53.7 4.8 %copy-start.8 = (bf16[384,768]{1,0:T(8,128)(2,1)S(1)}, bf16[384,768]{1,0:T(8,128)(2,1)}, u32[]{:S(2)}) copy-start(bf16[384,768]{1,0:T(8,128)(2,1)} %copy-done.7) | copy-start | bytes 1769476
  53.7 4.8 %copy-start.10 = (bf16[384,768]{1,0:T(8,128)(2,1)S(1)}, bf16[384,768]{1,0:T(8,128)(2,1)}, u32[]{:S(2)}) copy-start(bf16[384,768]{1,0:T(8,128)(2,1)} %copy-done.9) | copy-start | bytes 1769476
  53.7 4.8 %copy-start.12 = (bf16[384,768]{1,0:T(8,128)(2,1)S(1)}, bf16[384,768]{1,0:T(8,128)(2,1)}, u32[]{:S(2)}) copy-start(bf16[384,768]{1,0:T(8,128)(2,1)} %copy-done.11) | copy-start | bytes 1769476
  59.6 7.2 %collective-permute-start.6 = (bf16[48,2304]{1,0:T(8,128)(2,1)S(1)}, bf16[48,2304]{1,0:T(8,128)(2,1)S(1)}, u32[]{:S(2)}, u32[]{:S(2)}) collective-permute-start(bf16[48,2304]{1,0:T(8,128)(2,1)S(1)} %get-tuple-element.88), channel_id=1, source_target_pairs={{0,16},{16,32},{32,48},{48,64},{64,80},{80,96},{96,112},{112,0},{1... | collective-permute-start | bytes 663560 | tf_op jit(solution)/shard_map/ppermute | solution.py:34
  61.6 6.7 %collective-permute-start.7 = (bf16[48,2304]{1,0:T(8,128)(2,1)S(1)}, bf16[48,2304]{1,0:T(8,128)(2,1)S(1)}, u32[]{:S(2)}, u32[]{:S(2)}) collective-permute-start(bf16[48,2304]{1,0:T(8,128)(2,1)S(1)} %get-tuple-element.87), channel_id=1, source_target_pairs={{0,112},{16,0},{32,16},{48,32},{64,48},{80,64},{96,80},{112,96},{1... | collective-permute-start | bytes 663560 | tf_op jit(solution)/shard_map/ppermute | solution.py:34
  62.9 5.5 %collective-permute-start.8 = (f32[8,1024]{1,0:T(8,128)S(1)}, f32[8,1024]{1,0:T(8,128)S(1)}, u32[]{:S(2)}, u32[]{:S(2)}) collective-permute-start(f32[8,1024]{1,0:T(8,128)S(1)} %attention_stats.1.stats_ref), channel_id=1, source_target_pairs={{0,1},{1,0},{2,3},{3,2},{4,5},{5,4},{6,7},{7,6},{8,9},{9,8},{10,11... | collective-permute-start | bytes 98312 | tf_op jit(solution)/shard_map/ppermute | solution.py:28
  68.4 8.0 %collective-permute-start.10 = (bf16[48,2304]{1,0:T(8,128)(2,1)S(1)}, bf16[48,2304]{1,0:T(8,128)(2,1)S(1)}, u32[]{:S(2)}, u32[]{:S(2)}) collective-permute-start(bf16[48,2304]{1,0:T(8,128)(2,1)S(1)} %get-tuple-element.52), channel_id=1, source_target_pairs={{0,112},{16,0},{32,16},{48,32},{64,48},{80,64},{96,80},{112,96},{1... | collective-permute-start | bytes 663560 | tf_op jit(solution)/shard_map/ppermute | solution.py:34
  71.6 7.9 %collective-permute-start.9 = (bf16[48,2304]{1,0:T(8,128)(2,1)S(1)}, bf16[48,2304]{1,0:T(8,128)(2,1)S(1)}, u32[]{:S(2)}, u32[]{:S(2)}) collective-permute-start(bf16[48,2304]{1,0:T(8,128)(2,1)S(1)} %get-tuple-element.51), channel_id=1, source_target_pairs={{0,16},{16,32},{32,48},{48,64},{64,80},{80,96},{96,112},{112,0},{1... | collective-permute-start | bytes 663560 | tf_op jit(solution)/shard_map/ppermute | solution.py:34
  76.4 6.6 %copy-start.4 = (bf16[1024,128]{1,0:T(8,128)(2,1)S(1)}, bf16[1024,128]{1,0:T(8,128)(2,1)}, u32[]{:S(2)}) copy-start(bf16[1024,128]{1,0:T(8,128)(2,1)} %copy-done.3) | copy-start | bytes 786436
  79.6 8.8 %collective-permute-start.12 = (bf16[48,2304]{1,0:T(8,128)(2,1)S(1)}, bf16[48,2304]{1,0:T(8,128)(2,1)S(1)}, u32[]{:S(2)}, u32[]{:S(2)}) collective-permute-start(bf16[48,2304]{1,0:T(8,128)(2,1)S(1)} %get-tuple-element.58), channel_id=1, source_target_pairs={{0,16},{16,32},{32,48},{48,64},{64,80},{80,96},{96,112},{112,0},{1... | collective-permute-start | bytes 663560 | tf_op jit(solution)/shard_map/ppermute | solution.py:34
  79.9 8.5 %collective-permute-start.13 = (bf16[48,2304]{1,0:T(8,128)(2,1)S(1)}, bf16[48,2304]{1,0:T(8,128)(2,1)S(1)}, u32[]{:S(2)}, u32[]{:S(2)}) collective-permute-start(bf16[48,2304]{1,0:T(8,128)(2,1)S(1)} %get-tuple-element.59), channel_id=1, source_target_pairs={{0,112},{16,0},{32,16},{48,32},{64,48},{80,64},{96,80},{112,96},{1... | collective-permute-start | bytes 663560 | tf_op jit(solution)/shard_map/ppermute | solution.py:34
  88.5 7.5 %collective-permute-start.14 = (bf16[48,2304]{1,0:T(8,128)(2,1)S(1)}, bf16[48,2304]{1,0:T(8,128)(2,1)S(1)}, u32[]{:S(2)}, u32[]{:S(2)}) collective-permute-start(bf16[48,2304]{1,0:T(8,128)(2,1)S(1)} %convert_element_type.154), channel_id=1, source_target_pairs={{0,128},{16,144},{32,160},{48,176},{64,192},{80,208},{96,224},{112... | collective-permute-start | bytes 663560 | tf_op jit(solution)/shard_map/ppermute | solution.py:87
  89.2 15.6 %all-to-all-start.1 = ((bf16[4,512,256]{2,1,0:T(8,128)(2,1)}), bf16[4,512,256]{2,1,0:T(8,128)(2,1)}, u32[]{:S(2)}, u32[]{:S(2)}) async-start(bf16[4,512,256]{2,1,0:T(8,128)(2,1)} %bitcast.34), calls=%async_computation.1 | async-start | bytes 2097152 | tf_op jit(solution)/shard_map/all_to_all | solution.py:55
  96.2 7.2 %collective-permute-start.15 = (bf16[48,2304]{1,0:T(8,128)(2,1)S(1)}, bf16[48,2304]{1,0:T(8,128)(2,1)S(1)}, u32[]{:S(2)}, u32[]{:S(2)}) collective-permute-start(bf16[48,2304]{1,0:T(8,128)(2,1)S(1)} %pad_maximum_fusion.8.refs_0_), channel_id=1, source_target_pairs={{0,16},{16,32},{32,48},{48,64},{64,80},{80,96},{96,112},{112,0},{1... | collective-permute-start | bytes 663560 | tf_op jit(solution)/shard_map/ppermute | solution.py:34
  96.3 7.1 %collective-permute-start.16 = (bf16[48,2304]{1,0:T(8,128)(2,1)S(1)}, bf16[48,2304]{1,0:T(8,128)(2,1)S(1)}, u32[]{:S(2)}, u32[]{:S(2)}) collective-permute-start(bf16[48,2304]{1,0:T(8,128)(2,1)S(1)} %pad_maximum_fusion.8.refs_0_), channel_id=1, source_target_pairs={{0,112},{16,0},{32,16},{48,32},{64,48},{80,64},{96,80},{112,96},{1... | collective-permute-start | bytes 663560 | tf_op jit(solution)/shard_map/ppermute | solution.py:34
  103.5 11.2 %copy-start.5 = (bf16[48,2304]{1,0:T(8,128)(2,1)}, bf16[48,2304]{1,0:T(8,128)(2,1)S(1)}, u32[]{:S(2)}) copy-start(bf16[48,2304]{1,0:T(8,128)(2,1)S(1)} %collective-permute-done.16.refs_1_) | copy-start | bytes 663556
  106.2 14.2 %copy-start.14 = (bf16[8,48,512]{2,1,0:T(8,128)(2,1)S(1)}, bf16[8,48,512]{2,1,0:T(8,128)(2,1)}, u32[]{:S(2)}) copy-start(bf16[8,48,512]{2,1,0:T(8,128)(2,1)} %copy-done.13) | copy-start | bytes 1179652
  106.2 5.8 %collective-permute-start.17 = (bf16[256,256]{1,0:T(8,128)(2,1)S(1)}, bf16[256,256]{1,0:T(8,128)(2,1)S(1)}, u32[]{:S(2)}, u32[]{:S(2)}) collective-permute-start(bf16[256,256]{1,0:T(8,128)(2,1)S(1)} %slice.287), channel_id=1, source_target_pairs={{0,16},{16,0},{32,48},{48,32},{64,80},{80,64},{96,112},{112,96},{1... | collective-permute-start | bytes 393224 | tf_op jit(solution)/shard_map/ppermute | solution.py:63
  106.3 8.3 %collective-permute-start.11 = (bf16[512,128]{1,0:T(8,128)(2,1)S(1)}, bf16[512,128]{1,0:T(8,128)(2,1)S(1)}, u32[]{:S(2)}, u32[]{:S(2)}) collective-permute-start(bf16[512,128]{1,0:T(8,128)(2,1)S(1)} %slice.288), channel_id=1, source_target_pairs={{0,1},{1,0},{2,3},{3,2},{4,5},{5,4},{6,7},{7,6},{8,9},{9,8},{10,11... | collective-permute-start | bytes 393224 | tf_op jit(solution)/shard_map/ppermute | solution.py:28
  112.0 5.9 %collective-permute-start.18 = (bf16[128,256]{1,0:T(8,128)(2,1)S(1)}, bf16[128,256]{1,0:T(8,128)(2,1)S(1)}, u32[]{:S(2)}, u32[]{:S(2)}) collective-permute-start(bf16[128,256]{1,0:T(8,128)(2,1)S(1)} %slice.289), channel_id=1, source_target_pairs={{0,128},{16,144},{32,160},{48,176},{64,192},{80,208},{96,224},{112... | collective-permute-start | bytes 196616 | tf_op jit(solution)/shard_map/ppermute | solution.py:63
  114.7 6.6 %collective-permute-start.21 = (bf16[48,2304]{1,0:T(8,128)(2,1)S(1)}, bf16[48,2304]{1,0:T(8,128)(2,1)S(1)}, u32[]{:S(2)}, u32[]{:S(2)}) collective-permute-start(bf16[48,2304]{1,0:T(8,128)(2,1)S(1)} %collective-permute-done.16.refs_1_), channel_id=1, source_target_pairs={{0,112},{16,0},{32,16},{48,32},{64,48},{80,64},{96,80},{112,96},{1... | collective-permute-start | bytes 663560 | tf_op jit(solution)/shard_map/ppermute | solution.py:34
  116.5 8.3 %collective-permute-start.22 = (bf16[48,2304]{1,0:T(8,128)(2,1)S(1)}, bf16[48,2304]{1,0:T(8,128)(2,1)S(1)}, u32[]{:S(2)}, u32[]{:S(2)}) collective-permute-start(bf16[48,2304]{1,0:T(8,128)(2,1)S(1)} %collective-permute-done.15.refs_8_), channel_id=1, source_target_pairs={{0,16},{16,32},{32,48},{48,64},{64,80},{80,96},{96,112},{112,0},{1... | collective-permute-start | bytes 663560 | tf_op jit(solution)/shard_map/ppermute | solution.py:34
  117.9 20.4 %copy-start.6 = (bf16[48,2304]{1,0:T(8,128)(2,1)S(1)}, bf16[48,2304]{1,0:T(8,128)(2,1)}, u32[]{:S(2)}) copy-start(bf16[48,2304]{1,0:T(8,128)(2,1)} %copy-done.5) | copy-start | bytes 663556
  117.9 8.9 %collective-permute-start.19 = (f32[64,256]{1,0:T(8,128)S(1)}, f32[64,256]{1,0:T(8,128)S(1)}, u32[]{:S(2)}, u32[]{:S(2)}) collective-permute-start(f32[64,256]{1,0:T(8,128)S(1)} %slice.236), channel_id=1, source_target_pairs={{0,32},{16,48},{32,0},{48,16},{64,96},{80,112},{96,64},{112,80},{1... | collective-permute-start | bytes 196616 | tf_op jit(solution)/shard_map/ppermute | solution.py:63
  124.8 6.4 %collective-permute-start.23 = (bf16[48,2304]{1,0:T(8,128)(2,1)S(1)}, bf16[48,2304]{1,0:T(8,128)(2,1)S(1)}, u32[]{:S(2)}, u32[]{:S(2)}) collective-permute-start(bf16[48,2304]{1,0:T(8,128)(2,1)S(1)} %collective-permute-done.21.refs_2_), channel_id=1, source_target_pairs={{0,112},{16,0},{32,16},{48,32},{64,48},{80,64},{96,80},{112,96},{1... | collective-permute-start | bytes 663560 | tf_op jit(solution)/shard_map/ppermute | solution.py:34
  124.8 7.5 %collective-permute-start.24 = (bf16[48,2304]{1,0:T(8,128)(2,1)S(1)}, bf16[48,2304]{1,0:T(8,128)(2,1)S(1)}, u32[]{:S(2)}, u32[]{:S(2)}) collective-permute-start(bf16[48,2304]{1,0:T(8,128)(2,1)S(1)} %collective-permute-done.22.refs_7_), channel_id=1, source_target_pairs={{0,16},{16,32},{32,48},{48,64},{64,80},{80,96},{96,112},{112,0},{1... | collective-permute-start | bytes 663560 | tf_op jit(solution)/shard_map/ppermute | solution.py:34
  126.9 8.9 %collective-permute-start.20 = (f32[32,256]{1,0:T(8,128)S(1)}, f32[32,256]{1,0:T(8,128)S(1)}, u32[]{:S(2)}, u32[]{:S(2)}) collective-permute-start(f32[32,256]{1,0:T(8,128)S(1)} %slice.238), channel_id=1, source_target_pairs={{0,64},{16,80},{32,96},{48,112},{64,0},{80,16},{96,32},{112,48},{1... | collective-permute-start | bytes 98312 | tf_op jit(solution)/shard_map/ppermute | solution.py:63
  132.3 6.0 %collective-permute-start.25 = (bf16[48,1152]{1,0:T(8,128)(2,1)S(1)}, bf16[48,1152]{1,0:T(8,128)(2,1)S(1)}, u32[]{:S(2)}, u32[]{:S(2)}) collective-permute-start(bf16[48,1152]{1,0:T(8,128)(2,1)S(1)} %slice.210), channel_id=1, source_target_pairs={{0,16},{16,32},{32,48},{48,64},{64,80},{80,96},{96,112},{112,0},{1... | collective-permute-start | bytes 331784 | tf_op jit(solution)/shard_map/ppermute | solution.py:34
  132.9 5.5 %collective-permute-start.26 = (bf16[48,1152]{1,0:T(8,128)(2,1)S(1)}, bf16[48,1152]{1,0:T(8,128)(2,1)S(1)}, u32[]{:S(2)}, u32[]{:S(2)}) collective-permute-start(bf16[48,1152]{1,0:T(8,128)(2,1)S(1)} %slice.211), channel_id=1, source_target_pairs={{0,112},{16,0},{32,16},{48,32},{64,48},{80,64},{96,80},{112,96},{1... | collective-permute-start | bytes 331784 | tf_op jit(solution)/shard_map/ppermute | solution.py:34
  139.5 1.3 copy-start.1
  140.7 1.3 collective-permute-start.27
  142.7 10.3 %all-to-all-start.2 = ((bf16[8,48,128]{2,1,0:T(8,128)(2,1)}), bf16[8,48,128]{2,1,0:T(8,128)(2,1)S(1)}, u32[]{:S(2)}, u32[]{:S(2)}) async-start(bf16[8,48,128]{2,1,0:T(8,128)(2,1)} %add_convert_fusion.7), calls=%async_computation.2 | async-start | bytes 196608 | tf_op jit(solution)/shard_map/all_to_all | solution.py:452
  148.3 1.5 copy-start.2
  149.8 5.4 %copy-start.16 = (pred[512,384]{0,1:T(32,128)(4,1)S(1)}, pred[512,384]{0,1:T(32,128)(4,1)}, u32[]{:S(2)}) copy-start(pred[512,384]{0,1:T(32,128)(4,1)} %copy-done.15) | copy-start | bytes 589828
  153.0 0.6 copy-start.17

commit v12 on v9

--- a/solution.py
+++ b/solution.py
@@ -76,10 +76,11 @@
     shape = blocks.shape
     bits = shape[0].bit_length() - 1
     for bit in range(bits):
+        middle = blocks
         blocks = blocks.reshape((2**bit, 2, -1) + shape[1:])
         got = partner(blocks[:, 1], 2 ** (bits - 1 - bit))
         blocks = jnp.stack([blocks[:, 0], got], axis=1)
-    return blocks.reshape(shape)
+    return blocks.reshape(shape), middle
 
 
 def opposite(block):
@@ -101,11 +102,12 @@
     return parts[far][:, :cut], parts[far][:, cut:]
 
 
-def sum_step(move, parts, step, onward, back):
+def sum_step(move, parts, step, onward, back, waits=()):
     n = len(parts)
     far = n // 2
     cut = parts[0].shape[1] // 2
     onward, back = move(onward, 1), move(back, -1)
+    onward, back = both_after(onward, back, *waits)
     ahead, behind = parts[far - 1 - step], parts[(far + 1 + step) % n]
     if step == 0:
         onward = jnp.concatenate([add_low(onward, ahead[:, :cut]), ahead[:, cut:]], axis=1)
@@ -304,8 +306,8 @@
     picked = jnp.einsum("bs,bd->sd", placed_low, rows, preferred_element_type=F32)
     scaled = picked[:, width:] * slot_weight.reshape(-1, 1)
     sent = jnp.concatenate([picked[:, :width].astype(BF), scaled.astype(BF)], axis=1)
-    got = exchange(sent.reshape(exp_size, CAP, 2 * width))
-    return placed_low, got
+    got, middle = exchange(sent.reshape(exp_size, CAP, 2 * width))
+    return placed_low, got, middle
 
 
 def project(got, gate_weight, up_weight, down_weight):
@@ -423,7 +425,7 @@
     columns = mine.shape[1]
     mine = (mine + lax.ppermute(other, "head", [(0, 1), (1, 0)]).astype(F32)).astype(BF)
     mine = turn(mine.reshape(ring, -1, columns), (ring - at) % ring).reshape(exp_size, CAP, columns)
-    back_rows = exchange(mine)
+    back_rows, _ = exchange(mine)
     grad_input = jnp.dot(
         placed_low, back_rows.reshape(-1, columns), preferred_element_type=F32
     ).astype(BF)
@@ -447,8 +449,8 @@
     rows = tokens * queries.shape[1]
     size = queries.shape[2]
     pair = jnp.concatenate([key_rows[:, 0, :], value_vector_rows[:, 0, :]], axis=1)
-    flat = key_gather(pair)
-    placed_low, got = select(moe_input, moe_grad, expert_ids, router_weight)
+    placed_low, got, middle = select(moe_input, moe_grad, expert_ids, router_weight)
+    flat = key_gather(after(pair, middle))
     mine = jnp.concatenate([by_head(queries), by_head(grad_attn)], axis=0)
     theirs = beside(mine)
     queries = jnp.concatenate([mine[:rows], theirs[:rows]], axis=0)
@@ -457,16 +459,14 @@
         got, gate_weight, up_weight, down_weight
     )
     onward, back = both_after(*sum_start(parts), theirs)
+    onward, back = sum_step(z_move, parts, 0, onward, back)
     stats = attention_stats(own, tokens, queries, grads, after(flat, onward, back))
-    onward, back = sum_step(z_move, parts, 0, onward, back)
-    onward, back = both_after(onward, back, stats)
+    onward, back = sum_step(z_move, parts, 1, onward, back, (stats,))
     far_stats = beside(stats)
-    onward, back = sum_step(z_move, parts, 1, onward, back)
-    onward, back = both_after(onward, back, far_stats)
     half = flat.shape[0] // 2
     middle = lax.axis_size("ctx") // 2
     lower = attention_grads(
-        own, tokens, 0, queries, grads, after(flat[:half], onward, back), stats, far_stats
+        own, tokens, 0, queries, grads, flat[:half], after(stats, onward, back), far_stats
     )
     onward, back = sum_step(z_move, parts, 2, onward, back)
     onward, back = both_after(onward, back, *lower)

time: 154 us -> 159 us (1.032)
  waiting for transfers between devices: 47.6 us -> 55.2 us
  starting transfers between devices: 66.8 us -> 62.7 us
  other arithmetic: 10.1 us -> 12 us
    ppermute x16, waiting for transfers between devices: 23.5 us -> 33.6 us  [z_move(): return lax.ppermute(block, 'ctx', pairs)]
    ppermute x4, starting transfers between devices: 9.93 us -> 3.42 us  [ctx_sum(): both = both[:half] + lax.ppermute(sent, 'ctx', pairs).astype(F32)]
    ppermute x6, waiting for transfers between devices: 14.7 us -> 11.2 us  [partner(): lax.ppermute(block, 'exp', [(e, e ^ mask) for e in range(lax.axis_size('e...]
    ppermute x1, waiting for transfers between devices: 3.91 us -> 0.53 us  [opposite(): lax.ppermute(block, 'ctx', [(c, (c + n // X_HI) % n) for c in range(n)])]
    all_to_all x1, waiting for transfers between devices: 0.01 us -> 3.07 us  [y_parts(): lax.all_to_all(parts, 'exp', 0, 0, tiled=True, axis_index_groups=groups)]
    ppermute x4, waiting for transfers between devices: 4.52 us -> 6.81 us  [ctx_sum(): both = both[:half] + lax.ppermute(sent, 'ctx', pairs).astype(F32)]
    ppermute x1, starting transfers between devices: 0.77 us -> 2.39 us  [opposite(): lax.ppermute(block, 'ctx', [(c, (c + n // X_HI) % n) for c in range(n)])]
  transfers between devices with their start and end apart: 33 -> 33, of which waited for: 19 -> 17; matrix products, arithmetic and copies ran while one was open for 9% -> 9% of each run, Pallas kernels for 8% -> 10%
where the time goes in v12:
time: 159 us; the launch traced here: 157 us
  starting transfers between devices  62.7 us (39%)
  waiting for transfers between devices  55.2 us (35%)
  Pallas kernels  17 us (11%)
  other arithmetic  12 us (8%)
  local copies, waits for them, and re-layouts  5.81 us (4%)
  matrix products  3.43 us (2%)
    ppermute x16, waiting for transfers between devices, z_move(): return lax.ppermute(block, 'ctx', pairs)  33.6 us
    ppermute x16, starting transfers between devices, z_move(): return lax.ppermute(block, 'ctx', pairs)  24 us
    all_to_all x1, starting transfers between devices, key_gather(): lax.all_to_all(copies, ('ctx', 'exp'), 0, 0, tiled=True, axis_index_group...  13.3 us
    ppermute x6, starting transfers between devices, partner(): lax.ppermute(block, 'exp', [(e, e ^ mask) for e in range(lax.axis_size('e...  11.5 us
    ppermute x6, waiting for transfers between devices, partner(): lax.ppermute(block, 'exp', [(e, e ^ mask) for e in range(lax.axis_size('e...  11.2 us
    pallas_call x2, Pallas kernels, attention_grads(): pl.pallas_call(functools.partial(grads_body, own, rows, tokens), out_shap...  10.2 us
    ppermute x4, waiting for transfers between devices, ctx_sum(): both = both[:half] + lax.ppermute(sent, 'ctx', pairs).astype(F32)  6.81 us
    pallas_call x1, Pallas kernels, attention_stats(): pl.pallas_call(functools.partial(stats_body, own, lax.axis_size('exp') //...  4.78 us
  transfers between devices with their start and end apart: 33, of which 17 were waited for; matrix products, arithmetic and copies ran while one was open for 9% of the time, Pallas kernels for 10%

profile of v12, /device:TPU:2, one launch (start us, length us, event | category | flops | bytes accessed | tf_op | source)
XLA Modules:
  0.0 157.5 jit_solution(4282137249644530146)
XLA Ops:
  0.7 0.9 fusion.19
  1.6 1.1 reduce-window.6
  3.0 0.8 fusion.20
  4.5 1.4 fusion.2
  6.2 3.3 %collective-permute-start.1 = (bf16[1,4,48,512]{3,2,1,0:T(8,128)(2,1)S(1)}, bf16[1,4,48,512]{3,2,1,0:T(8,128)(2,1)S(1)}, u32[]{:S(2)}, u32[]{:S(2)}) collective-permute-start(bf16[1,4,48,512]{3,2,1,0:T(8,128)(2,1)S(1)} %get-tuple-element.101), channel_id=1, source_target_pairs={{0,4},{1,5},{2,6},{3,7},{4,0},{5,1},{6,2},{7,3},{8,12},{9,13},{10,... | collective-permute-start | bytes 589832 | tf_op jit(solution)/shard_map/ppermute | solution.py:72
  9.5 4.9 %collective-permute-done.1 = bf16[1,4,48,512]{3,2,1,0:T(8,128)(2,1)S(1)} collective-permute-done((bf16[1,4,48,512]{3,2,1,0:T(8,128)(2,1)S(1)}, bf16[1,4,48,512]{3,2,1,0:T(8,128)(2,1)S(1)}, u32[]{:S(2)}, u32[]{:S(2)}) %collective-permute-start.1) | collective-permute-done | bytes 196640 | tf_op jit(solution)/shard_map/ppermute | solution.py:72
  14.5 1.7 %collective-permute-start.2 = (bf16[2,2,48,512]{3,2,1,0:T(8,128)(2,1)S(1)}, bf16[2,2,48,512]{3,2,1,0:T(8,128)(2,1)S(1)}, u32[]{:S(2)}, u32[]{:S(2)}) collective-permute-start(bf16[2,2,48,512]{3,2,1,0:T(8,128)(2,1)S(1)} %get-tuple-element.99), channel_id=1, source_target_pairs={{0,2},{1,3},{2,0},{3,1},{4,6},{5,7},{6,4},{7,5},{8,10},{9,11},{10,... | collective-permute-start | bytes 589832 | tf_op jit(solution)/shard_map/ppermute | solution.py:72
  16.1 0.7 pad_maximum_fusion.3
  16.9 0.5 collective-permute-start
  17.4 2.9 %collective-permute-done.2 = bf16[2,2,48,512]{3,2,1,0:T(8,128)(2,1)S(1)} collective-permute-done((bf16[2,2,48,512]{3,2,1,0:T(8,128)(2,1)S(1)}, bf16[2,2,48,512]{3,2,1,0:T(8,128)(2,1)S(1)}, u32[]{:S(2)}, u32[]{:S(2)}) %collective-permute-start.2) | collective-permute-done | bytes 196640 | tf_op jit(solution)/shard_map/ppermute | solution.py:72
  20.4 0.7 slice_bitcast_fusion.1
  21.1 1.2 collective-permute-start.3
  22.5 1.1 broadcast_in_dim.47
  23.6 13.3 %all-to-all-start = ((bf16[64,32,256]{2,1,0:T(8,128)(2,1)}), bf16[64,32,256]{2,1,0:T(8,128)(2,1)S(1)}, u32[]{:S(2)}, u32[]{:S(2)}) async-start(bf16[64,32,256]{2,1,0:T(8,128)(2,1)} %broadcast_in_dim.47), calls=%async_computation | async-start | bytes 2097152 | tf_op jit(solution)/shard_map/all_to_all | solution.py:45
  36.9 1.0 pad_maximum_fusion.2
  39.2 1.6 %collective-permute-start.4 = (bf16[48,1152]{1,0:T(8,128)(2,1)S(1)}, bf16[48,1152]{1,0:T(8,128)(2,1)S(1)}, u32[]{:S(2)}, u32[]{:S(2)}) collective-permute-start(bf16[48,1152]{1,0:T(8,128)(2,1)S(1)} %get-tuple-element.44), channel_id=1, source_target_pairs={{0,16},{16,32},{32,48},{48,64},{64,80},{80,96},{96,112},{112,0},{1... | collective-permute-start | bytes 331784 | tf_op jit(solution)/shard_map/ppermute | solution.py:34
  40.8 1.7 %collective-permute-start.5 = (bf16[48,1152]{1,0:T(8,128)(2,1)S(1)}, bf16[48,1152]{1,0:T(8,128)(2,1)S(1)}, u32[]{:S(2)}, u32[]{:S(2)}) collective-permute-start(bf16[48,1152]{1,0:T(8,128)(2,1)S(1)} %get-tuple-element.45), channel_id=1, source_target_pairs={{0,112},{16,0},{32,16},{48,32},{64,48},{80,64},{96,80},{112,96},{1... | collective-permute-start | bytes 331784 | tf_op jit(solution)/shard_map/ppermute | solution.py:34
  42.5 19.6 %collective-permute-done.4 = bf16[48,1152]{1,0:T(8,128)(2,1)S(1)} collective-permute-done((bf16[48,1152]{1,0:T(8,128)(2,1)S(1)}, bf16[48,1152]{1,0:T(8,128)(2,1)S(1)}, u32[]{:S(2)}, u32[]{:S(2)}) %collective-permute-start.4) | collective-permute-done | bytes 110624 | tf_op jit(solution)/shard_map/ppermute | solution.py:34
  62.2 0.8 fusion.13
  63.2 3.1 %collective-permute-start.7 = (bf16[48,2304]{1,0:T(8,128)(2,1)}, bf16[48,2304]{1,0:T(8,128)(2,1)}, u32[]{:S(2)}, u32[]{:S(2)}) collective-permute-start(bf16[48,2304]{1,0:T(8,128)(2,1)} %get-tuple-element.85), channel_id=1, source_target_pairs={{0,112},{16,0},{32,16},{48,32},{64,48},{80,64},{96,80},{112,96},{1... | collective-permute-start | bytes 663560 | tf_op jit(solution)/shard_map/ppermute | solution.py:34
  66.4 4.8 %attention_stats.1.stats_ref = f32[8,1024]{1,0:T(8,128)S(1)} custom-call(s32[3]{0:T(128)S(1)} %pad_add_fusion.2.here_ref, bf16[1024,128]{1,0:T(8,128)(2,1)S(1)} %get-tuple-element.110.q_ref, bf16[1024,128]{1,0:T(8,128)(2,1)S(1)} %get-tuple-element.111.g_ref, bf16[2048,256]{1,0:T(8,128)(2,1)S(1)} %bitcast.83), custom_call_target="tpu_custom_call" | custom-call | flops 1073741824 | bytes 1048576 | tf_op jit(solution)/shard_map/attention_stats/pallas_call | solution.py:244
  71.1 1.9 %collective-permute-start.10 = (f32[8,1024]{1,0:T(8,128)S(1)}, f32[8,1024]{1,0:T(8,128)S(1)}, u32[]{:S(2)}, u32[]{:S(2)}) collective-permute-start(f32[8,1024]{1,0:T(8,128)S(1)} %attention_stats.1.stats_ref), channel_id=1, source_target_pairs={{0,1},{1,0},{2,3},{3,2},{4,5},{5,4},{6,7},{7,6},{8,9},{9,8},{10,11... | collective-permute-start | bytes 98312 | tf_op jit(solution)/shard_map/ppermute | solution.py:28
  73.0 1.1 add_convert_fusion.2
  74.2 1.9 %collective-permute-start.8 = (bf16[48,2304]{1,0:T(8,128)(2,1)S(1)}, bf16[48,2304]{1,0:T(8,128)(2,1)S(1)}, u32[]{:S(2)}, u32[]{:S(2)}) collective-permute-start(bf16[48,2304]{1,0:T(8,128)(2,1)S(1)} %get-tuple-element.82), channel_id=1, source_target_pairs={{0,16},{16,32},{32,48},{48,64},{64,80},{80,96},{96,112},{112,0},{1... | collective-permute-start | bytes 663560 | tf_op jit(solution)/shard_map/ppermute | solution.py:34
  76.1 1.5 collective-permute-start.9
  77.6 4.7 %attention_grads.2 = (bf16[4,16,32,256]{3,2,1,0:T(8,128)(2,1)S(1)}, f32[1024,128]{1,0:T(8,128)S(1)}) custom-call(s32[3]{0:T(128)S(1)} %pad_add_fusion.2.here_ref, bf16[1024,128]{1,0:T(8,128)(2,1)S(1)} %get-tuple-element.110.q_ref, bf16[1024,128]{1,0:T(8,128)(2,1)S(1)} %get-tuple-element.111.g_ref, bf16[1024,256]{1,0:T(8,128)(2,1)S(1)} %bitcast.85, ...), custom_call_target="tpu_custom_call" | custom-call | flops 1342177280 | bytes 1048576 | tf_op jit(solution)/shard_map/attention_grads/pallas_call | solution.py:263
  83.2 2.9 %collective-permute-start.13 = (bf16[48,2304]{1,0:T(8,128)(2,1)S(1)}, bf16[48,2304]{1,0:T(8,128)(2,1)S(1)}, u32[]{:S(2)}, u32[]{:S(2)}) collective-permute-start(bf16[48,2304]{1,0:T(8,128)(2,1)S(1)} %get-tuple-element.57), channel_id=1, source_target_pairs={{0,112},{16,0},{32,16},{48,32},{64,48},{80,64},{96,80},{112,96},{1... | collective-permute-start | bytes 663560 | tf_op jit(solution)/shard_map/ppermute | solution.py:34
  86.2 5.4 %attention_grads.3 = (bf16[4,16,32,256]{3,2,1,0:T(8,128)(2,1)}, f32[1024,128]{1,0:T(8,128)S(1)}) custom-call(s32[3]{0:T(128)S(1)} %pad_add_fusion.here_ref, bf16[1024,128]{1,0:T(8,128)(2,1)S(1)} %get-tuple-element.110.q_ref, bf16[1024,128]{1,0:T(8,128)(2,1)S(1)} %copy-done.2, bf16[1024,256]{1,0:T(8,128)(2,1)S(1)} %bitcast.84, ...), custom_call_target="tpu_custom_call" | custom-call | flops 1342177280 | bytes 1048576 | tf_op jit(solution)/shard_map/attention_grads/pallas_call | solution.py:263
  91.7 2.4 %collective-permute-start.14 = (bf16[48,2304]{1,0:T(8,128)(2,1)S(1)}, bf16[48,2304]{1,0:T(8,128)(2,1)S(1)}, u32[]{:S(2)}, u32[]{:S(2)}) collective-permute-start(bf16[48,2304]{1,0:T(8,128)(2,1)S(1)} %convert_element_type.154), channel_id=1, source_target_pairs={{0,128},{16,144},{32,160},{48,176},{64,192},{80,208},{96,224},{112... | collective-permute-start | bytes 663560 | tf_op jit(solution)/shard_map/ppermute | solution.py:88
  94.1 4.6 %all-to-all-start.1 = ((bf16[4,512,256]{2,1,0:T(8,128)(2,1)}), bf16[4,512,256]{2,1,0:T(8,128)(2,1)}, u32[]{:S(2)}, u32[]{:S(2)}) async-start(bf16[4,512,256]{2,1,0:T(8,128)(2,1)} %bitcast.34), calls=%async_computation.1 | async-start | bytes 2097152 | tf_op jit(solution)/shard_map/all_to_all | solution.py:55
  98.7 0.5 collective-permute-done.14
  99.5 3.2 %collective-permute-start.16 = (bf16[48,2304]{1,0:T(8,128)(2,1)S(1)}, bf16[48,2304]{1,0:T(8,128)(2,1)S(1)}, u32[]{:S(2)}, u32[]{:S(2)}) collective-permute-start(bf16[48,2304]{1,0:T(8,128)(2,1)S(1)} %pad_maximum_fusion.8.refs_0_), channel_id=1, source_target_pairs={{0,112},{16,0},{32,16},{48,32},{64,48},{80,64},{96,80},{112,96},{1... | collective-permute-start | bytes 663560 | tf_op jit(solution)/shard_map/ppermute | solution.py:34
  102.8 1.0 collective-permute-start.11
  103.8 2.9 %collective-permute-done.15.refs_8_ = bf16[48,2304]{1,0:T(8,128)(2,1)S(1)} collective-permute-done((bf16[48,2304]{1,0:T(8,128)(2,1)S(1)}, bf16[48,2304]{1,0:T(8,128)(2,1)S(1)}, u32[]{:S(2)}, u32[]{:S(2)}) %collective-permute-start.15) | collective-permute-done | bytes 221216 | tf_op jit(solution)/shard_map/ppermute | solution.py:34
  106.6 3.1 %all-to-all-done.1 = bf16[4,512,256]{2,1,0:T(8,128)(2,1)} async-done(((bf16[4,512,256]{2,1,0:T(8,128)(2,1)}), bf16[4,512,256]{2,1,0:T(8,128)(2,1)}, u32[]{:S(2)}, u32[]{:S(2)}) %all-to-all-start.1) | async-done | bytes 1048608 | tf_op jit(solution)/shard_map/all_to_all | solution.py:55
  109.7 1.4 convert_reduce_fusion
  111.3 2.0 %collective-permute-start.21 = (bf16[48,2304]{1,0:T(8,128)(2,1)S(1)}, bf16[48,2304]{1,0:T(8,128)(2,1)S(1)}, u32[]{:S(2)}, u32[]{:S(2)}) collective-permute-start(bf16[48,2304]{1,0:T(8,128)(2,1)S(1)} %collective-permute-done.16.refs_1_), channel_id=1, source_target_pairs={{0,112},{16,0},{32,16},{48,32},{64,48},{80,64},{96,80},{112,96},{1... | collective-permute-start | bytes 663560 | tf_op jit(solution)/shard_map/ppermute | solution.py:34
  113.4 4.2 %collective-permute-done.17 = bf16[256,256]{1,0:T(8,128)(2,1)S(1)} collective-permute-done((bf16[256,256]{1,0:T(8,128)(2,1)S(1)}, bf16[256,256]{1,0:T(8,128)(2,1)S(1)}, u32[]{:S(2)}, u32[]{:S(2)}) %collective-permute-start.17) | collective-permute-done | bytes 131104 | tf_op jit(solution)/shard_map/ppermute | solution.py:63
  117.6 0.6 slice.330
  118.7 0.8 fusion
  119.5 1.2 collective-permute-done.21.refs_2_
  120.8 2.0 %collective-permute-done.22.refs_7_ = bf16[48,2304]{1,0:T(8,128)(2,1)S(1)} collective-permute-done((bf16[48,2304]{1,0:T(8,128)(2,1)S(1)}, bf16[48,2304]{1,0:T(8,128)(2,1)S(1)}, u32[]{:S(2)}, u32[]{:S(2)}) %collective-permute-start.22) | collective-permute-done | bytes 221216 | tf_op jit(solution)/shard_map/ppermute | solution.py:34
  122.7 1.3 collective-permute-start.23
  124.0 0.7 collective-permute-start.24
  125.1 1.0 fusion.34
  126.1 3.0 %collective-permute-done.23.refs_3_ = bf16[48,2304]{1,0:T(8,128)(2,1)S(1)} collective-permute-done((bf16[48,2304]{1,0:T(8,128)(2,1)S(1)}, bf16[48,2304]{1,0:T(8,128)(2,1)S(1)}, u32[]{:S(2)}, u32[]{:S(2)}) %collective-permute-start.23) | collective-permute-done | bytes 221216 | tf_op jit(solution)/shard_map/ppermute | solution.py:34
  129.2 2.0 %collective-permute-done.24.refs_6_ = bf16[48,2304]{1,0:T(8,128)(2,1)S(1)} collective-permute-done((bf16[48,2304]{1,0:T(8,128)(2,1)S(1)}, bf16[48,2304]{1,0:T(8,128)(2,1)S(1)}, u32[]{:S(2)}, u32[]{:S(2)}) %collective-permute-start.24) | collective-permute-done | bytes 221216 | tf_op jit(solution)/shard_map/ppermute | solution.py:34
  131.3 3.3 %collective-permute-start.26 = (bf16[48,1152]{1,0:T(8,128)(2,1)S(1)}, bf16[48,1152]{1,0:T(8,128)(2,1)S(1)}, u32[]{:S(2)}, u32[]{:S(2)}) collective-permute-start(bf16[48,1152]{1,0:T(8,128)(2,1)S(1)} %slice.229), channel_id=1, source_target_pairs={{0,112},{16,0},{32,16},{48,32},{64,48},{80,64},{96,80},{112,96},{1... | collective-permute-start | bytes 331784 | tf_op jit(solution)/shard_map/ppermute | solution.py:34
  134.6 2.6 %collective-permute-done.25.refs_4_ = bf16[48,1152]{1,0:T(8,128)(2,1)S(1)} collective-permute-done((bf16[48,1152]{1,0:T(8,128)(2,1)S(1)}, bf16[48,1152]{1,0:T(8,128)(2,1)S(1)}, u32[]{:S(2)}, u32[]{:S(2)}) %collective-permute-start.25) | collective-permute-done | bytes 110624 | tf_op jit(solution)/shard_map/ppermute | solution.py:34
  137.2 0.5 expert_contrib.1
  137.8 0.9 add_convert_fusion.4
  138.8 0.8 copy.51
  139.6 2.6 %collective-permute-start.20 = (f32[32,256]{1,0:T(8,128)S(1)}, f32[32,256]{1,0:T(8,128)S(1)}, u32[]{:S(2)}, u32[]{:S(2)}) collective-permute-start(f32[32,256]{1,0:T(8,128)S(1)} %slice.262), channel_id=1, source_target_pairs={{0,64},{16,80},{32,96},{48,112},{64,0},{80,16},{96,32},{112,48},{1... | collective-permute-start | bytes 98312 | tf_op jit(solution)/shard_map/ppermute | solution.py:63
  142.3 2.5 %collective-permute-start.28 = (bf16[1,4,48,128]{3,2,1,0:T(8,128)(2,1)S(1)}, bf16[1,4,48,128]{3,2,1,0:T(8,128)(2,1)S(1)}, u32[]{:S(2)}, u32[]{:S(2)}) collective-permute-start(bf16[1,4,48,128]{3,2,1,0:T(8,128)(2,1)S(1)} %get-tuple-element.109), channel_id=1, source_target_pairs={{0,4},{1,5},{2,6},{3,7},{4,0},{5,1},{6,2},{7,3},{8,12},{9,13},{10,... | collective-permute-start | bytes 147464 | tf_op jit(solution)/shard_map/ppermute | solution.py:72
  144.8 2.6 %collective-permute-done.20 = f32[32,256]{1,0:T(8,128)S(1)} collective-permute-done((f32[32,256]{1,0:T(8,128)S(1)}, f32[32,256]{1,0:T(8,128)S(1)}, u32[]{:S(2)}, u32[]{:S(2)}) %collective-permute-start.20) | collective-permute-done | bytes 32800 | tf_op jit(solution)/shard_map/ppermute | solution.py:63
  147.4 0.6 collective-permute-done.28
  148.0 1.3 collective-permute-start.29
  149.2 0.6 fusion.26
  149.8 2.3 %collective-permute-done.29 = bf16[2,2,48,128]{3,2,1,0:T(8,128)(2,1)S(1)} collective-permute-done((bf16[2,2,48,128]{3,2,1,0:T(8,128)(2,1)S(1)}, bf16[2,2,48,128]{3,2,1,0:T(8,128)(2,1)S(1)}, u32[]{:S(2)}, u32[]{:S(2)}) %collective-permute-start.29) | collective-permute-done | bytes 49184 | tf_op jit(solution)/shard_map/ppermute | solution.py:72
  152.2 1.6 collective-permute-start.30
  153.7 0.6 fusion.27
  154.3 1.5 expert_weight_grads.1
  155.9 0.5 collective-permute-done.30
  156.4 1.0 convolution_convert_fusion.3
  (121 shorter events, 5.7 us)
Async XLA Ops:
  0.6 38.2 %copy-start = (bf16[1,1536,256]{2,1,0:T(8,128)(2,1)S(1)}, bf16[1,1536,256]{2,1,0:T(8,128)(2,1)}, u32[]{:S(2)}) copy-start(bf16[1,1536,256]{2,1,0:T(8,128)(2,1)} %param.21) | copy-start | bytes 2359300
  6.0 3.5 %copy-start.15 = (bf16[256,2,128]{2,1,0:T(2,128)(2,1)S(1)}, bf16[256,2,128]{2,1,0:T(2,128)(2,1)}, u32[]{:S(2)}) copy-start(bf16[256,2,128]{2,1,0:T(2,128)(2,1)} %param.11) | copy-start | bytes 393220
  6.0 3.5 %copy-start.16 = (bf16[256,2,128]{2,1,0:T(2,128)(2,1)S(1)}, bf16[256,2,128]{2,1,0:T(2,128)(2,1)}, u32[]{:S(2)}) copy-start(bf16[256,2,128]{2,1,0:T(2,128)(2,1)} %param.14) | copy-start | bytes 393220
  6.1 11.2 %copy-start.17 = (bf16[32,1,128]{2,0,1:T(8,128)(2,1)S(1)}, bf16[32,1,128]{2,0,1:T(8,128)(2,1)}, u32[]{:S(2)}) copy-start(bf16[32,1,128]{2,0,1:T(8,128)(2,1)} %param.13) | copy-start | bytes 24580
  6.2 11.2 %copy-start.18 = (bf16[32,1,128]{2,0,1:T(8,128)(2,1)S(1)}, bf16[32,1,128]{2,0,1:T(8,128)(2,1)}, u32[]{:S(2)}) copy-start(bf16[32,1,128]{2,0,1:T(8,128)(2,1)} %param.12) | copy-start | bytes 24580
  6.2 8.2 %collective-permute-start.1 = (bf16[1,4,48,512]{3,2,1,0:T(8,128)(2,1)S(1)}, bf16[1,4,48,512]{3,2,1,0:T(8,128)(2,1)S(1)}, u32[]{:S(2)}, u32[]{:S(2)}) collective-permute-start(bf16[1,4,48,512]{3,2,1,0:T(8,128)(2,1)S(1)} %get-tuple-element.101), channel_id=1, source_target_pairs={{0,4},{1,5},{2,6},{3,7},{4,0},{5,1},{6,2},{7,3},{8,12},{9,13},{10,... | collective-permute-start | bytes 589832 | tf_op jit(solution)/shard_map/ppermute | solution.py:72
  14.5 5.9 %collective-permute-start.2 = (bf16[2,2,48,512]{3,2,1,0:T(8,128)(2,1)S(1)}, bf16[2,2,48,512]{3,2,1,0:T(8,128)(2,1)S(1)}, u32[]{:S(2)}, u32[]{:S(2)}) collective-permute-start(bf16[2,2,48,512]{3,2,1,0:T(8,128)(2,1)S(1)} %get-tuple-element.99), channel_id=1, source_target_pairs={{0,2},{1,3},{2,0},{3,1},{4,6},{5,7},{6,4},{7,5},{8,10},{9,11},{10,... | collective-permute-start | bytes 589832 | tf_op jit(solution)/shard_map/ppermute | solution.py:72
  16.9 22.3 %collective-permute-start = (bf16[1024,128]{1,0:T(8,128)(2,1)}, bf16[1024,128]{1,0:T(8,128)(2,1)S(1)}, u32[]{:S(2)}, u32[]{:S(2)}) collective-permute-start(bf16[1024,128]{1,0:T(8,128)(2,1)} %pad_maximum_fusion.3), channel_id=1, source_target_pairs={{0,1},{1,0},{2,3},{3,2},{4,5},{5,4},{6,7},{7,6},{8,9},{9,8},{10,11... | collective-permute-start | bytes 786440 | tf_op jit(solution)/shard_map/ppermute | solution.py:28
  20.3 2.1 %copy-start.13 = (bf16[1,256,1536]{2,1,0:T(8,128)(2,1)S(1)}, bf16[1,256,1536]{2,1,0:T(8,128)(2,1)}, u32[]{:S(2)}) copy-start(bf16[1,256,1536]{2,1,0:T(8,128)(2,1)} %param.20) | copy-start | bytes 2359300
  20.3 2.1 %copy-start.14 = (bf16[1,256,1536]{2,1,0:T(8,128)(2,1)S(1)}, bf16[1,256,1536]{2,1,0:T(8,128)(2,1)}, u32[]{:S(2)}) copy-start(bf16[1,256,1536]{2,1,0:T(8,128)(2,1)} %param.19) | copy-start | bytes 2359300
  21.1 15.8 %collective-permute-start.3 = (bf16[4,1,48,512]{3,2,0,1:T(8,128)(2,1)}, bf16[4,1,48,512]{3,2,0,1:T(8,128)(2,1)}, u32[]{:S(2)}, u32[]{:S(2)}) collective-permute-start(bf16[4,1,48,512]{3,2,0,1:T(8,128)(2,1)} %get-tuple-element.97), channel_id=1, source_target_pairs={{0,1},{1,0},{2,3},{3,2},{4,5},{5,4},{6,7},{7,6},{8,9},{9,8},{10,11... | collective-permute-start | bytes 589832 | tf_op jit(solution)/shard_map/ppermute | solution.py:72
  23.6 42.7 %all-to-all-start = ((bf16[64,32,256]{2,1,0:T(8,128)(2,1)}), bf16[64,32,256]{2,1,0:T(8,128)(2,1)S(1)}, u32[]{:S(2)}, u32[]{:S(2)}) async-start(bf16[64,32,256]{2,1,0:T(8,128)(2,1)} %broadcast_in_dim.47), calls=%async_computation | async-start | bytes 2097152 | tf_op jit(solution)/shard_map/all_to_all | solution.py:45
  38.0 0.7 copy-start.11
  38.4 23.9 %copy-start.5 = (bf16[384,768]{1,0:T(8,128)(2,1)}, bf16[384,768]{1,0:T(8,128)(2,1)S(1)}, u32[]{:S(2)}) copy-start(bf16[384,768]{1,0:T(8,128)(2,1)S(1)} %convolution_convert_fusion.2) | copy-start | bytes 1769476
  38.8 23.4 %copy-start.7 = (bf16[384,768]{1,0:T(8,128)(2,1)}, bf16[384,768]{1,0:T(8,128)(2,1)S(1)}, u32[]{:S(2)}) copy-start(bf16[384,768]{1,0:T(8,128)(2,1)S(1)} %convolution_convert_fusion.1) | copy-start | bytes 1769476
  39.1 23.1 %copy-start.9 = (bf16[384,768]{1,0:T(8,128)(2,1)}, bf16[384,768]{1,0:T(8,128)(2,1)S(1)}, u32[]{:S(2)}) copy-start(bf16[384,768]{1,0:T(8,128)(2,1)S(1)} %convolution_convert_fusion) | copy-start | bytes 1769476
  39.2 23.0 %collective-permute-start.4 = (bf16[48,1152]{1,0:T(8,128)(2,1)S(1)}, bf16[48,1152]{1,0:T(8,128)(2,1)S(1)}, u32[]{:S(2)}, u32[]{:S(2)}) collective-permute-start(bf16[48,1152]{1,0:T(8,128)(2,1)S(1)} %get-tuple-element.44), channel_id=1, source_target_pairs={{0,16},{16,32},{32,48},{48,64},{64,80},{80,96},{96,112},{112,0},{1... | collective-permute-start | bytes 331784 | tf_op jit(solution)/shard_map/ppermute | solution.py:34
  40.8 21.3 %collective-permute-start.5 = (bf16[48,1152]{1,0:T(8,128)(2,1)S(1)}, bf16[48,1152]{1,0:T(8,128)(2,1)S(1)}, u32[]{:S(2)}, u32[]{:S(2)}) collective-permute-start(bf16[48,1152]{1,0:T(8,128)(2,1)S(1)} %get-tuple-element.45), channel_id=1, source_target_pairs={{0,112},{16,0},{32,16},{48,32},{64,48},{80,64},{96,80},{112,96},{1... | collective-permute-start | bytes 331784 | tf_op jit(solution)/shard_map/ppermute | solution.py:34
  63.0 10.0 %collective-permute-start.6 = (bf16[48,2304]{1,0:T(8,128)(2,1)}, bf16[48,2304]{1,0:T(8,128)(2,1)}, u32[]{:S(2)}, u32[]{:S(2)}) collective-permute-start(bf16[48,2304]{1,0:T(8,128)(2,1)} %get-tuple-element.86), channel_id=1, source_target_pairs={{0,16},{16,32},{32,48},{48,64},{64,80},{80,96},{96,112},{112,0},{1... | collective-permute-start | bytes 663560 | tf_op jit(solution)/shard_map/ppermute | solution.py:34
  63.2 9.8 %collective-permute-start.7 = (bf16[48,2304]{1,0:T(8,128)(2,1)}, bf16[48,2304]{1,0:T(8,128)(2,1)}, u32[]{:S(2)}, u32[]{:S(2)}) collective-permute-start(bf16[48,2304]{1,0:T(8,128)(2,1)} %get-tuple-element.85), channel_id=1, source_target_pairs={{0,112},{16,0},{32,16},{48,32},{64,48},{80,64},{96,80},{112,96},{1... | collective-permute-start | bytes 663560 | tf_op jit(solution)/shard_map/ppermute | solution.py:34
  66.3 11.3 %copy-start.1 = (bf16[1024,128]{1,0:T(8,128)(2,1)}, bf16[1024,128]{1,0:T(8,128)(2,1)S(1)}, u32[]{:S(2)}) copy-start(bf16[1024,128]{1,0:T(8,128)(2,1)S(1)} %get-tuple-element.111.g_ref) | copy-start | bytes 786436
  66.3 6.7 %copy-start.6 = (bf16[384,768]{1,0:T(8,128)(2,1)S(1)}, bf16[384,768]{1,0:T(8,128)(2,1)}, u32[]{:S(2)}) copy-start(bf16[384,768]{1,0:T(8,128)(2,1)} %copy-done.5) | copy-start | bytes 1769476
  66.3 6.7 %copy-start.8 = (bf16[384,768]{1,0:T(8,128)(2,1)S(1)}, bf16[384,768]{1,0:T(8,128)(2,1)}, u32[]{:S(2)}) copy-start(bf16[384,768]{1,0:T(8,128)(2,1)} %copy-done.7) | copy-start | bytes 1769476
  66.4 6.7 %copy-start.10 = (bf16[384,768]{1,0:T(8,128)(2,1)S(1)}, bf16[384,768]{1,0:T(8,128)(2,1)}, u32[]{:S(2)}) copy-start(bf16[384,768]{1,0:T(8,128)(2,1)} %copy-done.9) | copy-start | bytes 1769476
  71.1 6.4 %collective-permute-start.10 = (f32[8,1024]{1,0:T(8,128)S(1)}, f32[8,1024]{1,0:T(8,128)S(1)}, u32[]{:S(2)}, u32[]{:S(2)}) collective-permute-start(f32[8,1024]{1,0:T(8,128)S(1)} %attention_stats.1.stats_ref), channel_id=1, source_target_pairs={{0,1},{1,0},{2,3},{3,2},{4,5},{5,4},{6,7},{7,6},{8,9},{9,8},{10,11... | collective-permute-start | bytes 98312 | tf_op jit(solution)/shard_map/ppermute | solution.py:28
  74.2 8.2 %collective-permute-start.8 = (bf16[48,2304]{1,0:T(8,128)(2,1)S(1)}, bf16[48,2304]{1,0:T(8,128)(2,1)S(1)}, u32[]{:S(2)}, u32[]{:S(2)}) collective-permute-start(bf16[48,2304]{1,0:T(8,128)(2,1)S(1)} %get-tuple-element.82), channel_id=1, source_target_pairs={{0,16},{16,32},{32,48},{48,64},{64,80},{80,96},{96,112},{112,0},{1... | collective-permute-start | bytes 663560 | tf_op jit(solution)/shard_map/ppermute | solution.py:34
  76.1 6.6 %collective-permute-start.9 = (bf16[48,2304]{1,0:T(8,128)(2,1)S(1)}, bf16[48,2304]{1,0:T(8,128)(2,1)S(1)}, u32[]{:S(2)}, u32[]{:S(2)}) collective-permute-start(bf16[48,2304]{1,0:T(8,128)(2,1)S(1)} %get-tuple-element.81), channel_id=1, source_target_pairs={{0,112},{16,0},{32,16},{48,32},{64,48},{80,64},{96,80},{112,96},{1... | collective-permute-start | bytes 663560 | tf_op jit(solution)/shard_map/ppermute | solution.py:34
  82.4 3.8 %copy-start.2 = (bf16[1024,128]{1,0:T(8,128)(2,1)S(1)}, bf16[1024,128]{1,0:T(8,128)(2,1)}, u32[]{:S(2)}) copy-start(bf16[1024,128]{1,0:T(8,128)(2,1)} %copy-done.1) | copy-start | bytes 786436
  82.8 8.8 %collective-permute-start.12 = (bf16[48,2304]{1,0:T(8,128)(2,1)S(1)}, bf16[48,2304]{1,0:T(8,128)(2,1)S(1)}, u32[]{:S(2)}, u32[]{:S(2)}) collective-permute-start(bf16[48,2304]{1,0:T(8,128)(2,1)S(1)} %get-tuple-element.56), channel_id=1, source_target_pairs={{0,16},{16,32},{32,48},{48,64},{64,80},{80,96},{96,112},{112,0},{1... | collective-permute-start | bytes 663560 | tf_op jit(solution)/shard_map/ppermute | solution.py:34
  83.2 8.4 %collective-permute-start.13 = (bf16[48,2304]{1,0:T(8,128)(2,1)S(1)}, bf16[48,2304]{1,0:T(8,128)(2,1)S(1)}, u32[]{:S(2)}, u32[]{:S(2)}) collective-permute-start(bf16[48,2304]{1,0:T(8,128)(2,1)S(1)} %get-tuple-element.57), channel_id=1, source_target_pairs={{0,112},{16,0},{32,16},{48,32},{64,48},{80,64},{96,80},{112,96},{1... | collective-permute-start | bytes 663560 | tf_op jit(solution)/shard_map/ppermute | solution.py:34
  91.7 7.5 %collective-permute-start.14 = (bf16[48,2304]{1,0:T(8,128)(2,1)S(1)}, bf16[48,2304]{1,0:T(8,128)(2,1)S(1)}, u32[]{:S(2)}, u32[]{:S(2)}) collective-permute-start(bf16[48,2304]{1,0:T(8,128)(2,1)S(1)} %convert_element_type.154), channel_id=1, source_target_pairs={{0,128},{16,144},{32,160},{48,176},{64,192},{80,208},{96,224},{112... | collective-permute-start | bytes 663560 | tf_op jit(solution)/shard_map/ppermute | solution.py:88
  94.1 15.6 %all-to-all-start.1 = ((bf16[4,512,256]{2,1,0:T(8,128)(2,1)}), bf16[4,512,256]{2,1,0:T(8,128)(2,1)}, u32[]{:S(2)}, u32[]{:S(2)}) async-start(bf16[4,512,256]{2,1,0:T(8,128)(2,1)} %bitcast.34), calls=%async_computation.1 | async-start | bytes 2097152 | tf_op jit(solution)/shard_map/all_to_all | solution.py:55
  99.4 7.2 %collective-permute-start.15 = (bf16[48,2304]{1,0:T(8,128)(2,1)S(1)}, bf16[48,2304]{1,0:T(8,128)(2,1)S(1)}, u32[]{:S(2)}, u32[]{:S(2)}) collective-permute-start(bf16[48,2304]{1,0:T(8,128)(2,1)S(1)} %pad_maximum_fusion.8.refs_0_), channel_id=1, source_target_pairs={{0,16},{16,32},{32,48},{48,64},{64,80},{80,96},{96,112},{112,0},{1... | collective-permute-start | bytes 663560 | tf_op jit(solution)/shard_map/ppermute | solution.py:34
  99.5 7.1 %collective-permute-start.16 = (bf16[48,2304]{1,0:T(8,128)(2,1)S(1)}, bf16[48,2304]{1,0:T(8,128)(2,1)S(1)}, u32[]{:S(2)}, u32[]{:S(2)}) collective-permute-start(bf16[48,2304]{1,0:T(8,128)(2,1)S(1)} %pad_maximum_fusion.8.refs_0_), channel_id=1, source_target_pairs={{0,112},{16,0},{32,16},{48,32},{64,48},{80,64},{96,80},{112,96},{1... | collective-permute-start | bytes 663560 | tf_op jit(solution)/shard_map/ppermute | solution.py:34
  102.8 8.5 %collective-permute-start.11 = (bf16[512,128]{1,0:T(8,128)(2,1)S(1)}, bf16[512,128]{1,0:T(8,128)(2,1)}, u32[]{:S(2)}, u32[]{:S(2)}) collective-permute-start(bf16[512,128]{1,0:T(8,128)(2,1)S(1)} %slice.329), channel_id=1, source_target_pairs={{0,1},{1,0},{2,3},{3,2},{4,5},{5,4},{6,7},{7,6},{8,9},{9,8},{10,11... | collective-permute-start | bytes 393224 | tf_op jit(solution)/shard_map/ppermute | solution.py:28
  106.6 11.0 %copy-start.3 = (bf16[48,2304]{1,0:T(8,128)(2,1)}, bf16[48,2304]{1,0:T(8,128)(2,1)S(1)}, u32[]{:S(2)}) copy-start(bf16[48,2304]{1,0:T(8,128)(2,1)S(1)} %collective-permute-done.16.refs_1_) | copy-start | bytes 663556
  111.2 6.4 %collective-permute-start.17 = (bf16[256,256]{1,0:T(8,128)(2,1)S(1)}, bf16[256,256]{1,0:T(8,128)(2,1)S(1)}, u32[]{:S(2)}, u32[]{:S(2)}) collective-permute-start(bf16[256,256]{1,0:T(8,128)(2,1)S(1)} %slice.328), channel_id=1, source_target_pairs={{0,16},{16,0},{32,48},{48,32},{64,80},{80,64},{96,112},{112,96},{1... | collective-permute-start | bytes 393224 | tf_op jit(solution)/shard_map/ppermute | solution.py:63
  111.3 9.5 %collective-permute-start.21 = (bf16[48,2304]{1,0:T(8,128)(2,1)S(1)}, bf16[48,2304]{1,0:T(8,128)(2,1)S(1)}, u32[]{:S(2)}, u32[]{:S(2)}) collective-permute-start(bf16[48,2304]{1,0:T(8,128)(2,1)S(1)} %collective-permute-done.16.refs_1_), channel_id=1, source_target_pairs={{0,112},{16,0},{32,16},{48,32},{64,48},{80,64},{96,80},{112,96},{1... | collective-permute-start | bytes 663560 | tf_op jit(solution)/shard_map/ppermute | solution.py:34
  113.3 9.4 %collective-permute-start.22 = (bf16[48,2304]{1,0:T(8,128)(2,1)S(1)}, bf16[48,2304]{1,0:T(8,128)(2,1)S(1)}, u32[]{:S(2)}, u32[]{:S(2)}) collective-permute-start(bf16[48,2304]{1,0:T(8,128)(2,1)S(1)} %collective-permute-done.15.refs_8_), channel_id=1, source_target_pairs={{0,16},{16,32},{32,48},{48,64},{64,80},{80,96},{96,112},{112,0},{1... | collective-permute-start | bytes 663560 | tf_op jit(solution)/shard_map/ppermute | solution.py:34
  118.3 6.5 %collective-permute-start.18 = (bf16[128,256]{1,0:T(8,128)(2,1)}, bf16[128,256]{1,0:T(8,128)(2,1)S(1)}, u32[]{:S(2)}, u32[]{:S(2)}) collective-permute-start(bf16[128,256]{1,0:T(8,128)(2,1)} %slice.330), channel_id=1, source_target_pairs={{0,128},{16,144},{32,160},{48,176},{64,192},{80,208},{96,224},{112... | collective-permute-start | bytes 196616 | tf_op jit(solution)/shard_map/ppermute | solution.py:63
  119.5 17.7 %copy-start.4 = (bf16[48,2304]{1,0:T(8,128)(2,1)S(1)}, bf16[48,2304]{1,0:T(8,128)(2,1)}, u32[]{:S(2)}) copy-start(bf16[48,2304]{1,0:T(8,128)(2,1)} %copy-done.3) | copy-start | bytes 663556
  122.7 6.5 %collective-permute-start.23 = (bf16[48,2304]{1,0:T(8,128)(2,1)S(1)}, bf16[48,2304]{1,0:T(8,128)(2,1)S(1)}, u32[]{:S(2)}, u32[]{:S(2)}) collective-permute-start(bf16[48,2304]{1,0:T(8,128)(2,1)S(1)} %collective-permute-done.21.refs_2_), channel_id=1, source_target_pairs={{0,112},{16,0},{32,16},{48,32},{64,48},{80,64},{96,80},{112,96},{1... | collective-permute-start | bytes 663560 | tf_op jit(solution)/shard_map/ppermute | solution.py:34
  124.0 7.1 %collective-permute-start.24 = (bf16[48,2304]{1,0:T(8,128)(2,1)S(1)}, bf16[48,2304]{1,0:T(8,128)(2,1)S(1)}, u32[]{:S(2)}, u32[]{:S(2)}) collective-permute-start(bf16[48,2304]{1,0:T(8,128)(2,1)S(1)} %collective-permute-done.22.refs_7_), channel_id=1, source_target_pairs={{0,16},{16,32},{32,48},{48,64},{64,80},{80,96},{96,112},{112,0},{1... | collective-permute-start | bytes 663560 | tf_op jit(solution)/shard_map/ppermute | solution.py:34
  124.8 9.8 %collective-permute-start.19 = (f32[64,256]{1,0:T(8,128)S(1)}, f32[64,256]{1,0:T(8,128)S(1)}, u32[]{:S(2)}, u32[]{:S(2)}) collective-permute-start(f32[64,256]{1,0:T(8,128)S(1)} %slice.260), channel_id=1, source_target_pairs={{0,32},{16,48},{32,0},{48,16},{64,96},{80,112},{96,64},{112,80},{1... | collective-permute-start | bytes 196616 | tf_op jit(solution)/shard_map/ppermute | solution.py:63
  131.2 6.0 %collective-permute-start.25 = (bf16[48,1152]{1,0:T(8,128)(2,1)S(1)}, bf16[48,1152]{1,0:T(8,128)(2,1)S(1)}, u32[]{:S(2)}, u32[]{:S(2)}) collective-permute-start(bf16[48,1152]{1,0:T(8,128)(2,1)S(1)} %slice.228), channel_id=1, source_target_pairs={{0,16},{16,32},{32,48},{48,64},{64,80},{80,96},{96,112},{112,0},{1... | collective-permute-start | bytes 331784 | tf_op jit(solution)/shard_map/ppermute | solution.py:34
  131.3 5.9 %collective-permute-start.26 = (bf16[48,1152]{1,0:T(8,128)(2,1)S(1)}, bf16[48,1152]{1,0:T(8,128)(2,1)S(1)}, u32[]{:S(2)}, u32[]{:S(2)}) collective-permute-start(bf16[48,1152]{1,0:T(8,128)(2,1)S(1)} %slice.229), channel_id=1, source_target_pairs={{0,112},{16,0},{32,16},{48,32},{64,48},{80,64},{96,80},{112,96},{1... | collective-permute-start | bytes 331784 | tf_op jit(solution)/shard_map/ppermute | solution.py:34
  137.7 4.4 %collective-permute-start.27 = (bf16[384,128]{1,0:T(8,128)(2,1)S(1)}, bf16[384,128]{1,0:T(8,128)(2,1)S(1)}, u32[]{:S(2)}, u32[]{:S(2)}) collective-permute-start(bf16[384,128]{1,0:T(8,128)(2,1)S(1)} %get-tuple-element.73), channel_id=1, source_target_pairs={{0,8},{8,0},{1,9},{9,1},{2,10},{10,2},{3,11},{11,3},{4,12},{12,4},... | collective-permute-start | bytes 294920 | tf_op jit(solution)/shard_map/ppermute | solution.py:426
  139.6 7.8 %collective-permute-start.20 = (f32[32,256]{1,0:T(8,128)S(1)}, f32[32,256]{1,0:T(8,128)S(1)}, u32[]{:S(2)}, u32[]{:S(2)}) collective-permute-start(f32[32,256]{1,0:T(8,128)S(1)} %slice.262), channel_id=1, source_target_pairs={{0,64},{16,80},{32,96},{48,112},{64,0},{80,16},{96,32},{112,48},{1... | collective-permute-start | bytes 98312 | tf_op jit(solution)/shard_map/ppermute | solution.py:63
  142.3 5.7 %collective-permute-start.28 = (bf16[1,4,48,128]{3,2,1,0:T(8,128)(2,1)S(1)}, bf16[1,4,48,128]{3,2,1,0:T(8,128)(2,1)S(1)}, u32[]{:S(2)}, u32[]{:S(2)}) collective-permute-start(bf16[1,4,48,128]{3,2,1,0:T(8,128)(2,1)S(1)} %get-tuple-element.109), channel_id=1, source_target_pairs={{0,4},{1,5},{2,6},{3,7},{4,0},{5,1},{6,2},{7,3},{8,12},{9,13},{10,... | collective-permute-start | bytes 147464 | tf_op jit(solution)/shard_map/ppermute | solution.py:72
  148.0 4.2 %collective-permute-start.29 = (bf16[2,2,48,128]{3,2,1,0:T(8,128)(2,1)S(1)}, bf16[2,2,48,128]{3,2,1,0:T(8,128)(2,1)S(1)}, u32[]{:S(2)}, u32[]{:S(2)}) collective-permute-start(bf16[2,2,48,128]{3,2,1,0:T(8,128)(2,1)S(1)} %get-tuple-element.107), channel_id=1, source_target_pairs={{0,2},{1,3},{2,0},{3,1},{4,6},{5,7},{6,4},{7,5},{8,10},{9,11},{10,... | collective-permute-start | bytes 147464 | tf_op jit(solution)/shard_map/ppermute | solution.py:72
  152.2 4.2 %collective-permute-start.30 = (bf16[4,1,48,128]{3,2,0,1:T(8,128)(2,1)S(1)}, bf16[4,1,48,128]{3,2,0,1:T(8,128)(2,1)S(1)}, u32[]{:S(2)}, u32[]{:S(2)}) collective-permute-start(bf16[4,1,48,128]{3,2,0,1:T(8,128)(2,1)S(1)} %get-tuple-element.105), channel_id=1, source_target_pairs={{0,1},{1,0},{2,3},{3,2},{4,5},{5,4},{6,7},{7,6},{8,9},{9,8},{10,11... | collective-permute-start | bytes 147464 | tf_op jit(solution)/shard_map/ppermute | solution.py:72
  154.3 2.1 %copy-start.12 = (pred[512,8,48]{0,2,1:T(8,128)(4,1)S(1)}, pred[512,8,48]{0,2,1:T(8,128)(4,1)}, u32[]{:S(2)}) copy-start(pred[512,8,48]{0,2,1:T(8,128)(4,1)} %fusion) | copy-start | bytes 589828
